TPU v7x, 128 devices: a whole 4x4x4 slice. The times are simulated.
128 devices in a mesh: seq: 16 (over y_hi, x, core), fsdp: 8 (over z, y_lo).
Axes of the slice: x: 4, y: 4 (y_hi: 2, y_lo: 2; y = y_hi * 2 + y_lo), z: 4, core: 2. Of those that a mesh axis runs over, the one named last changes fastest.
Arguments:
- input_token_index: int32 [2, 8, 1024], P(None, None, 'seq'), may hold values from 0 to 31999
- target_token_index: int32 [2, 8, 512], P(None, None, 'seq'), may hold values from 0 to 31999
- loss_position_index: int32 [2, 8, 512], replicated, may hold values from 0 to 63, as said below
- document_slot_index: int32 [2, 8, 1024], replicated, may hold values from 0 to 2, as said below
- row_used_length: int32 [2, 8], replicated, may hold values from 512 to 1024, as said below
- head_group_offsets: int32 [4], replicated, may hold values from 0 to 128, as said below
- embedding: float32 [32000, 2048], P('fsdp', 'seq'), may hold values from -6 to 6
- embedding_first_moment: float32 [32000, 2048], P('fsdp', 'seq'), may hold values from -2.3841858e-06 to 2.3841858e-06
- embedding_second_moment: float32 [32000, 2048], P('fsdp', 'seq'), may hold values from 2.9802322e-14 to 1.1920929e-13
- frozen_output_table: bfloat16 [32000, 2048], P('fsdp', 'seq')
- frozen_query_key_value_weight: bfloat16 [2048, 2560], P(('seq', 'fsdp')), may hold values from -0.125 to 0.125
- frozen_attention_output_weight: bfloat16 [2048, 2048], P(('seq', 'fsdp')), may hold values from -0.25 to 0.25
- frozen_gate_up_weight: bfloat16 [2048, 11264], P(('seq', 'fsdp')), may hold values from -0.125 to 0.125
- frozen_down_weight: bfloat16 [5632, 2048], P(('seq', 'fsdp')), may hold values from -0.078125 to 0.078125
- norm_gain_vectors: float32 [3, 2048], P(None, ('seq', 'fsdp')), as said below
- norm_gain_first_moment: float32 [3, 2048], P(None, ('seq', 'fsdp')), may hold values from -1.9073486e-05 to 1.9073486e-05
- norm_gain_second_moment: float32 [3, 2048], P(None, ('seq', 'fsdp')), may hold values from 1.9073486e-12 to 7.6293945e-12
- adapter_down_factors: float32 [32, 2048], P(None, ('seq', 'fsdp')), may hold values from -0.125 to 0.125
- adapter_up_factors: float32 [8, 4608], P(None, ('seq', 'fsdp')), may hold values from -1.5 to 1.5
- rank_side_statistics: float32 [8, 8, 8], replicated, as said below
- down_width_statistics: float32 [4, 2048], P(None, ('seq', 'fsdp')), may hold values from 2.3841857e-11 to 3.8146972e-10
- up_width_statistics: float32 [4608], P(('seq', 'fsdp')), may hold values from 2.3841858e-13 to 9.536743e-13
Outputs:
- document_loss_sum: float32 [], replicated
- document_total: float32 [], replicated
- global_gradient_norm: float32 [], replicated
- clipped_embedding_gradient: float32 [32000, 2048], P('fsdp', 'seq')
- updated_embedding_second_moment: float32 [32000, 2048], P('fsdp', 'seq')
- updated_embedding_table: float32 [32000, 2048], P('fsdp', 'seq')
- updated_gain_first_moment: float32 [3, 2048], P(None, ('seq', 'fsdp'))
- updated_gain_second_moment: float32 [3, 2048], P(None, ('seq', 'fsdp'))
- updated_norm_gains: float32 [3, 2048], P(None, ('seq', 'fsdp'))
- lora_a_grad: float32 [32, 2048], P(None, ('seq', 'fsdp'))
- lora_b_grad: float32 [8, 4608], P(None, ('seq', 'fsdp'))
- updated_rank_statistics: float32 [8, 8, 8], replicated
- updated_down_width_statistics: float32 [4, 2048], P(None, ('seq', 'fsdp'))
- updated_up_width_statistics: float32 [4608], P(('seq', 'fsdp'))
- updated_down_factors: float32 [32, 2048], P(None, ('seq', 'fsdp'))
- updated_up_factors: float32 [8, 4608], P(None, ('seq', 'fsdp'))
Inputs may be any that keep to these rules, and one draw needn't show every extreme that they name: `loss_position_index`: each block of 32 entries holds distinct increasing offsets. `document_slot_index`: ids never fall along a row; slots at or beyond the row's length have id 2. `row_used_length`: for every row index, one of the micro-batches uses all 1024 slots. `head_group_offsets`: half of the key-value heads have a nonzero offset, one of them exactly 128; the others 0. `norm_gain_vectors`: positive. `rank_side_statistics`: diagonal with positive diagonal.
All inputs are finite; a program needn't handle non-finite values.
Results may differ from a plain program's by a relative error of at most 0.02.
Values may be sent and summed in bfloat16 or wider, within the bound.
A program may use at most 384 MiB of HBM per device.

v0:
```python
import jax
import jax.numpy as jnp
from jax import lax
from jax.sharding import Mesh
from jax.sharding import PartitionSpec as P

STEP = 5
GROUP = 256
SEQ = ("seq_0", "seq_1", "seq_2")
SEQ_FSDP = ("seq_0", "seq_1", "seq_2", "fsdp_0", "fsdp_1")
FSDP = ("fsdp_0", "fsdp_1")


NORM_EPS = 1e-05
ADAPTER_SCALE = 2.0
ROPE_BASE = 10000.0
CLIP_MAX = 0.001
FIRST_DECAY = 0.5
SECOND_DECAY = 0.5
RATE_EMBED = 0.3
RATE_GAIN = 0.1
LEARN_RATE_DOWN = 0.1
LEARN_RATE_UP = 0.5
WEIGHT_DECAY = 0.01
ADAM_EPS = 1e-12
HIGHEST = lax.Precision.HIGHEST


def from_behind(block, axis, distance):
    devices = range(lax.axis_size(axis))
    route = [(i - distance, i) for i in devices if i - distance in devices]
    return lax.ppermute(block, axis, route)


def side_by_side(arrays, axis, dim, along):
    widths = [a.shape[along] for a in arrays]
    both = jnp.concatenate(arrays, axis=along)
    whole = lax.all_gather(both, axis, axis=dim, tiled=True)
    return tuple(jnp.split(whole, [sum(widths[:k]) for k in range(1, len(widths))], axis=along))


def in_order(pieces, dim):
    pieces = jnp.moveaxis(pieces, 0, dim)
    dims = pieces.shape
    return pieces.reshape(*dims[:dim], dims[dim] * dims[dim + 1], *dims[dim + 2 :])


def gather_together(arrays, axis, dims):
    vector = jnp.concatenate([a.reshape(-1) for a in arrays])
    lines, at, outs = (lax.all_gather(vector, axis), 0, [])
    for a, dim in zip(arrays, dims):
        pieces = lines[:, at : at + a.size].reshape(-1, *a.shape)
        outs.append(in_order(pieces, dim))
        at += a.size
    return tuple(outs)


def copy_for_each(shard, axis):
    count = lax.axis_size(axis)
    return lax.all_to_all(
        jnp.broadcast_to(shard[None], (count, *shard.shape)), axis, 0, 0, tiled=True
    )


def gathered_copies(shard, axis, dim):
    return in_order(copy_for_each(shard, axis), dim)


def all_in_one(shard, axis):
    leaves = jax.tree.leaves(shard)
    sequence = sorted(range(len(leaves)), key=lambda k: -leaves[k].size)
    width = (1, *leaves[sequence[0]].shape)[-1]
    lines = [
        jnp.pad(leaves[k].reshape(-1), (0, -leaves[k].size % width)).reshape(-1, width)
        for k in sequence
    ]
    both, at, found = (copy_for_each(jnp.concatenate(lines), axis), 0, {})
    for k, line in zip(sequence, lines):
        slab = both[:, at : at + len(line)].reshape(len(both), -1)
        found[k] = slab[:, : leaves[k].size].reshape(-1, *leaves[k].shape)
        at += len(line)
    numbers = iter(range(len(leaves)))
    return jax.tree.map(lambda _: found[next(numbers)], shard)


def joined_by_halves(pieces, combine):
    while len(jax.tree.leaves(pieces)[0]) > 1:
        pieces = jax.vmap(combine)(
            *(jax.tree.map(lambda part: part[side::2], pieces) for side in (0, 1))
        )
    return jax.tree.map(lambda part: part[0], pieces)


def combined_all(shard, axis, combine):
    pieces = all_in_one(shard, axis)
    return joined_by_halves(pieces, combine)


def split_up(shard, dim, count):
    dims = shard.shape
    pieces = shard.reshape(*dims[:dim], count, dims[dim] // count, *dims[dim + 1 :])
    return jnp.moveaxis(pieces, dim, 0)


def sum_together(arrays, axis, dims):
    count = lax.axis_size(axis)
    pieces = [split_up(a, dim, count) for a, dim in zip(arrays, dims)]
    lines = jnp.concatenate([b.reshape(count, -1) for b in pieces], axis=1)
    rows = max(16, -(-lines.shape[1] // 1024) * 8)
    lines = jnp.pad(lines, ((0, 0), (0, rows * 128 - lines.shape[1]))).reshape(-1, 128)
    vector, at, outs = (lax.psum_scatter(lines, axis, tiled=True).reshape(-1), 0, [])
    for b in pieces:
        part = b[0]
        outs.append(vector[at : at + part.size].reshape(part.shape))
        at += part.size
    return tuple(outs)


def over_axes(shard, axes):
    for axis in axes:
        shard = lax.psum(shard, axis)
    return shard


def contract_simple(left_op, right_op):
    return jnp.dot(left_op, right_op, preferred_element_type=jnp.float32)


def contract_transposed(left_op, right_op):
    return lax.dot_general(
        left_op, right_op, (((1,), (1,)), ((), ())), preferred_element_type=jnp.float32
    )


def contract_leading(left_op, right_op):
    return lax.dot_general(
        left_op, right_op, (((0,), (0,)), ((), ())), preferred_element_type=jnp.float32
    )


def norm_scale(values):
    return lax.rsqrt(jnp.mean(values * values, axis=-1, keepdims=True) + NORM_EPS)


def norm_back(values, gain, upstream):
    scale_of = norm_scale(values)
    scaled = gain * upstream
    inward = scale_of * scaled - values * scale_of**3 * jnp.mean(
        scaled * values, axis=-1, keepdims=True
    )
    return (inward, jnp.sum(upstream * values * scale_of, axis=0))


def rotate(values, places):
    half_dim = values.shape[-1] // 2
    freqs = ROPE_BASE ** (-2.0 * jnp.arange(half_dim).astype(jnp.float32) / values.shape[-1])
    angles = places[:, None] * freqs[None, :]
    cosine = jnp.cos(angles)[:, None, :]
    sine_of = jnp.sin(angles)[:, None, :]
    first_half = values[..., :half_dim]
    second_half = values[..., half_dim:]
    return jnp.concatenate(
        [first_half * cosine - second_half * sine_of, second_half * cosine + first_half * sine_of],
        -1,
    )


def score_mask(query_pos, key_pos, query_seg, key_seg, shifts):
    query_gid = (query_pos[None, :] + shifts[:, None]) // GROUP
    key_gid = (key_pos[None, :] + shifts[:, None]) // GROUP
    causal = (key_pos[None, :] <= query_pos[:, None])[None]
    same_seg = (query_seg[:, None] == key_seg[None, :])[None]
    return (causal & same_seg & (query_gid[:, :, None] == key_gid[:, None, :]))[:, None]


def layer_forward(
    x_start, segments, seq_at, shifts, frozen, down_factor_reduced, up_factor_reduced, gain_full
):
    (
        frozen_query_key_value_weight,
        frozen_attention_output_weight,
        frozen_gate_up_weight,
        frozen_down_weight,
    ) = frozen
    tokens_n, model_width_value = x_start.shape
    adapter_rank_value = down_factor_reduced.shape[0] // 4
    key_value_width = (frozen_query_key_value_weight.shape[1] - model_width_value) // 2
    kv_heads = shifts.shape[0]
    head_dim = key_value_width // kv_heads
    heads_n = model_width_value // head_dim
    query_pos = seq_at * tokens_n + jnp.arange(tokens_n)
    places = query_pos.astype(jnp.float32)
    normalized_rows = (x_start * norm_scale(x_start) * gain_full[0]).astype(jnp.bfloat16)
    adapter_input = contract_transposed(
        normalized_rows, down_factor_reduced[: 3 * adapter_rank_value]
    ).astype(jnp.bfloat16)
    adapter_output = jnp.concatenate(
        [
            contract_simple(
                adapter_input[:, :adapter_rank_value], up_factor_reduced[:, :model_width_value]
            ),
            contract_simple(
                adapter_input[:, adapter_rank_value : 2 * adapter_rank_value],
                up_factor_reduced[:, model_width_value : model_width_value + key_value_width],
            ),
            contract_simple(
                adapter_input[:, 2 * adapter_rank_value :],
                up_factor_reduced[
                    :, model_width_value + key_value_width : model_width_value + 2 * key_value_width
                ],
            ),
        ],
        1,
    )
    packed_rows = (
        contract_simple(normalized_rows, frozen_query_key_value_weight)
        + ADAPTER_SCALE * adapter_output
    )
    queries = rotate(
        packed_rows[:, :model_width_value].reshape(tokens_n, heads_n, head_dim), places
    ).astype(jnp.bfloat16)
    key_rows = rotate(
        packed_rows[:, model_width_value : model_width_value + key_value_width].reshape(
            tokens_n, kv_heads, head_dim
        ),
        places,
    ).astype(jnp.bfloat16)
    value_rows = packed_rows[:, model_width_value + key_value_width :].astype(jnp.bfloat16)
    local_kv = jnp.concatenate([key_rows.reshape(tokens_n, key_value_width), value_rows], 1)
    reach = GROUP // tokens_n
    earlier = [from_behind(local_kv, SEQ, distance) for distance in range(reach, 0, -1)]
    window_kv = jnp.concatenate(earlier + [local_kv], 0)
    window_len = window_kv.shape[0]
    key_pos = (seq_at - reach) * tokens_n + jnp.arange(window_len)
    padded_seg = jnp.concatenate([jnp.full((reach * tokens_n,), -1, segments.dtype), segments])
    key_seg = lax.dynamic_slice_in_dim(padded_seg, seq_at * tokens_n, window_len)
    query_seg = lax.dynamic_slice_in_dim(segments, seq_at * tokens_n, tokens_n)
    allowed = score_mask(query_pos, key_pos, query_seg, key_seg, shifts)
    grouped = queries.reshape(tokens_n, kv_heads, heads_n // kv_heads, head_dim)
    all_keys = window_kv[:, :key_value_width].reshape(window_len, kv_heads, head_dim)
    all_vals = window_kv[:, key_value_width:].reshape(window_len, kv_heads, head_dim)
    scores = (
        jnp.einsum("ihgd,jhd->hgij", grouped, all_keys, preferred_element_type=jnp.float32) * 0.125
    )
    scores = jnp.where(allowed, scores, -1e30)
    top_score = jnp.max(scores, axis=-1, keepdims=True)
    weights_exp = jnp.where(allowed, jnp.exp(scores - top_score), 0.0)
    totals = jnp.sum(weights_exp, axis=-1, keepdims=True)
    probs = (weights_exp / totals).astype(jnp.bfloat16)
    log_total = top_score + jnp.log(totals)
    attention_output = (
        jnp.einsum("hgij,jhd->ihgd", probs, all_vals, preferred_element_type=jnp.float32)
        .reshape(tokens_n, model_width_value)
        .astype(jnp.bfloat16)
    )
    adapter_middle = contract_transposed(
        attention_output, down_factor_reduced[3 * adapter_rank_value :]
    ).astype(jnp.bfloat16)
    x_mid = (
        x_start
        + contract_simple(attention_output, frozen_attention_output_weight)
        + ADAPTER_SCALE
        * contract_simple(
            adapter_middle, up_factor_reduced[:, model_width_value + 2 * key_value_width :]
        )
    )
    normed_two = (x_mid * norm_scale(x_mid) * gain_full[1]).astype(jnp.bfloat16)
    gate_up = contract_simple(normed_two, frozen_gate_up_weight)
    ff_width = gate_up.shape[1] // 2
    hidden = (jax.nn.silu(gate_up[:, :ff_width]) * gate_up[:, ff_width:]).astype(jnp.bfloat16)
    x_end = x_mid + contract_simple(hidden, frozen_down_weight)
    final_norm = (x_end * norm_scale(x_end) * gain_full[2]).astype(jnp.bfloat16)
    kept = (
        x_start,
        x_mid,
        x_end,
        normalized_rows,
        adapter_input,
        grouped,
        window_kv,
        allowed,
        log_total,
        attention_output,
        adapter_middle,
        normed_two,
        gate_up,
        hidden,
        places,
    )
    return (final_norm, kept)


def layer_backward(upstream, kept, frozen, down_factor_reduced, up_factor_reduced, gain_full):
    (
        x_start,
        x_mid,
        x_end,
        normalized_rows,
        adapter_input,
        grouped,
        window_kv,
        allowed,
        log_total,
        attention_output,
        adapter_middle,
        normed_two,
        gate_up,
        hidden,
        places,
    ) = kept
    (
        frozen_query_key_value_weight,
        frozen_attention_output_weight,
        frozen_gate_up_weight,
        frozen_down_weight,
    ) = frozen
    tokens_n, model_width_value = x_start.shape
    adapter_rank_value = down_factor_reduced.shape[0] // 4
    key_value_width = window_kv.shape[1] // 2
    kv_heads = grouped.shape[1]
    head_dim = grouped.shape[3]
    window_len = window_kv.shape[0]
    reach = window_len // tokens_n - 1
    d_end, gain_end = norm_back(x_end, gain_full[2], upstream)
    d_hidden = contract_transposed(d_end.astype(jnp.bfloat16), frozen_down_weight)
    ff_width = gate_up.shape[1] // 2
    gate_part = gate_up[:, :ff_width]
    up_part = gate_up[:, ff_width:]
    sigmoid_of = jax.nn.sigmoid(gate_part)
    d_gate = d_hidden * up_part * sigmoid_of * (1.0 + gate_part * (1.0 - sigmoid_of))
    d_up = d_hidden * gate_part * sigmoid_of
    d_gate_up = jnp.concatenate([d_gate, d_up], 1).astype(jnp.bfloat16)
    back_two, gain_mid = norm_back(
        x_mid, gain_full[1], contract_transposed(d_gate_up, frozen_gate_up_weight)
    )
    d_mid = d_end + back_two
    adapter_branch_gradient = d_mid.astype(jnp.bfloat16)
    up_factor_output = up_factor_reduced[:, model_width_value + 2 * key_value_width :]
    adapter_middle_gradient = (
        ADAPTER_SCALE * contract_transposed(adapter_branch_gradient, up_factor_output)
    ).astype(jnp.bfloat16)
    attention_output_gradient = (
        contract_transposed(adapter_branch_gradient, frozen_attention_output_weight)
        + contract_simple(adapter_middle_gradient, down_factor_reduced[3 * adapter_rank_value :])
    ).astype(jnp.bfloat16)
    up_factor_gradient_output = ADAPTER_SCALE * contract_leading(
        adapter_middle, adapter_branch_gradient
    )
    down_factor_gradient_output = contract_leading(adapter_middle_gradient, attention_output)
    all_keys = window_kv[:, :key_value_width].reshape(window_len, kv_heads, head_dim)
    all_vals = window_kv[:, key_value_width:].reshape(window_len, kv_heads, head_dim)
    scores = (
        jnp.einsum("ihgd,jhd->hgij", grouped, all_keys, preferred_element_type=jnp.float32) * 0.125
    )
    probs = jnp.where(allowed, jnp.exp(scores - log_total), 0.0)
    d_grouped = attention_output_gradient.reshape(tokens_n, kv_heads, -1, head_dim)
    d_probs = jnp.einsum("ihgd,jhd->hgij", d_grouped, all_vals, preferred_element_type=jnp.float32)
    d_vals = jnp.einsum(
        "hgij,ihgd->jhd", probs.astype(jnp.bfloat16), d_grouped, preferred_element_type=jnp.float32
    )
    d_scores = (
        0.125 * probs * (d_probs - jnp.sum(probs * d_probs, axis=-1, keepdims=True))
    ).astype(jnp.bfloat16)
    d_queries = jnp.einsum(
        "hgij,jhd->ihgd", d_scores, all_keys, preferred_element_type=jnp.float32
    ).reshape(tokens_n, -1, head_dim)
    d_keys = jnp.einsum("hgij,ihgd->jhd", d_scores, grouped, preferred_element_type=jnp.float32)
    d_window = jnp.concatenate(
        [d_keys.reshape(window_len, key_value_width), d_vals.reshape(window_len, key_value_width)],
        1,
    )
    d_kv = d_window[reach * tokens_n :]
    for distance in range(1, reach + 1):
        block = d_window[(reach - distance) * tokens_n : (reach - distance + 1) * tokens_n]
        d_kv = d_kv + from_behind(block.astype(jnp.bfloat16), SEQ, -distance).astype(block.dtype)
    packed_rows_gradient = jnp.concatenate(
        [
            rotate(d_queries, -places).reshape(tokens_n, model_width_value),
            rotate(
                d_kv[:, :key_value_width].reshape(tokens_n, kv_heads, head_dim), -places
            ).reshape(tokens_n, key_value_width),
            d_kv[:, key_value_width:],
        ],
        1,
    ).astype(jnp.bfloat16)
    adapter_input_gradient = (
        ADAPTER_SCALE
        * jnp.concatenate(
            [
                contract_transposed(
                    packed_rows_gradient[:, :model_width_value],
                    up_factor_reduced[:, :model_width_value],
                ),
                contract_transposed(
                    packed_rows_gradient[
                        :, model_width_value : model_width_value + key_value_width
                    ],
                    up_factor_reduced[:, model_width_value : model_width_value + key_value_width],
                ),
                contract_transposed(
                    packed_rows_gradient[:, model_width_value + key_value_width :],
                    up_factor_reduced[
                        :,
                        model_width_value
                        + key_value_width : model_width_value
                        + 2 * key_value_width,
                    ],
                ),
            ],
            1,
        )
    ).astype(jnp.bfloat16)
    up_factor_gradient_input = ADAPTER_SCALE * jnp.concatenate(
        [
            contract_leading(
                adapter_input[:, :adapter_rank_value], packed_rows_gradient[:, :model_width_value]
            ),
            contract_leading(
                adapter_input[:, adapter_rank_value : 2 * adapter_rank_value],
                packed_rows_gradient[:, model_width_value : model_width_value + key_value_width],
            ),
            contract_leading(
                adapter_input[:, 2 * adapter_rank_value :],
                packed_rows_gradient[:, model_width_value + key_value_width :],
            ),
        ],
        1,
    )
    down_factor_gradient_input = contract_leading(adapter_input_gradient, normalized_rows)
    back_one, gain_start = norm_back(
        x_start,
        gain_full[0],
        contract_transposed(packed_rows_gradient, frozen_query_key_value_weight)
        + contract_simple(adapter_input_gradient, down_factor_reduced[: 3 * adapter_rank_value]),
    )
    d_start = d_mid + back_one
    down_factor_gradient = jnp.concatenate(
        [down_factor_gradient_input, down_factor_gradient_output], 0
    )
    up_factor_gradient = jnp.concatenate([up_factor_gradient_input, up_factor_gradient_output], 1)
    grad_gain = jnp.stack([gain_start, gain_mid, gain_end])
    return (d_start, down_factor_gradient, up_factor_gradient, grad_gain)


def merge_stats(first_set, second_set):
    top_a, sum_a = first_set
    top_b, sum_b = second_set
    top_new = jnp.maximum(top_a, top_b)
    return (top_new, sum_a * jnp.exp(top_a - top_new) + sum_b * jnp.exp(top_b - top_new))


def adam_update(weight_vals, first_old, second_old, gradient, rate):
    first_new = FIRST_DECAY * first_old + (1.0 - FIRST_DECAY) * gradient
    second_new = SECOND_DECAY * second_old + (1.0 - SECOND_DECAY) * gradient * gradient
    first_hat = first_new / (1.0 - FIRST_DECAY**STEP)
    second_hat = second_new / (1.0 - SECOND_DECAY**STEP)
    step_vals = first_hat / (jnp.sqrt(second_hat) + ADAM_EPS) + WEIGHT_DECAY * weight_vals
    return (first_new, second_new, weight_vals - rate * step_vals)


def factor_onehot(columns, model_width_value, key_value_width):
    factor_id = (
        (columns >= model_width_value).astype(jnp.int32)
        + (columns >= model_width_value + key_value_width).astype(jnp.int32)
        + (columns >= model_width_value + 2 * key_value_width).astype(jnp.int32)
    )
    return (factor_id[None, :] == jnp.arange(4)[:, None]).astype(jnp.float32)


def shampoo_parts(down_factor_gradient, up_factor_gradient, onehot):
    left_three = down_factor_gradient.reshape(4, up_factor_gradient.shape[0], -1)
    stats_left = jnp.einsum("krd,ksd->krs", left_three, left_three, precision=HIGHEST)
    stats_right = jnp.einsum(
        "rc,sc,kc->krs", up_factor_gradient, up_factor_gradient, onehot, precision=HIGHEST
    )
    return jnp.concatenate([stats_left, stats_right], 0)


def inverse_root(stats):
    unit_mat = jnp.eye(stats.shape[-1], dtype=stats.dtype)[None]
    norm_of = jnp.sqrt(jnp.sum(stats * stats, axis=(1, 2), keepdims=True))
    matrix = stats / norm_of
    root_mat = unit_mat * lax.rsqrt(jnp.sqrt(norm_of))
    for iteration in range(10):
        factor = (5.0 * unit_mat - matrix) * 0.25
        root_mat = jnp.einsum("kab,kbc->kac", root_mat, factor, precision=HIGHEST)
        square = jnp.einsum("kab,kbc->kac", factor, factor, precision=HIGHEST)
        fourth = jnp.einsum("kab,kbc->kac", square, square, precision=HIGHEST)
        matrix = jnp.einsum("kab,kbc->kac", fourth, matrix, precision=HIGHEST)
    return root_mat


def shampoo_apply(
    stats_new, width_left, width_right, down_factor_gradient, up_factor_gradient, onehot
):
    roots = inverse_root(stats_new)
    left_three = down_factor_gradient.reshape(4, up_factor_gradient.shape[0], -1)
    down_factor_step = (
        jnp.einsum("krs,ksd->krd", roots[:4], left_three, precision=HIGHEST)
        * lax.rsqrt(jnp.sqrt(width_left))[:, None, :]
    )
    up_factor_step = (
        jnp.einsum("krs,sc,kc->rc", roots[4:], up_factor_gradient, onehot, precision=HIGHEST)
        * lax.rsqrt(jnp.sqrt(width_right))[None, :]
    )
    return (down_factor_step.reshape(down_factor_gradient.shape), up_factor_step)


def per_device(
    input_token_index,
    target_token_index,
    loss_position_index,
    document_slot_index,
    row_used_length,
    head_group_offsets,
    embedding,
    embedding_first_moment,
    embedding_second_moment,
    frozen_output_table,
    frozen_query_key_value_weight,
    frozen_attention_output_weight,
    frozen_gate_up_weight,
    frozen_down_weight,
    norm_gain_vectors,
    norm_gain_first_moment,
    norm_gain_second_moment,
    adapter_down_factors,
    adapter_up_factors,
    rank_side_statistics,
    down_width_statistics,
    up_width_statistics,
):
    frozen = (
        *side_by_side(
            (frozen_query_key_value_weight, frozen_attention_output_weight, frozen_gate_up_weight),
            SEQ_FSDP,
            0,
            1,
        ),
        lax.all_gather(frozen_down_weight, SEQ_FSDP, axis=0, tiled=True),
    )
    left_full, right_full, gain_full = gather_together(
        (adapter_down_factors, adapter_up_factors, norm_gain_vectors), SEQ_FSDP, (1, 1, 1)
    )
    down_factor_reduced = left_full.astype(jnp.bfloat16)
    up_factor_reduced = right_full.astype(jnp.bfloat16)
    table_low, head_full = side_by_side(
        (embedding.astype(jnp.bfloat16), frozen_output_table), SEQ, 1, 0
    )
    fsdp_at = lax.axis_index(FSDP)
    seq_at = lax.axis_index(SEQ)
    micro_n, rows_n, tokens_n = input_token_index.shape
    vocab_dev, model_width_value = table_low.shape
    loss_dev = target_token_index.shape[2]
    blocks = jnp.arange(loss_position_index.shape[2]) // loss_dev
    spot_rows = blocks * tokens_n + loss_position_index
    counted = spot_rows < row_used_length[..., None]
    seg_at = jnp.take_along_axis(document_slot_index, spot_rows, axis=2)
    member = seg_at[..., None] == jnp.arange(3)
    counts = jnp.sum((counted[..., None] & member).astype(jnp.int32), axis=2)
    document_total = jnp.sum((counts > 0).astype(jnp.float32))
    per_doc = jnp.sum(jnp.where(member, counts[:, :, None, :], 0), axis=-1)
    doc_weight = jnp.where(counted, 1.0 / jnp.maximum(per_doc, 1).astype(jnp.float32), 0.0)
    own_weight = lax.dynamic_slice_in_dim(doc_weight, seq_at * loss_dev, loss_dev, 2)
    own_spots = lax.dynamic_slice_in_dim(loss_position_index, seq_at * loss_dev, loss_dev, 2)
    local_ids = input_token_index - fsdp_at * vocab_dev
    inside = (local_ids >= 0) & (local_ids < vocab_dev)
    looked = jnp.take(table_low, jnp.where(inside, local_ids, 0), axis=0) * inside[
        ..., None
    ].astype(jnp.bfloat16)
    x_starts = lax.psum_scatter(
        looked.astype(jnp.float32).astype(jnp.bfloat16), FSDP, scatter_dimension=1, tiled=True
    ).astype(jnp.float32)[:, 0]
    own_segments = lax.dynamic_index_in_dim(document_slot_index, fsdp_at, 1, keepdims=False)
    finals = []
    keeps = []
    for micro_at in range(micro_n):
        final_norm, kept = layer_forward(
            x_starts[micro_at],
            own_segments[micro_at],
            seq_at,
            head_group_offsets,
            frozen,
            down_factor_reduced,
            up_factor_reduced,
            gain_full,
        )
        finals.append(final_norm)
        keeps.append(kept)
    own_rows = lax.dynamic_index_in_dim(own_spots, fsdp_at, 1, keepdims=False)
    chosen = jnp.stack(
        [jnp.take(finals[micro_at], own_rows[micro_at], axis=0) for micro_at in range(micro_n)]
    )
    gathered = gathered_copies(chosen[:, None], FSDP, 1)
    flat_rows = gathered.reshape(-1, model_width_value)
    logits = contract_transposed(flat_rows, head_full)
    local_target = target_token_index.reshape(-1) - fsdp_at * vocab_dev
    is_target = jnp.arange(vocab_dev)[None, :] == local_target[:, None]
    top_local = jnp.max(logits, axis=1)
    exp_local = jnp.sum(jnp.exp(logits - top_local[:, None]), axis=1)
    target_local = jnp.sum(jnp.where(is_target, logits, 0.0), axis=1)
    top_all, exp_all = combined_all((top_local, exp_local), FSDP, merge_stats)
    log_norm = top_all + jnp.log(exp_all)
    weight_flat = own_weight.reshape(-1)
    peer_of = jnp.arange(weight_flat.shape[0]) // loss_dev % rows_n
    loss_part = jnp.sum(jnp.where(peer_of == fsdp_at, log_norm * weight_flat, 0.0)) - jnp.sum(
        weight_flat * target_local
    )
    d_logits = (
        (weight_flat / document_total)[:, None]
        * (jnp.exp(logits - log_norm[:, None]) - is_target.astype(jnp.float32))
    ).astype(jnp.bfloat16)
    d_rows = lax.psum_scatter(
        contract_simple(d_logits, head_full)
        .reshape(micro_n, rows_n, loss_dev, model_width_value)
        .astype(jnp.bfloat16),
        FSDP,
        scatter_dimension=1,
        tiled=True,
    ).astype(jnp.float32)[:, 0]
    back_frozen = (
        *side_by_side(
            (frozen_query_key_value_weight, frozen_attention_output_weight, frozen_gate_up_weight),
            SEQ_FSDP,
            0,
            1,
        ),
        lax.all_gather(frozen_down_weight, SEQ_FSDP, axis=0, tiled=True),
    )
    acc_left = jnp.zeros(left_full.shape, jnp.float32)
    acc_right = jnp.zeros(right_full.shape, jnp.float32)
    acc_gain = jnp.zeros(gain_full.shape, jnp.float32)
    d_starts = [None] * micro_n
    for micro_at in reversed(range(micro_n)):
        upstream = (
            jnp.zeros((tokens_n, model_width_value), jnp.float32)
            .at[own_rows[micro_at]]
            .add(d_rows[micro_at])
        )
        d_start, down_factor_gradient, up_factor_gradient, grad_gain = layer_backward(
            upstream,
            keeps[micro_at],
            back_frozen,
            down_factor_reduced,
            up_factor_reduced,
            gain_full,
        )
        d_starts[micro_at] = d_start
        acc_left = acc_left + down_factor_gradient
        acc_right = acc_right + up_factor_gradient
        acc_gain = acc_gain + grad_gain
    d_gathered = lax.all_gather(
        jnp.stack(d_starts)[:, None].astype(jnp.bfloat16), FSDP, axis=1, tiled=True
    ).astype(jnp.float32)
    embed_part = (
        jnp.zeros((vocab_dev, model_width_value), jnp.float32)
        .at[jnp.where(inside, local_ids, vocab_dev)]
        .add(d_gathered, mode="drop")
    )
    grad_embed = lax.psum_scatter(
        embed_part.astype(jnp.bfloat16), SEQ, scatter_dimension=1, tiled=True
    ).astype(jnp.float32)
    down_factor_gradient, up_factor_gradient, grad_gain = sum_together(
        (acc_left, acc_right, acc_gain), SEQ_FSDP, (1, 1, 1)
    )
    shard_cols = up_factor_gradient.shape[1]
    columns = lax.axis_index(SEQ_FSDP) * shard_cols + jnp.arange(shard_cols)
    onehot = factor_onehot(
        columns, model_width_value, (right_full.shape[1] - 2 * model_width_value) // 2
    )
    stats_part = shampoo_parts(down_factor_gradient, up_factor_gradient, onehot)
    squares = (
        jnp.sum(grad_embed * grad_embed)
        + jnp.sum(grad_gain * grad_gain)
        + jnp.sum(down_factor_gradient * down_factor_gradient)
        + jnp.sum(up_factor_gradient * up_factor_gradient)
    )
    squares_all, document_loss_sum, stats_all = (
        over_axes(squares, SEQ_FSDP),
        over_axes(loss_part, SEQ_FSDP),
        over_axes(stats_part, SEQ_FSDP),
    )
    global_gradient_norm = jnp.sqrt(squares_all)
    clip_factor = CLIP_MAX / jnp.maximum(global_gradient_norm, CLIP_MAX)
    grad_embed = grad_embed * clip_factor
    grad_gain = grad_gain * clip_factor
    down_factor_gradient = down_factor_gradient * clip_factor
    up_factor_gradient = up_factor_gradient * clip_factor
    unused_first, updated_embedding_second_moment, updated_embedding_table = adam_update(
        embedding, embedding_first_moment, embedding_second_moment, grad_embed, RATE_EMBED
    )
    updated_gain_first_moment, updated_gain_second_moment, updated_norm_gains = adam_update(
        norm_gain_vectors, norm_gain_first_moment, norm_gain_second_moment, grad_gain, RATE_GAIN
    )
    adapter_rank_value = up_factor_gradient.shape[0]
    updated_rank_statistics = (
        SECOND_DECAY * rank_side_statistics
        + (1.0 - SECOND_DECAY) * (clip_factor * clip_factor) * stats_all
    )
    updated_down_width_statistics = SECOND_DECAY * down_width_statistics + (
        1.0 - SECOND_DECAY
    ) * jnp.sum(down_factor_gradient.reshape(4, adapter_rank_value, -1) ** 2, axis=1)
    updated_up_width_statistics = SECOND_DECAY * up_width_statistics + (
        1.0 - SECOND_DECAY
    ) * jnp.sum(up_factor_gradient * up_factor_gradient, axis=0)
    down_factor_step, up_factor_step = shampoo_apply(
        updated_rank_statistics,
        updated_down_width_statistics,
        updated_up_width_statistics,
        down_factor_gradient,
        up_factor_gradient,
        onehot,
    )
    updated_down_factors = adapter_down_factors - LEARN_RATE_DOWN * down_factor_step
    updated_up_factors = adapter_up_factors - LEARN_RATE_UP * up_factor_step
    return (
        document_loss_sum,
        document_total,
        global_gradient_norm,
        grad_embed,
        updated_embedding_second_moment,
        updated_embedding_table,
        updated_gain_first_moment,
        updated_gain_second_moment,
        updated_norm_gains,
        down_factor_gradient,
        up_factor_gradient,
        updated_rank_statistics,
        updated_down_width_statistics,
        updated_up_width_statistics,
        updated_down_factors,
        updated_up_factors,
    )


def solution(mesh):
    torus = Mesh(
        mesh.devices.reshape(2, 4, 2, 4, 2), ("seq_0", "seq_1", "seq_2", "fsdp_0", "fsdp_1")
    )
    return jax.shard_map(
        per_device,
        mesh=torus,
        in_specs=(
            P(None, None, SEQ),
            P(None, None, SEQ),
            P(),
            P(),
            P(),
            P(),
            P(FSDP, SEQ),
            P(FSDP, SEQ),
            P(FSDP, SEQ),
            P(FSDP, SEQ),
            P(SEQ_FSDP, None),
            P(SEQ_FSDP, None),
            P(SEQ_FSDP, None),
            P(SEQ_FSDP, None),
            P(None, SEQ_FSDP),
            P(None, SEQ_FSDP),
            P(None, SEQ_FSDP),
            P(None, SEQ_FSDP),
            P(None, SEQ_FSDP),
            P(),
            P(None, SEQ_FSDP),
            P(SEQ_FSDP),
        ),
        out_specs=(
            P(),
            P(),
            P(),
            P(FSDP, SEQ),
            P(FSDP, SEQ),
            P(FSDP, SEQ),
            P(None, SEQ_FSDP),
            P(None, SEQ_FSDP),
            P(None, SEQ_FSDP),
            P(None, SEQ_FSDP),
            P(None, SEQ_FSDP),
            P(),
            P(None, SEQ_FSDP),
            P(SEQ_FSDP),
            P(None, SEQ_FSDP),
            P(None, SEQ_FSDP),
        ),
        check_vma=False,
    )
```

profile of v0, /device:TPU:1, one launch (start us, length us, event | category | flops | bytes accessed | tf_op | source)
XLA Modules:
  0.0 2584.0 jit_solution(3367365304543782120)
XLA Ops:
  13.7 208.2 %all-gather.7.cloned.1.call-done = bf16[8000,2048]{1,0:T(8,128)(2,1)} async-done(((bf16[8000,128]{1,0:T(8,128)(2,1)}), bf16[8000,2048]{1,0:T(8,128)(2,1)}) %all-gather.7.cloned.1.call-update) | async-done | bytes 32768016 | tf_op jit(solution)/shard_map/all_gather | solution.py:38
  221.9 13.7 split.23
  235.6 16.8 gather_fusion
  264.1 50.8 %all-reduce.15.cloned.1.call-done = f32[108544]{0:T(1024)} async-done(((f32[108544]{0:T(1024)}), f32[108544]{0:T(1024)}) %all-reduce.15.cloned.1.call-update) | async-done | bytes 434192
  320.1 369.3 %all-gather.13.cloned.1.call-done = bf16[128,44,2048]{2,1,0:T(8,128)(2,1)} async-done(((bf16[1,44,2048]{2,1,0:T(8,128)(2,1)}), bf16[128,44,2048]{2,1,0:T(8,128)(2,1)}) %all-gather.13.cloned.1.call-update) | async-done | bytes 23068688 | tf_op jit(solution)/shard_map/all_gather | solution.py:540
  689.4 27.7 %reshape.1017 = bf16[5632,2048]{1,0:T(8,128)(2,1)} reshape(bf16[128,44,2048]{2,1,0:T(8,128)(2,1)} %all-gather.13.cloned.1.call-done) | data formatting | bytes 46137344
  723.6 357.5 %all-gather.9.cloned.1.call-done = bf16[2048,15872]{1,0:T(8,128)(2,1)} async-done(((bf16[16,15872]{1,0:T(8,128)(2,1)}), bf16[2048,15872]{1,0:T(8,128)(2,1)}) %all-gather.9.cloned.1.call-update) | async-done | bytes 65011728 | tf_op jit(solution)/shard_map/all_gather | solution.py:38
  1152.5 16.7 fusion.4
  1169.3 10.9 multiply_reduce_fusion.12
  1191.2 18.1 fusion.6
  1209.4 10.9 multiply_reduce_fusion.15
  1235.5 63.4 %gather_fusion.1 = s32[8192]{0:T(1024)S(1)} fusion(s32[2,8,1024]{2,1,0:T(8,128)S(1)} %copy-done, s32[8192]{0:T(1024)S(1)} %bitcast.407), kind=kCustom, calls=%fused_computation.3 | custom fusion | bytes 163840 | tf_op jit(solution)/shard_map/jit(take_along_axis)/gather | solution.py:558
  1302.5 12.5 fusion.363
  1332.0 15.9 fusion.50
  1349.2 112.7 %all-reduce.19.cloned.1.call-done = bf16[2,8,32,2048]{3,2,1,0:T(8,128)(2,1)} async-done(((bf16[2,8,32,2048]{3,2,1,0:T(8,128)(2,1)}), bf16[2,8,32,2048]{3,2,1,0:T(8,128)(2,1)}) %all-reduce.19.cloned.1.call-update) | async-done | bytes 2097168
  1470.7 13.9 multiply_convert_fusion.7
  1484.7 21.4 multiply_reduce_fusion.1
  1525.6 12.3 multiply_convert_fusion.5
  1537.8 20.2 multiply_reduce_fusion.4
  1559.4 6.2 fusion.23
  1590.6 6.3 collective-permute-done.15
  1634.4 77.1 %all-gather.11.cloned.1.call-done = bf16[2,8,64,2048]{3,2,1,0:T(8,128)(2,1)} async-done(((bf16[2,1,64,2048]{3,2,1,0:T(8,128)(2,1)}), bf16[2,8,64,2048]{3,2,1,0:T(8,128)(2,1)}) %all-gather.11.cloned.1.call-update) | async-done | bytes 4194320 | tf_op jit(solution)/shard_map/all_gather | solution.py:652
  1711.5 27.6 %scatter_custom_fusion.2 = f32[4000,2048]{1,0:T(8,128)} fusion(s32[1024]{0:T(1024)S(1)} %reshape.996, f32[]{:T(128)} %constant.237.clone.1, bf16[1024,2048]{1,0:T(8,128)(2,1)} %bitcast.430), kind=kCustom, calls=%fused_computation.15 | custom fusion | flops 4194304 | bytes 36962308 | tf_op jit(solution)/shard_map/scatter-add | solution.py:658
  1739.1 17.3 convert_element_type.348
  1756.4 21.1 copy.299
  1778.7 557.8 %reduce-scatter.11.cloned.1.call-done = f32[16,128]{1,0:T(8,128)} async-done(((f32[2048,128]{1,0:T(8,128)}), f32[16,128]{1,0:T(8,128)}) %reduce-scatter.11.cloned.1.call-update) | async-done | bytes 8208 | tf_op jit(solution)/shard_map/reduce_scatter | solution.py:111
  2341.0 155.5 %reduce-scatter.13.cloned.1.call-done = bf16[128,4000]{1,0:T(8,128)(2,1)} async-done(((bf16[2048,4000]{1,0:T(8,128)(2,1)}), bf16[128,4000]{1,0:T(8,128)(2,1)}) %reduce-scatter.13.cloned.1.call-update) | async-done | bytes 1024016
  2502.4 7.4 all-reduce.10
  2509.9 13.0 all-reduce.7
  2522.9 11.6 all-reduce.9
  2534.5 14.8 all-reduce.6
  2549.3 7.5 all-reduce.8
  (703 shorter events, 263.9 us)
Async XLA Ops:
  8.0 213.9 %all-gather.7.cloned.1.call-start = ((), (), s32[]{:S(2)}) async-start(), calls=%async_computation.4 | async-start | bytes 34816000 | tf_op jit(solution)/shard_map/all_gather | solution.py:38
  11.3 303.6 %all-reduce.15.cloned.1.call-start = ((), (), s32[]{:S(2)}) async-start(), calls=%async_computation.8 | async-start | bytes 868352
  12.8 676.7 %all-gather.13.cloned.1.call-start = ((), (), s32[]{:S(2)}) async-start(), calls=%async_computation.9 | async-start | bytes 25362432 | tf_op jit(solution)/shard_map/all_gather | solution.py:540
  13.5 703.6 %all-reduce.17.cloned.1.call-start = ((), (), s32[]{:S(2)}) async-start(), calls=%async_computation.11 | async-start | bytes 8388608
  256.3 824.9 %all-gather.9.cloned.1.call-start = ((), (), s32[]{:S(2)}) async-start(), calls=%async_computation.5 | async-start | bytes 65519616 | tf_op jit(solution)/shard_map/all_gather | solution.py:38
  259.0 834.7 %copy-start.72 = (f32[64,32]{1,0:T(8,128)}, f32[64,32]{1,0:T(8,128)S(1)}, u32[]{:S(2)}) copy-start(f32[64,32]{1,0:T(8,128)S(1)} %copy.245) | copy-start | bytes 24580
  264.1 879.9 %copy-start.36 = (pred[4,64,320]{2,1,0:T(8,128)(4,1)}, pred[4,64,320]{2,1,0:T(8,128)(4,1)S(1)}, u32[]{:S(2)}) copy-start(pred[4,64,320]{2,1,0:T(8,128)(4,1)S(1)} %get-tuple-element.221) | copy-start | bytes 245764
  264.1 918.8 %copy-start.38 = (pred[4,64,320]{2,1,0:T(8,128)(4,1)}, pred[4,64,320]{2,1,0:T(8,128)(4,1)S(1)}, u32[]{:S(2)}) copy-start(pred[4,64,320]{2,1,0:T(8,128)(4,1)S(1)} %get-tuple-element.220) | copy-start | bytes 245764
  317.9 872.3 %copy-start.54 = (bf16[8,4608]{1,0:T(8,128)(2,1)}, bf16[8,4608]{1,0:T(8,128)(2,1)S(1)}, u32[]{:S(2)}) copy-start(bf16[8,4608]{1,0:T(8,128)(2,1)S(1)} %convert_element_type.294) | copy-start | bytes 221188
  318.5 1197.2 %copy-start.63 = (bf16[8,2048]{1,0:T(8,128)(2,1)}, bf16[8,2048]{1,0:T(8,128)(2,1)S(1)}, u32[]{:S(2)}) copy-start(bf16[8,2048]{1,0:T(8,128)(2,1)S(1)} %slice.385) | copy-start | bytes 98308
  1094.9 45.7 %collective-permute-start.7 = (bf16[64,512]{1,0:T(8,128)(2,1)}, bf16[64,512]{1,0:T(8,128)(2,1)}, u32[]{:S(2)}, u32[]{:S(2)}) collective-permute-start(bf16[64,512]{1,0:T(8,128)(2,1)} %pad_maximum_fusion.18), channel_id=1, source_target_pairs={{0,8},{8,16},{16,24},{24,32},{32,40},{40,48},{48,56},{56,64},{64,7... | collective-permute-start | bytes 196616 | tf_op jit(solution)/shard_map/ppermute | solution.py:32
  1097.3 42.4 %collective-permute-start.6 = (bf16[64,512]{1,0:T(8,128)(2,1)}, bf16[64,512]{1,0:T(8,128)(2,1)}, u32[]{:S(2)}, u32[]{:S(2)}) collective-permute-start(bf16[64,512]{1,0:T(8,128)(2,1)} %pad_maximum_fusion.18), channel_id=1, source_target_pairs={{0,16},{8,24},{16,32},{24,40},{32,48},{40,56},{48,64},{56,72},{64,... | collective-permute-start | bytes 196616 | tf_op jit(solution)/shard_map/ppermute | solution.py:32
  1101.0 37.9 %collective-permute-start.5 = (bf16[64,512]{1,0:T(8,128)(2,1)}, bf16[64,512]{1,0:T(8,128)(2,1)}, u32[]{:S(2)}, u32[]{:S(2)}) collective-permute-start(bf16[64,512]{1,0:T(8,128)(2,1)} %pad_maximum_fusion.18), channel_id=1, source_target_pairs={{0,24},{8,32},{16,40},{24,48},{32,56},{40,64},{48,72},{56,80},{64,... | collective-permute-start | bytes 196616 | tf_op jit(solution)/shard_map/ppermute | solution.py:32
  1105.4 32.6 %collective-permute-start.4 = (bf16[64,512]{1,0:T(8,128)(2,1)}, bf16[64,512]{1,0:T(8,128)(2,1)}, u32[]{:S(2)}, u32[]{:S(2)}) collective-permute-start(bf16[64,512]{1,0:T(8,128)(2,1)} %pad_maximum_fusion.18), channel_id=1, source_target_pairs={{0,32},{8,40},{16,48},{24,56},{32,64},{40,72},{48,80},{56,88},{64,... | collective-permute-start | bytes 196616 | tf_op jit(solution)/shard_map/ppermute | solution.py:32
  1111.8 9.4 collective-permute-start
  1121.2 3.6 collective-permute-start.1
  1124.9 4.9 collective-permute-start.2
  1129.7 6.6 collective-permute-start.3
  1231.0 68.3 %all-to-all-start = ((bf16[8,2,1,32,2048]{4,3,1,2,0:T(8,128)(2,1)}), bf16[8,2,1,32,2048]{4,3,1,2,0:T(8,128)(2,1)}, u32[]{:S(2)}, u32[]{:S(2)}) async-start(bf16[8,2,1,32,2048]{4,3,1,2,0:T(8,128)(2,1)} %broadcast_in_dim.102), calls=%async_computation | async-start | bytes 4194304 | tf_op jit(solution)/shard_map/all_to_all | solution.py:60
  1318.8 10.1 all-to-all-start.1
  1323.8 138.1 %all-reduce.19.cloned.1.call-start = ((), (), s32[]{:S(2)}) async-start(), calls=%async_computation.12 | async-start | bytes 4194304
  1347.9 363.6 %all-gather.11.cloned.1.call-start = ((), (), s32[]{:S(2)}) async-start(), calls=%async_computation.6 | async-start | bytes 4718592 | tf_op jit(solution)/shard_map/all_gather | solution.py:652
  1575.7 10.5 collective-permute-start.8
  1579.0 8.8 collective-permute-start.11
  1580.3 8.8 collective-permute-start.10
  1581.6 8.8 collective-permute-start.9
  1583.9 6.7 collective-permute-start.12
  1586.2 10.7 collective-permute-start.15
  1587.7 10.3 collective-permute-start.14
  1589.0 9.0 collective-permute-start.13
  1613.9 722.7 %reduce-scatter.11.cloned.1.call-start = ((), (), s32[]{:S(2)}) async-start(), calls=%async_computation.7 | async-start | bytes 1056768 | tf_op jit(solution)/shard_map/reduce_scatter | solution.py:111
  1633.9 862.7 %reduce-scatter.13.cloned.1.call-start = ((), (), s32[]{:S(2)}) async-start(), calls=%async_computation.10 | async-start | bytes 17825792
  (153 other events, 6353.3 us)
Sparse Core Ops, SparseCore 0:
  11.9 209.9 all-gather.6
  223.7 465.6 all-gather.12
  691.2 389.8 all-gather.8
Sparse Core Ops, SparseCore 1:
  17.2 297.7 all-reduce.14
  317.5 188.7 all-reduce.16
  1348.0 113.9 all-reduce.18
  1613.9 97.5 all-gather.10
  1714.5 621.9 reduce-scatter.10
  2340.9 155.6 reduce-scatter.12
where the time goes:
time: 2600 us; the launch traced here: 2580 us
  waiting for transfers between devices  1910 us (73%)
  matrix products  241 us (9%)
  local copies, waits for them, and re-layouts  197 us (8%)
  other arithmetic  109 us (4%)
  blocking collectives  54.4 us (2%)
  starting transfers between devices  53.4 us (2%)
    all_gather x2, waiting for transfers between devices, side_by_side(): whole = lax.all_gather(both, axis, axis=dim, tiled=True)  566 us
    reduce_scatter x1, waiting for transfers between devices, sum_together(): lax.psum_scatter(lines, axis, tiled=True).reshape(-1)  558 us
    all_gather x1, waiting for transfers between devices, per_device(): lax.all_gather(frozen_down_weight, SEQ_FSDP, axis=0, tiled=True)  369 us
    unnamed x13, waiting for transfers between devices  320 us
    dot_general x21, matrix products, contract_transposed(): lax.dot_general(left_op, right_op, (((1,), (1,)), ((), ())), preferred_el...  108 us
    dot_general x21, matrix products, contract_simple(): return jnp.dot(left_op, right_op, preferred_element_type=jnp.float32)  100 us
    all_gather x1, waiting for transfers between devices, per_device(): lax.all_gather(jnp.stack(d_starts)[:, None].astype(jnp.bfloat16), FSDP, a...  77.1 us
    gather x2, local copies, waits for them, and re-layouts, per_device(): seg_at = jnp.take_along_axis(document_slot_index, spot_rows, axis=2)  63.4 us
  transfers between devices with their start and end apart: 27, of which 15 were waited for; matrix products, arithmetic and copies ran while one was open for 10% of the time, Pallas kernels for 0%

commit v1 on v0

v1 whole, which is shorter than its diff:
```python
import functools

import jax
import jax.numpy as jnp
from jax import lax
from jax.experimental import pallas as pl
from jax.experimental.pallas import tpu as pltpu
from jax.sharding import Mesh
from jax.sharding import PartitionSpec as P

STEP = 5
GROUP = 256
SEQ = ("seq_0", "seq_1", "seq_2")
FSDP = ("fsdp_0", "fsdp_1")
SEQ_FSDP = SEQ + FSDP
SEQ_N = 16
FSDP_N = 8
TOK = 64
PAD_FF = 6144
NORM_EPS = 1e-05
ADAPTER_SCALE = 2.0
ROPE_BASE = 10000.0
CLIP_MAX = 0.001
FIRST_DECAY = 0.5
SECOND_DECAY = 0.5
RATE_EMBED = 0.3
RATE_GAIN = 0.1
LEARN_RATE_DOWN = 0.1
LEARN_RATE_UP = 0.5
WEIGHT_DECAY = 0.01
ADAM_EPS = 1e-12
HIGHEST = lax.Precision.HIGHEST
MESH_ID = pl.DeviceIdType.MESH
ANY = pl.BlockSpec(memory_space=pl.ANY)
VMEM = pl.BlockSpec(memory_space=pltpu.VMEM)
SMEM = pl.BlockSpec(memory_space=pltpu.SMEM)
DMA = pltpu.SemaphoreType.DMA
VMEM_LIMIT = 56 * 1024 * 1024


def seq_me():
    return lax.axis_index("seq_0") * 8 + lax.axis_index("seq_1") * 2 + lax.axis_index("seq_2")


def fsdp_me():
    return lax.axis_index("fsdp_0") * 2 + lax.axis_index("fsdp_1")


def seq_at(i):
    return {"seq_0": i // 8, "seq_1": (i // 2) % 4, "seq_2": i % 2}


def fsdp_at(i):
    return {"fsdp_0": i // 2, "fsdp_1": i % 2}


RINGS = {"seq": (SEQ_N, seq_me, seq_at), "fsdp": (FSDP_N, fsdp_me, fsdp_at)}


def greet(kind, offsets):
    count, where, at = RINGS[kind]
    me = where()
    barrier = pltpu.get_barrier_semaphore()
    for k in offsets:
        pl.semaphore_signal(
            barrier, inc=1, device_id=at((me + count - k) % count), device_id_type=MESH_ID
        )
    pl.semaphore_wait(barrier, len(offsets))
    return me


def send_each(kind, me, offsets, src_of, dst_of, send_sem, recv_sem):
    count, _, at = RINGS[kind]
    copies = []
    for n, k in enumerate(offsets):
        peer = (me + k) % count
        copy = pltpu.make_async_remote_copy(
            src_ref=src_of(k, peer),
            dst_ref=dst_of(k, peer),
            send_sem=send_sem.at[n],
            recv_sem=recv_sem.at[n],
            device_id=at(peer),
            device_id_type=MESH_ID,
        )
        copy.start()
        copies.append(copy)
    return copies


def remote_call(body, out_shape, in_specs, out_specs, scratch, collective_id, name):
    return pl.pallas_call(
        body,
        out_shape=out_shape,
        in_specs=in_specs,
        out_specs=out_specs,
        scratch_shapes=scratch,
        compiler_params=pltpu.CompilerParams(
            collective_id=collective_id, has_side_effects=True, vmem_limit_bytes=VMEM_LIMIT
        ),
        name=name,
    )


def sems(n):
    return [DMA((n,)), DMA((n,))]


ALL16 = range(1, SEQ_N)
ALL8 = range(1, FSDP_N)


def gather_fsdp(blocks, collective_id, name):
    count = len(blocks)

    def body(*refs):
        ins, outs = refs[:count], refs[count : 2 * count]
        ssem, rsem, lsem = refs[2 * count :]
        me = greet("fsdp", ALL8)
        copies = []
        for n in range(count):
            copies += send_each(
                "fsdp", me, ALL8, lambda k, p: ins[n], lambda k, p: outs[n].at[me],
                ssem.at[pl.ds(7 * n, 7)], rsem.at[pl.ds(7 * n, 7)],
            )
            own = pltpu.make_async_copy(ins[n], outs[n].at[me], lsem.at[n])
            own.start()
            copies.append(own)
        for copy in copies:
            copy.wait()

    return remote_call(
        body,
        [jax.ShapeDtypeStruct((FSDP_N, *b.shape), b.dtype) for b in blocks],
        [ANY] * count,
        [ANY] * count,
        sems(7 * count) + [DMA((count,))],
        collective_id,
        name,
    )(*blocks)


def sum_over(kind, block, collective_id, name, scatter):
    count = RINGS[kind][0]
    offsets = ALL16 if kind == "seq" else ALL8
    part = block.shape[1:] if scatter else block.shape

    def body(src, out, held, ssem, rsem):
        me = greet(kind, offsets)
        copies = send_each(
            kind, me, offsets,
            (lambda k, p: src.at[p]) if scatter else (lambda k, p: src),
            lambda k, p: held.at[k - 1], ssem, rsem,
        )
        total = (src[me] if scatter else src[...]).astype(jnp.float32)
        for n, copy in enumerate(copies):
            copy.wait_recv()
            total = total + held[n].astype(jnp.float32)
        out[...] = total
        for copy in copies:
            copy.wait_send()

    return remote_call(
        body,
        jax.ShapeDtypeStruct(part, jnp.float32),
        [VMEM],
        VMEM,
        [pltpu.VMEM((count - 1, *part), block.dtype)] + sems(count - 1),
        collective_id,
        name,
    )(block)


def sum_rows(block, collective_id, name):
    _, rows, width = block.shape

    def body(src, out, held, ssem, rsem):
        me = greet("fsdp", ALL8)
        copies = send_each(
            "fsdp", me, ALL8, lambda k, p: src.at[p], lambda k, p: held.at[k - 1], ssem, rsem
        )
        out[...] = src[me].astype(jnp.float32)
        for n, copy in enumerate(copies):
            copy.wait_recv()
            out[...] += held[n].astype(jnp.float32)
        for copy in copies:
            copy.wait_send()

    return remote_call(
        body,
        jax.ShapeDtypeStruct((rows, width), jnp.float32),
        [VMEM],
        VMEM,
        [pltpu.VMEM((7, rows, width), block.dtype)] + sems(7),
        collective_id,
        name,
    )(block)


def columns_to_rows(block, collective_id, name):
    _, rows, width = block.shape

    def body(src, out, ssem, rsem, lsem):
        me = greet("seq", ALL16)
        spot = pl.ds(pl.multiple_of(me * width, width), width)
        copies = send_each(
            "seq", me, ALL16, lambda k, p: src.at[p], lambda k, p: out.at[:, spot], ssem, rsem
        )
        own = pltpu.make_async_copy(src.at[me], out.at[:, spot], lsem)
        own.start()
        for copy in copies:
            copy.wait()
        own.wait()

    return remote_call(
        body,
        jax.ShapeDtypeStruct((rows, SEQ_N * width), block.dtype),
        [ANY],
        ANY,
        sems(15) + [DMA],
        collective_id,
        name,
    )(block)


def rows_to_columns(block, summed, collective_id, name):
    rows = block.shape[0]
    width = block.shape[1] // SEQ_N
    part = summed.shape[1:]

    def body(src, part_src, out, total_out, held, ssem, rsem, psem, qsem, lsem):
        me = greet("seq", ALL16)

        def cols(p):
            return pl.ds(pl.multiple_of(p * width, width), width)

        copies = send_each(
            "seq", me, ALL16, lambda k, p: src.at[:, cols(p)], lambda k, p: out.at[me], ssem, rsem
        )
        parts = send_each(
            "seq", me, ALL16, lambda k, p: part_src.at[p], lambda k, p: held.at[k - 1], psem, qsem
        )
        own = pltpu.make_async_copy(src.at[:, cols(me)], out.at[me], lsem)
        own.start()
        total = part_src[me]
        for n, copy in enumerate(parts):
            copy.wait_recv()
            total = total + held[n]
        total_out[...] = total
        for copy in copies:
            copy.wait()
        for copy in parts:
            copy.wait_send()
        own.wait()

    return remote_call(
        body,
        [
            jax.ShapeDtypeStruct((SEQ_N, rows, width), block.dtype),
            jax.ShapeDtypeStruct(part, jnp.float32),
        ],
        [ANY, VMEM],
        [ANY, VMEM],
        [pltpu.VMEM((15, *part), jnp.float32)] + sems(15) + sems(15) + [DMA],
        collective_id,
        name,
    )(block, summed)


def gather_and_sum(block, summed, collective_id, name):
    def body(src, part_src, out, total_out, held, ssem, rsem, psem, qsem, lsem):
        me = greet("fsdp", ALL8)
        parts = send_each(
            "fsdp", me, ALL8, lambda k, p: part_src, lambda k, p: held.at[k - 1], psem, qsem
        )
        copies = send_each(
            "fsdp", me, ALL8, lambda k, p: src, lambda k, p: out.at[me], ssem, rsem
        )
        own = pltpu.make_async_copy(src, out.at[me], lsem)
        own.start()
        total = part_src[...]
        for n, copy in enumerate(parts):
            copy.wait_recv()
            total = total + held[n]
        total_out[...] = total
        for copy in copies:
            copy.wait()
        for copy in parts:
            copy.wait_send()
        own.wait()

    return remote_call(
        body,
        [
            jax.ShapeDtypeStruct((FSDP_N, *block.shape), block.dtype),
            jax.ShapeDtypeStruct(summed.shape, jnp.float32),
        ],
        [ANY, VMEM],
        [ANY, VMEM],
        [pltpu.VMEM((7, *summed.shape), jnp.float32)] + sems(7) + sems(7) + [DMA],
        collective_id,
        name,
    )(block, summed)


class Piece:
    def __init__(self, block, order, whole, halves):
        self.block, self.order, self.whole, self.halves = block, order, whole, halves


def gather_weights(qkvo, gate_up, down, small, head, table, ids):
    out_shape = [
        jax.ShapeDtypeStruct((2, 4, 2, 4, 2, *qkvo.shape), qkvo.dtype),
        jax.ShapeDtypeStruct((2, 4, 2, 4, 2, *gate_up.shape), gate_up.dtype),
        jax.ShapeDtypeStruct((2, 4, 2, 4, 2, *down.shape), down.dtype),
        jax.ShapeDtypeStruct((2, 4, 2, 4, 2, *small.shape), small.dtype),
        jax.ShapeDtypeStruct((head.shape[0], SEQ_N * head.shape[1]), head.dtype),
        jax.ShapeDtypeStruct((4, 2, *table.shape), table.dtype),
        jax.ShapeDtypeStruct((SEQ_N, *ids.shape), ids.dtype),
    ]
    sem_count = 400

    def body(*refs):
        ins, outs, sem = refs[:7], refs[7:14], refs[14]
        yh, x, c, z, yl = (lax.axis_index(a) for a in SEQ_FSDP)
        y = 2 * yh + yl
        where = {"x": x, "y": y, "z": z}
        seq = seq_me()
        used = [0]

        def fresh():
            used[0] += 1
            return sem.at[used[0] - 1]

        def beside(axis, step):
            at = (where[axis] + step + 4) % 4
            if axis == "x":
                return {"seq_1": at}
            if axis == "z":
                return {"fsdp_0": at}
            return {"seq_0": at // 2, "fsdp_1": at % 2}

        other = {"seq_2": 1 - c}

        barrier = pltpu.get_barrier_semaphore()
        greeted = [beside("y", 1), beside("y", -1), beside("z", 1), beside("z", -1)]
        greeted += [seq_at((seq + k) % SEQ_N) for k in ALL16]
        for device in greeted:
            pl.semaphore_signal(barrier, inc=1, device_id=device, device_id_type=MESH_ID)

        late = []

        def remote(src, dst, ssem, rsem, device):
            pltpu.make_async_remote_copy(
                src_ref=src, dst_ref=dst, send_sem=ssem, recv_sem=rsem,
                device_id=device, device_id_type=MESH_ID,
            ).start()

        def arrived(ref, rsem):
            pltpu.make_async_copy(ref, ref, rsem).wait()

        def weight_stream(ref, order, whole, halves):
            def block(done, axis, at, tail, core=c):
                place = {"yh": yh, "x": x, "z": z, "yl": yl}
                for a, value in [(a, slice(None)) for a in done] + [(axis, at)]:
                    if a == "y":
                        if isinstance(value, slice):
                            place["yh"] = place["yl"] = value
                        else:
                            place["yh"], place["yl"] = value // 2, value % 2
                    elif a is not None:
                        place[a] = value
                return ref.at[(place["yh"], place["x"], core, place["z"], place["yl"]) + tail]

            send = [fresh() for _ in order]
            across_s, across_r = fresh(), fresh()
            late.append((send[0], ref.at[(0, 0, 0, pl.ds(0, 3), 0) + whole]))
            late.append((send[1], ref.at[(0, pl.ds(0, 2), 0, pl.ds(0, 3), slice(None)) + whole]))
            late.append(
                (send[2], ref.at[(slice(None), slice(None), 0, pl.ds(0, 3), slice(None)) + whole])
            )
            late.append((across_s, ref.at[(slice(None), slice(None), c, slice(None), slice(None)) + whole]))
            late.append((across_r, ref.at[(slice(None), slice(None), 1 - c, slice(None), slice(None)) + whole]))

            def across(view):
                remote(view, view, across_s, across_r, other)

            across(block([], None, None, whole))
            for n, axis in enumerate(order):
                done = order[:n]
                at = where[axis]
                before, after, far = (at + 3) % 4, (at + 1) % 4, (at + 2) % 4
                from_before, from_after = fresh(), fresh()
                own = block(done, axis, at, whole)
                remote(own, own, send[n], from_before, beside(axis, 1))
                remote(own, own, send[n], from_after, beside(axis, -1))
                yield
                got = block(done, axis, before, whole)
                arrived(got, from_before)
                far_first = fresh()
                half = block(done, axis, before, halves[0])
                remote(half, half, send[n], far_first, beside(axis, 1))
                across(got)
                got = block(done, axis, after, whole)
                arrived(got, from_after)
                if len(halves) > 1:
                    far_second = fresh()
                    half = block(done, axis, after, halves[1])
                    remote(half, half, send[n], far_second, beside(axis, -1))
                across(got)
                yield
                arrived(block(done, axis, far, halves[0]), far_first)
                if len(halves) > 1:
                    arrived(block(done, axis, far, halves[1]), far_second)
                across(block(done, axis, far, whole))

        def table_stream(ref):
            send_y, send_z, recv_y = fresh(), fresh(), fresh()
            late.append((send_y, ref.at[0, 0]))
            late.append((send_z, ref.at[pl.ds(0, 3)]))
            own = ref.at[z, yl]
            remote(own, own, send_y, recv_y, {"fsdp_1": 1 - yl})
            yield
            arrived(ref.at[z, 1 - yl], recv_y)
            half_rows = ref.shape[2] // 2
            first, second = pl.ds(0, half_rows), pl.ds(half_rows, half_rows)
            before, after, far = (z + 3) % 4, (z + 1) % 4, (z + 2) % 4
            from_before, from_after, far_first, far_second = (fresh() for _ in range(4))
            remote(ref.at[z], ref.at[z], send_z, from_before, beside("z", 1))
            remote(ref.at[z], ref.at[z], send_z, from_after, beside("z", -1))
            yield
            arrived(ref.at[before], from_before)
            half = ref.at[before, :, first]
            remote(half, half, send_z, far_first, beside("z", 1))
            arrived(ref.at[after], from_after)
            half = ref.at[after, :, second]
            remote(half, half, send_z, far_second, beside("z", -1))
            yield
            arrived(ref.at[far, :, first], far_first)
            arrived(ref.at[far, :, second], far_second)

        def head_stream(ref):
            width = head.shape[1]
            rows = ref.shape[0]

            def cols(h, at, take=slice(None)):
                start = pl.multiple_of(((h * 4 + at) * 2 + c) * width, width)
                return ref.at[take, pl.ds(start, width)]

            send_y, send_x, recv_y, across_s, across_r = (fresh() for _ in range(5))
            late.append((send_y, ref.at[:, pl.ds(0, width)]))
            late.append((send_x, ref.at[:, pl.ds(0, 6 * width)]))
            late.append((across_s, ref.at[:, pl.ds(0, 8 * width)]))
            late.append((across_r, ref.at[:, pl.ds(0, 8 * width)]))

            def across(view):
                remote(view, view, across_s, across_r, other)

            own = cols(yh, x)
            remote(own, own, send_y, recv_y, {"seq_0": 1 - yh})
            across(own)
            yield
            got = cols(1 - yh, x)
            arrived(got, recv_y)
            across(got)
            first, second = pl.ds(0, rows // 2), pl.ds(rows // 2, rows // 2)
            before, after, far = (x + 3) % 4, (x + 1) % 4, (x + 2) % 4
            marks = [[fresh() for _ in range(4)] for _ in range(2)]
            for h in range(2):
                own = cols(h, x)
                remote(own, own, send_x, marks[h][0], beside("x", 1))
                remote(own, own, send_x, marks[h][1], beside("x", -1))
            yield
            for h in range(2):
                got = cols(h, before)
                arrived(got, marks[h][0])
                half = cols(h, before, first)
                remote(half, half, send_x, marks[h][2], beside("x", 1))
                across(got)
                got = cols(h, after)
                arrived(got, marks[h][1])
                half = cols(h, after, second)
                remote(half, half, send_x, marks[h][3], beside("x", -1))
                across(got)
            yield
            for h in range(2):
                arrived(cols(h, far, first), marks[h][2])
                arrived(cols(h, far, second), marks[h][3])
                across(cols(h, far))

        def ids_stream(src, ref):
            send, recv = fresh(), fresh()
            for k in ALL16:
                remote(src, ref.at[seq], send, recv, seq_at((seq + k) % SEQ_N))
            late.append((send, ref.at[pl.ds(0, 15)]))
            late.append((recv, ref.at[pl.ds(0, 15)]))
            return
            yield

        own_views = [
            outs[0].at[yh, x, c, z, yl],
            outs[1].at[yh, x, c, z, yl],
            outs[2].at[yh, x, c, z, yl],
            outs[3].at[yh, x, c, z, yl],
            outs[4].at[:, pl.ds(pl.multiple_of(seq * head.shape[1], head.shape[1]), head.shape[1])],
            outs[5].at[z, yl],
            outs[6].at[seq],
        ]
        local = []
        for src, dst in zip(ins, own_views):
            copy = pltpu.make_async_copy(src, dst, fresh())
            copy.start()
            local.append(copy)
        for copy in local:
            copy.wait()
        pl.semaphore_wait(barrier, len(greeted))

        turns = (("x", "y", "z"), ("y", "z", "x"), ("z", "x", "y"))

        def column_streams(ref, start, width):
            third = width // 3
            for n, order in enumerate(turns):
                at = start + n * third
                yield weight_stream(
                    ref, order,
                    (slice(None), pl.ds(at, third)),
                    [(slice(None), pl.ds(at + k * third // 2, third // 2)) for k in range(2)],
                )

        def down_streams(ref):
            width = ref.shape[-1]
            for n, order in enumerate(turns):
                yield weight_stream(
                    ref, order,
                    (n, slice(None), slice(None)),
                    [(n, slice(None), pl.ds(k * width // 2, width // 2)) for k in range(2)],
                )

        small_all = (slice(None), slice(None))
        wide = gate_up.shape[1]
        starts = [
            [ids_stream(ins[6], outs[6]), table_stream(outs[5])]
            + list(column_streams(outs[0], 0, qkvo.shape[1]))
            + [weight_stream(outs[3], turns[0], small_all, [small_all])],
            [head_stream(outs[4])] + list(column_streams(outs[1], 0, wide // 2)),
            list(column_streams(outs[1], wide // 2, wide // 2)),
            list(down_streams(outs[2])),
        ]
        active = []
        while starts or active:
            if starts:
                active += starts.pop(0)
            still = []
            for stream in active:
                try:
                    next(stream)
                    still.append(stream)
                except StopIteration:
                    pass
            active = still
        for mark, view in late:
            arrived(view, mark)
        assert used[0] <= sem_count, used[0]

    return remote_call(
        body, out_shape, [ANY] * 7, [ANY] * 7, [DMA((sem_count,))], 1, "gather_weights"
    )(qkvo, gate_up, down, small, head, table, ids)


def look_up(table, ids):
    vocab, width = table.shape

    def body(ids_ref, table_ref, out_ref, wide, rows):
        wide[...] = table_ref[...].astype(jnp.float32)
        for s in range(SEQ_N):

            def step(t, carry):
                rows[pl.ds(t, 1), :] = wide[pl.ds(ids_ref[s, t], 1), :]
                return carry

            lax.fori_loop(0, 128, step, 0, unroll=16)
            out_ref[s] = rows[...].astype(jnp.bfloat16)

    return pl.pallas_call(
        body,
        out_shape=jax.ShapeDtypeStruct((SEQ_N, 128, width), jnp.bfloat16),
        in_specs=[SMEM, VMEM],
        out_specs=VMEM,
        scratch_shapes=[
            pltpu.VMEM((vocab, width), jnp.float32),
            pltpu.VMEM((128, width), jnp.float32),
        ],
        compiler_params=pltpu.CompilerParams(vmem_limit_bytes=VMEM_LIMIT),
        name="look_up",
    )(ids, table)


def add_rows(gradient, local_ids, vocab):
    count, width = gradient.shape
    tile = 512
    padded = -(-vocab // 512) * 512

    def body(ids_ref, grad_ref, out_ref):
        @pl.when(pl.program_id(0) == 0)
        def _():
            out_ref[...] = jnp.zeros_like(out_ref)

        ids = ids_ref[...]
        grad = grad_ref[...]

        def step(n, carry):
            start = pl.multiple_of(n * 512, 512)
            row = lax.broadcasted_iota(jnp.int32, (512, tile), 0) + start
            hot = (row == ids).astype(jnp.float32).astype(jnp.bfloat16)
            out_ref[pl.ds(start, 512), :] += jnp.dot(
                hot, grad, preferred_element_type=jnp.float32
            )
            return carry

        lax.fori_loop(0, padded // 512, step, 0)

    return pl.pallas_call(
        body,
        out_shape=jax.ShapeDtypeStruct((padded, width), jnp.float32),
        grid=(count // tile,),
        in_specs=[
            pl.BlockSpec((1, tile), lambda i: (0, i)),
            pl.BlockSpec((tile, width), lambda i: (i, 0)),
        ],
        out_specs=pl.BlockSpec((padded, width), lambda i: (0, 0)),
        compiler_params=pltpu.CompilerParams(vmem_limit_bytes=VMEM_LIMIT),
        name="add_rows",
    )(local_ids.reshape(1, count), gradient)


def turn(values, cosine, sine):
    width = values.shape[-1]
    lane = lax.broadcasted_iota(jnp.int32, values.shape, values.ndim - 1)
    swapped = jnp.where(
        lane % 64 < 32,
        pltpu.roll(values, width - 32, values.ndim - 1),
        pltpu.roll(values, 32, values.ndim - 1),
    )
    return values * cosine + swapped * sine


def key_value_window(key_value, cosine, sine, collective_id):
    def body(kv_ref, cos_ref, sin_ref, out, held, ssem, rsem, lsem):
        me = greet("seq", range(1, 5))
        for m in range(2):
            rows = kv_ref[pl.ds(m * TOK, TOK), :]
            held[m, :, 0:256] = turn(rows[:, 0:256], cos_ref[:, 0:256], sin_ref[:, 0:256]).astype(
                jnp.bfloat16
            )
            held[m, :, 256:512] = rows[:, 256:512].astype(jnp.bfloat16)
        copies = send_each(
            "seq", me, range(1, 5), lambda k, p: held,
            lambda k, p: out.at[:, pl.ds((4 - k) * TOK, TOK), :], ssem, rsem,
        )
        own = pltpu.make_async_copy(held, out.at[:, pl.ds(4 * TOK, TOK), :], lsem)
        own.start()
        for copy in copies:
            copy.wait()
        own.wait()

    return remote_call(
        body,
        jax.ShapeDtypeStruct((2, 5 * TOK, 512), jnp.bfloat16),
        [VMEM] * 3,
        VMEM,
        [pltpu.VMEM((2, TOK, 512), jnp.bfloat16)] + sems(4) + [DMA],
        collective_id,
        "key_value_window",
    )(key_value, cosine, sine)


def key_value_back(far, own, cosine, sine, collective_id):
    def body(far_ref, own_ref, cos_ref, sin_ref, out, held, ssem, rsem):
        me = greet("seq", range(12, 16))
        copies = send_each(
            "seq", me, range(12, 16),
            lambda k, p: far_ref.at[:, pl.ds((k - 12) * TOK, TOK), :],
            lambda k, p: held.at[k - 12], ssem, rsem,
        )
        for copy in copies:
            copy.wait_recv()
        for m in range(2):
            total = own_ref[m]
            for n in range(3, -1, -1):
                total = total + held[n, m].astype(jnp.float32)
            keys = turn(total[:, 0:256], cos_ref[:, 0:256], -sin_ref[:, 0:256])
            out[pl.ds(m * TOK, TOK), 0:256] = keys.astype(jnp.bfloat16)
            out[pl.ds(m * TOK, TOK), 256:512] = total[:, 256:512].astype(jnp.bfloat16)
        for copy in copies:
            copy.wait_send()

    return remote_call(
        body,
        jax.ShapeDtypeStruct((2 * TOK, 512), jnp.bfloat16),
        [VMEM] * 4,
        VMEM,
        [pltpu.VMEM((4, 2, TOK, 512), jnp.bfloat16)] + sems(4),
        collective_id,
        "key_value_back",
    )(far, own, cosine, sine)


def spread_heads(block):
    return jnp.concatenate([block[:, 64 * g : 64 * g + 64] for g in range(8)], axis=0)


def join_heads(block):
    return jnp.concatenate([block[64 * g : 64 * g + 64, :] for g in range(8)], axis=1)


def window_mask(start_ref, query_seg, key_seg, shift):
    start = start_ref[0]
    query = start + lax.broadcasted_iota(jnp.int32, (TOK, 5 * TOK), 0)
    key = start - 4 * TOK + lax.broadcasted_iota(jnp.int32, (TOK, 5 * TOK), 1)
    allowed = (
        (key <= query)
        & (key >= 0)
        & (query_seg == key_seg)
        & (((query + shift) >> 8) == ((key + shift) >> 8))
    )
    return jnp.concatenate([allowed.astype(jnp.float32)] * 8, axis=0) > 0.5


def nt(left, right):
    return lax.dot_general(
        left, right, (((1,), (1,)), ((), ())), preferred_element_type=jnp.float32
    )


def tn(left, right):
    return lax.dot_general(
        left, right, (((0,), (0,)), ((), ())), preferred_element_type=jnp.float32
    )


def probabilities(queries, keys, mask):
    scores = jnp.where(mask, nt(queries, keys) * 0.125, -1e30)
    top = jnp.max(scores, axis=-1, keepdims=True)
    raised = jnp.where(mask, jnp.exp(scores - top), 0.0)
    return raised / jnp.sum(raised, axis=-1, keepdims=True)


def attend(queries, window, cosine, sine, query_seg, key_seg, start, shifts):
    def body(start_ref, shift_ref, q_ref, kv_ref, cos_ref, sin_ref, qs_ref, ks_ref, q_out, a_out):
        for h in range(4):
            cols = slice(512 * h, 512 * h + 512)
            turned = turn(q_ref[:, cols], cos_ref[...], sin_ref[...]).astype(jnp.bfloat16)
            q_out[:, cols] = turned
            mask = window_mask(start_ref, qs_ref[0], ks_ref[0], shift_ref[h])
            probs = probabilities(spread_heads(turned), kv_ref[0, :, 64 * h : 64 * h + 64], mask)
            values = kv_ref[0, :, 256 + 64 * h : 256 + 64 * h + 64]
            mixed = jnp.dot(probs.astype(jnp.bfloat16), values, preferred_element_type=jnp.float32)
            a_out[:, cols] = join_heads(mixed).astype(jnp.bfloat16)

    wide = pl.BlockSpec((TOK, 2048), lambda m: (m, 0))
    return pl.pallas_call(
        body,
        out_shape=[jax.ShapeDtypeStruct((2 * TOK, 2048), jnp.bfloat16)] * 2,
        grid=(2,),
        in_specs=[
            SMEM,
            SMEM,
            wide,
            pl.BlockSpec((1, 5 * TOK, 512), lambda m: (m, 0, 0)),
            pl.BlockSpec((TOK, 512), lambda m: (0, 0)),
            pl.BlockSpec((TOK, 512), lambda m: (0, 0)),
            pl.BlockSpec((1, TOK, 1), lambda m: (m, 0, 0)),
            pl.BlockSpec((1, 1, 5 * TOK), lambda m: (m, 0, 0)),
        ],
        out_specs=[wide, wide],
        compiler_params=pltpu.CompilerParams(vmem_limit_bytes=VMEM_LIMIT),
        name="attend",
    )(start, shifts, queries, window, cosine, sine, query_seg, key_seg)


def attend_back(queries, window, upstream, cosine, sine, query_seg, key_seg, start, shifts):
    def body(
        start_ref, shift_ref, q_ref, kv_ref, g_ref, cos_ref, sin_ref, qs_ref, ks_ref,
        dq_out, far_out, own_out,
    ):
        for h in range(4):
            cols = slice(512 * h, 512 * h + 512)
            mask = window_mask(start_ref, qs_ref[0], ks_ref[0], shift_ref[h])
            spread = spread_heads(q_ref[:, cols])
            keys = kv_ref[0, :, 64 * h : 64 * h + 64]
            values = kv_ref[0, :, 256 + 64 * h : 256 + 64 * h + 64]
            probs = probabilities(spread, keys, mask)
            grads = spread_heads(g_ref[:, cols])
            d_probs = nt(grads, values)
            d_values = tn(probs.astype(jnp.bfloat16), grads)
            inner = jnp.sum(probs * d_probs, axis=-1, keepdims=True)
            d_scores = (0.125 * probs * (d_probs - inner)).astype(jnp.bfloat16)
            d_queries = join_heads(jnp.dot(d_scores, keys, preferred_element_type=jnp.float32))
            dq_out[:, cols] = turn(d_queries, cos_ref[...], -sin_ref[...]).astype(jnp.bfloat16)
            d_keys = tn(d_scores, spread)
            for at, part in ((64 * h, d_keys), (256 + 64 * h, d_values)):
                far_out[0, :, at : at + 64] = part[0 : 4 * TOK].astype(jnp.bfloat16)
                own_out[0, :, at : at + 64] = part[4 * TOK :]

    wide = pl.BlockSpec((TOK, 2048), lambda m: (m, 0))
    return pl.pallas_call(
        body,
        out_shape=[
            jax.ShapeDtypeStruct((2 * TOK, 2048), jnp.bfloat16),
            jax.ShapeDtypeStruct((2, 4 * TOK, 512), jnp.bfloat16),
            jax.ShapeDtypeStruct((2, TOK, 512), jnp.float32),
        ],
        grid=(2,),
        in_specs=[
            SMEM,
            SMEM,
            wide,
            pl.BlockSpec((1, 5 * TOK, 512), lambda m: (m, 0, 0)),
            wide,
            pl.BlockSpec((TOK, 512), lambda m: (0, 0)),
            pl.BlockSpec((TOK, 512), lambda m: (0, 0)),
            pl.BlockSpec((1, TOK, 1), lambda m: (m, 0, 0)),
            pl.BlockSpec((1, 1, 5 * TOK), lambda m: (m, 0, 0)),
        ],
        out_specs=[
            wide,
            pl.BlockSpec((1, 4 * TOK, 512), lambda m: (m, 0, 0)),
            pl.BlockSpec((1, TOK, 512), lambda m: (m, 0, 0)),
        ],
        compiler_params=pltpu.CompilerParams(vmem_limit_bytes=VMEM_LIMIT),
        name="attend_back",
    )(start, shifts, queries, window, upstream, cosine, sine, query_seg, key_seg)


def dot(left, right):
    return jnp.dot(left, right, preferred_element_type=jnp.float32)


def dot_exact(left, right):
    return jnp.dot(left, right, precision=HIGHEST)


def norm_scale(values):
    return lax.rsqrt(jnp.mean(values * values, axis=-1, keepdims=True) + NORM_EPS)


def norm_back(values, gain, upstream):
    scale_of = norm_scale(values)
    scaled = gain * upstream
    inward = scale_of * scaled - values * scale_of**3 * jnp.mean(
        scaled * values, axis=-1, keepdims=True
    )
    return (inward, jnp.sum(upstream * values * scale_of, axis=0))


def adam_update(weight_vals, first_old, second_old, gradient, rate):
    first_new = FIRST_DECAY * first_old + (1.0 - FIRST_DECAY) * gradient
    second_new = SECOND_DECAY * second_old + (1.0 - SECOND_DECAY) * gradient * gradient
    first_hat = first_new / (1.0 - FIRST_DECAY**STEP)
    second_hat = second_new / (1.0 - SECOND_DECAY**STEP)
    step_vals = first_hat / (jnp.sqrt(second_hat) + ADAM_EPS) + WEIGHT_DECAY * weight_vals
    return (first_new, second_new, weight_vals - rate * step_vals)


def factor_onehot(columns):
    factor_id = (
        (columns >= 2048).astype(jnp.int32)
        + (columns >= 2048 + 256).astype(jnp.int32)
        + (columns >= 2048 + 512).astype(jnp.int32)
    )
    return (factor_id[None, :] == jnp.arange(4)[:, None]).astype(jnp.float32)


def shampoo_parts(down_factor_gradient, up_factor_gradient, onehot):
    left_three = down_factor_gradient.reshape(4, up_factor_gradient.shape[0], -1)
    stats_left = jnp.einsum("krd,ksd->krs", left_three, left_three, precision=HIGHEST)
    stats_right = jnp.einsum(
        "rc,sc,kc->krs", up_factor_gradient, up_factor_gradient, onehot, precision=HIGHEST
    )
    return jnp.concatenate([stats_left, stats_right], 0)


def inverse_root(stats):
    unit_mat = jnp.eye(stats.shape[-1], dtype=stats.dtype)[None]
    norm_of = jnp.sqrt(jnp.sum(stats * stats, axis=(1, 2), keepdims=True))
    matrix = stats / norm_of
    root_mat = unit_mat * lax.rsqrt(jnp.sqrt(norm_of))
    for iteration in range(10):
        factor = (5.0 * unit_mat - matrix) * 0.25
        root_mat = jnp.einsum("kab,kbc->kac", root_mat, factor, precision=HIGHEST)
        square = jnp.einsum("kab,kbc->kac", factor, factor, precision=HIGHEST)
        fourth = jnp.einsum("kab,kbc->kac", square, square, precision=HIGHEST)
        matrix = jnp.einsum("kab,kbc->kac", fourth, matrix, precision=HIGHEST)
    return root_mat


def shampoo_apply(
    stats_new, width_left, width_right, down_factor_gradient, up_factor_gradient, onehot
):
    roots = inverse_root(stats_new)
    left_three = down_factor_gradient.reshape(4, up_factor_gradient.shape[0], -1)
    down_factor_step = (
        jnp.einsum("krs,ksd->krd", roots[:4], left_three, precision=HIGHEST)
        * lax.rsqrt(jnp.sqrt(width_left))[:, None, :]
    )
    up_factor_step = (
        jnp.einsum("krs,sc,kc->rc", roots[4:], up_factor_gradient, onehot, precision=HIGHEST)
        * lax.rsqrt(jnp.sqrt(width_right))[None, :]
    )
    return (down_factor_step.reshape(down_factor_gradient.shape), up_factor_step)


def per_device(
    input_token_index,
    target_token_index,
    loss_position_index,
    document_slot_index,
    row_used_length,
    head_group_offsets,
    embedding,
    embedding_first_moment,
    embedding_second_moment,
    frozen_output_table,
    frozen_query_key_value_weight,
    frozen_attention_output_weight,
    frozen_gate_up_weight,
    frozen_down_weight,
    norm_gain_vectors,
    norm_gain_first_moment,
    norm_gain_second_moment,
    adapter_down_factors,
    adapter_up_factors,
    rank_side_statistics,
    down_width_statistics,
    up_width_statistics,
):
    fsdp_here = lax.axis_index(FSDP)
    seq_here = lax.axis_index(SEQ)
    vocab_dev = embedding.shape[0]

    qkvo_own = jnp.concatenate([frozen_query_key_value_weight, frozen_attention_output_weight], 1)
    gate_up_own = jnp.pad(
        frozen_gate_up_weight.reshape(16, 256, 44), ((0, 0), (0, 0), (0, 4))
    ).reshape(16, 2 * PAD_FF)
    down_own = jnp.pad(frozen_down_weight, ((0, 4), (0, 0))).reshape(3, 16, 2048)
    small_own = jnp.pad(
        jnp.concatenate(
            [
                adapter_down_factors.reshape(-1),
                norm_gain_vectors.reshape(-1),
                adapter_up_factors.reshape(-1),
            ]
        ),
        (0, 1024 - 848),
    ).reshape(8, 128)
    ids_own = jnp.pad(input_token_index.reshape(16, TOK), ((0, 0), (0, 64)))
    qkvo, gate_up_w, down_w, small, head, table, ids = gather_weights(
        qkvo_own,
        gate_up_own,
        down_own,
        small_own,
        frozen_output_table,
        embedding.astype(jnp.bfloat16),
        ids_own,
    )
    qkvo = qkvo.reshape(2048, 4608)
    w_qkv, w_out = qkvo[:, :2560], qkvo[:, 2560:]
    gate_up_w = gate_up_w.reshape(2048, 2 * PAD_FF)
    down_w = down_w.reshape(PAD_FF, 2048)
    small = small.reshape(128, 1024)
    down_full = small[:, :512].reshape(128, 32, 16).transpose(1, 0, 2).reshape(32, 2048)
    gain = small[:, 512:560].reshape(128, 3, 16).transpose(1, 0, 2).reshape(3, 2048)
    up_full = small[:, 560:848].reshape(128, 8, 36).transpose(1, 0, 2).reshape(8, 4608)
    a_low = down_full.astype(jnp.bfloat16)
    b_low = up_full.astype(jnp.bfloat16)
    a_in, a_out = a_low[:24], a_low[24:]
    factor_of = (jnp.arange(2560) >= 2048).astype(jnp.int32) + (jnp.arange(2560) >= 2304)
    b_in = jnp.where(
        (jnp.arange(24) // 8)[:, None] == factor_of[None, :],
        jnp.concatenate([b_low[:, :2560]] * 3, 0),
        jnp.zeros((), jnp.bfloat16),
    )
    b_out = b_low[:, 2560:]

    places = loss_position_index.reshape(2, 8, SEQ_N, 32)
    spots = jnp.arange(SEQ_N)[:, None] * TOK + places
    counted = spots < row_used_length[..., None, None]
    seg_blocks = document_slot_index.reshape(2, 8, SEQ_N, 1, TOK)
    seg_at = jnp.sum(
        jnp.where(places[..., None] == jnp.arange(TOK), seg_blocks, 0), axis=-1
    )
    member = counted[..., None] & (seg_at[..., None] == jnp.arange(3))
    counts = jnp.sum(member.astype(jnp.int32), axis=(2, 3))
    document_total = jnp.sum((counts > 0).astype(jnp.float32))
    own_places = lax.dynamic_index_in_dim(places, seq_here, 2, keepdims=False)
    own_counted = lax.dynamic_index_in_dim(counted, seq_here, 2, keepdims=False)
    own_seg = lax.dynamic_index_in_dim(seg_at, seq_here, 2, keepdims=False)
    per_doc = jnp.sum(
        jnp.where(own_seg[..., None] == jnp.arange(3), counts[:, :, None, :], 0), axis=-1
    )
    own_weight = jnp.where(own_counted, 1.0 / jnp.maximum(per_doc, 1).astype(jnp.float32), 0.0)
    weight_flat = own_weight.transpose(1, 0, 2).reshape(-1)
    row_places = lax.dynamic_index_in_dim(own_places, fsdp_here, 1, keepdims=False)
    chosen_at = (row_places + jnp.arange(2)[:, None] * TOK).reshape(64)
    pick = (chosen_at[:, None] == jnp.arange(128)[None, :]).astype(jnp.float32)

    ids = ids[:, :, :TOK].reshape(SEQ_N, 2, 8, TOK)
    row_ids = lax.dynamic_index_in_dim(ids, fsdp_here, 2, keepdims=False).reshape(SEQ_N, 128)
    x_start = columns_to_rows(
        look_up(table.reshape(8 * vocab_dev, 128), row_ids), 2, "rows_of_tokens"
    ).astype(jnp.float32)

    half = 32
    freqs = ROPE_BASE ** (-2.0 * jnp.arange(half).astype(jnp.float32) / 64)
    angles = (seq_here * TOK + jnp.arange(TOK)).astype(jnp.float32)[:, None] * freqs[None, :]
    cosine = jnp.tile(jnp.cos(angles), (1, 16))
    sine = jnp.sin(angles)
    sine = jnp.tile(jnp.concatenate([-sine, sine], 1), (1, 8))
    own_docs = lax.dynamic_index_in_dim(document_slot_index, fsdp_here, 1, keepdims=False)
    padded = jnp.concatenate([jnp.full((2, 4 * TOK), -1, jnp.int32), own_docs], 1)
    key_seg = lax.dynamic_slice_in_dim(padded, seq_here * TOK, 5 * TOK, 1)[:, None, :]
    query_seg = key_seg[:, 0, 4 * TOK :][:, :, None]
    start = (seq_here * TOK).reshape(1)
    normed_one = (x_start * norm_scale(x_start) * gain[0]).astype(jnp.bfloat16)
    adapter_in = nt(normed_one, a_in).astype(jnp.bfloat16)
    packed = dot(normed_one, w_qkv) + ADAPTER_SCALE * dot(adapter_in, b_in)
    window = key_value_window(packed[:, 2048:], cosine, sine, 3)
    queries, attended = attend(
        packed, window, cosine, sine, query_seg, key_seg, start, head_group_offsets
    )
    adapter_mid = nt(attended, a_out).astype(jnp.bfloat16)
    x_mid = x_start + dot(attended, w_out) + ADAPTER_SCALE * dot(adapter_mid, b_out)

    normed_two = (x_mid * norm_scale(x_mid) * gain[1]).astype(jnp.bfloat16)
    gate_up = dot(normed_two, gate_up_w)
    gate, up = gate_up[:, :PAD_FF], gate_up[:, PAD_FF:]
    hidden = (jax.nn.silu(gate) * up).astype(jnp.bfloat16)
    x_end = x_mid + dot(hidden, down_w)
    normed_end = (x_end * norm_scale(x_end) * gain[2]).astype(jnp.bfloat16)

    chosen = dot(pick.astype(jnp.bfloat16), normed_end).astype(jnp.bfloat16)
    (rows,) = gather_fsdp([chosen], 4, "chosen_rows")
    rows = rows.reshape(512, 2048)
    logits = nt(rows, head)
    local_target = target_token_index.transpose(1, 0, 2).reshape(-1) - fsdp_here * vocab_dev
    is_target = jnp.arange(vocab_dev)[None, :] == local_target[:, None]
    top_local = jnp.max(logits, axis=1)
    exp_local = jnp.sum(jnp.exp(logits - top_local[:, None]), axis=1)
    target_local = jnp.sum(jnp.where(is_target, logits, 0.0), axis=1)
    (stats,) = gather_fsdp(
        [jnp.pad(jnp.stack([top_local, exp_local]), ((0, 6), (0, 0)))], 5, "softmax_parts"
    )
    top_all = jnp.max(stats[:, 0], axis=0)
    exp_all = jnp.sum(stats[:, 1] * jnp.exp(stats[:, 0] - top_all[None, :]), axis=0)
    log_norm = top_all + jnp.log(exp_all)
    peer_of = jnp.arange(512) // 64
    loss_part = jnp.sum(jnp.where(peer_of == fsdp_here, log_norm * weight_flat, 0.0)) - jnp.sum(
        weight_flat * target_local
    )
    d_logits = (
        (weight_flat / document_total)[:, None]
        * (jnp.exp(logits - log_norm[:, None]) - is_target.astype(jnp.float32))
    ).astype(jnp.bfloat16)
    d_chosen = sum_rows(
        dot(d_logits, head).astype(jnp.bfloat16).reshape(8, 64, 2048), 6, "row_gradients"
    )

    upstream = lax.dot_general(pick, d_chosen, (((0,), (0,)), ((), ())), precision=HIGHEST)
    d_end, gain_end = norm_back(x_end, gain[2], upstream)
    d_hidden = nt(d_end.astype(jnp.bfloat16), down_w)
    sigmoid_of = jax.nn.sigmoid(gate)
    d_gate = d_hidden * up * sigmoid_of * (1.0 + gate * (1.0 - sigmoid_of))
    d_up = d_hidden * gate * sigmoid_of
    d_gate_up = jnp.concatenate([d_gate.astype(jnp.bfloat16), d_up.astype(jnp.bfloat16)], 1)
    back_two, gain_mid = norm_back(x_mid, gain[1], nt(d_gate_up, gate_up_w))
    d_mid = d_end + back_two

    d_branch = d_mid.astype(jnp.bfloat16)
    d_adapter_mid = (ADAPTER_SCALE * nt(d_branch, b_out)).astype(jnp.bfloat16)
    d_attended = (nt(d_branch, w_out) + dot(d_adapter_mid, a_out)).astype(jnp.bfloat16)
    up_gradient_out = ADAPTER_SCALE * tn(adapter_mid, d_branch)
    down_gradient_out = tn(d_adapter_mid, attended)
    d_queries, d_far, d_own = attend_back(
        queries, window, d_attended, cosine, sine, query_seg, key_seg, start, head_group_offsets
    )
    d_key_value = key_value_back(d_far, d_own, cosine, sine, 7)
    d_packed = jnp.concatenate([d_queries, d_key_value], 1)
    d_adapter_in = (ADAPTER_SCALE * nt(d_packed, b_in)).astype(jnp.bfloat16)
    up_gradient_in = ADAPTER_SCALE * jnp.concatenate(
        [
            tn(adapter_in[:, 0:8], d_packed[:, :2048]),
            tn(adapter_in[:, 8:16], d_packed[:, 2048:2304]),
            tn(adapter_in[:, 16:24], d_packed[:, 2304:]),
        ],
        1,
    )
    down_gradient_in = tn(d_adapter_in, normed_one)
    back_one, gain_start = norm_back(
        x_start, gain[0], nt(d_packed, w_qkv) + dot(d_adapter_in, a_in)
    )
    d_start = (d_mid + back_one).astype(jnp.bfloat16)

    left = jnp.concatenate(
        [
            down_gradient_in,
            down_gradient_out,
            jnp.stack([gain_start, gain_mid, gain_end]),
            jnp.zeros((5, 2048), jnp.float32),
        ],
        0,
    )
    left = left.reshape(40, 16, 128).transpose(1, 0, 2)
    right = jnp.concatenate([up_gradient_in, up_gradient_out], 1).reshape(8, 16, 288)
    right = jnp.pad(right, ((0, 0), (0, 0), (0, 96))).transpose(1, 0, 2).reshape(16, 24, 128)
    d_columns, small_sum = rows_to_columns(
        d_start, jnp.concatenate([left, right], 1), 8, "token_gradients"
    )
    d_tokens, small_sum = gather_and_sum(d_columns, small_sum, 9, "token_gradients_all")
    all_ids = ids.transpose(2, 0, 1, 3).reshape(-1) - fsdp_here * vocab_dev
    grad_embed = add_rows(d_tokens.reshape(-1, 128), all_ids, vocab_dev)[:vocab_dev]
    left_sum = small_sum[:40]
    right_sum = small_sum[40:].reshape(8, 384)[:, :288]
    group_onehot = factor_onehot(seq_here * 288 + jnp.arange(288))
    stats_part = shampoo_parts(left_sum[:32], right_sum, group_onehot)
    first = (fsdp_here == 0).astype(jnp.float32)
    squares = jnp.sum(grad_embed * grad_embed) + first * (
        jnp.sum(left_sum[:35] * left_sum[:35]) + jnp.sum(right_sum * right_sum)
    )
    totals = jnp.concatenate(
        [
            (first * stats_part).reshape(-1),
            squares.reshape(1),
            loss_part.reshape(1),
            jnp.zeros((510,), jnp.float32),
        ]
    ).reshape(8, 128)
    totals = sum_over("seq", totals, 10, "totals_seq", False)
    totals = sum_over("fsdp", totals, 11, "totals_fsdp", False)
    stats_all = totals[:4].reshape(8, 8, 8)
    document_loss_sum = totals[4, 1]
    global_gradient_norm = jnp.sqrt(totals[4, 0])
    clip_factor = CLIP_MAX / jnp.maximum(global_gradient_norm, CLIP_MAX)

    own_left = lax.dynamic_slice_in_dim(left_sum, fsdp_here * 16, 16, 1)
    down_factor_gradient = own_left[:32] * clip_factor
    grad_gain = own_left[32:35] * clip_factor
    up_factor_gradient = (
        lax.dynamic_slice_in_dim(right_sum, fsdp_here * 36, 36, 1) * clip_factor
    )
    grad_embed = grad_embed * clip_factor
    unused_first, updated_embedding_second_moment, updated_embedding_table = adam_update(
        embedding, embedding_first_moment, embedding_second_moment, grad_embed, RATE_EMBED
    )
    updated_gain_first_moment, updated_gain_second_moment, updated_norm_gains = adam_update(
        norm_gain_vectors, norm_gain_first_moment, norm_gain_second_moment, grad_gain, RATE_GAIN
    )
    updated_rank_statistics = (
        SECOND_DECAY * rank_side_statistics
        + (1.0 - SECOND_DECAY) * (clip_factor * clip_factor) * stats_all
    )
    updated_down_width_statistics = SECOND_DECAY * down_width_statistics + (
        1.0 - SECOND_DECAY
    ) * jnp.sum(down_factor_gradient.reshape(4, 8, -1) ** 2, axis=1)
    updated_up_width_statistics = SECOND_DECAY * up_width_statistics + (
        1.0 - SECOND_DECAY
    ) * jnp.sum(up_factor_gradient * up_factor_gradient, axis=0)
    onehot = factor_onehot((seq_here * 8 + fsdp_here) * 36 + jnp.arange(36))
    down_factor_step, up_factor_step = shampoo_apply(
        updated_rank_statistics,
        updated_down_width_statistics,
        updated_up_width_statistics,
        down_factor_gradient,
        up_factor_gradient,
        onehot,
    )
    updated_down_factors = adapter_down_factors - LEARN_RATE_DOWN * down_factor_step
    updated_up_factors = adapter_up_factors - LEARN_RATE_UP * up_factor_step
    return (
        document_loss_sum,
        document_total,
        global_gradient_norm,
        grad_embed,
        updated_embedding_second_moment,
        updated_embedding_table,
        updated_gain_first_moment,
        updated_gain_second_moment,
        updated_norm_gains,
        down_factor_gradient,
        up_factor_gradient,
        updated_rank_statistics,
        updated_down_width_statistics,
        updated_up_width_statistics,
        updated_down_factors,
        updated_up_factors,
    )


def solution(mesh):
    torus = Mesh(
        mesh.devices.reshape(2, 4, 2, 4, 2), SEQ_FSDP
    )
    return jax.shard_map(
        per_device,
        mesh=torus,
        in_specs=(
            P(None, None, SEQ),
            P(None, None, SEQ),
            P(),
            P(),
            P(),
            P(),
            P(FSDP, SEQ),
            P(FSDP, SEQ),
            P(FSDP, SEQ),
            P(FSDP, SEQ),
            P(SEQ_FSDP, None),
            P(SEQ_FSDP, None),
            P(SEQ_FSDP, None),
            P(SEQ_FSDP, None),
            P(None, SEQ_FSDP),
            P(None, SEQ_FSDP),
            P(None, SEQ_FSDP),
            P(None, SEQ_FSDP),
            P(None, SEQ_FSDP),
            P(),
            P(None, SEQ_FSDP),
            P(SEQ_FSDP),
        ),
        out_specs=(
            P(),
            P(),
            P(),
            P(FSDP, SEQ),
            P(FSDP, SEQ),
            P(FSDP, SEQ),
            P(None, SEQ_FSDP),
            P(None, SEQ_FSDP),
            P(None, SEQ_FSDP),
            P(None, SEQ_FSDP),
            P(None, SEQ_FSDP),
            P(),
            P(None, SEQ_FSDP),
            P(SEQ_FSDP),
            P(None, SEQ_FSDP),
            P(None, SEQ_FSDP),
        ),
        check_vma=False,
    )
```

time: 2600 us -> 936 us (0.36)
  waiting for transfers between devices: 1910 us -> 0 us
  Pallas kernels: 0 us -> 711 us
  local copies, waits for them, and re-layouts: 197 us -> 28.1 us
  matrix products: 241 us -> 140 us
  other arithmetic: 109 us -> 38.1 us
  blocking collectives: 54.4 us -> 0 us
  starting transfers between devices: 53.4 us -> 0 us
    all_gather x4 -> x0, waiting for transfers between devices: 1010 us -> none  [the longest x2 566 us: side_by_side(): whole = lax.all_gather(both, axis, axis=dim, tiled=True)]
    pallas_call x0 -> x15, Pallas kernels: none -> 711 us  [the longest x1 402 us: gather_weights(): remote_call(body, out_shape, [ANY] * 7, [ANY] * 7, [DMA((sem_count,))], 1...]
    reduce_scatter x1 -> x0, waiting for transfers between devices: 558 us -> none  [sum_together(): lax.psum_scatter(lines, axis, tiled=True).reshape(-1)]
    unnamed x13 -> x0, waiting for transfers between devices: 320 us -> none
    dot_general x66 -> x26, matrix products: 232 us -> 132 us  [the longest x9 68.6 us: nt(): lax.dot_general(left, right, (((1,), (1,)), ((), ())), preferred_element_...]
    gather x5 -> x0, local copies, waits for them, and re-layouts: 84.1 us -> none  [the longest x2 63.4 us: per_device(): seg_at = jnp.take_along_axis(document_slot_index, spot_rows, axis=2)]
    unnamed x333 -> x52, local copies, waits for them, and re-layouts: 62 us -> 3.79 us
    psum x5 -> x0, blocking collectives: 54.4 us -> none  [over_axes(): shard = lax.psum(shard, axis)]
  transfers between devices with their start and end apart: 27 -> 0, of which waited for: 15 -> 0; matrix products, arithmetic and copies ran while one was open for 10% -> 0% of each run, Pallas kernels for 0% -> 0%
where the time goes in v1:
time: 936 us; the launch traced here: 925 us
  Pallas kernels  711 us (76%)
  matrix products  140 us (15%)
  other arithmetic  38.1 us (4%)
  local copies, waits for them, and re-layouts  28.1 us (3%)
    pallas_call x1, Pallas kernels, gather_weights(): remote_call(body, out_shape, [ANY] * 7, [ANY] * 7, [DMA((sem_count,))], 1...  402 us
    pallas_call x1, Pallas kernels, add_rows(): pl.pallas_call(body, out_shape=jax.ShapeDtypeStruct((padded, width), jnp....  80.4 us
    dot_general x9, matrix products, nt(): lax.dot_general(left, right, (((1,), (1,)), ((), ())), preferred_element_...  68.6 us
    dot_general x10, matrix products, dot(): return jnp.dot(left, right, preferred_element_type=jnp.float32)  60.2 us
    pallas_call x1, Pallas kernels, gather_and_sum(): remote_call(body, [jax.ShapeDtypeStruct((FSDP_N, *block.shape), block.dty...  53 us
    pallas_call x2, Pallas kernels, gather_fsdp(): remote_call(body, [jax.ShapeDtypeStruct((FSDP_N, *b.shape), b.dtype) for...  32.9 us
    pallas_call x1, Pallas kernels, sum_rows(): remote_call(body, jax.ShapeDtypeStruct((rows, width), jnp.float32), [VMEM...  30 us
    pallas_call x1, Pallas kernels, rows_to_columns(): remote_call(body, [jax.ShapeDtypeStruct((SEQ_N, rows, width), block.dtype...  20 us

profile of v1, /device:TPU:1, one launch (start us, length us, event | category | flops | bytes accessed | tf_op | source)
XLA Modules:
  0.0 925.1 jit_solution(8903988808258874034)
XLA Ops:
  10.9 5.8 select_reduce_fusion.1
  24.3 3.0 reshape.420
  27.6 2.8 reshape.421.refs_1_
  30.3 402.3 %gather_weights.1 = (bf16[2,4,2,4,2,16,4608]{6,5,4,3,2,1,0:T(8,128)(2,1)}, bf16[2,4,2,4,2,16,12288]{6,5,4,3,2,1,0:T(8,128)(2,1)}, bf16[2,4,2,4,2,3,16,2048]{7,6,...) custom-call(bf16[16,4608]{1,0:T(8,128)(2,1)} %pad_maximum_fusion.4.r, ...), custom_call_target="tpu_custom_call" | custom-call | tf_op jit(solution)/shard_map/gather_weights/pallas_call | solution.py:564
  435.5 10.5 %look_up.1.src = bf16[16,128,128]{2,1,0:T(8,128)(2,1)} custom-call(s32[16,128]{1,0:T(8,128)} %reshape.429.ids_ref, bf16[32000,128]{1,0:T(8,128)(2,1)} %bitcast.198), custom_call_target="tpu_custom_call" | custom-call | tf_op jit(solution)/shard_map/look_up/pallas_call | solution.py:583
  446.0 12.5 %rows_of_tokens.1 = bf16[128,2048]{1,0:T(8,128)(2,1)} custom-call(bf16[16,128,128]{2,1,0:T(8,128)(2,1)} %look_up.1.src), custom_call_target="tpu_custom_call" | custom-call | tf_op jit(solution)/shard_map/rows_of_tokens/pallas_call | solution.py:214
  463.6 5.0 fusion.2
  469.8 18.5 %key_value_window.1.kv_ref = bf16[2,320,512]{2,1,0:T(8,128)(2,1)} custom-call(f32[128,512]{1,0:T(8,128)} %slice.178.kv_ref, f32[64,512]{1,0:T(8,128)} %copy.139.cos_ref, f32[64,512]{1,0:T(8,128)} %tile.21.sin_ref), custom_call_target="tpu_custom_call" | custom-call | tf_op jit(solution)/shard_map/key_value_window/pallas_call | solution.py:665
  488.3 8.0 attend.1
  497.6 4.8 fusion.19
  502.9 18.0 %fusion.48 = f32[128,12288]{1,0:T(8,128)S(1)} fusion(bf16[2048,12288]{1,0:T(8,128)(2,1)} %bitcast.196, f32[128,2048]{1,0:T(8,128)S(1)} %get-tuple-element.180, f32[2048]{0:T(1024)S(1)} %mul.596, f32[128]{0:T(128)S(1)} %get-tuple-element.176), kind=kOutput, calls=%fused_computation.92 | convolution fusion | flops 6443237376 | bytes 57680384 | tf_op jit(solution)/shard_map/dot_general | solution.py:835
  520.9 12.6 %multiply_reduce_fusion.5 = (f32[128]{0:T(128)S(1)}, f32[128,2048]{1,0:T(8,128)S(1)}) fusion(f32[128,2048]{1,0:T(8,128)S(1)} %get-tuple-element.180, bf16[6144,2048]{1,0:T(8,128)(2,1)} %bitcast.222, f32[128,12288]{1,0:T(8,128)S(1)} %fusion.48), kind=kOutput, calls=%fused_computation.88 | convolution fusion | flops 3226730496 | bytes 33554944 | tf_op jit(solution)/shard_map/dot_general | solution.py:835
  534.5 26.9 %chosen_rows.1 = bf16[8,64,2048]{2,1,0:T(8,128)(2,1)} custom-call(bf16[64,2048]{1,0:T(8,128)(2,1)} %convolution_convert_fusion.refs_0_), custom_call_target="tpu_custom_call" | custom-call | tf_op jit(solution)/shard_map/chosen_rows/pallas_call | solution.py:131
  561.4 12.5 %fusion.200 = (f32[512]{0:T(512)S(1)}, f32[512,4000]{0,1:T(8,128)S(1)}) fusion(bf16[512,2048]{1,0:T(8,128)(2,1)} %bitcast.201, bf16[4000,2048]{1,0:T(8,128)(2,1)} %get-tuple-element.39), kind=kOutput, calls=%fused_computation.347 | convolution fusion | flops 8390655488 | bytes 26675200 | tf_op jit(solution)/shard_map/dot_general | solution.py:729
  573.9 2.2 select_reduce_fusion
  577.8 6.0 softmax_parts.1
  587.6 16.2 %fusion.17 = bf16[512,2048]{1,0:T(8,128)(2,1)} fusion(bf16[4000,2048]{1,0:T(8,128)(2,1)} %get-tuple-element.39, f32[512,4000]{0,1:T(8,128)} %copy-done.3, s32[512]{0:T(512)S(1)} %sub.189, f32[512]{0:T(512)S(1)} %log_add_fusion, f32[512]{0:T(512)S(1)} %div.112), kind=kOutput, calls=%fused_computation.28 | convolution fusion | flops 8401944576 | bytes 26679296 | tf_op jit(solution)/shard_map/dot_general | solution.py:835
  603.9 30.0 %row_gradients.1 = f32[64,2048]{1,0:T(8,128)} custom-call(bf16[8,64,2048]{2,1,0:T(8,128)(2,1)} %bitcast.200), custom_call_target="tpu_custom_call" | custom-call | tf_op jit(solution)/shard_map/row_gradients/pallas_call | solution.py:188
  635.9 16.1 %multiply_convert_fusion.3 = (bf16[128,6144]{1,0:T(8,128)(2,1)}, bf16[128,6144]{1,0:T(8,128)(2,1)}) fusion(f32[128,12288]{1,0:T(8,128)} %copy-done.5, bf16[6144,2048]{1,0:T(8,128)(2,1)} %bitcast.223, f32[128]{0:T(128)S(1)} %broadcast_multiply_fusion.2, f32[128,2048]{1,0:T(8,128)S(1)} %get-tuple-element.182, f32[128]{0:T(128)S(1)} %get-tuple-element.177, ...), kind=kOutput, calls=%fused_computation.25 | convolution fusion | flops 3233021952 | bytes 36709888 | tf_op jit(solution)/shard_map/dot_general | solution.py:729
  652.0 24.0 %multiply_reduce_fusion.2 = (f32[2048]{0:T(1024)S(1)}, f32[128]{0:T(128)S(1)}, f32[128,2048]{1,0:T(8,128)}) fusion(f32[128,2048]{1,0:T(8,128)S(1)} %get-tuple-element.180, f32[128]{0:T(128)S(1)} %get-tuple-element.176, f32[2048]{0:T(1024)S(1)} %mul.596, bf16[2048,12288]{1,0:T(8,128)(2,1)} %bitcast.197, bf16[128,6144]{1,0:T(8,128)(2,1)} %get-tuple-element.155, ...), kind=kOutput, calls=%fused_computation.82 | convolution fusion | flops 6450313216 | bytes 55591936 | tf_op jit(solution)/shard_map/dot_general | solution.py:729
  676.0 2.2 subtract_add_fusion
  678.8 6.3 fusion.4
  686.2 11.5 %attend_back.1 = (bf16[128,2048]{1,0:T(8,128)(2,1)}, bf16[2,256,512]{2,1,0:T(8,128)(2,1)}, f32[2,64,512]{2,1,0:T(8,128)}) custom-call(s32[1]{0:T(128)} %bitcast.5.start_ref, s32[4]{0:T(128)} %shift_ref.3, bf16[128,2048]{1,0:T(8,128)(2,1)} %get-tuple-element.40.q_ref, bf16[2,320,512]{2,1,0:T(8,128)(2,1)} %key_value_window.1.kv_ref, ...), custom_call_target="tpu_custom_call" | custom-call | tf_op jit(solution)/shard_map/attend_back/pallas_call | solution.py:805
  697.6 14.9 %key_value_back.1 = bf16[128,512]{1,0:T(8,128)(2,1)} custom-call(bf16[2,256,512]{2,1,0:T(8,128)(2,1)} %get-tuple-element.42.far_ref, f32[2,64,512]{2,1,0:T(8,128)} %get-tuple-element.43.own_ref, f32[64,512]{1,0:T(8,128)} %copy.139.cos_ref, f32[64,512]{1,0:T(8,128)} %tile.21.sin_ref), custom_call_target="tpu_custom_call" | custom-call | tf_op jit(solution)/shard_map/key_value_back/pallas_call | solution.py:696
  712.6 7.6 fusion
  724.4 20.0 %token_gradients.1 = (bf16[16,128,128]{2,1,0:T(8,128)(2,1)}, f32[64,128]{1,0:T(8,128)}) custom-call(bf16[128,2048]{1,0:T(8,128)(2,1)} %fusion.44.src, f32[16,64,128]{2,1,0:T(8,128)} %pad_maximum_fusion.1.part_src), custom_call_target="tpu_custom_call" | custom-call | tf_op jit(solution)/shard_map/token_gradients/pallas_call | solution.py:255
  744.5 53.0 %token_gradients_all.1 = (bf16[8,16,128,128]{3,2,1,0:T(8,128)(2,1)}, f32[64,128]{1,0:T(8,128)}) custom-call(bf16[16,128,128]{2,1,0:T(8,128)(2,1)} %get-tuple-element.44.src, f32[64,128]{1,0:T(8,128)} %get-tuple-element.45.part_src), custom_call_target="tpu_custom_call" | custom-call | tf_op jit(solution)/shard_map/token_gradients_all/pallas_call | solution.py:291
  798.9 80.4 %add_rows.1 = f32[4096,128]{1,0:T(8,128)} custom-call(s32[1,16384]{1,0:T(1,128)} %sub.198.ids_ref, bf16[16384,128]{1,0:T(8,128)(2,1)} %bitcast.199), custom_call_target="tpu_custom_call" | custom-call | tf_op jit(solution)/shard_map/add_rows/pallas_call | solution.py:621
  879.4 2.9 multiply_reduce_fusion
  885.9 10.7 %totals_seq.1.src = f32[8,128]{1,0:T(8,128)} custom-call(f32[8,128]{1,0:T(8,128)} %maximum_bitcast_fusion.src), custom_call_target="tpu_custom_call" | custom-call | tf_op jit(solution)/shard_map/totals_seq/pallas_call | solution.py:162
  896.6 6.4 totals_fsdp.1
  917.8 6.0 fusion.28
  (236 shorter events, 58.7 us)
Async XLA Ops:
  0.6 22.6 %copy-start.2 = (f32[4000,128]{1,0:T(8,128)S(1)}, f32[4000,128]{1,0:T(8,128)}, u32[]{:S(2)}) copy-start(f32[4000,128]{1,0:T(8,128)} %param.28) | copy-start | bytes 6144004
  5.6 18.7 %copy-start.13 = (s32[2,1,320]{2,1,0:T(1,128)}, s32[2,1,320]{2,1,0:T(1,128)S(1)}, u32[]{:S(2)}) copy-start(s32[2,1,320]{2,1,0:T(1,128)S(1)} %broadcast_in_dim.48.ks_ref) | copy-start | bytes 7684
  8.2 16.2 %copy-start.11 = (bf16[16,11264]{1,0:T(8,128)(2,1)S(1)}, bf16[16,11264]{1,0:T(8,128)(2,1)}, u32[]{:S(2)}) copy-start(bf16[16,11264]{1,0:T(8,128)(2,1)} %param.34) | copy-start | bytes 1081348
  432.6 2.1 copy-start.10
  458.5 4.8 copy-start.1
  469.0 19.3 %copy-start.4 = (f32[128,2560]{1,0:T(8,128)}, f32[128,2560]{1,0:T(8,128)S(1)}, u32[]{:S(2)}) copy-start(f32[128,2560]{1,0:T(8,128)S(1)} %fusion.12.q_ref) | copy-start | bytes 3932164
  520.9 12.6 %copy-start.5 = (f32[128,12288]{1,0:T(8,128)}, f32[128,12288]{1,0:T(8,128)S(1)}, u32[]{:S(2)}) copy-start(f32[128,12288]{1,0:T(8,128)S(1)} %fusion.48) | copy-start | bytes 18874372
  573.9 3.2 copy-start.3
  635.8 16.1 %copy-start.6 = (f32[128,2048]{1,0:T(8,128)}, f32[128,2048]{1,0:T(8,128)S(1)}, u32[]{:S(2)}) copy-start(f32[128,2048]{1,0:T(8,128)S(1)} %get-tuple-element.185) | copy-start | bytes 3145732
  676.0 2.4 copy-start.7
  712.6 7.7 copy-start.8
  712.6 7.7 copy-start.9
  798.8 83.4 %copy-start.12 = (f32[64,128]{1,0:T(8,128)S(1)}, f32[64,128]{1,0:T(8,128)}, u32[]{:S(2)}) copy-start(f32[64,128]{1,0:T(8,128)} %get-tuple-element.46) | copy-start | bytes 98308
  798.8 107.0 %copy-start.23 = (f32[36]{0:T(128)S(1)}, f32[36]{0:T(128)}, u32[]{:S(2)}) copy-start(f32[36]{0:T(128)} %param.43) | copy-start | bytes 436
  798.9 107.5 %copy-start.19 = (f32[3,16]{1,0:T(4,128)S(1)}, f32[3,16]{1,0:T(4,128)}, u32[]{:S(2)}) copy-start(f32[3,16]{1,0:T(4,128)} %param.36) | copy-start | bytes 580
  798.9 107.5 %copy-start.21 = (f32[3,16]{1,0:T(4,128)S(1)}, f32[3,16]{1,0:T(4,128)}, u32[]{:S(2)}) copy-start(f32[3,16]{1,0:T(4,128)} %param.38) | copy-start | bytes 580
  798.9 107.5 %copy-start.22 = (f32[3,16]{1,0:T(4,128)S(1)}, f32[3,16]{1,0:T(4,128)}, u32[]{:S(2)}) copy-start(f32[3,16]{1,0:T(4,128)} %param.37) | copy-start | bytes 580
  798.9 108.3 %copy-start.20 = (f32[4,16]{1,0:T(4,128)S(1)}, f32[4,16]{1,0:T(4,128)}, u32[]{:S(2)}) copy-start(f32[4,16]{1,0:T(4,128)} %param.42) | copy-start | bytes 772
  798.9 109.6 %copy-start.14 = (f32[8,8,8]{2,1,0:T(8,128)S(1)}, f32[8,8,8]{2,1,0:T(8,128)}, u32[]{:S(2)}) copy-start(f32[8,8,8]{2,1,0:T(8,128)} %param.41) | copy-start | bytes 6148
  879.3 36.9 %copy-start.17 = (f32[8,36]{1,0:T(8,128)S(1)}, f32[8,36]{1,0:T(8,128)}, u32[]{:S(2)}) copy-start(f32[8,36]{1,0:T(8,128)} %param.40) | copy-start | bytes 3460
  879.4 37.8 %copy-start.16 = (f32[32,16]{0,1:T(8,128)S(1)}, f32[32,16]{0,1:T(8,128)}, u32[]{:S(2)}) copy-start(f32[32,16]{0,1:T(8,128)} %param.39) | copy-start | bytes 6148
  879.4 38.4 %copy-start = (f32[4096,128]{1,0:T(8,128)S(1)}, f32[4096,128]{1,0:T(8,128)}, u32[]{:S(2)}) copy-start(f32[4096,128]{1,0:T(8,128)} %add_rows.1) | copy-start | bytes 6291460
  905.2 18.7 %copy-start.18 = (f32[8,36]{1,0:T(8,128)}, f32[8,36]{1,0:T(8,128)S(1)}, u32[]{:S(2)}) copy-start(f32[8,36]{1,0:T(8,128)S(1)} %get-tuple-element.145) | copy-start | bytes 3460
  908.6 15.2 %copy-start.15 = (f32[8,8,8]{2,1,0:T(8,128)}, f32[8,8,8]{2,1,0:T(8,128)S(1)}, u32[]{:S(2)}) copy-start(f32[8,8,8]{2,1,0:T(8,128)S(1)} %get-tuple-element.143) | copy-start | bytes 6148

commit v2 on v1

--- a/solution.py
+++ b/solution.py
@@ -302,25 +302,32 @@
     )(block, summed)
 
 
-class Piece:
-    def __init__(self, block, order, whole, halves):
-        self.block, self.order, self.whole, self.halves = block, order, whole, halves
-
-
-def gather_weights(qkvo, gate_up, down, small, head, table, ids):
+ORDER = (
+    "s", "q0", "q1", "q2", "t", "g0", "g1", "d0", "d1", "s", "s", "q0",
+    "q0", "q1", "q1", "s", "q0", "q1", "s", "s", "s", "q2", "q2", "q0",
+    "q0", "q2", "d0", "d1", "s", "s", "q0", "g0", "g1", "q1", "q1", "s",
+    "q2", "q2", "d1", "d1", "d0", "d0", "q1", "q2", "t", "d1", "d0", "g1",
+    "g1", "g0", "g0", "q0", "q0", "g1", "g0", "q0", "q2", "q2", "q1", "q1",
+    "d0", "d0", "d1", "d1", "t", "t", "q2", "d0", "q1", "d1", "t", "g0",
+    "g0", "g1", "g1", "g0", "g1",
+)
+
+
+def gather_weights(qkvo, gate_up, down, small, table, ids):
+    quarter = gate_up.shape[1] // 4
     out_shape = [
         jax.ShapeDtypeStruct((2, 4, 2, 4, 2, *qkvo.shape), qkvo.dtype),
-        jax.ShapeDtypeStruct((2, 4, 2, 4, 2, *gate_up.shape), gate_up.dtype),
-        jax.ShapeDtypeStruct((2, 4, 2, 4, 2, *down.shape), down.dtype),
+        jax.ShapeDtypeStruct((2, 4, 2, 4, 2, gate_up.shape[0], quarter), gate_up.dtype),
+        jax.ShapeDtypeStruct((2, 4, 2, 2, *down.shape), down.dtype),
         jax.ShapeDtypeStruct((2, 4, 2, 4, 2, *small.shape), small.dtype),
-        jax.ShapeDtypeStruct((head.shape[0], SEQ_N * head.shape[1]), head.dtype),
         jax.ShapeDtypeStruct((4, 2, *table.shape), table.dtype),
         jax.ShapeDtypeStruct((SEQ_N, *ids.shape), ids.dtype),
     ]
-    sem_count = 400
+    sem_count = 300
+    every = slice(None)
 
     def body(*refs):
-        ins, outs, sem = refs[:7], refs[7:14], refs[14]
+        ins, outs, sem = refs[:6], refs[6:12], refs[12]
         yh, x, c, z, yl = (lax.axis_index(a) for a in SEQ_FSDP)
         y = 2 * yh + yl
         where = {"x": x, "y": y, "z": z}
@@ -340,9 +347,16 @@
             return {"seq_0": at // 2, "fsdp_1": at % 2}
 
         other = {"seq_2": 1 - c}
+        column = [
+            (dz, dc, {"fsdp_0": (z + dz) % 4, "seq_2": (c + dc) % 2})
+            for dz in range(4)
+            for dc in range(2)
+            if dz or dc
+        ]
 
         barrier = pltpu.get_barrier_semaphore()
-        greeted = [beside("y", 1), beside("y", -1), beside("z", 1), beside("z", -1)]
+        greeted = [beside("y", 1), beside("y", -1)]
+        greeted += [device for dz, dc, device in column if dz]
         greeted += [seq_at((seq + k) % SEQ_N) for k in ALL16]
         for device in greeted:
             pl.semaphore_signal(barrier, inc=1, device_id=device, device_id_type=MESH_ID)
@@ -358,155 +372,160 @@
         def arrived(ref, rsem):
             pltpu.make_async_copy(ref, ref, rsem).wait()
 
-        def weight_stream(ref, order, whole, halves):
-            def block(done, axis, at, tail, core=c):
-                place = {"yh": yh, "x": x, "z": z, "yl": yl}
-                for a, value in [(a, slice(None)) for a in done] + [(axis, at)]:
-                    if a == "y":
-                        if isinstance(value, slice):
-                            place["yh"] = place["yl"] = value
-                        else:
-                            place["yh"], place["yl"] = value // 2, value % 2
-                    elif a is not None:
-                        place[a] = value
-                return ref.at[(place["yh"], place["x"], core, place["z"], place["yl"]) + tail]
-
-            send = [fresh() for _ in order]
-            across_s, across_r = fresh(), fresh()
-            late.append((send[0], ref.at[(0, 0, 0, pl.ds(0, 3), 0) + whole]))
-            late.append((send[1], ref.at[(0, pl.ds(0, 2), 0, pl.ds(0, 3), slice(None)) + whole]))
-            late.append(
-                (send[2], ref.at[(slice(None), slice(None), 0, pl.ds(0, 3), slice(None)) + whole])
-            )
-            late.append((across_s, ref.at[(slice(None), slice(None), c, slice(None), slice(None)) + whole]))
-            late.append((across_r, ref.at[(slice(None), slice(None), 1 - c, slice(None), slice(None)) + whole]))
-
-            def across(view):
-                remote(view, view, across_s, across_r, other)
-
-            across(block([], None, None, whole))
+        def rings(block, order, sizes, halves, across):
             for n, axis in enumerate(order):
                 done = order[:n]
                 at = where[axis]
                 before, after, far = (at + 3) % 4, (at + 1) % 4, (at + 2) % 4
-                from_before, from_after = fresh(), fresh()
-                own = block(done, axis, at, whole)
-                remote(own, own, send[n], from_before, beside(axis, 1))
-                remote(own, own, send[n], from_after, beside(axis, -1))
+                send, from_before, from_after, far_first = (fresh() for _ in range(4))
+                late.append((send, sizes[n]))
+                own = block(done, axis, at, None)
+                remote(own, own, send, from_before, beside(axis, 1))
+                remote(own, own, send, from_after, beside(axis, -1))
                 yield
-                got = block(done, axis, before, whole)
+                got = block(done, axis, before, None)
                 arrived(got, from_before)
-                far_first = fresh()
-                half = block(done, axis, before, halves[0])
-                remote(half, half, send[n], far_first, beside(axis, 1))
-                across(got)
-                got = block(done, axis, after, whole)
-                arrived(got, from_after)
-                if len(halves) > 1:
-                    far_second = fresh()
-                    half = block(done, axis, after, halves[1])
-                    remote(half, half, send[n], far_second, beside(axis, -1))
+                half = block(done, axis, before, 0)
+                remote(half, half, send, far_first, beside(axis, 1))
                 across(got)
                 yield
-                arrived(block(done, axis, far, halves[0]), far_first)
-                if len(halves) > 1:
-                    arrived(block(done, axis, far, halves[1]), far_second)
-                across(block(done, axis, far, whole))
+                got = block(done, axis, after, None)
+                arrived(got, from_after)
+                if halves:
+                    far_second = fresh()
+                    half = block(done, axis, after, 1)
+                    remote(half, half, send, far_second, beside(axis, -1))
+                across(got)
+                yield
+                arrived(block(done, axis, far, 0), far_first)
+                if halves:
+                    arrived(block(done, axis, far, 1), far_second)
+                across(block(done, axis, far, None))
+
+        def place(done, axis, at):
+            spot = {"yh": yh, "x": x, "z": z, "yl": yl}
+            for a in done:
+                if a == "y":
+                    spot["yh"] = spot["yl"] = every
+                else:
+                    spot[a] = every
+            if axis == "y":
+                spot["yh"], spot["yl"] = at // 2, at % 2
+            elif axis is not None:
+                spot[axis] = at
+            return spot
+
+        def all_stream(ref, order, tails, halves=True):
+            def block(done, axis, at, half):
+                spot = place(done, axis, at)
+                tail = tails[0 if half is None else half + 1]
+                return ref.at[(spot["yh"], spot["x"], c, spot["z"], spot["yl"]) + tail]
+
+            across_s, across_r = fresh(), fresh()
+            late.append((across_s, ref.at[(every, every, c, every, every) + tails[0]]))
+            late.append((across_r, ref.at[(every, every, 1 - c, every, every) + tails[0]]))
+
+            def across(view):
+                remote(view, view, across_s, across_r, other)
+
+            three = pl.ds(0, 3)
+            sizes = [
+                ref.at[(0, 0, 0, three, 0) + tails[0]],
+                ref.at[(0, pl.ds(0, 2), 0, three, every) + tails[0]],
+                ref.at[(every, every, 0, three, every) + tails[0]],
+            ]
+            across(block([], None, None, None))
+            yield from rings(block, order, sizes, halves, across)
+
+        def nothing(view):
+            return None
+
+        def gate_up_stream(src, ref, order, start, width):
+            tails = [
+                (every, pl.ds(start, width)),
+                (every, pl.ds(start, width // 2)),
+                (every, pl.ds(start + width // 2, width // 2)),
+            ]
+
+            def block(done, axis, at, half):
+                spot = place(done, axis, at)
+                tail = tails[0 if half is None else half + 1]
+                return ref.at[(spot["yh"], spot["x"], every, every, spot["yl"]) + tail]
+
+            marks = []
+            for dz, dc, device in column:
+                send, recv = fresh(), fresh()
+                first = pl.multiple_of(
+                    (2 * (device["fsdp_0"] % 2) + device["seq_2"]) * quarter + start, 128
+                )
+                here = ref.at[(yh, x, c, z, yl) + tails[0]]
+                remote(src.at[:, pl.ds(first, width)], here, send, recv, device)
+                late.append((send, here))
+                marks.append((ref.at[(yh, x, (c + dc) % 2, (z + 4 - dz) % 4, yl) + tails[0]], recv))
+            yield
+            for view, recv in marks:
+                arrived(view, recv)
+            three = pl.ds(0, 3)
+            sizes = [
+                ref.at[(0, three, every, every, 0) + tails[0]],
+                ref.at[(every, three, every, every, every) + tails[0]],
+            ]
+            yield from rings(block, order, sizes, True, nothing)
+
+        def down_stream(ref, order, start, width):
+            tails = [
+                (every, pl.ds(start, width)),
+                (every, pl.ds(start, width // 2)),
+                (every, pl.ds(start + width // 2, width // 2)),
+            ]
+            zh = z // 2
+
+            def block(done, axis, at, half):
+                spot = place(done, axis, at)
+                tail = tails[0 if half is None else half + 1]
+                return ref.at[(spot["yh"], spot["x"], every, spot["yl"]) + tail]
+
+            send, recv = fresh(), fresh()
+            here = ref.at[(yh, x, zh, yl) + tails[0]]
+            remote(here, here, send, recv, {"fsdp_0": (z + 2) % 4})
+            late.append((send, here))
+            yield
+            arrived(ref.at[(yh, x, 1 - zh, yl) + tails[0]], recv)
+            three = pl.ds(0, 3)
+            sizes = [
+                ref.at[(0, three, every, 0) + tails[0]],
+                ref.at[(every, three, every, every) + tails[0]],
+            ]
+            yield from rings(block, order, sizes, True, nothing)
 
         def table_stream(ref):
-            send_y, send_z, recv_y = fresh(), fresh(), fresh()
+            send_y, recv_y = fresh(), fresh()
             late.append((send_y, ref.at[0, 0]))
-            late.append((send_z, ref.at[pl.ds(0, 3)]))
             own = ref.at[z, yl]
             remote(own, own, send_y, recv_y, {"fsdp_1": 1 - yl})
             yield
             arrived(ref.at[z, 1 - yl], recv_y)
             half_rows = ref.shape[2] // 2
-            first, second = pl.ds(0, half_rows), pl.ds(half_rows, half_rows)
-            before, after, far = (z + 3) % 4, (z + 1) % 4, (z + 2) % 4
-            from_before, from_after, far_first, far_second = (fresh() for _ in range(4))
-            remote(ref.at[z], ref.at[z], send_z, from_before, beside("z", 1))
-            remote(ref.at[z], ref.at[z], send_z, from_after, beside("z", -1))
-            yield
-            arrived(ref.at[before], from_before)
-            half = ref.at[before, :, first]
-            remote(half, half, send_z, far_first, beside("z", 1))
-            arrived(ref.at[after], from_after)
-            half = ref.at[after, :, second]
-            remote(half, half, send_z, far_second, beside("z", -1))
-            yield
-            arrived(ref.at[far, :, first], far_first)
-            arrived(ref.at[far, :, second], far_second)
-
-        def head_stream(ref):
-            width = head.shape[1]
-            rows = ref.shape[0]
-
-            def cols(h, at, take=slice(None)):
-                start = pl.multiple_of(((h * 4 + at) * 2 + c) * width, width)
-                return ref.at[take, pl.ds(start, width)]
-
-            send_y, send_x, recv_y, across_s, across_r = (fresh() for _ in range(5))
-            late.append((send_y, ref.at[:, pl.ds(0, width)]))
-            late.append((send_x, ref.at[:, pl.ds(0, 6 * width)]))
-            late.append((across_s, ref.at[:, pl.ds(0, 8 * width)]))
-            late.append((across_r, ref.at[:, pl.ds(0, 8 * width)]))
-
-            def across(view):
-                remote(view, view, across_s, across_r, other)
-
-            own = cols(yh, x)
-            remote(own, own, send_y, recv_y, {"seq_0": 1 - yh})
-            across(own)
-            yield
-            got = cols(1 - yh, x)
-            arrived(got, recv_y)
-            across(got)
-            first, second = pl.ds(0, rows // 2), pl.ds(rows // 2, rows // 2)
-            before, after, far = (x + 3) % 4, (x + 1) % 4, (x + 2) % 4
-            marks = [[fresh() for _ in range(4)] for _ in range(2)]
-            for h in range(2):
-                own = cols(h, x)
-                remote(own, own, send_x, marks[h][0], beside("x", 1))
-                remote(own, own, send_x, marks[h][1], beside("x", -1))
-            yield
-            for h in range(2):
-                got = cols(h, before)
-                arrived(got, marks[h][0])
-                half = cols(h, before, first)
-                remote(half, half, send_x, marks[h][2], beside("x", 1))
-                across(got)
-                got = cols(h, after)
-                arrived(got, marks[h][1])
-                half = cols(h, after, second)
-                remote(half, half, send_x, marks[h][3], beside("x", -1))
-                across(got)
-            yield
-            for h in range(2):
-                arrived(cols(h, far, first), marks[h][2])
-                arrived(cols(h, far, second), marks[h][3])
-                across(cols(h, far))
-
-        def ids_stream(src, ref):
-            send, recv = fresh(), fresh()
-            for k in ALL16:
-                remote(src, ref.at[seq], send, recv, seq_at((seq + k) % SEQ_N))
-            late.append((send, ref.at[pl.ds(0, 15)]))
-            late.append((recv, ref.at[pl.ds(0, 15)]))
-            return
-            yield
+            part = (every, pl.ds(0, half_rows), pl.ds(half_rows, half_rows))
+
+            def block(done, axis, at, half):
+                return ref.at[at, :, part[0 if half is None else half + 1]]
+
+            yield from rings(block, ("z",), [ref.at[pl.ds(0, 3)]], True, nothing)
 
         own_views = [
-            outs[0].at[yh, x, c, z, yl],
-            outs[1].at[yh, x, c, z, yl],
-            outs[2].at[yh, x, c, z, yl],
-            outs[3].at[yh, x, c, z, yl],
-            outs[4].at[:, pl.ds(pl.multiple_of(seq * head.shape[1], head.shape[1]), head.shape[1])],
-            outs[5].at[z, yl],
-            outs[6].at[seq],
+            (ins[0], outs[0].at[yh, x, c, z, yl]),
+            (
+                ins[1].at[:, pl.ds(pl.multiple_of((2 * (z % 2) + c) * quarter, 128), quarter)],
+                outs[1].at[yh, x, c, z, yl],
+            ),
+            (ins[2], outs[2].at[yh, x, z // 2, yl]),
+            (ins[3], outs[3].at[yh, x, c, z, yl]),
+            (ins[4], outs[4].at[z, yl]),
+            (ins[5], outs[5].at[seq]),
         ]
         local = []
-        for src, dst in zip(ins, own_views):
+        for src, dst in own_views:
             copy = pltpu.make_async_copy(src, dst, fresh())
             copy.start()
             local.append(copy)
@@ -514,56 +533,212 @@
             copy.wait()
         pl.semaphore_wait(barrier, len(greeted))
 
-        turns = (("x", "y", "z"), ("y", "z", "x"), ("z", "x", "y"))
-
-        def column_streams(ref, start, width):
-            third = width // 3
-            for n, order in enumerate(turns):
-                at = start + n * third
-                yield weight_stream(
-                    ref, order,
-                    (slice(None), pl.ds(at, third)),
-                    [(slice(None), pl.ds(at + k * third // 2, third // 2)) for k in range(2)],
-                )
-
-        def down_streams(ref):
-            width = ref.shape[-1]
-            for n, order in enumerate(turns):
-                yield weight_stream(
-                    ref, order,
-                    (n, slice(None), slice(None)),
-                    [(n, slice(None), pl.ds(k * width // 2, width // 2)) for k in range(2)],
-                )
-
-        small_all = (slice(None), slice(None))
-        wide = gate_up.shape[1]
-        starts = [
-            [ids_stream(ins[6], outs[6]), table_stream(outs[5])]
-            + list(column_streams(outs[0], 0, qkvo.shape[1]))
-            + [weight_stream(outs[3], turns[0], small_all, [small_all])],
-            [head_stream(outs[4])] + list(column_streams(outs[1], 0, wide // 2)),
-            list(column_streams(outs[1], wide // 2, wide // 2)),
-            list(down_streams(outs[2])),
-        ]
-        active = []
-        while starts or active:
-            if starts:
-                active += starts.pop(0)
-            still = []
-            for stream in active:
-                try:
-                    next(stream)
-                    still.append(stream)
-                except StopIteration:
-                    pass
-            active = still
+        send, recv = fresh(), fresh()
+        for k in ALL16:
+            remote(ins[5], outs[5].at[seq], send, recv, seq_at((seq + k) % SEQ_N))
+        late.append((send, outs[5].at[pl.ds(0, 15)]))
+        late.append((recv, outs[5].at[pl.ds(0, 15)]))
+
+        third = qkvo.shape[1] // 3
+        half = quarter // 2
+        wide = down.shape[1] // 2
+        streams = {
+            "s": all_stream(outs[3], "xyz", [(every, every)] * 2, False),
+            "t": table_stream(outs[4]),
+            "g0": gate_up_stream(ins[1], outs[1], "xy", 0, half),
+            "g1": gate_up_stream(ins[1], outs[1], "yx", half, half),
+            "d0": down_stream(outs[2], "xy", 0, wide),
+            "d1": down_stream(outs[2], "yx", wide, wide),
+        }
+        for n, order in enumerate(("xyz", "yzx", "zxy")):
+            streams["q%d" % n] = all_stream(
+                outs[0], order,
+                [
+                    (every, pl.ds(n * third, third)),
+                    (every, pl.ds(n * third, third // 2)),
+                    (every, pl.ds(n * third + third // 2, third // 2)),
+                ],
+            )
+        for name in ORDER:
+            next(streams[name], None)
+        for name in sorted(streams):
+            assert next(streams[name], "end") == "end", name
         for mark, view in late:
             arrived(view, mark)
         assert used[0] <= sem_count, used[0]
 
     return remote_call(
-        body, out_shape, [ANY] * 7, [ANY] * 7, [DMA((sem_count,))], 1, "gather_weights"
-    )(qkvo, gate_up, down, small, head, table, ids)
+        body, out_shape, [ANY] * 6, [ANY] * 6, [DMA((sem_count,))], 1, "gather_weights"
+    )(qkvo, gate_up, down, small, table, ids)
+
+
+def feed_forward(rows, gate_up_w, down_w, saved, collective_id, name):
+    forward = saved is None
+    count, width = rows.shape
+    quarter = gate_up_w.shape[1]
+    units = quarter // 2
+    chunk = count // 2
+    tile = 512
+
+    def body(*refs):
+        if forward:
+            (src, gu_hbm, dn_hbm, out, gu_out, held, gu, dn, saved_v, mid, part, give, got, sem) = refs
+        else:
+            (src, gu_hbm, dn_hbm, gu_in, out, held, gu, dn, saved_v, mid, part, give, got, sem) = refs
+        c, z = lax.axis_index("seq_2"), lax.axis_index("fsdp_0")
+        sibling = {"seq_2": 1 - c}
+        partner = {"fsdp_0": z + 1 - 2 * (z % 2)}
+        used = [0]
+
+        def fresh():
+            used[0] += 1
+            return sem.at[used[0] - 1]
+
+        loads = [pltpu.make_async_copy(gu_hbm, gu, fresh()), pltpu.make_async_copy(dn_hbm, dn, fresh())]
+        if not forward:
+            loads.append(pltpu.make_async_copy(gu_in, saved_v, fresh()))
+            loads = [loads[1], loads[2], loads[0]]
+        for load in loads:
+            load.start()
+
+        barrier = pltpu.get_barrier_semaphore()
+        for device in (sibling, partner):
+            pl.semaphore_signal(barrier, inc=1, device_id=device, device_id_type=MESH_ID)
+        pl.semaphore_wait(barrier, 2)
+
+        started = []
+
+        def remote(src_ref, dst_ref, device):
+            copy = pltpu.make_async_remote_copy(
+                src_ref=src_ref, dst_ref=dst_ref, send_sem=fresh(), recv_sem=fresh(),
+                device_id=device, device_id_type=MESH_ID,
+            )
+            copy.start()
+            started.append(copy)
+            return copy
+
+        def lines(block, k=None):
+            if k is None:
+                return pl.ds(block * count, count)
+            return pl.ds(block * count + k * chunk, chunk)
+
+        along = [
+            remote(src.at[pl.ds(k * chunk, chunk)], held.at[lines(2, k)], partner) for k in range(2)
+        ]
+        beside = remote(src, held.at[lines(1)], sibling)
+        held[lines(0), :] = src[...]
+
+        def first_product(pair):
+            mine = pl.ds(pair * 2 * count, 2 * count)
+
+            def step(n, carry):
+                at = pl.multiple_of(n * tile, tile)
+                low, high = pl.ds(at, tile), pl.ds(pl.multiple_of(at + units, tile), tile)
+                block = held[mine, :]
+                if forward:
+                    gate = jnp.dot(block, gu[:, low], preferred_element_type=jnp.float32)
+                    up = jnp.dot(block, gu[:, high], preferred_element_type=jnp.float32)
+                    saved_v[mine, low] = gate
+                    saved_v[mine, high] = up
+                    mid[:, low] = (gate * jax.nn.sigmoid(gate) * up).astype(jnp.bfloat16)
+                else:
+                    d_hidden = nt(block, dn[low, :])
+                    gate, up = saved_v[mine, low], saved_v[mine, high]
+                    sigmoid_of = jax.nn.sigmoid(gate)
+                    mid[:, low] = (
+                        d_hidden * up * sigmoid_of * (1.0 + gate * (1.0 - sigmoid_of))
+                    ).astype(jnp.bfloat16)
+                    mid[:, high] = (d_hidden * gate * sigmoid_of).astype(jnp.bfloat16)
+                return carry
+
+            lax.fori_loop(0, units // tile, step, 0)
+
+        def second_product(pair):
+            def step(n, carry):
+                at = pl.ds(pl.multiple_of(n * tile, tile), tile)
+                if forward:
+                    part[pair, :, at] = jnp.dot(
+                        mid[...], dn[:, at], preferred_element_type=jnp.float32
+                    )
+                else:
+                    part[pair, :, at] = nt(mid[...], gu[at, :])
+                return carry
+
+            lax.fori_loop(0, width // tile, step, 0)
+
+        loads[0].wait()
+        if not forward:
+            loads[1].wait()
+        beside.wait_recv()
+        first_product(0)
+        along[0].wait_recv()
+        passed = [remote(held.at[lines(2, 0)], held.at[lines(3, 0)], sibling)]
+        loads[-1].wait()
+        second_product(0)
+        along[1].wait_recv()
+        passed.append(remote(held.at[lines(2, 1)], held.at[lines(3, 1)], sibling))
+        give[0] = part[0, count:, :].astype(jnp.bfloat16)
+        home = remote(give.at[0], got.at[0], sibling)
+        if forward:
+            stores = [
+                pltpu.make_async_copy(
+                    saved_v.at[pl.ds(0, 2 * count)], gu_out.at[pl.ds(0, 2 * count)], fresh()
+                )
+            ]
+            stores[0].start()
+        for copy in passed:
+            copy.wait_recv()
+        first_product(1)
+        if forward:
+            stores.append(
+                pltpu.make_async_copy(
+                    saved_v.at[pl.ds(2 * count, 2 * count)], gu_out.at[pl.ds(2 * count, 2 * count)], fresh()
+                )
+            )
+            stores[1].start()
+        second_product(1)
+        give[1] = part[1, count:, :].astype(jnp.bfloat16)
+        over = remote(give.at[1], got.at[1], sibling)
+        over.wait_recv()
+        back = []
+        for k in range(2):
+            some = pl.ds(k * chunk, chunk)
+            give[2, some, :] = (part[1, some, :] + got[1, some, :].astype(jnp.float32)).astype(
+                jnp.bfloat16
+            )
+            back.append(remote(give.at[2, some], got.at[2, some], partner))
+        home.wait_recv()
+        out[...] = part[0, 0:count, :] + got[0].astype(jnp.float32)
+        for k in range(2):
+            some = pl.ds(k * chunk, chunk)
+            back[k].wait_recv()
+            out[some, :] += got[2, some, :].astype(jnp.float32)
+        for copy in started:
+            copy.wait_send()
+        if forward:
+            for copy in stores:
+                copy.wait()
+
+    scratch = [
+        pltpu.VMEM((4 * count, width), jnp.bfloat16),
+        pltpu.VMEM(gate_up_w.shape, jnp.bfloat16),
+        pltpu.VMEM(down_w.shape, jnp.bfloat16),
+        pltpu.VMEM((4 * count, quarter), jnp.float32),
+        pltpu.VMEM((2 * count, units if forward else quarter), jnp.bfloat16),
+        pltpu.VMEM((2, 2 * count, width), jnp.float32),
+        pltpu.VMEM((3, count, width), jnp.bfloat16),
+        pltpu.VMEM((3, count, width), jnp.bfloat16),
+        DMA((24,)),
+    ]
+    total = jax.ShapeDtypeStruct((count, width), jnp.float32)
+    if forward:
+        products = jax.ShapeDtypeStruct((4 * count, quarter), jnp.float32)
+        return remote_call(
+            body, [total, products], [VMEM, ANY, ANY], [VMEM, ANY], scratch, collective_id, name
+        )(rows, gate_up_w, down_w)
+    return remote_call(
+        body, total, [VMEM, ANY, ANY, ANY], VMEM, scratch, collective_id, name
+    )(rows, gate_up_w, down_w, saved)
 
 
 def look_up(table, ids):
@@ -596,37 +771,53 @@
 
 def add_rows(gradient, local_ids, vocab):
     count, width = gradient.shape
-    tile = 512
-    padded = -(-vocab // 512) * 512
-
-    def body(ids_ref, grad_ref, out_ref):
+    tile, low_n = 1024, 1024
+
+    def body(ids_ref, grad_ref, out_ref, total, spread):
         @pl.when(pl.program_id(0) == 0)
         def _():
-            out_ref[...] = jnp.zeros_like(out_ref)
+            total[...] = jnp.zeros_like(total)
 
         ids = ids_ref[...]
+        high, low = ids >> 10, ids & 1023
+        part = lax.broadcasted_iota(jnp.int32, (8, tile), 0)
+        which = jnp.transpose((part == high).astype(jnp.float32))
         grad = grad_ref[...]
+        for h in range(4):
+            spread[:, h * width : (h + 1) * width] = jnp.where(
+                which[:, h : h + 1] > 0.5, grad.astype(jnp.float32), 0.0
+            ).astype(jnp.bfloat16)
 
         def step(n, carry):
-            start = pl.multiple_of(n * 512, 512)
-            row = lax.broadcasted_iota(jnp.int32, (512, tile), 0) + start
-            hot = (row == ids).astype(jnp.float32).astype(jnp.bfloat16)
-            out_ref[pl.ds(start, 512), :] += jnp.dot(
-                hot, grad, preferred_element_type=jnp.float32
+            start = pl.multiple_of(n * 256, 256)
+            row = lax.broadcasted_iota(jnp.int32, (256, tile), 0) + start
+            hot = (row == low).astype(jnp.float32).astype(jnp.bfloat16)
+            total[pl.ds(start, 256), :] += jnp.dot(
+                hot, spread[...], preferred_element_type=jnp.float32
             )
             return carry
 
-        lax.fori_loop(0, padded // 512, step, 0)
+        lax.fori_loop(0, low_n // 256, step, 0)
+
+        @pl.when(pl.program_id(0) == count // tile - 1)
+        def _():
+            for h in range(4):
+                rows = min(low_n, vocab - h * low_n)
+                out_ref[h * low_n : h * low_n + rows, :] = total[0:rows, h * width : (h + 1) * width]
 
     return pl.pallas_call(
         body,
-        out_shape=jax.ShapeDtypeStruct((padded, width), jnp.float32),
+        out_shape=jax.ShapeDtypeStruct((vocab, width), jnp.float32),
         grid=(count // tile,),
         in_specs=[
             pl.BlockSpec((1, tile), lambda i: (0, i)),
             pl.BlockSpec((tile, width), lambda i: (i, 0)),
         ],
-        out_specs=pl.BlockSpec((padded, width), lambda i: (0, 0)),
+        out_specs=pl.BlockSpec((vocab, width), lambda i: (0, 0)),
+        scratch_shapes=[
+            pltpu.VMEM((low_n, 4 * width), jnp.float32),
+            pltpu.VMEM((tile, 4 * width), jnp.bfloat16),
+        ],
         compiler_params=pltpu.CompilerParams(vmem_limit_bytes=VMEM_LIMIT),
         name="add_rows",
     )(local_ids.reshape(1, count), gradient)
@@ -938,10 +1129,11 @@
     vocab_dev = embedding.shape[0]
 
     qkvo_own = jnp.concatenate([frozen_query_key_value_weight, frozen_attention_output_weight], 1)
-    gate_up_own = jnp.pad(
-        frozen_gate_up_weight.reshape(16, 256, 44), ((0, 0), (0, 0), (0, 4))
-    ).reshape(16, 2 * PAD_FF)
-    down_own = jnp.pad(frozen_down_weight, ((0, 4), (0, 0))).reshape(3, 16, 2048)
+    gate_up_own = frozen_gate_up_weight.reshape(16, 2, 8, 2, 2, 2, 2, 44).transpose(
+        0, 5, 3, 1, 2, 4, 6, 7
+    )
+    gate_up_own = jnp.pad(gate_up_own, [(0, 0)] * 7 + [(0, 4)]).reshape(16, 2 * PAD_FF)
+    down_own = jnp.pad(frozen_down_weight, ((0, 4), (0, 0)))
     small_own = jnp.pad(
         jnp.concatenate(
             [
@@ -953,19 +1145,20 @@
         (0, 1024 - 848),
     ).reshape(8, 128)
     ids_own = jnp.pad(input_token_index.reshape(16, TOK), ((0, 0), (0, 64)))
-    qkvo, gate_up_w, down_w, small, head, table, ids = gather_weights(
+    qkvo, gate_up_w, down_w, small, table, ids = gather_weights(
         qkvo_own,
         gate_up_own,
         down_own,
         small_own,
-        frozen_output_table,
         embedding.astype(jnp.bfloat16),
         ids_own,
     )
     qkvo = qkvo.reshape(2048, 4608)
     w_qkv, w_out = qkvo[:, :2560], qkvo[:, 2560:]
-    gate_up_w = gate_up_w.reshape(2048, 2 * PAD_FF)
-    down_w = down_w.reshape(PAD_FF, 2048)
+    gate_up_w = gate_up_w.reshape(2048, PAD_FF // 2)
+    down_w = down_w.reshape(PAD_FF // 4, 2048)
+    head_own, ids = lax.optimization_barrier((frozen_output_table, ids))
+    head = lax.all_gather(head_own, SEQ, axis=1, tiled=True)
     small = small.reshape(128, 1024)
     down_full = small[:, :512].reshape(128, 32, 16).transpose(1, 0, 2).reshape(32, 2048)
     gain = small[:, 512:560].reshape(128, 3, 16).transpose(1, 0, 2).reshape(3, 2048)
@@ -1031,10 +1224,8 @@
     x_mid = x_start + dot(attended, w_out) + ADAPTER_SCALE * dot(adapter_mid, b_out)
 
     normed_two = (x_mid * norm_scale(x_mid) * gain[1]).astype(jnp.bfloat16)
-    gate_up = dot(normed_two, gate_up_w)
-    gate, up = gate_up[:, :PAD_FF], gate_up[:, PAD_FF:]
-    hidden = (jax.nn.silu(gate) * up).astype(jnp.bfloat16)
-    x_end = x_mid + dot(hidden, down_w)
+    hidden_sum, gate_up = feed_forward(normed_two, gate_up_w, down_w, None, 12, "feed_forward")
+    x_end = x_mid + hidden_sum
     normed_end = (x_end * norm_scale(x_end) * gain[2]).astype(jnp.bfloat16)
 
     chosen = dot(pick.astype(jnp.bfloat16), normed_end).astype(jnp.bfloat16)
@@ -1066,12 +1257,10 @@
 
     upstream = lax.dot_general(pick, d_chosen, (((0,), (0,)), ((), ())), precision=HIGHEST)
     d_end, gain_end = norm_back(x_end, gain[2], upstream)
-    d_hidden = nt(d_end.astype(jnp.bfloat16), down_w)
-    sigmoid_of = jax.nn.sigmoid(gate)
-    d_gate = d_hidden * up * sigmoid_of * (1.0 + gate * (1.0 - sigmoid_of))
-    d_up = d_hidden * gate * sigmoid_of
-    d_gate_up = jnp.concatenate([d_gate.astype(jnp.bfloat16), d_up.astype(jnp.bfloat16)], 1)
-    back_two, gain_mid = norm_back(x_mid, gain[1], nt(d_gate_up, gate_up_w))
+    d_normed = feed_forward(
+        d_end.astype(jnp.bfloat16), gate_up_w, down_w, gate_up, 13, "feed_forward_back"
+    )
+    back_two, gain_mid = norm_back(x_mid, gain[1], d_normed)
     d_mid = d_end + back_two
 
     d_branch = d_mid.astype(jnp.bfloat16)

time: 936 us -> 754 us (0.81)
  Pallas kernels: 711 us -> 576 us
  matrix products: 140 us -> 74.1 us
  between operations: 7 us -> 20.7 us
    pallas_call x2 -> x4, Pallas kernels: 483 us -> 338 us  [the longest x1 217 us: gather_weights(): remote_call(body, out_shape, [ANY] * 6, [ANY] * 6, [DMA((sem_count,))], 1...]
    dot_general x9 -> x7, matrix products: 68.6 us -> 28.9 us  [nt(): lax.dot_general(left, right, (((1,), (1,)), ((), ())), preferred_element_...]
    dot_general x10 -> x8, matrix products: 60.2 us -> 31.6 us  [dot(): return jnp.dot(left, right, preferred_element_type=jnp.float32)]
  transfers between devices with their start and end apart: 0 -> 1, of which waited for: 0 -> 0; matrix products, arithmetic and copies ran while one was open for 0% -> 5% of each run, Pallas kernels for 0% -> 17%
where the time goes in v2:
time: 754 us; the launch traced here: 745 us
  Pallas kernels  576 us (76%)
  matrix products  74.1 us (10%)
  other arithmetic  44.7 us (6%)
  local copies, waits for them, and re-layouts  30 us (4%)
  between operations  20.7 us (3%)
    pallas_call x1, Pallas kernels, gather_weights(): remote_call(body, out_shape, [ANY] * 6, [ANY] * 6, [DMA((sem_count,))], 1...  217 us
    pallas_call x1, Pallas kernels, gather_and_sum(): remote_call(body, [jax.ShapeDtypeStruct((FSDP_N, *block.shape), block.dty...  53.7 us
    pallas_call x1, Pallas kernels, add_rows(): pl.pallas_call(body, out_shape=jax.ShapeDtypeStruct((vocab, width), jnp.f...  42.6 us
    pallas_call x1, Pallas kernels, feed_forward(): remote_call(body, [total, products], [VMEM, ANY, ANY], [VMEM, ANY], scrat...  40 us
    pallas_call x1, Pallas kernels, feed_forward(): remote_call(body, total, [VMEM, ANY, ANY, ANY], VMEM, scratch, collective...  38.2 us
    pallas_call x2, Pallas kernels, gather_fsdp(): remote_call(body, [jax.ShapeDtypeStruct((FSDP_N, *b.shape), b.dtype) for...  32.8 us
    dot_general x8, matrix products, dot(): return jnp.dot(left, right, preferred_element_type=jnp.float32)  31.6 us
    pallas_call x1, Pallas kernels, sum_rows(): remote_call(body, jax.ShapeDtypeStruct((rows, width), jnp.float32), [VMEM...  29.8 us
  transfers between devices with their start and end apart: 1, of which 0 were waited for; matrix products, arithmetic and copies ran while one was open for 5% of the time, Pallas kernels for 17%

profile of v2, /device:TPU:1, one launch (start us, length us, event | category | flops | bytes accessed | tf_op | source)
XLA Modules:
  0.0 745.0 jit_solution(8840825501737118868)
XLA Ops:
  9.7 2.6 convert_element_type.178.refs_4_
  12.3 4.0 reshape.417
  19.4 2.8 reshape.418.refs_1_
  24.1 217.4 %gather_weights.1 = (bf16[2,4,2,4,2,16,4608]{6,5,4,3,2,1,0:T(8,128)(2,1)}, bf16[2,4,2,4,2,16,3072]{6,5,4,3,2,1,0:T(8,128)(2,1)}, bf16[2,4,2,2,48,2048]{5,4,3,2,1...) custom-call(bf16[16,4608]{1,0:T(8,128)(2,1)} %pad_maximum_fusion.4.r, ...), custom_call_target="tpu_custom_call" | custom-call | tf_op jit(solution)/shard_map/gather_weights/pallas_call | solution.py:570
  244.8 6.0 select_reduce_fusion.1
  254.3 10.1 %look_up.1.src = bf16[16,128,128]{2,1,0:T(8,128)(2,1)} custom-call(s32[16,128]{1,0:T(8,128)} %reshape.425.ids_ref, bf16[32000,128]{1,0:T(8,128)(2,1)} %bitcast.198), custom_call_target="tpu_custom_call" | custom-call | tf_op jit(solution)/shard_map/look_up/pallas_call | solution.py:758
  264.4 18.6 %rows_of_tokens.1 = bf16[128,2048]{1,0:T(8,128)(2,1)} custom-call(bf16[16,128,128]{2,1,0:T(8,128)(2,1)} %look_up.1.src), custom_call_target="tpu_custom_call" | custom-call | tf_op jit(solution)/shard_map/rows_of_tokens/pallas_call | solution.py:214
  288.2 6.5 fusion.2
  295.9 20.7 %key_value_window.1.kv_ref = bf16[2,320,512]{2,1,0:T(8,128)(2,1)} custom-call(f32[128,512]{1,0:T(8,128)} %slice.166.kv_ref, f32[64,512]{1,0:T(8,128)} %copy.144.cos_ref, f32[64,512]{1,0:T(8,128)} %tile.21.sin_ref), custom_call_target="tpu_custom_call" | custom-call | tf_op jit(solution)/shard_map/key_value_window/pallas_call | solution.py:856
  316.7 8.3 %attend.1 = (bf16[128,2048]{1,0:T(8,128)(2,1)}, bf16[128,2048]{1,0:T(8,128)(2,1)}) custom-call(s32[1]{0:T(128)} %bitcast.5.start_ref, s32[4]{0:T(128)} %shift_ref.3, f32[128,2560]{1,0:T(8,128)} %copy-done.4, bf16[2,320,512]{2,1,0:T(8,128)(2,1)} %key_value_window.1.kv_ref, f32[64,512]{1,0:T(8,128)} %copy.144.cos_ref, f32[64,512]{1,0:T(8,128)} %tile.21.sin_ref, ...), custom_call_target="tpu_custom_call" | custom-call | tf_op jit(solution)/shard_map/attend/pallas_call | solution.py:951
  326.3 4.8 fusion.15
  332.5 40.0 %feed_forward.1 = (f32[128,2048]{1,0:T(8,128)}, f32[512,3072]{1,0:T(8,128)}) custom-call(bf16[128,2048]{1,0:T(8,128)(2,1)} %multiply_convert_fusion.5.refs_0_, bf16[2048,3072]{1,0:T(8,128)(2,1)} %bitcast.194, bf16[1536,2048]{1,0:T(8,128)(2,1)} %bitcast.196), custom_call_target="tpu_custom_call" | custom-call | tf_op jit(solution)/shard_map/feed_forward/pallas_call | solution.py:736
  375.0 26.9 %chosen_rows.1 = bf16[8,64,2048]{2,1,0:T(8,128)(2,1)} custom-call(bf16[64,2048]{1,0:T(8,128)(2,1)} %convolution_convert_fusion.refs_0_), custom_call_target="tpu_custom_call" | custom-call | tf_op jit(solution)/shard_map/chosen_rows/pallas_call | solution.py:131
  403.9 12.5 %fusion.189 = (f32[512]{0:T(512)S(1)}, f32[512,4000]{0,1:T(8,128)S(1)}) fusion(bf16[512,2048]{1,0:T(8,128)(2,1)} %bitcast.202, bf16[4000,2048]{1,0:T(8,128)(2,1)} %all-gather.2.cloned.1.call-done), kind=kOutput, calls=%fused_computation.332 | convolution fusion | flops 8390655488 | bytes 26675200 | tf_op jit(solution)/shard_map/dot_general | solution.py:920
  416.4 2.2 select_reduce_fusion
  420.3 5.9 softmax_parts.1
  428.7 16.1 %fusion.13 = bf16[512,2048]{1,0:T(8,128)(2,1)} fusion(bf16[4000,2048]{1,0:T(8,128)(2,1)} %all-gather.2.cloned.1.call-done, f32[512,4000]{0,1:T(8,128)} %copy-done.3, s32[512]{0:T(512)S(1)} %sub.186, f32[512]{0:T(512)S(1)} %log_add_fusion, f32[512]{0:T(512)S(1)} %div.106), kind=kOutput, calls=%fused_computation.20 | convolution fusion | flops 8401944576 | bytes 26679296 | tf_op jit(solution)/shard_map/dot_general | solution.py:1026
  444.8 29.8 %row_gradients.1 = f32[64,2048]{1,0:T(8,128)} custom-call(bf16[8,64,2048]{2,1,0:T(8,128)(2,1)} %bitcast.201), custom_call_target="tpu_custom_call" | custom-call | tf_op jit(solution)/shard_map/row_gradients/pallas_call | solution.py:188
  474.6 2.6 multiply_reduce_fusion.1
  478.2 38.2 %feed_forward_back.1 = f32[128,2048]{1,0:T(8,128)} custom-call(bf16[128,2048]{1,0:T(8,128)(2,1)} %fusion.178.refs_0_, bf16[2048,3072]{1,0:T(8,128)(2,1)} %bitcast.195, bf16[1536,2048]{1,0:T(8,128)(2,1)} %bitcast.197, f32[512,3072]{1,0:T(8,128)} %get-tuple-element.45.refs_3_), custom_call_target="tpu_custom_call" | custom-call | tf_op jit(solution)/shard_map/feed_forward_back/pallas_call | solution.py:739
  516.4 2.1 multiply_reduce_fusion.2
  520.8 6.3 fusion.4
  529.1 11.1 %attend_back.1 = (bf16[128,2048]{1,0:T(8,128)(2,1)}, bf16[2,256,512]{2,1,0:T(8,128)(2,1)}, f32[2,64,512]{2,1,0:T(8,128)}) custom-call(s32[1]{0:T(128)} %bitcast.5.start_ref, s32[4]{0:T(128)} %shift_ref.3, bf16[128,2048]{1,0:T(8,128)(2,1)} %get-tuple-element.46.q_ref, bf16[2,320,512]{2,1,0:T(8,128)(2,1)} %key_value_window.1.kv_ref, ...), custom_call_target="tpu_custom_call" | custom-call | tf_op jit(solution)/shard_map/attend_back/pallas_call | solution.py:996
  540.1 15.5 %key_value_back.1 = bf16[128,512]{1,0:T(8,128)(2,1)} custom-call(bf16[2,256,512]{2,1,0:T(8,128)(2,1)} %get-tuple-element.48.far_ref, f32[2,64,512]{2,1,0:T(8,128)} %get-tuple-element.49.own_ref, f32[64,512]{1,0:T(8,128)} %copy.144.cos_ref, f32[64,512]{1,0:T(8,128)} %tile.21.sin_ref), custom_call_target="tpu_custom_call" | custom-call | tf_op jit(solution)/shard_map/key_value_back/pallas_call | solution.py:887
  555.7 7.9 %fusion = f32[128,2048]{1,0:T(8,128)S(1)} fusion(bf16[2048,4608]{1,0:T(8,128)(2,1)} %bitcast.225, bf16[128,512]{1,0:T(8,128)(2,1)} %key_value_back.1, bf16[128,2048]{1,0:T(8,128)(2,1)} %get-tuple-element.47), kind=kOutput, calls=%fused_computation | convolution fusion | flops 1343488000 | bytes 12189696 | tf_op jit(solution)/shard_map/dot_general | solution.py:920
  571.2 19.9 %token_gradients.1 = (bf16[16,128,128]{2,1,0:T(8,128)(2,1)}, f32[64,128]{1,0:T(8,128)}) custom-call(bf16[128,2048]{1,0:T(8,128)(2,1)} %fusion.39.src, f32[16,64,128]{2,1,0:T(8,128)} %pad_maximum_fusion.1.part_src), custom_call_target="tpu_custom_call" | custom-call | tf_op jit(solution)/shard_map/token_gradients/pallas_call | solution.py:255
  591.1 53.7 %token_gradients_all.1 = (bf16[8,16,128,128]{3,2,1,0:T(8,128)(2,1)}, f32[64,128]{1,0:T(8,128)}) custom-call(bf16[16,128,128]{2,1,0:T(8,128)(2,1)} %get-tuple-element.50.src, f32[64,128]{1,0:T(8,128)} %get-tuple-element.51.part_src), custom_call_target="tpu_custom_call" | custom-call | tf_op jit(solution)/shard_map/token_gradients_all/pallas_call | solution.py:291
  648.5 42.6 %add_rows.1 = f32[4000,128]{1,0:T(8,128)} custom-call(s32[1,16384]{1,0:T(1,128)} %sub.194.ids_ref, bf16[16384,128]{1,0:T(8,128)(2,1)} %bitcast.199), custom_call_target="tpu_custom_call" | custom-call | tf_op jit(solution)/shard_map/add_rows/pallas_call | solution.py:808
  691.1 2.9 multiply_reduce_fusion
  698.8 10.4 %totals_seq.1.src = f32[8,128]{1,0:T(8,128)} custom-call(f32[8,128]{1,0:T(8,128)} %maximum_bitcast_fusion.src), custom_call_target="tpu_custom_call" | custom-call | tf_op jit(solution)/shard_map/totals_seq/pallas_call | solution.py:162
  709.2 6.5 totals_fsdp.1
  729.0 6.1 fusion.24
  (256 shorter events, 63.4 us)
Async XLA Ops:
  7.2 10.2 %copy-start.9 = (bf16[44,2048]{1,0:T(8,128)(2,1)S(1)}, bf16[44,2048]{1,0:T(8,128)(2,1)}, u32[]{:S(2)}) copy-start(bf16[44,2048]{1,0:T(8,128)(2,1)} %param.35) | copy-start | bytes 540676
  7.2 396.7 %all-gather.2.cloned.1.call-start = ((), (), s32[]{:S(2)}) async-start(), calls=%async_computation | async-start | bytes 17408000 | tf_op jit(solution)/shard_map/all_gather | solution.py:1161
  12.3 9.8 %copy-start.21 = (s32[2,8,64]{2,1,0:T(8,128)S(1)}, s32[2,8,64]{2,1,0:T(8,128)}, u32[]{:S(2)}) copy-start(s32[2,8,64]{2,1,0:T(8,128)} %param.22) | copy-start | bytes 12292
  12.3 10.4 %copy-start.11 = (bf16[16,2560]{1,0:T(8,128)(2,1)S(1)}, bf16[16,2560]{1,0:T(8,128)(2,1)}, u32[]{:S(2)}) copy-start(bf16[16,2560]{1,0:T(8,128)(2,1)} %param.32) | copy-start | bytes 245764
  12.3 10.4 %copy-start.12 = (bf16[16,2048]{1,0:T(8,128)(2,1)S(1)}, bf16[16,2048]{1,0:T(8,128)(2,1)}, u32[]{:S(2)}) copy-start(bf16[16,2048]{1,0:T(8,128)(2,1)} %param.33) | copy-start | bytes 196612
  19.3 223.9 %copy-start.22 = (s32[2,8,32]{2,1,0:T(8,128)S(1)}, s32[2,8,32]{2,1,0:T(8,128)}, u32[]{:S(2)}) copy-start(s32[2,8,32]{2,1,0:T(8,128)} %param.23) | copy-start | bytes 6148
  19.3 224.0 %copy-start.10 = (s32[2,8,1024]{2,1,0:T(8,128)S(1)}, s32[2,8,1024]{2,1,0:T(8,128)}, u32[]{:S(2)}) copy-start(s32[2,8,1024]{2,1,0:T(8,128)} %param.25) | copy-start | bytes 196612
  19.3 225.2 %copy-start.14 = (s32[2,8,512]{2,1,0:T(8,128)S(1)}, s32[2,8,512]{2,1,0:T(8,128)}, u32[]{:S(2)}) copy-start(s32[2,8,512]{2,1,0:T(8,128)} %param.24) | copy-start | bytes 98308
  22.1 222.6 %copy-start.29 = (s32[2,8]{1,0:T(2,128)S(1)}, s32[2,8]{1,0:T(2,128)}, u32[]{:S(2)}) copy-start(s32[2,8]{1,0:T(2,128)} %param.26) | copy-start | bytes 196
  241.5 12.0 %copy-start.8 = (s32[16,16,128]{2,1,0:T(8,128)S(1)}, s32[16,16,128]{2,1,0:T(8,128)}, u32[]{:S(2)}) copy-start(s32[16,16,128]{2,1,0:T(8,128)} %get-tuple-element.36) | copy-start | bytes 393220
  243.5 20.8 %copy-start.13 = (s32[2,1,320]{2,1,0:T(1,128)}, s32[2,1,320]{2,1,0:T(1,128)S(1)}, u32[]{:S(2)}) copy-start(s32[2,1,320]{2,1,0:T(1,128)S(1)} %broadcast_in_dim.48.ks_ref) | copy-start | bytes 7684
  283.0 4.2 copy-start.1
  287.9 276.9 %copy-start.25 = (f32[128]{0:T(128)}, f32[128]{0:T(128)S(1)}, u32[]{:S(2)}) copy-start(f32[128]{0:T(128)S(1)} %get-tuple-element.180) | copy-start | bytes 1540
  295.1 21.5 %copy-start.4 = (f32[128,2560]{1,0:T(8,128)}, f32[128,2560]{1,0:T(8,128)S(1)}, u32[]{:S(2)}) copy-start(f32[128,2560]{1,0:T(8,128)S(1)} %fusion.12.q_ref) | copy-start | bytes 3932164
  416.4 3.2 copy-start.3
  520.8 6.3 copy-start.5
  555.7 8.0 %copy-start.6 = (bf16[128,512]{1,0:T(8,128)(2,1)S(1)}, bf16[128,512]{1,0:T(8,128)(2,1)}, u32[]{:S(2)}) copy-start(bf16[128,512]{1,0:T(8,128)(2,1)} %key_value_back.1) | copy-start | bytes 393220
  555.7 8.0 %copy-start.7 = (bf16[128,2048]{1,0:T(8,128)(2,1)S(1)}, bf16[128,2048]{1,0:T(8,128)(2,1)}, u32[]{:S(2)}) copy-start(bf16[128,2048]{1,0:T(8,128)(2,1)} %get-tuple-element.47) | copy-start | bytes 1572868
  555.7 8.7 %copy-start.2 = (bf16[128,2048]{1,0:T(8,128)(2,1)S(1)}, bf16[128,2048]{1,0:T(8,128)(2,1)}, u32[]{:S(2)}) copy-start(bf16[128,2048]{1,0:T(8,128)(2,1)} %rows_of_tokens.1) | copy-start | bytes 1572868
  648.5 47.4 %copy-start.18 = (f32[288,4]{0,1:T(4,128)S(1)}, f32[288,4]{0,1:T(4,128)}, u32[]{:S(2)}) copy-start(f32[288,4]{0,1:T(4,128)} %convert_bitcast_fusion) | copy-start | bytes 13828
  648.5 70.8 %copy-start.15 = (f32[8,8,8]{2,1,0:T(8,128)S(1)}, f32[8,8,8]{2,1,0:T(8,128)}, u32[]{:S(2)}) copy-start(f32[8,8,8]{2,1,0:T(8,128)} %param.41) | copy-start | bytes 6148
  648.5 71.9 %copy-start.24 = (f32[8,8]{1,0:T(8,128)S(1)}, f32[8,8]{1,0:T(8,128)}, u32[]{:S(2)}) copy-start(f32[8,8]{1,0:T(8,128)} %fusion.141) | copy-start | bytes 772
  691.1 35.7 %copy-start.26 = (f32[4,16]{1,0:T(4,128)S(1)}, f32[4,16]{1,0:T(4,128)}, u32[]{:S(2)}) copy-start(f32[4,16]{1,0:T(4,128)} %param.42) | copy-start | bytes 772
  691.1 36.7 %copy-start.17 = (f32[32,16]{0,1:T(8,128)S(1)}, f32[32,16]{0,1:T(8,128)}, u32[]{:S(2)}) copy-start(f32[32,16]{0,1:T(8,128)} %param.39) | copy-start | bytes 6148
  691.1 37.4 %copy-start.30 = (f32[36]{0:T(128)S(1)}, f32[36]{0:T(128)}, u32[]{:S(2)}) copy-start(f32[36]{0:T(128)} %param.43) | copy-start | bytes 436
  691.1 37.9 %copy-start = (f32[4000,128]{1,0:T(8,128)S(1)}, f32[4000,128]{1,0:T(8,128)}, u32[]{:S(2)}) copy-start(f32[4000,128]{1,0:T(8,128)} %add_rows.1) | copy-start | bytes 6144004
  719.5 15.6 %copy-start.16 = (f32[8,8,8]{2,1,0:T(8,128)}, f32[8,8,8]{2,1,0:T(8,128)S(1)}, u32[]{:S(2)}) copy-start(f32[8,8,8]{2,1,0:T(8,128)S(1)} %get-tuple-element.149) | copy-start | bytes 6148
  728.5 7.3 copy-start.20
  729.0 6.1 copy-start.23
  729.0 6.1 copy-start.27
  729.0 6.1 copy-start.28
  729.0 6.8 copy-start.19
Sparse Core Ops, SparseCore 0:
  241.7 132.9 all-gather.1

commit v3 on v2

--- a/solution.py
+++ b/solution.py
@@ -11,7 +11,7 @@
 STEP = 5
 GROUP = 256
 SEQ = ("seq_0", "seq_1", "seq_2")
-FSDP = ("fsdp_0", "fsdp_1")
+FSDP = ("fsdp_0", "fsdp_1", "fsdp_2")
 SEQ_FSDP = SEQ + FSDP
 SEQ_N = 16
 FSDP_N = 8
@@ -42,8 +42,16 @@
     return lax.axis_index("seq_0") * 8 + lax.axis_index("seq_1") * 2 + lax.axis_index("seq_2")
 
 
+def z_me():
+    return lax.axis_index("fsdp_0") * 2 + lax.axis_index("fsdp_1")
+
+
+def z_at(i):
+    return {"fsdp_0": i // 2, "fsdp_1": i % 2}
+
+
 def fsdp_me():
-    return lax.axis_index("fsdp_0") * 2 + lax.axis_index("fsdp_1")
+    return z_me() * 2 + lax.axis_index("fsdp_2")
 
 
 def seq_at(i):
@@ -51,7 +59,7 @@
 
 
 def fsdp_at(i):
-    return {"fsdp_0": i // 2, "fsdp_1": i % 2}
+    return {**z_at(i // 2), "fsdp_2": i % 2}
 
 
 RINGS = {"seq": (SEQ_N, seq_me, seq_at), "fsdp": (FSDP_N, fsdp_me, fsdp_at)}
@@ -109,36 +117,6 @@
 ALL8 = range(1, FSDP_N)
 
 
-def gather_fsdp(blocks, collective_id, name):
-    count = len(blocks)
-
-    def body(*refs):
-        ins, outs = refs[:count], refs[count : 2 * count]
-        ssem, rsem, lsem = refs[2 * count :]
-        me = greet("fsdp", ALL8)
-        copies = []
-        for n in range(count):
-            copies += send_each(
-                "fsdp", me, ALL8, lambda k, p: ins[n], lambda k, p: outs[n].at[me],
-                ssem.at[pl.ds(7 * n, 7)], rsem.at[pl.ds(7 * n, 7)],
-            )
-            own = pltpu.make_async_copy(ins[n], outs[n].at[me], lsem.at[n])
-            own.start()
-            copies.append(own)
-        for copy in copies:
-            copy.wait()
-
-    return remote_call(
-        body,
-        [jax.ShapeDtypeStruct((FSDP_N, *b.shape), b.dtype) for b in blocks],
-        [ANY] * count,
-        [ANY] * count,
-        sems(7 * count) + [DMA((count,))],
-        collective_id,
-        name,
-    )(*blocks)
-
-
 def sum_over(kind, block, collective_id, name, scatter):
     count = RINGS[kind][0]
     offsets = ALL16 if kind == "seq" else ALL8
@@ -170,204 +148,163 @@
     )(block)
 
 
-def sum_rows(block, collective_id, name):
-    _, rows, width = block.shape
-
-    def body(src, out, held, ssem, rsem):
-        me = greet("fsdp", ALL8)
-        copies = send_each(
-            "fsdp", me, ALL8, lambda k, p: src.at[p], lambda k, p: held.at[k - 1], ssem, rsem
+ORDER = (
+    "s", "t", "q0", "q1", "q2", "s", "s", "q0", "q0", "s", "q1", "q2",
+    "q1", "q2", "s", "s", "q0", "s", "q1", "q2", "s", "s", "q2", "q2",
+    "q1", "q1", "q2", "q0", "q0", "s", "q1", "t", "q0", "q2", "q2", "t",
+    "t", "t", "t", "q2", "q1", "q1", "q0", "q0", "t", "q1", "t", "q0",
+)
+
+
+class Post:
+    def __init__(self, sem, count):
+        self.sem, self.count, self.used, self.sent, self.late = sem, count, 0, [], []
+
+    def fresh(self):
+        self.used += 1
+        assert self.used <= self.count, self.used
+        return self.sem.at[self.used - 1]
+
+    def start(self, src, dst, ssem, rsem, device):
+        copy = pltpu.make_async_remote_copy(
+            src_ref=src, dst_ref=dst, send_sem=ssem, recv_sem=rsem,
+            device_id=device, device_id_type=MESH_ID,
         )
-        out[...] = src[me].astype(jnp.float32)
-        for n, copy in enumerate(copies):
+        copy.start()
+        return copy
+
+    def send(self, src, dst, device):
+        copy = self.start(src, dst, self.fresh(), self.fresh(), device)
+        self.sent.append(copy)
+        return copy
+
+    def finish(self):
+        for copy in self.sent:
+            copy.wait_send()
+        for mark, view in self.late:
+            pltpu.make_async_copy(view, view, mark).wait()
+
+
+def greet_devices(devices):
+    barrier = pltpu.get_barrier_semaphore()
+    for device in devices:
+        pl.semaphore_signal(barrier, inc=1, device_id=device, device_id_type=MESH_ID)
+    pl.semaphore_wait(barrier, len(devices))
+
+
+def fsdp_peers():
+    me = fsdp_me()
+    return [fsdp_at((me + k) % FSDP_N) for k in ALL8]
+
+
+def seq_peers():
+    me = seq_me()
+    return [seq_at((me + k) % SEQ_N) for k in ALL16]
+
+
+def relay(post, out, first, second, first_a, first_b):
+    z, yl = z_me(), lax.axis_index("fsdp_2")
+    partner, up, down = {"fsdp_2": 1 - yl}, z_at((z + 1) % 4), z_at((z + 3) % 4)
+    before, after, far = (z + 3) % 4, (z + 1) % 4, (z + 2) % 4
+
+    def at(zz, y, part=()):
+        return out.at[(zz * 2 + y,) + part]
+
+    def send(zz, y, part, device):
+        view = at(zz, y, part)
+        return post.send(view, view, device)
+
+    to_partner = send(z, yl, (), partner)
+    ring_up = send(z, yl, (), up)
+    ring_down = send(z, yl, (), down)
+    yield
+    to_partner.wait_recv()
+    other_up = send(z, 1 - yl, first, up)
+    other_down = send(z, 1 - yl, first, down)
+    yield
+    ring_up.wait_recv()
+    far_up = send(before, yl, first, up)
+    across = [send(before, yl, second, partner)]
+    yield
+    ring_down.wait_recv()
+    far_down = send(after, yl, second, down)
+    across.append(send(after, yl, second, partner))
+    yield
+    other_up.wait_recv()
+    last_up = send(before, 1 - yl, first_a, up)
+    yield
+    other_down.wait_recv()
+    last_down = send(after, 1 - yl, first_b, down)
+    yield
+    far_up.wait_recv()
+    far_down.wait_recv()
+    across.append(send(far, yl, second, partner))
+    yield
+    last_up.wait_recv()
+    last_down.wait_recv()
+    for copy in across:
+        copy.wait_recv()
+
+
+def spread_gate_up(gate_up, collective_id):
+    rows = gate_up.shape[0]
+    quarter = gate_up.shape[1] // 4
+
+    def body(src, out, sem, lsem):
+        post = Post(sem, 14)
+        z, c = z_me(), lax.axis_index("seq_2")
+        column = [((z + dz) % 4, (c + dc) % 2) for dz in range(4) for dc in range(2) if dz or dc]
+        greet_devices([{**z_at(zz), "seq_2": cc} for zz, cc in column])
+
+        def part(zz, cc):
+            first = pl.multiple_of((2 * (zz % 2) + cc) * quarter, 128)
+            return src.at[:, pl.ds(first, quarter)]
+
+        for zz, cc in column:
+            post.send(part(zz, cc), out.at[c, z], {**z_at(zz), "seq_2": cc})
+        own = pltpu.make_async_copy(part(z, c), out.at[c, z], lsem)
+        own.start()
+        for copy in post.sent:
             copy.wait_recv()
-            out[...] += held[n].astype(jnp.float32)
-        for copy in copies:
-            copy.wait_send()
+        post.finish()
+        own.wait()
 
     return remote_call(
         body,
-        jax.ShapeDtypeStruct((rows, width), jnp.float32),
-        [VMEM],
-        VMEM,
-        [pltpu.VMEM((7, rows, width), block.dtype)] + sems(7),
-        collective_id,
-        name,
-    )(block)
-
-
-def columns_to_rows(block, collective_id, name):
-    _, rows, width = block.shape
-
-    def body(src, out, ssem, rsem, lsem):
-        me = greet("seq", ALL16)
-        spot = pl.ds(pl.multiple_of(me * width, width), width)
-        copies = send_each(
-            "seq", me, ALL16, lambda k, p: src.at[p], lambda k, p: out.at[:, spot], ssem, rsem
-        )
-        own = pltpu.make_async_copy(src.at[me], out.at[:, spot], lsem)
-        own.start()
-        for copy in copies:
-            copy.wait()
-        own.wait()
-
-    return remote_call(
-        body,
-        jax.ShapeDtypeStruct((rows, SEQ_N * width), block.dtype),
-        [ANY],
-        ANY,
-        sems(15) + [DMA],
-        collective_id,
-        name,
-    )(block)
-
-
-def rows_to_columns(block, summed, collective_id, name):
-    rows = block.shape[0]
-    width = block.shape[1] // SEQ_N
-    part = summed.shape[1:]
-
-    def body(src, part_src, out, total_out, held, ssem, rsem, psem, qsem, lsem):
-        me = greet("seq", ALL16)
-
-        def cols(p):
-            return pl.ds(pl.multiple_of(p * width, width), width)
-
-        copies = send_each(
-            "seq", me, ALL16, lambda k, p: src.at[:, cols(p)], lambda k, p: out.at[me], ssem, rsem
-        )
-        parts = send_each(
-            "seq", me, ALL16, lambda k, p: part_src.at[p], lambda k, p: held.at[k - 1], psem, qsem
-        )
-        own = pltpu.make_async_copy(src.at[:, cols(me)], out.at[me], lsem)
-        own.start()
-        total = part_src[me]
-        for n, copy in enumerate(parts):
-            copy.wait_recv()
-            total = total + held[n]
-        total_out[...] = total
-        for copy in copies:
-            copy.wait()
-        for copy in parts:
-            copy.wait_send()
-        own.wait()
-
-    return remote_call(
-        body,
-        [
-            jax.ShapeDtypeStruct((SEQ_N, rows, width), block.dtype),
-            jax.ShapeDtypeStruct(part, jnp.float32),
-        ],
-        [ANY, VMEM],
-        [ANY, VMEM],
-        [pltpu.VMEM((15, *part), jnp.float32)] + sems(15) + sems(15) + [DMA],
-        collective_id,
-        name,
-    )(block, summed)
-
-
-def gather_and_sum(block, summed, collective_id, name):
-    def body(src, part_src, out, total_out, held, ssem, rsem, psem, qsem, lsem):
-        me = greet("fsdp", ALL8)
-        parts = send_each(
-            "fsdp", me, ALL8, lambda k, p: part_src, lambda k, p: held.at[k - 1], psem, qsem
-        )
-        copies = send_each(
-            "fsdp", me, ALL8, lambda k, p: src, lambda k, p: out.at[me], ssem, rsem
-        )
-        own = pltpu.make_async_copy(src, out.at[me], lsem)
-        own.start()
-        total = part_src[...]
-        for n, copy in enumerate(parts):
-            copy.wait_recv()
-            total = total + held[n]
-        total_out[...] = total
-        for copy in copies:
-            copy.wait()
-        for copy in parts:
-            copy.wait_send()
-        own.wait()
-
-    return remote_call(
-        body,
-        [
-            jax.ShapeDtypeStruct((FSDP_N, *block.shape), block.dtype),
-            jax.ShapeDtypeStruct(summed.shape, jnp.float32),
-        ],
-        [ANY, VMEM],
-        [ANY, VMEM],
-        [pltpu.VMEM((7, *summed.shape), jnp.float32)] + sems(7) + sems(7) + [DMA],
-        collective_id,
-        name,
-    )(block, summed)
-
-
-ORDER = (
-    "s", "q0", "q1", "q2", "t", "g0", "g1", "d0", "d1", "s", "s", "q0",
-    "q0", "q1", "q1", "s", "q0", "q1", "s", "s", "s", "q2", "q2", "q0",
-    "q0", "q2", "d0", "d1", "s", "s", "q0", "g0", "g1", "q1", "q1", "s",
-    "q2", "q2", "d1", "d1", "d0", "d0", "q1", "q2", "t", "d1", "d0", "g1",
-    "g1", "g0", "g0", "q0", "q0", "g1", "g0", "q0", "q2", "q2", "q1", "q1",
-    "d0", "d0", "d1", "d1", "t", "t", "q2", "d0", "q1", "d1", "t", "g0",
-    "g0", "g1", "g1", "g0", "g1",
-)
-
-
-def gather_weights(qkvo, gate_up, down, small, table, ids):
-    quarter = gate_up.shape[1] // 4
+        jax.ShapeDtypeStruct((2, 4, rows, quarter), gate_up.dtype),
+        [ANY], ANY, [DMA((14,)), DMA], collective_id, "spread_gate_up",
+    )(gate_up)
+
+
+def gather_weights(qkvo, small, table, ids):
     out_shape = [
         jax.ShapeDtypeStruct((2, 4, 2, 4, 2, *qkvo.shape), qkvo.dtype),
-        jax.ShapeDtypeStruct((2, 4, 2, 4, 2, gate_up.shape[0], quarter), gate_up.dtype),
-        jax.ShapeDtypeStruct((2, 4, 2, 2, *down.shape), down.dtype),
         jax.ShapeDtypeStruct((2, 4, 2, 4, 2, *small.shape), small.dtype),
-        jax.ShapeDtypeStruct((4, 2, *table.shape), table.dtype),
+        jax.ShapeDtypeStruct((FSDP_N, *table.shape), table.dtype),
         jax.ShapeDtypeStruct((SEQ_N, *ids.shape), ids.dtype),
     ]
-    sem_count = 300
+    sem_count = 160
     every = slice(None)
 
     def body(*refs):
-        ins, outs, sem = refs[:6], refs[6:12], refs[12]
-        yh, x, c, z, yl = (lax.axis_index(a) for a in SEQ_FSDP)
-        y = 2 * yh + yl
-        where = {"x": x, "y": y, "z": z}
+        ins, outs, sem = refs[:4], refs[4:8], refs[8]
+        post = Post(sem, sem_count)
+        yh, x, c, z, yl = (
+            lax.axis_index("seq_0"), lax.axis_index("seq_1"), lax.axis_index("seq_2"), z_me(),
+            lax.axis_index("fsdp_2"),
+        )
+        where = {"x": x, "y": 2 * yh + yl, "z": z}
         seq = seq_me()
-        used = [0]
-
-        def fresh():
-            used[0] += 1
-            return sem.at[used[0] - 1]
 
         def beside(axis, step):
             at = (where[axis] + step + 4) % 4
             if axis == "x":
                 return {"seq_1": at}
             if axis == "z":
-                return {"fsdp_0": at}
-            return {"seq_0": at // 2, "fsdp_1": at % 2}
+                return z_at(at)
+            return {"seq_0": at // 2, "fsdp_2": at % 2}
 
         other = {"seq_2": 1 - c}
-        column = [
-            (dz, dc, {"fsdp_0": (z + dz) % 4, "seq_2": (c + dc) % 2})
-            for dz in range(4)
-            for dc in range(2)
-            if dz or dc
-        ]
-
-        barrier = pltpu.get_barrier_semaphore()
-        greeted = [beside("y", 1), beside("y", -1)]
-        greeted += [device for dz, dc, device in column if dz]
-        greeted += [seq_at((seq + k) % SEQ_N) for k in ALL16]
-        for device in greeted:
-            pl.semaphore_signal(barrier, inc=1, device_id=device, device_id_type=MESH_ID)
-
-        late = []
-
-        def remote(src, dst, ssem, rsem, device):
-            pltpu.make_async_remote_copy(
-                src_ref=src, dst_ref=dst, send_sem=ssem, recv_sem=rsem,
-                device_id=device, device_id_type=MESH_ID,
-            ).start()
 
         def arrived(ref, rsem):
             pltpu.make_async_copy(ref, ref, rsem).wait()
@@ -377,24 +314,24 @@
                 done = order[:n]
                 at = where[axis]
                 before, after, far = (at + 3) % 4, (at + 1) % 4, (at + 2) % 4
-                send, from_before, from_after, far_first = (fresh() for _ in range(4))
-                late.append((send, sizes[n]))
+                send, from_before, from_after, far_first = (post.fresh() for _ in range(4))
+                post.late.append((send, sizes[axis, n]))
                 own = block(done, axis, at, None)
-                remote(own, own, send, from_before, beside(axis, 1))
-                remote(own, own, send, from_after, beside(axis, -1))
+                post.start(own, own, send, from_before, beside(axis, 1))
+                post.start(own, own, send, from_after, beside(axis, -1))
                 yield
                 got = block(done, axis, before, None)
                 arrived(got, from_before)
                 half = block(done, axis, before, 0)
-                remote(half, half, send, far_first, beside(axis, 1))
+                post.start(half, half, send, far_first, beside(axis, 1))
                 across(got)
                 yield
                 got = block(done, axis, after, None)
                 arrived(got, from_after)
                 if halves:
-                    far_second = fresh()
+                    far_second = post.fresh()
                     half = block(done, axis, after, 1)
-                    remote(half, half, send, far_second, beside(axis, -1))
+                    post.start(half, half, send, far_second, beside(axis, -1))
                 across(got)
                 yield
                 arrived(block(done, axis, far, 0), far_first)
@@ -402,155 +339,69 @@
                     arrived(block(done, axis, far, 1), far_second)
                 across(block(done, axis, far, None))
 
-        def place(done, axis, at):
-            spot = {"yh": yh, "x": x, "z": z, "yl": yl}
-            for a in done:
-                if a == "y":
-                    spot["yh"] = spot["yl"] = every
-                else:
-                    spot[a] = every
-            if axis == "y":
-                spot["yh"], spot["yl"] = at // 2, at % 2
-            elif axis is not None:
-                spot[axis] = at
-            return spot
-
         def all_stream(ref, order, tails, halves=True):
             def block(done, axis, at, half):
-                spot = place(done, axis, at)
+                spot = {"yh": yh, "x": x, "z": z, "yl": yl}
+                for a in done:
+                    if a == "y":
+                        spot["yh"] = spot["yl"] = every
+                    else:
+                        spot[a] = every
+                if axis == "y":
+                    spot["yh"], spot["yl"] = at // 2, at % 2
+                elif axis is not None:
+                    spot[axis] = at
                 tail = tails[0 if half is None else half + 1]
                 return ref.at[(spot["yh"], spot["x"], c, spot["z"], spot["yl"]) + tail]
 
-            across_s, across_r = fresh(), fresh()
-            late.append((across_s, ref.at[(every, every, c, every, every) + tails[0]]))
-            late.append((across_r, ref.at[(every, every, 1 - c, every, every) + tails[0]]))
+            across_s, across_r = post.fresh(), post.fresh()
+            post.late.append((across_s, ref.at[(every, every, c, every, every) + tails[0]]))
+            post.late.append((across_r, ref.at[(every, every, 1 - c, every, every) + tails[0]]))
 
             def across(view):
-                remote(view, view, across_s, across_r, other)
+                post.start(view, view, across_s, across_r, other)
 
             three = pl.ds(0, 3)
-            sizes = [
-                ref.at[(0, 0, 0, three, 0) + tails[0]],
-                ref.at[(0, pl.ds(0, 2), 0, three, every) + tails[0]],
-                ref.at[(every, every, 0, three, every) + tails[0]],
-            ]
+            sizes = {}
+            for axis in "xyz":
+                sizes[axis, 0] = ref.at[(0, 0, 0, three, 0) + tails[0]]
+                sizes[axis, 1] = ref.at[(0, pl.ds(0, 2), 0, three, every) + tails[0]]
+                sizes[axis, 2] = ref.at[(every, every, 0, three, every) + tails[0]]
             across(block([], None, None, None))
             yield from rings(block, order, sizes, halves, across)
 
-        def nothing(view):
-            return None
-
-        def gate_up_stream(src, ref, order, start, width):
-            tails = [
-                (every, pl.ds(start, width)),
-                (every, pl.ds(start, width // 2)),
-                (every, pl.ds(start + width // 2, width // 2)),
-            ]
-
-            def block(done, axis, at, half):
-                spot = place(done, axis, at)
-                tail = tails[0 if half is None else half + 1]
-                return ref.at[(spot["yh"], spot["x"], every, every, spot["yl"]) + tail]
-
-            marks = []
-            for dz, dc, device in column:
-                send, recv = fresh(), fresh()
-                first = pl.multiple_of(
-                    (2 * (device["fsdp_0"] % 2) + device["seq_2"]) * quarter + start, 128
-                )
-                here = ref.at[(yh, x, c, z, yl) + tails[0]]
-                remote(src.at[:, pl.ds(first, width)], here, send, recv, device)
-                late.append((send, here))
-                marks.append((ref.at[(yh, x, (c + dc) % 2, (z + 4 - dz) % 4, yl) + tails[0]], recv))
-            yield
-            for view, recv in marks:
-                arrived(view, recv)
-            three = pl.ds(0, 3)
-            sizes = [
-                ref.at[(0, three, every, every, 0) + tails[0]],
-                ref.at[(every, three, every, every, every) + tails[0]],
-            ]
-            yield from rings(block, order, sizes, True, nothing)
-
-        def down_stream(ref, order, start, width):
-            tails = [
-                (every, pl.ds(start, width)),
-                (every, pl.ds(start, width // 2)),
-                (every, pl.ds(start + width // 2, width // 2)),
-            ]
-            zh = z // 2
-
-            def block(done, axis, at, half):
-                spot = place(done, axis, at)
-                tail = tails[0 if half is None else half + 1]
-                return ref.at[(spot["yh"], spot["x"], every, spot["yl"]) + tail]
-
-            send, recv = fresh(), fresh()
-            here = ref.at[(yh, x, zh, yl) + tails[0]]
-            remote(here, here, send, recv, {"fsdp_0": (z + 2) % 4})
-            late.append((send, here))
-            yield
-            arrived(ref.at[(yh, x, 1 - zh, yl) + tails[0]], recv)
-            three = pl.ds(0, 3)
-            sizes = [
-                ref.at[(0, three, every, 0) + tails[0]],
-                ref.at[(every, three, every, every) + tails[0]],
-            ]
-            yield from rings(block, order, sizes, True, nothing)
-
-        def table_stream(ref):
-            send_y, recv_y = fresh(), fresh()
-            late.append((send_y, ref.at[0, 0]))
-            own = ref.at[z, yl]
-            remote(own, own, send_y, recv_y, {"fsdp_1": 1 - yl})
-            yield
-            arrived(ref.at[z, 1 - yl], recv_y)
-            half_rows = ref.shape[2] // 2
-            part = (every, pl.ds(0, half_rows), pl.ds(half_rows, half_rows))
-
-            def block(done, axis, at, half):
-                return ref.at[at, :, part[0 if half is None else half + 1]]
-
-            yield from rings(block, ("z",), [ref.at[pl.ds(0, 3)]], True, nothing)
-
         own_views = [
             (ins[0], outs[0].at[yh, x, c, z, yl]),
-            (
-                ins[1].at[:, pl.ds(pl.multiple_of((2 * (z % 2) + c) * quarter, 128), quarter)],
-                outs[1].at[yh, x, c, z, yl],
-            ),
-            (ins[2], outs[2].at[yh, x, z // 2, yl]),
-            (ins[3], outs[3].at[yh, x, c, z, yl]),
-            (ins[4], outs[4].at[z, yl]),
-            (ins[5], outs[5].at[seq]),
+            (ins[1], outs[1].at[yh, x, c, z, yl]),
+            (ins[2], outs[2].at[z * 2 + yl]),
+            (ins[3], outs[3].at[seq]),
         ]
         local = []
         for src, dst in own_views:
-            copy = pltpu.make_async_copy(src, dst, fresh())
+            copy = pltpu.make_async_copy(src, dst, post.fresh())
             copy.start()
             local.append(copy)
+        greet_devices(
+            [beside(axis, step) for axis in "yz" for step in (1, -1)] + seq_peers()
+        )
         for copy in local:
             copy.wait()
-        pl.semaphore_wait(barrier, len(greeted))
-
-        send, recv = fresh(), fresh()
-        for k in ALL16:
-            remote(ins[5], outs[5].at[seq], send, recv, seq_at((seq + k) % SEQ_N))
-        late.append((send, outs[5].at[pl.ds(0, 15)]))
-        late.append((recv, outs[5].at[pl.ds(0, 15)]))
+
+        send, recv = post.fresh(), post.fresh()
+        for device in seq_peers():
+            post.start(ins[3], outs[3].at[seq], send, recv, device)
+        post.late.append((send, outs[3].at[pl.ds(0, 15)]))
+        post.late.append((recv, outs[3].at[pl.ds(0, 15)]))
 
         third = qkvo.shape[1] // 3
-        half = quarter // 2
-        wide = down.shape[1] // 2
         streams = {
-            "s": all_stream(outs[3], "xyz", [(every, every)] * 2, False),
-            "t": table_stream(outs[4]),
-            "g0": gate_up_stream(ins[1], outs[1], "xy", 0, half),
-            "g1": gate_up_stream(ins[1], outs[1], "yx", half, half),
-            "d0": down_stream(outs[2], "xy", 0, wide),
-            "d1": down_stream(outs[2], "yx", wide, wide),
+            "s": all_stream(outs[1], "xyz", [(every, every)] * 2, False),
+            "t": relay(
+                post, outs[2], (pl.ds(0, 2000),), (pl.ds(2000, 2000),), (pl.ds(0, 1008),),
+                (pl.ds(1008, 992),),
+            ),
         }
-        for n, order in enumerate(("xyz", "yzx", "zxy")):
+        for n, order in enumerate(("yzx", "zyx", "zxy")):
             streams["q%d" % n] = all_stream(
                 outs[0], order,
                 [
@@ -563,42 +414,328 @@
             next(streams[name], None)
         for name in sorted(streams):
             assert next(streams[name], "end") == "end", name
-        for mark, view in late:
-            arrived(view, mark)
-        assert used[0] <= sem_count, used[0]
+        post.finish()
 
     return remote_call(
-        body, out_shape, [ANY] * 6, [ANY] * 6, [DMA((sem_count,))], 1, "gather_weights"
-    )(qkvo, gate_up, down, small, table, ids)
+        body, out_shape, [ANY] * 4, [ANY] * 4, [DMA((sem_count,))], 1, "gather_weights"
+    )(qkvo, small, table, ids)
+
+
+def rows_of_tokens(table, ids, collective_id):
+    vocab, width = table.shape
+
+    def body(ids_ref, table_ref, out, wide, rows, block, sem, lsem):
+        post = Post(sem, 30)
+        me = seq_me()
+        wide[...] = table_ref[...].astype(jnp.float32)
+        spot = pl.ds(pl.multiple_of(me * width, width), width)
+        greet_devices(seq_peers())
+
+        def fetch(s):
+            def step(t, carry):
+                rows[pl.ds(t, 1), :] = wide[pl.ds(ids_ref[s, t], 1), :]
+                return carry
+
+            lax.fori_loop(0, 128, step, 0, unroll=16)
+
+        for k in list(ALL16) + [0]:
+            peer = (me + k) % SEQ_N
+            fetch(peer)
+            block[k] = rows[...].astype(jnp.bfloat16)
+            if k:
+                post.send(block.at[k], out.at[:, spot], seq_at(peer))
+        own = pltpu.make_async_copy(block.at[0], out.at[:, spot], lsem)
+        own.start()
+        for copy in post.sent:
+            copy.wait_recv()
+        post.finish()
+        own.wait()
+
+    return remote_call(
+        body,
+        jax.ShapeDtypeStruct((128, SEQ_N * width), jnp.bfloat16),
+        [SMEM, VMEM],
+        VMEM,
+        [
+            pltpu.VMEM((vocab, width), jnp.float32),
+            pltpu.VMEM((128, width), jnp.float32),
+            pltpu.VMEM((SEQ_N, 128, width), jnp.bfloat16),
+            DMA((30,)),
+            DMA,
+        ],
+        collective_id,
+        "rows_of_tokens",
+    )(ids, table)
+
+
+def head_step(chosen, head, target, weight, scaled, collective_id):
+    vocab, width = head.shape
+    padded = -(-vocab // 512) * 512
+    tiles = padded // 512
+
+    def body(
+        chosen_ref, head_hbm, target_ref, weight_ref, scaled_ref, out, loss, hd, held, raised, d_logits,
+        prod, got, stat, stats, sem, lsem,
+    ):
+        post = Post(sem, 60)
+        me = fsdp_me()
+        load = pltpu.make_async_copy(head_hbm, hd.at[pl.ds(0, vocab)], lsem)
+        load.start()
+        held[me] = chosen_ref[...]
+        greet_devices(fsdp_peers())
+        for _ in relay(
+            post, held, (pl.ds(0, 32),), (pl.ds(32, 32),), (pl.ds(0, 16),), (pl.ds(16, 16),)
+        ):
+            pass
+        hd[vocab:, :] = jnp.zeros((padded - vocab, width), jnp.bfloat16)
+        load.wait()
+        rows = held[...].reshape(512, width)
+        target_at = target_ref[...]
+
+        def logits(n, carry):
+            top, picked = carry
+            at = pl.multiple_of(n * 512, 512)
+            tile = nt(held[...].reshape(512, width), hd[pl.ds(at, 512), :])
+            column = lax.broadcasted_iota(jnp.int32, (512, 512), 1) + at
+            tile = jnp.where(column < vocab, tile, -1e30)
+            raised[:, pl.ds(at, 512)] = tile
+            top = jnp.maximum(top, jnp.max(tile, axis=1, keepdims=True))
+            hit = jnp.where(column == target_at, tile, 0.0)
+            return top, picked + jnp.sum(hit, axis=1, keepdims=True)
+
+        top, picked = lax.fori_loop(
+            0, tiles, logits, (jnp.full((512, 1), -1e30, jnp.float32), jnp.zeros((512, 1), jnp.float32))
+        )
+
+        def exponents(n, total):
+            at = pl.ds(pl.multiple_of(n * 512, 512), 512)
+            tile = jnp.exp(raised[:, at] - top)
+            raised[:, at] = tile
+            return total + jnp.sum(tile, axis=1, keepdims=True)
+
+        total = lax.fori_loop(0, tiles, exponents, jnp.zeros((512, 1), jnp.float32))
+        lane = lax.broadcasted_iota(jnp.int32, (512, 128), 1)
+        both = jnp.where(lane == 0, top, jnp.where(lane == 1, total, 0.0))
+        stat[...] = jnp.transpose(both)[0:8, :]
+        copies = [
+            post.send(stat, stats.at[k - 1], fsdp_at((me + k) % FSDP_N)) for k in ALL8
+        ]
+        for copy in copies:
+            copy.wait_recv()
+        top_all = stat[0:1, :]
+        for n in range(7):
+            top_all = jnp.maximum(top_all, stats[n, 0:1, :])
+        sum_all = stat[1:2, :] * jnp.exp(stat[0:1, :] - top_all)
+        for n in range(7):
+            sum_all = sum_all + stats[n, 1:2, :] * jnp.exp(stats[n, 0:1, :] - top_all)
+        log_row = top_all + jnp.log(sum_all)
+        log_norm = jnp.transpose(jnp.broadcast_to(log_row, (128, 512)))[:, 0:1]
+        weights = weight_ref[...]
+        mine = lax.broadcasted_iota(jnp.int32, (512, 1), 0) // 64 == me
+        value = jnp.sum(jnp.where(mine, log_norm * weights, 0.0) - weights * picked, axis=0, keepdims=True)
+        loss[...] = jnp.broadcast_to(value, (8, 128))
+        scale = scaled_ref[...]
+        factor = scale * jnp.exp(top - log_norm)
+
+        def slopes(n, carry):
+            at = pl.multiple_of(n * 512, 512)
+            column = lax.broadcasted_iota(jnp.int32, (512, 512), 1) + at
+            hit = jnp.where(column == target_at, scale, 0.0)
+            d_logits[:, pl.ds(at, 512)] = (factor * raised[:, pl.ds(at, 512)] - hit).astype(jnp.bfloat16)
+            return carry
+
+        lax.fori_loop(0, tiles, slopes, 0)
+        half, inner = lax.axis_index("fsdp_0"), me % 4
+        sums = []
+        for n, part in enumerate((1 - half, half)):
+            start = pl.multiple_of(part * 256, 256)
+
+            def product(t, carry):
+                at = pl.ds(pl.multiple_of(t * 512, 512), 512)
+                tile = jnp.dot(
+                    d_logits[pl.ds(start, 256), :], hd[:, at], preferred_element_type=jnp.float32
+                )
+                prod[pl.ds(part * 4, 4), :, at] = tile.astype(jnp.bfloat16).reshape(4, 64, 512)
+                return carry
+
+            lax.fori_loop(0, width // 512, product, 0)
+            for j in range(n, 4):
+                peer = part * 4 + (inner + j) % 4
+                sums.append(post.send(prod.at[peer], got.at[4 * n + j - n], fsdp_at(peer)))
+        out[...] = prod[me].astype(jnp.float32)
+        for n, copy in enumerate(sums):
+            copy.wait_recv()
+            out[...] += got[n].astype(jnp.float32)
+        post.finish()
+
+    return remote_call(
+        body,
+        [
+            jax.ShapeDtypeStruct((64, width), jnp.float32),
+            jax.ShapeDtypeStruct((8, 128), jnp.float32),
+        ],
+        [VMEM, ANY, VMEM, VMEM, VMEM],
+        [VMEM, VMEM],
+        [
+            pltpu.VMEM((padded, width), jnp.bfloat16),
+            pltpu.VMEM((8, 64, width), jnp.bfloat16),
+            pltpu.VMEM((512, padded), jnp.float32),
+            pltpu.VMEM((512, padded), jnp.bfloat16),
+            pltpu.VMEM((8, 64, width), jnp.bfloat16),
+            pltpu.VMEM((7, 64, width), jnp.bfloat16),
+            pltpu.VMEM((8, 512), jnp.float32),
+            pltpu.VMEM((7, 8, 512), jnp.float32),
+            DMA((60,)),
+            DMA,
+        ],
+        collective_id,
+        "head_step",
+    )(chosen, head, target, weight, scaled)
+
+
+def token_gradients(d_start, small, ids, vocab, collective_id):
+    width = 128
+    low_n, tile = 1024, 1024
+    rows = small.shape[1]
+
+    def body(src, small_ref, ids_ref, out, small_out, held, parts, mid, parts_b, total, spread, sem, lsem):
+        post = Post(sem, 120)
+        f, s = fsdp_me(), seq_me()
+        z, yl = z_me(), lax.axis_index("fsdp_2")
+        greet_devices(seq_peers() + fsdp_peers())
+
+        def cols(p):
+            return pl.ds(pl.multiple_of(p * width, width), width)
+
+        moves, sums = [], []
+        for k in ALL16:
+            peer = (s + k) % SEQ_N
+            sums.append(post.send(small_ref.at[peer], parts.at[k - 1], seq_at(peer)))
+            moves.append(post.send(src.at[:, cols(peer)], held.at[f, s], seq_at(peer)))
+        own = pltpu.make_async_copy(src.at[:, cols(s)], held.at[f, s], lsem)
+        own.start()
+        total[...] = jnp.zeros_like(total)
+        amount = small_ref[s]
+        for n, copy in enumerate(sums):
+            copy.wait_recv()
+            amount = amount + parts[n]
+        mid[...] = amount
+        shares = [post.send(mid, parts_b.at[k - 1], fsdp_at((f + k) % FSDP_N)) for k in ALL8]
+        for copy in moves:
+            copy.wait_recv()
+        own.wait()
+
+        def add(block):
+            def one(t, carry):
+                ids_row = ids_ref[pl.ds(block * 2 + t, 1), :]
+                high, low = ids_row >> 10, ids_row & 1023
+                part = lax.broadcasted_iota(jnp.int32, (8, tile), 0)
+                which = jnp.transpose((part == high).astype(jnp.float32))
+                grad = held[block, pl.ds(t * 8, 8)].reshape(tile, width).astype(jnp.float32)
+                for h in range(4):
+                    spread[:, h * width : (h + 1) * width] = jnp.where(
+                        which[:, h : h + 1] > 0.5, grad, 0.0
+                    ).astype(jnp.bfloat16)
+
+                def step(n, inner):
+                    start = pl.multiple_of(n * 256, 256)
+                    row = lax.broadcasted_iota(jnp.int32, (256, tile), 0) + start
+                    hot = (row == low).astype(jnp.float32).astype(jnp.bfloat16)
+                    total[pl.ds(start, 256), :] += jnp.dot(
+                        hot, spread[...], preferred_element_type=jnp.float32
+                    )
+                    return inner
+
+                lax.fori_loop(0, low_n // 256, step, 0)
+                return carry
+
+            lax.fori_loop(0, 2, one, 0)
+
+        every = slice(None)
+        steps = relay(
+            post, held, (pl.ds(0, 8),), (pl.ds(8, 8),), (pl.ds(0, 4),), (pl.ds(4, 4),)
+        )
+        before, after, far = (z + 3) % 4, (z + 1) % 4, (z + 2) % 4
+        next(steps)
+        add(f)
+        next(steps)
+        next(steps)
+        next(steps)
+        add(z * 2 + 1 - yl)
+        next(steps)
+        next(steps)
+        add(before * 2 + yl)
+        next(steps)
+        add(after * 2 + yl)
+        add(far * 2 + yl)
+        assert next(steps, "end") == "end"
+        for zz in (before, after, far):
+            add(zz * 2 + 1 - yl)
+        for n, copy in enumerate(shares):
+            copy.wait_recv()
+            mid_part = parts_b[n]
+            amount = amount + mid_part
+        small_out[...] = amount
+        for h in range(4):
+            count = min(low_n, vocab - h * low_n)
+            out[h * low_n : h * low_n + count, :] = total[0:count, h * width : (h + 1) * width]
+        post.finish()
+
+    return remote_call(
+        body,
+        [
+            jax.ShapeDtypeStruct((vocab, width), jnp.float32),
+            jax.ShapeDtypeStruct((rows, width), jnp.float32),
+        ],
+        [VMEM, VMEM, VMEM],
+        [VMEM, VMEM],
+        [
+            pltpu.VMEM((FSDP_N, SEQ_N, 128, width), jnp.bfloat16),
+            pltpu.VMEM((15, rows, width), jnp.float32),
+            pltpu.VMEM((rows, width), jnp.float32),
+            pltpu.VMEM((7, rows, width), jnp.float32),
+            pltpu.VMEM((low_n, 4 * width), jnp.float32),
+            pltpu.VMEM((tile, 4 * width), jnp.bfloat16),
+            DMA((120,)),
+            DMA,
+        ],
+        collective_id,
+        "token_gradients",
+    )(d_start, small, ids)
 
 
 def feed_forward(rows, gate_up_w, down_w, saved, collective_id, name):
     forward = saved is None
     count, width = rows.shape
-    quarter = gate_up_w.shape[1]
+    quarter = gate_up_w.shape[-1]
     units = quarter // 2
     chunk = count // 2
     tile = 512
 
     def body(*refs):
         if forward:
-            (src, gu_hbm, dn_hbm, out, gu_out, held, gu, dn, saved_v, mid, part, give, got, sem) = refs
+            (src, gu_hbm, dn_hbm, out, gu_out, held, gu_blocks, dn, saved_v, mid, part, give, got, sem) = refs
         else:
-            (src, gu_hbm, dn_hbm, gu_in, out, held, gu, dn, saved_v, mid, part, give, got, sem) = refs
-        c, z = lax.axis_index("seq_2"), lax.axis_index("fsdp_0")
+            (src, gu_hbm, dn_hbm, gu_in, out, held, gu_blocks, dn, saved_v, mid, part, give, got, sem) = refs
+        c = lax.axis_index("seq_2")
         sibling = {"seq_2": 1 - c}
-        partner = {"fsdp_0": z + 1 - 2 * (z % 2)}
+        partner = {"fsdp_1": 1 - lax.axis_index("fsdp_1")}
         used = [0]
 
         def fresh():
             used[0] += 1
             return sem.at[used[0] - 1]
 
-        loads = [pltpu.make_async_copy(gu_hbm, gu, fresh()), pltpu.make_async_copy(dn_hbm, dn, fresh())]
+        gu = gu_blocks.reshape(width, quarter)
+        load_gu = [
+            pltpu.make_async_copy(gu_hbm.at[:, k], gu_blocks.at[:, :, k], fresh()) for k in range(2)
+        ]
+        load_dn = [pltpu.make_async_copy(dn_hbm, dn, fresh())]
+        loads = [load_gu, load_dn]
         if not forward:
-            loads.append(pltpu.make_async_copy(gu_in, saved_v, fresh()))
-            loads = [loads[1], loads[2], loads[0]]
-        for load in loads:
+            load_dn.append(pltpu.make_async_copy(gu_in, saved_v, fresh()))
+            loads = [load_dn, load_gu]
+        for load in loads[0] + loads[1]:
             load.start()
 
         barrier = pltpu.get_barrier_semaphore()
@@ -666,14 +803,14 @@
 
             lax.fori_loop(0, width // tile, step, 0)
 
-        loads[0].wait()
-        if not forward:
-            loads[1].wait()
+        for load in loads[0]:
+            load.wait()
         beside.wait_recv()
         first_product(0)
         along[0].wait_recv()
         passed = [remote(held.at[lines(2, 0)], held.at[lines(3, 0)], sibling)]
-        loads[-1].wait()
+        for load in loads[1]:
+            load.wait()
         second_product(0)
         along[1].wait_recv()
         passed.append(remote(held.at[lines(2, 1)], held.at[lines(3, 1)], sibling))
@@ -721,7 +858,7 @@
 
     scratch = [
         pltpu.VMEM((4 * count, width), jnp.bfloat16),
-        pltpu.VMEM(gate_up_w.shape, jnp.bfloat16),
+        pltpu.VMEM((8, 8, 2, 16, quarter), jnp.bfloat16),
         pltpu.VMEM(down_w.shape, jnp.bfloat16),
         pltpu.VMEM((4 * count, quarter), jnp.float32),
         pltpu.VMEM((2 * count, units if forward else quarter), jnp.bfloat16),
@@ -739,88 +876,6 @@
     return remote_call(
         body, total, [VMEM, ANY, ANY, ANY], VMEM, scratch, collective_id, name
     )(rows, gate_up_w, down_w, saved)
-
-
-def look_up(table, ids):
-    vocab, width = table.shape
-
-    def body(ids_ref, table_ref, out_ref, wide, rows):
-        wide[...] = table_ref[...].astype(jnp.float32)
-        for s in range(SEQ_N):
-
-            def step(t, carry):
-                rows[pl.ds(t, 1), :] = wide[pl.ds(ids_ref[s, t], 1), :]
-                return carry
-
-            lax.fori_loop(0, 128, step, 0, unroll=16)
-            out_ref[s] = rows[...].astype(jnp.bfloat16)
-
-    return pl.pallas_call(
-        body,
-        out_shape=jax.ShapeDtypeStruct((SEQ_N, 128, width), jnp.bfloat16),
-        in_specs=[SMEM, VMEM],
-        out_specs=VMEM,
-        scratch_shapes=[
-            pltpu.VMEM((vocab, width), jnp.float32),
-            pltpu.VMEM((128, width), jnp.float32),
-        ],
-        compiler_params=pltpu.CompilerParams(vmem_limit_bytes=VMEM_LIMIT),
-        name="look_up",
-    )(ids, table)
-
-
-def add_rows(gradient, local_ids, vocab):
-    count, width = gradient.shape
-    tile, low_n = 1024, 1024
-
-    def body(ids_ref, grad_ref, out_ref, total, spread):
-        @pl.when(pl.program_id(0) == 0)
-        def _():
-            total[...] = jnp.zeros_like(total)
-
-        ids = ids_ref[...]
-        high, low = ids >> 10, ids & 1023
-        part = lax.broadcasted_iota(jnp.int32, (8, tile), 0)
-        which = jnp.transpose((part == high).astype(jnp.float32))
-        grad = grad_ref[...]
-        for h in range(4):
-            spread[:, h * width : (h + 1) * width] = jnp.where(
-                which[:, h : h + 1] > 0.5, grad.astype(jnp.float32), 0.0
-            ).astype(jnp.bfloat16)
-
-        def step(n, carry):
-            start = pl.multiple_of(n * 256, 256)
-            row = lax.broadcasted_iota(jnp.int32, (256, tile), 0) + start
-            hot = (row == low).astype(jnp.float32).astype(jnp.bfloat16)
-            total[pl.ds(start, 256), :] += jnp.dot(
-                hot, spread[...], preferred_element_type=jnp.float32
-            )
-            return carry
-
-        lax.fori_loop(0, low_n // 256, step, 0)
-
-        @pl.when(pl.program_id(0) == count // tile - 1)
-        def _():
-            for h in range(4):
-                rows = min(low_n, vocab - h * low_n)
-                out_ref[h * low_n : h * low_n + rows, :] = total[0:rows, h * width : (h + 1) * width]
-
-    return pl.pallas_call(
-        body,
-        out_shape=jax.ShapeDtypeStruct((vocab, width), jnp.float32),
-        grid=(count // tile,),
-        in_specs=[
-            pl.BlockSpec((1, tile), lambda i: (0, i)),
-            pl.BlockSpec((tile, width), lambda i: (i, 0)),
-        ],
-        out_specs=pl.BlockSpec((vocab, width), lambda i: (0, 0)),
-        scratch_shapes=[
-            pltpu.VMEM((low_n, 4 * width), jnp.float32),
-            pltpu.VMEM((tile, 4 * width), jnp.bfloat16),
-        ],
-        compiler_params=pltpu.CompilerParams(vmem_limit_bytes=VMEM_LIMIT),
-        name="add_rows",
-    )(local_ids.reshape(1, count), gradient)
 
 
 def turn(values, cosine, sine):
@@ -1145,18 +1200,23 @@
         (0, 1024 - 848),
     ).reshape(8, 128)
     ids_own = jnp.pad(input_token_index.reshape(16, TOK), ((0, 0), (0, 64)))
-    qkvo, gate_up_w, down_w, small, table, ids = gather_weights(
+    gate_up_w = lax.all_gather(
+        spread_gate_up(gate_up_own, 14).reshape(128, PAD_FF // 2),
+        ("seq_0", "seq_1", "fsdp_2"),
+        axis=0,
+        tiled=True,
+    ).reshape(8, 2, 8, 16, PAD_FF // 2)
+    down_w = lax.all_gather(
+        down_own, ("seq_0", "seq_1", "fsdp_0", "fsdp_2"), axis=0, tiled=True
+    )
+    qkvo, small, table, ids = gather_weights(
         qkvo_own,
-        gate_up_own,
-        down_own,
         small_own,
         embedding.astype(jnp.bfloat16),
         ids_own,
     )
     qkvo = qkvo.reshape(2048, 4608)
     w_qkv, w_out = qkvo[:, :2560], qkvo[:, 2560:]
-    gate_up_w = gate_up_w.reshape(2048, PAD_FF // 2)
-    down_w = down_w.reshape(PAD_FF // 4, 2048)
     head_own, ids = lax.optimization_barrier((frozen_output_table, ids))
     head = lax.all_gather(head_own, SEQ, axis=1, tiled=True)
     small = small.reshape(128, 1024)
@@ -1177,9 +1237,11 @@
     places = loss_position_index.reshape(2, 8, SEQ_N, 32)
     spots = jnp.arange(SEQ_N)[:, None] * TOK + places
     counted = spots < row_used_length[..., None, None]
-    seg_blocks = document_slot_index.reshape(2, 8, SEQ_N, 1, TOK)
+    below = jnp.sum(
+        (document_slot_index[..., None] < jnp.arange(1, 3)).astype(jnp.int32), axis=2
+    )
     seg_at = jnp.sum(
-        jnp.where(places[..., None] == jnp.arange(TOK), seg_blocks, 0), axis=-1
+        (spots[..., None] >= below[:, :, None, None, :]).astype(jnp.int32), axis=-1
     )
     member = counted[..., None] & (seg_at[..., None] == jnp.arange(3))
     counts = jnp.sum(member.astype(jnp.int32), axis=(2, 3))
@@ -1198,9 +1260,7 @@
 
     ids = ids[:, :, :TOK].reshape(SEQ_N, 2, 8, TOK)
     row_ids = lax.dynamic_index_in_dim(ids, fsdp_here, 2, keepdims=False).reshape(SEQ_N, 128)
-    x_start = columns_to_rows(
-        look_up(table.reshape(8 * vocab_dev, 128), row_ids), 2, "rows_of_tokens"
-    ).astype(jnp.float32)
+    x_start = rows_of_tokens(table.reshape(8 * vocab_dev, 128), row_ids, 2).astype(jnp.float32)
 
     half = 32
     freqs = ROPE_BASE ** (-2.0 * jnp.arange(half).astype(jnp.float32) / 64)
@@ -1229,31 +1289,13 @@
     normed_end = (x_end * norm_scale(x_end) * gain[2]).astype(jnp.bfloat16)
 
     chosen = dot(pick.astype(jnp.bfloat16), normed_end).astype(jnp.bfloat16)
-    (rows,) = gather_fsdp([chosen], 4, "chosen_rows")
-    rows = rows.reshape(512, 2048)
-    logits = nt(rows, head)
-    local_target = target_token_index.transpose(1, 0, 2).reshape(-1) - fsdp_here * vocab_dev
-    is_target = jnp.arange(vocab_dev)[None, :] == local_target[:, None]
-    top_local = jnp.max(logits, axis=1)
-    exp_local = jnp.sum(jnp.exp(logits - top_local[:, None]), axis=1)
-    target_local = jnp.sum(jnp.where(is_target, logits, 0.0), axis=1)
-    (stats,) = gather_fsdp(
-        [jnp.pad(jnp.stack([top_local, exp_local]), ((0, 6), (0, 0)))], 5, "softmax_parts"
-    )
-    top_all = jnp.max(stats[:, 0], axis=0)
-    exp_all = jnp.sum(stats[:, 1] * jnp.exp(stats[:, 0] - top_all[None, :]), axis=0)
-    log_norm = top_all + jnp.log(exp_all)
-    peer_of = jnp.arange(512) // 64
-    loss_part = jnp.sum(jnp.where(peer_of == fsdp_here, log_norm * weight_flat, 0.0)) - jnp.sum(
-        weight_flat * target_local
-    )
-    d_logits = (
-        (weight_flat / document_total)[:, None]
-        * (jnp.exp(logits - log_norm[:, None]) - is_target.astype(jnp.float32))
-    ).astype(jnp.bfloat16)
-    d_chosen = sum_rows(
-        dot(d_logits, head).astype(jnp.bfloat16).reshape(8, 64, 2048), 6, "row_gradients"
-    )
+    local_target = target_token_index.transpose(1, 0, 2).reshape(512, 1) - fsdp_here * vocab_dev
+    local_target = jnp.where(local_target < vocab_dev, local_target, -1)
+    weight_column = weight_flat.reshape(512, 1)
+    d_chosen, loss_tile = head_step(
+        chosen, head, local_target, weight_column, weight_column / document_total, 4
+    )
+    loss_part = loss_tile[0, 0]
 
     upstream = lax.dot_general(pick, d_chosen, (((0,), (0,)), ((), ())), precision=HIGHEST)
     d_end, gain_end = norm_back(x_end, gain[2], upstream)
@@ -1300,12 +1342,10 @@
     left = left.reshape(40, 16, 128).transpose(1, 0, 2)
     right = jnp.concatenate([up_gradient_in, up_gradient_out], 1).reshape(8, 16, 288)
     right = jnp.pad(right, ((0, 0), (0, 0), (0, 96))).transpose(1, 0, 2).reshape(16, 24, 128)
-    d_columns, small_sum = rows_to_columns(
-        d_start, jnp.concatenate([left, right], 1), 8, "token_gradients"
-    )
-    d_tokens, small_sum = gather_and_sum(d_columns, small_sum, 9, "token_gradients_all")
-    all_ids = ids.transpose(2, 0, 1, 3).reshape(-1) - fsdp_here * vocab_dev
-    grad_embed = add_rows(d_tokens.reshape(-1, 128), all_ids, vocab_dev)[:vocab_dev]
+    all_ids = ids.transpose(2, 0, 1, 3).reshape(16, 1024) - fsdp_here * vocab_dev
+    grad_embed, small_sum = token_gradients(
+        d_start, jnp.concatenate([left, right], 1), all_ids, vocab_dev, 8
+    )
     left_sum = small_sum[:40]
     right_sum = small_sum[40:].reshape(8, 384)[:, :288]
     group_onehot = factor_onehot(seq_here * 288 + jnp.arange(288))
@@ -1385,7 +1425,7 @@
 
 def solution(mesh):
     torus = Mesh(
-        mesh.devices.reshape(2, 4, 2, 4, 2), SEQ_FSDP
+        mesh.devices.reshape(2, 4, 2, 2, 2, 2), SEQ_FSDP
     )
     return jax.shard_map(
         per_device,

time: 754 us -> 960 us (1.27)
  waiting for transfers between devices: 0.02 us -> 251 us
  matrix products: 74.1 us -> 46.9 us
  other arithmetic: 44.7 us -> 34.9 us
    all_gather x0 -> x2, waiting for transfers between devices: none -> 166 us  [the longest x1 166 us: per_device(): lax.all_gather(spread_gate_up(gate_up_own, 14).reshape(128, PAD_FF // 2),...]
    all_gather x1, waiting for transfers between devices: 0.01 us -> 84.9 us  [per_device(): head = lax.all_gather(head_own, SEQ, axis=1, tiled=True)]
    dot_general x8 -> x7, matrix products: 31.6 us -> 14.9 us  [dot(): return jnp.dot(left, right, preferred_element_type=jnp.float32)]
    dot_general x7 -> x6, matrix products: 28.9 us -> 18.3 us  [nt(): lax.dot_general(left, right, (((1,), (1,)), ((), ())), preferred_element_...]
    pallas_call x9 -> x5, Pallas kernels: 425 us -> 421 us  [the longest x1 223 us: gather_weights(): remote_call(body, out_shape, [ANY] * 4, [ANY] * 4, [DMA((sem_count,))], 1...]
  transfers between devices with their start and end apart: 1 -> 3, of which waited for: 0 -> 2; matrix products, arithmetic and copies ran while one was open for 5% -> 5% of each run, Pallas kernels for 17% -> 35%
where the time goes in v3:
time: 960 us; the launch traced here: 954 us
  Pallas kernels  572 us (60%)
  waiting for transfers between devices  251 us (26%)
  matrix products  46.9 us (5%)
  other arithmetic  34.9 us (4%)
  local copies, waits for them, and re-layouts  29.4 us (3%)
  between operations  19 us (2%)
    pallas_call x1, Pallas kernels, gather_weights(): remote_call(body, out_shape, [ANY] * 4, [ANY] * 4, [DMA((sem_count,))], 1...  223 us
    all_gather x1, waiting for transfers between devices, per_device(): lax.all_gather(spread_gate_up(gate_up_own, 14).reshape(128, PAD_FF // 2),...  166 us
    all_gather x1, waiting for transfers between devices, per_device(): head = lax.all_gather(head_own, SEQ, axis=1, tiled=True)  84.9 us
    pallas_call x1, Pallas kernels, token_gradients(): remote_call(body, [jax.ShapeDtypeStruct((vocab, width), jnp.float32), jax...  76.6 us
    pallas_call x1, Pallas kernels, head_step(): remote_call(body, [jax.ShapeDtypeStruct((64, width), jnp.float32), jax.Sh...  74.3 us
    pallas_call x1, Pallas kernels, feed_forward(): remote_call(body, total, [VMEM, ANY, ANY, ANY], VMEM, scratch, collective...  38.7 us
    pallas_call x1, Pallas kernels, feed_forward(): remote_call(body, [total, products], [VMEM, ANY, ANY], [VMEM, ANY], scrat...  36.8 us
    pallas_call x1, Pallas kernels, rows_of_tokens(): remote_call(body, jax.ShapeDtypeStruct((128, SEQ_N * width), jnp.bfloat16...  26 us
  transfers between devices with their start and end apart: 3, of which 2 were waited for; matrix products, arithmetic and copies ran while one was open for 5% of the time, Pallas kernels for 35%

profile of v3, /device:TPU:1, one launch (start us, length us, event | category | flops | bytes accessed | tf_op | source)
XLA Modules:
  0.0 953.9 jit_solution(12082232736302173304)
XLA Ops:
  7.2 1.6 pad.24
  8.9 3.9 reshape.411
  15.3 2.8 reshape.412.src
  18.1 20.9 %spread_gate_up.1 = bf16[2,4,16,3072]{3,2,1,0:T(8,128)(2,1)} custom-call(bf16[16,12288]{1,0:T(8,128)(2,1)} %reshape.412.src), custom_call_target="tpu_custom_call" | custom-call | tf_op jit(solution)/shard_map/spread_gate_up/pallas_call | solution.py:272
  42.7 223.0 %gather_weights.1 = (bf16[2,4,2,4,2,16,4608]{6,5,4,3,2,1,0:T(8,128)(2,1)}, f32[2,4,2,4,2,8,128]{6,5,4,3,2,1,0:T(8,128)}, bf16[8,4000,128]{2,1,0:T(8,128)(2,1)}, s32[16,16,128]{2,1,0:T(8,128)}) custom-call(bf16[16,4608]{1,0:T(8,128)(2,1)} %pad_maximum_fusion.4.refs_0_, f32[8,128]{1,0:T(8,128)} %fusion.123.refs_1_, ...), custom_call_target="tpu_custom_call" | custom-call | tf_op jit(solution)/shard_map/gather_weights/pallas_call | solution.py:419
  270.5 26.0 %rows_of_tokens.1 = bf16[128,2048]{1,0:T(8,128)(2,1)} custom-call(s32[16,128]{1,0:T(8,128)} %reshape.405.ids_ref, bf16[32000,128]{1,0:T(8,128)(2,1)} %bitcast.165), custom_call_target="tpu_custom_call" | custom-call | tf_op jit(solution)/shard_map/rows_of_tokens/pallas_call | solution.py:454
  299.6 5.2 fusion.2
  313.3 23.6 %key_value_window.1.kv_ref = bf16[2,320,512]{2,1,0:T(8,128)(2,1)} custom-call(f32[128,512]{1,0:T(8,128)} %slice.161.kv_ref, f32[64,512]{1,0:T(8,128)} %copy.122.cos_ref, f32[64,512]{1,0:T(8,128)} %tile.21.sin_ref), custom_call_target="tpu_custom_call" | custom-call | tf_op jit(solution)/shard_map/key_value_window/pallas_call | solution.py:911
  336.9 7.9 attend.1
  347.3 4.9 fusion.10
  354.6 1.4 broadcast_divide_fusion.scaled_ref
  357.0 166.3 %all-gather.4.cloned.1.call-done = bf16[2048,3072]{1,0:T(8,128)(2,1)} async-done(((bf16[128,3072]{1,0:T(8,128)(2,1)}), bf16[2048,3072]{1,0:T(8,128)(2,1)}) %all-gather.4.cloned.1.call-update) | async-done | bytes 12582928 | tf_op jit(solution)/shard_map/all_gather | solution.py:1203
  523.3 36.8 %feed_forward.1 = (f32[128,2048]{1,0:T(8,128)}, f32[512,3072]{1,0:T(8,128)}) custom-call(bf16[128,2048]{1,0:T(8,128)(2,1)} %multiply_convert_fusion.1.refs_0_, bf16[8,2,8,16,3072]{4,3,2,1,0:T(8,128)(2,1)} %bitcast.163, bf16[1536,2048]{1,0:T(8,128)(2,1)} %all-gather.6.cloned.1.call-done.refs_2_), custom_call_target="tpu_custom_call" | custom-call | tf_op jit(solution)/shard_map/feed_forward/pallas_call | solution.py:873
  560.1 1.4 multiply_reduce_fusion.5
  562.6 84.9 %all-gather.8.cloned.1.call-done.head_hbm = bf16[4000,2048]{1,0:T(8,128)(2,1)} async-done(((bf16[4000,128]{1,0:T(8,128)(2,1)}), bf16[4000,2048]{1,0:T(8,128)(2,1)}) %all-gather.8.cloned.1.call-update) | async-done | bytes 16384016 | tf_op jit(solution)/shard_map/all_gather | solution.py:1221
  647.5 74.3 %head_step.1 = (f32[64,2048]{1,0:T(8,128)}, f32[8,128]{1,0:T(8,128)}) custom-call(bf16[64,2048]{1,0:T(8,128)(2,1)} %convolution_convert_fusion.chosen_ref, bf16[4000,2048]{1,0:T(8,128)(2,1)} %all-gather.8.cloned.1.call-done.head_hbm, s32[512,1]{1,0:T(8,128)} %compare_select_fusion.target_ref, f32[512,1]{1,0:T(8,128)} %copy-done.6, ...), custom_call_target="tpu_custom_call" | custom-call | tf_op jit(solution)/shard_map/head_step/pallas_call | solution.py:571
  721.8 2.6 multiply_reduce_fusion.1
  725.5 38.7 %feed_forward_back.1 = f32[128,2048]{1,0:T(8,128)} custom-call(bf16[128,2048]{1,0:T(8,128)(2,1)} %fusion.161.refs_0_, bf16[8,2,8,16,3072]{4,3,2,1,0:T(8,128)(2,1)} %bitcast.164, bf16[1536,2048]{1,0:T(8,128)(2,1)} %all-gather.6.cloned.1.call-done.refs_2_, f32[512,3072]{1,0:T(8,128)} %get-tuple-element.42.refs_3_), custom_call_target="tpu_custom_call" | custom-call | tf_op jit(solution)/shard_map/feed_forward_back/pallas_call | solution.py:876
  764.2 2.2 multiply_reduce_fusion.2
  767.2 6.3 fusion.4
  775.5 11.1 %attend_back.1 = (bf16[128,2048]{1,0:T(8,128)(2,1)}, bf16[2,256,512]{2,1,0:T(8,128)(2,1)}, f32[2,64,512]{2,1,0:T(8,128)}) custom-call(s32[1]{0:T(128)} %bitcast.4.start_ref, s32[4]{0:T(128)} %shift_ref.3, bf16[128,2048]{1,0:T(8,128)(2,1)} %get-tuple-element.43.q_ref, bf16[2,320,512]{2,1,0:T(8,128)(2,1)} %key_value_window.1.kv_ref, ...), custom_call_target="tpu_custom_call" | custom-call | tf_op jit(solution)/shard_map/attend_back/pallas_call | solution.py:1051
  786.6 16.4 %key_value_back.1 = bf16[128,512]{1,0:T(8,128)(2,1)} custom-call(bf16[2,256,512]{2,1,0:T(8,128)(2,1)} %get-tuple-element.45.far_ref, f32[2,64,512]{2,1,0:T(8,128)} %get-tuple-element.46.own_ref, f32[64,512]{1,0:T(8,128)} %copy.122.cos_ref, f32[64,512]{1,0:T(8,128)} %tile.21.sin_ref), custom_call_target="tpu_custom_call" | custom-call | tf_op jit(solution)/shard_map/key_value_back/pallas_call | solution.py:942
  803.0 1.4 fusion.23
  804.5 7.7 fusion
  813.1 1.8 fusion.37
  815.3 1.6 concatenate.58
  817.8 2.0 fusion.34.src
  819.7 76.6 %token_gradients.1 = (f32[4000,128]{1,0:T(8,128)}, f32[64,128]{1,0:T(8,128)}) custom-call(bf16[128,2048]{1,0:T(8,128)(2,1)} %fusion.34.src, f32[16,64,128]{2,1,0:T(8,128)} %pad_maximum_fusion.1.small_ref, s32[16,1024]{1,0:T(8,128)} %sub.146.ids_ref), custom_call_target="tpu_custom_call" | custom-call | tf_op jit(solution)/shard_map/token_gradients/pallas_call | solution.py:684
  902.3 2.7 multiply_reduce_fusion
  908.3 9.7 %totals_seq.1.src = f32[8,128]{1,0:T(8,128)} custom-call(f32[8,128]{1,0:T(8,128)} %maximum_bitcast_fusion.src), custom_call_target="tpu_custom_call" | custom-call | tf_op jit(solution)/shard_map/totals_seq/pallas_call | solution.py:140
  918.0 7.0 totals_fsdp.1
  938.4 6.1 fusion.19
  (263 shorter events, 55.8 us)
Async XLA Ops:
  7.2 349.8 %all-gather.6.cloned.1.call-start = ((), (), s32[]{:S(2)}) async-start(), calls=%async_computation.1 | async-start | bytes 6488064 | tf_op jit(solution)/shard_map/all_gather | solution.py:1209
  8.9 514.4 %all-gather.4.cloned.1.call-start = ((), (), s32[]{:S(2)}) async-start(), calls=%async_computation | async-start | bytes 13369344 | tf_op jit(solution)/shard_map/all_gather | solution.py:1203
  15.3 24.1 %copy-start.3 = (f32[4000,128]{1,0:T(8,128)S(1)}, f32[4000,128]{1,0:T(8,128)}, u32[]{:S(2)}) copy-start(f32[4000,128]{1,0:T(8,128)} %param.28) | copy-start | bytes 6144004
  39.1 3.0 copy-start.12
  39.1 2.9 copy-start.13
  39.2 608.4 %all-gather.8.cloned.1.call-start = ((), (), s32[]{:S(2)}) async-start(), calls=%async_computation.2 | async-start | bytes 17408000 | tf_op jit(solution)/shard_map/all_gather | solution.py:1221
  298.3 514.5 %copy-start.29 = (f32[128]{0:T(128)}, f32[128]{0:T(128)S(1)}, u32[]{:S(2)}) copy-start(f32[128]{0:T(128)S(1)} %get-tuple-element.154) | copy-start | bytes 1540
  304.9 3.0 copy-start.11
  305.3 5.4 copy-start.5
  305.3 4.2 copy-start.15
  305.3 4.7 copy-start.33
  306.3 5.8 copy-start.25
  308.0 28.9 %copy-start.14 = (s32[2,1,320]{2,1,0:T(1,128)}, s32[2,1,320]{2,1,0:T(1,128)S(1)}, u32[]{:S(2)}) copy-start(s32[2,1,320]{2,1,0:T(1,128)S(1)} %broadcast_in_dim.30.ks_ref) | copy-start | bytes 7684
  312.1 42.5 %copy-start.6 = (f32[512,1]{1,0:T(8,128)}, f32[512,1]{1,0:T(8,128)S(1)}, u32[]{:S(2)}) copy-start(f32[512,1]{1,0:T(8,128)S(1)} %reshape_reshape.4.weight_ref) | copy-start | bytes 6148
  313.3 34.0 %copy-start.1 = (bf16[128,2048]{1,0:T(8,128)(2,1)S(1)}, bf16[128,2048]{1,0:T(8,128)(2,1)}, u32[]{:S(2)}) copy-start(bf16[128,2048]{1,0:T(8,128)(2,1)} %rows_of_tokens.1) | copy-start | bytes 1572868
  767.2 6.3 copy-start.7
  786.5 17.9 %copy-start.9 = (bf16[128,2048]{1,0:T(8,128)(2,1)S(1)}, bf16[128,2048]{1,0:T(8,128)(2,1)}, u32[]{:S(2)}) copy-start(bf16[128,2048]{1,0:T(8,128)(2,1)} %get-tuple-element.44) | copy-start | bytes 1572868
  804.5 7.9 copy-start.8
  804.5 8.3 copy-start.2
  817.8 82.9 %copy-start.20 = (f32[288,4]{0,1:T(4,128)S(1)}, f32[288,4]{0,1:T(4,128)}, u32[]{:S(2)}) copy-start(f32[288,4]{0,1:T(4,128)} %convert_bitcast_fusion) | copy-start | bytes 13828
  819.7 108.1 %copy-start.16 = (f32[8,8,8]{2,1,0:T(8,128)S(1)}, f32[8,8,8]{2,1,0:T(8,128)}, u32[]{:S(2)}) copy-start(f32[8,8,8]{2,1,0:T(8,128)} %param.41) | copy-start | bytes 6148
  902.3 31.2 %copy-start.28 = (f32[8,8]{1,0:T(8,128)S(1)}, f32[8,8]{1,0:T(8,128)}, u32[]{:S(2)}) copy-start(f32[8,8]{1,0:T(8,128)} %fusion.125) | copy-start | bytes 772
  905.0 31.3 %copy-start.30 = (f32[4,16]{1,0:T(4,128)S(1)}, f32[4,16]{1,0:T(4,128)}, u32[]{:S(2)}) copy-start(f32[4,16]{1,0:T(4,128)} %param.42) | copy-start | bytes 772
  905.0 32.1 %copy-start.19 = (f32[32,16]{0,1:T(8,128)S(1)}, f32[32,16]{0,1:T(8,128)}, u32[]{:S(2)}) copy-start(f32[32,16]{0,1:T(8,128)} %param.39) | copy-start | bytes 6148
  905.0 32.8 %copy-start.34 = (f32[36]{0:T(128)S(1)}, f32[36]{0:T(128)}, u32[]{:S(2)}) copy-start(f32[36]{0:T(128)} %param.43) | copy-start | bytes 436
  905.0 33.3 %copy-start.4 = (f32[4000,128]{1,0:T(8,128)S(1)}, f32[4000,128]{1,0:T(8,128)}, u32[]{:S(2)}) copy-start(f32[4000,128]{1,0:T(8,128)} %param.28) | copy-start | bytes 6144004
  928.0 16.4 %copy-start.17 = (f32[8,8,8]{2,1,0:T(8,128)}, f32[8,8,8]{2,1,0:T(8,128)S(1)}, u32[]{:S(2)}) copy-start(f32[8,8,8]{2,1,0:T(8,128)S(1)} %get-tuple-element.125) | copy-start | bytes 6148
  937.8 6.6 copy-start.22
  938.3 6.1 copy-start.23
  938.3 6.9 copy-start.27
  938.3 6.9 copy-start.31
  938.3 6.9 copy-start.32
  (6 other events, 9.9 us)
Sparse Core Ops, SparseCore 0:
  9.7 219.4 all-gather.5
  230.8 292.4 all-gather.3
  525.6 121.9 all-gather.7

commit v4 on v3

--- a/solution.py
+++ b/solution.py
@@ -149,10 +149,13 @@
 
 
 ORDER = (
-    "s", "t", "q0", "q1", "q2", "s", "s", "q0", "q0", "s", "q1", "q2",
-    "q1", "q2", "s", "s", "q0", "s", "q1", "q2", "s", "s", "q2", "q2",
-    "q1", "q1", "q2", "q0", "q0", "s", "q1", "t", "q0", "q2", "q2", "t",
-    "t", "t", "t", "q2", "q1", "q1", "q0", "q0", "t", "q1", "t", "q0",
+    "s", "g0", "g1", "d0", "d1", "q0", "q1", "q2", "t", "s", "s", "q1",
+    "q1", "q0", "q0", "s", "q1", "q0", "s", "s", "s", "q2", "q2", "q0",
+    "q0", "q2", "q0", "d0", "d1", "t", "s", "s", "g0", "g1", "s", "q2",
+    "q2", "q1", "q1", "d1", "d1", "d0", "d0", "q1", "q2", "d1", "d0", "q0",
+    "q0", "g1", "g1", "g0", "g0", "q0", "g1", "g0", "q1", "q1", "t", "d1",
+    "d1", "q2", "q2", "d0", "d0", "q1", "d1", "q2", "d0", "g1", "g1", "t",
+    "t", "g0", "g0", "g1", "g0", "t",
 )
 
 
@@ -246,48 +249,21 @@
         copy.wait_recv()
 
 
-def spread_gate_up(gate_up, collective_id):
-    rows = gate_up.shape[0]
+def gather_weights(qkvo, small, table, ids, gate_up, down):
     quarter = gate_up.shape[1] // 4
-
-    def body(src, out, sem, lsem):
-        post = Post(sem, 14)
-        z, c = z_me(), lax.axis_index("seq_2")
-        column = [((z + dz) % 4, (c + dc) % 2) for dz in range(4) for dc in range(2) if dz or dc]
-        greet_devices([{**z_at(zz), "seq_2": cc} for zz, cc in column])
-
-        def part(zz, cc):
-            first = pl.multiple_of((2 * (zz % 2) + cc) * quarter, 128)
-            return src.at[:, pl.ds(first, quarter)]
-
-        for zz, cc in column:
-            post.send(part(zz, cc), out.at[c, z], {**z_at(zz), "seq_2": cc})
-        own = pltpu.make_async_copy(part(z, c), out.at[c, z], lsem)
-        own.start()
-        for copy in post.sent:
-            copy.wait_recv()
-        post.finish()
-        own.wait()
-
-    return remote_call(
-        body,
-        jax.ShapeDtypeStruct((2, 4, rows, quarter), gate_up.dtype),
-        [ANY], ANY, [DMA((14,)), DMA], collective_id, "spread_gate_up",
-    )(gate_up)
-
-
-def gather_weights(qkvo, small, table, ids):
     out_shape = [
         jax.ShapeDtypeStruct((2, 4, 2, 4, 2, *qkvo.shape), qkvo.dtype),
         jax.ShapeDtypeStruct((2, 4, 2, 4, 2, *small.shape), small.dtype),
         jax.ShapeDtypeStruct((FSDP_N, *table.shape), table.dtype),
         jax.ShapeDtypeStruct((SEQ_N, *ids.shape), ids.dtype),
+        jax.ShapeDtypeStruct((2, 4, 2, 4, 2, gate_up.shape[0], quarter), gate_up.dtype),
+        jax.ShapeDtypeStruct((2, 4, 2, 2, *down.shape), down.dtype),
     ]
-    sem_count = 160
+    sem_count = 300
     every = slice(None)
 
     def body(*refs):
-        ins, outs, sem = refs[:4], refs[4:8], refs[8]
+        ins, outs, sem = refs[:6], refs[6:12], refs[12]
         post = Post(sem, sem_count)
         yh, x, c, z, yl = (
             lax.axis_index("seq_0"), lax.axis_index("seq_1"), lax.axis_index("seq_2"), z_me(),
@@ -305,6 +281,9 @@
             return {"seq_0": at // 2, "fsdp_2": at % 2}
 
         other = {"seq_2": 1 - c}
+        column = [
+            ((z + dz) % 4, (c + dc) % 2, dz, dc) for dz in range(4) for dc in range(2) if dz or dc
+        ]
 
         def arrived(ref, rsem):
             pltpu.make_async_copy(ref, ref, rsem).wait()
@@ -339,18 +318,22 @@
                     arrived(block(done, axis, far, 1), far_second)
                 across(block(done, axis, far, None))
 
+        def place(done, axis, at):
+            spot = {"yh": yh, "x": x, "z": z, "yl": yl}
+            for a in done:
+                if a == "y":
+                    spot["yh"] = spot["yl"] = every
+                else:
+                    spot[a] = every
+            if axis == "y":
+                spot["yh"], spot["yl"] = at // 2, at % 2
+            elif axis is not None:
+                spot[axis] = at
+            return spot
+
         def all_stream(ref, order, tails, halves=True):
             def block(done, axis, at, half):
-                spot = {"yh": yh, "x": x, "z": z, "yl": yl}
-                for a in done:
-                    if a == "y":
-                        spot["yh"] = spot["yl"] = every
-                    else:
-                        spot[a] = every
-                if axis == "y":
-                    spot["yh"], spot["yl"] = at // 2, at % 2
-                elif axis is not None:
-                    spot[axis] = at
+                spot = place(done, axis, at)
                 tail = tails[0 if half is None else half + 1]
                 return ref.at[(spot["yh"], spot["x"], c, spot["z"], spot["yl"]) + tail]
 
@@ -370,11 +353,92 @@
             across(block([], None, None, None))
             yield from rings(block, order, sizes, halves, across)
 
+        def nothing(view):
+            return None
+
+        def gate_up_stream(src, ref, order, start, width):
+            tails = [
+                (every, pl.ds(start, width)),
+                (every, pl.ds(start, width // 2)),
+                (every, pl.ds(start + width // 2, width // 2)),
+            ]
+
+            def block(done, axis, at, half):
+                spot = place(done, axis, at)
+                tail = tails[0 if half is None else half + 1]
+                return ref.at[(spot["yh"], spot["x"], every, every, spot["yl"]) + tail]
+
+            marks = []
+            for zz, cc, dz, dc in column:
+                send, recv = post.fresh(), post.fresh()
+                first = pl.multiple_of(
+                    (2 * (zz % 2) + cc) * quarter + start, 128
+                )
+                here = ref.at[(yh, x, c, z, yl) + tails[0]]
+                post.start(src.at[:, pl.ds(first, width)], here, send, recv, {**z_at(zz), "seq_2": cc})
+                post.late.append((send, here))
+                marks.append((ref.at[(yh, x, (c + dc) % 2, (z + 4 - dz) % 4, yl) + tails[0]], recv))
+            yield
+            for view, recv in marks:
+                arrived(view, recv)
+            three = pl.ds(0, 3)
+            sizes = {}
+            for axis in "xy":
+                sizes[axis, 0] = ref.at[(0, three, every, every, 0) + tails[0]]
+                sizes[axis, 1] = ref.at[(every, three, every, every, every) + tails[0]]
+            yield from rings(block, order, sizes, True, nothing)
+
+        def down_stream(ref, order, start, width):
+            tails = [
+                (every, pl.ds(start, width)),
+                (every, pl.ds(start, width // 2)),
+                (every, pl.ds(start + width // 2, width // 2)),
+            ]
+            zh = z // 2
+
+            def block(done, axis, at, half):
+                spot = place(done, axis, at)
+                tail = tails[0 if half is None else half + 1]
+                return ref.at[(spot["yh"], spot["x"], every, spot["yl"]) + tail]
+
+            send, recv = post.fresh(), post.fresh()
+            here = ref.at[(yh, x, zh, yl) + tails[0]]
+            post.start(here, here, send, recv, z_at((z + 2) % 4))
+            post.late.append((send, here))
+            yield
+            arrived(ref.at[(yh, x, 1 - zh, yl) + tails[0]], recv)
+            three = pl.ds(0, 3)
+            sizes = {}
+            for axis in "xy":
+                sizes[axis, 0] = ref.at[(0, three, every, 0) + tails[0]]
+                sizes[axis, 1] = ref.at[(every, three, every, every) + tails[0]]
+            yield from rings(block, order, sizes, True, nothing)
+
+        def table_stream(ref):
+            send_y, recv_y = post.fresh(), post.fresh()
+            post.late.append((send_y, ref.at[0]))
+            own = ref.at[2 * z + yl]
+            post.start(own, own, send_y, recv_y, {"fsdp_2": 1 - yl})
+            yield
+            arrived(ref.at[2 * z + 1 - yl], recv_y)
+            half_rows = ref.shape[1] // 2
+            part = (every, pl.ds(0, half_rows), pl.ds(half_rows, half_rows))
+
+            def block(done, axis, at, half):
+                return ref.at[pl.ds(2 * at, 2), part[0 if half is None else half + 1]]
+
+            yield from rings(block, ("z",), {("z", 0): ref.at[pl.ds(0, 6)]}, True, nothing)
+
         own_views = [
             (ins[0], outs[0].at[yh, x, c, z, yl]),
             (ins[1], outs[1].at[yh, x, c, z, yl]),
             (ins[2], outs[2].at[z * 2 + yl]),
             (ins[3], outs[3].at[seq]),
+            (
+                ins[4].at[:, pl.ds(pl.multiple_of((2 * (z % 2) + c) * quarter, 128), quarter)],
+                outs[4].at[yh, x, c, z, yl],
+            ),
+            (ins[5], outs[5].at[yh, x, z // 2, yl]),
         ]
         local = []
         for src, dst in own_views:
@@ -382,7 +446,9 @@
             copy.start()
             local.append(copy)
         greet_devices(
-            [beside(axis, step) for axis in "yz" for step in (1, -1)] + seq_peers()
+            [beside("y", 1), beside("y", -1)]
+            + [{**z_at(zz), "seq_2": cc} for zz, cc, dz, dc in column if dz]
+            + seq_peers()
         )
         for copy in local:
             copy.wait()
@@ -396,12 +462,14 @@
         third = qkvo.shape[1] // 3
         streams = {
             "s": all_stream(outs[1], "xyz", [(every, every)] * 2, False),
-            "t": relay(
-                post, outs[2], (pl.ds(0, 2000),), (pl.ds(2000, 2000),), (pl.ds(0, 1008),),
-                (pl.ds(1008, 992),),
-            ),
+            "t": table_stream(outs[2]),
         }
-        for n, order in enumerate(("yzx", "zyx", "zxy")):
+        half, wide = quarter // 2, down.shape[1] // 2
+        streams["g0"] = gate_up_stream(ins[4], outs[4], "xy", 0, half)
+        streams["g1"] = gate_up_stream(ins[4], outs[4], "yx", half, half)
+        streams["d0"] = down_stream(outs[5], "xy", 0, wide)
+        streams["d1"] = down_stream(outs[5], "yx", wide, wide)
+        for n, order in enumerate(('xyz', 'yzx', 'zxy')):
             streams["q%d" % n] = all_stream(
                 outs[0], order,
                 [
@@ -417,8 +485,8 @@
         post.finish()
 
     return remote_call(
-        body, out_shape, [ANY] * 4, [ANY] * 4, [DMA((sem_count,))], 1, "gather_weights"
-    )(qkvo, small, table, ids)
+        body, out_shape, [ANY] * 6, [ANY] * 6, [DMA((sem_count,))], 1, "gather_weights"
+    )(qkvo, small, table, ids, gate_up, down)
 
 
 def rows_of_tokens(table, ids, collective_id):
@@ -714,9 +782,9 @@
 
     def body(*refs):
         if forward:
-            (src, gu_hbm, dn_hbm, out, gu_out, held, gu_blocks, dn, saved_v, mid, part, give, got, sem) = refs
+            (src, gu_hbm, dn_hbm, out, gu_out, held, gu, dn, saved_v, mid, part, give, got, sem) = refs
         else:
-            (src, gu_hbm, dn_hbm, gu_in, out, held, gu_blocks, dn, saved_v, mid, part, give, got, sem) = refs
+            (src, gu_hbm, dn_hbm, gu_in, out, held, gu, dn, saved_v, mid, part, give, got, sem) = refs
         c = lax.axis_index("seq_2")
         sibling = {"seq_2": 1 - c}
         partner = {"fsdp_1": 1 - lax.axis_index("fsdp_1")}
@@ -726,10 +794,7 @@
             used[0] += 1
             return sem.at[used[0] - 1]
 
-        gu = gu_blocks.reshape(width, quarter)
-        load_gu = [
-            pltpu.make_async_copy(gu_hbm.at[:, k], gu_blocks.at[:, :, k], fresh()) for k in range(2)
-        ]
+        load_gu = [pltpu.make_async_copy(gu_hbm, gu, fresh())]
         load_dn = [pltpu.make_async_copy(dn_hbm, dn, fresh())]
         loads = [load_gu, load_dn]
         if not forward:
@@ -858,7 +923,7 @@
 
     scratch = [
         pltpu.VMEM((4 * count, width), jnp.bfloat16),
-        pltpu.VMEM((8, 8, 2, 16, quarter), jnp.bfloat16),
+        pltpu.VMEM(gate_up_w.shape, jnp.bfloat16),
         pltpu.VMEM(down_w.shape, jnp.bfloat16),
         pltpu.VMEM((4 * count, quarter), jnp.float32),
         pltpu.VMEM((2 * count, units if forward else quarter), jnp.bfloat16),
@@ -1200,21 +1265,16 @@
         (0, 1024 - 848),
     ).reshape(8, 128)
     ids_own = jnp.pad(input_token_index.reshape(16, TOK), ((0, 0), (0, 64)))
-    gate_up_w = lax.all_gather(
-        spread_gate_up(gate_up_own, 14).reshape(128, PAD_FF // 2),
-        ("seq_0", "seq_1", "fsdp_2"),
-        axis=0,
-        tiled=True,
-    ).reshape(8, 2, 8, 16, PAD_FF // 2)
-    down_w = lax.all_gather(
-        down_own, ("seq_0", "seq_1", "fsdp_0", "fsdp_2"), axis=0, tiled=True
-    )
-    qkvo, small, table, ids = gather_weights(
+    qkvo, small, table, ids, gate_up_w, down_w = gather_weights(
         qkvo_own,
         small_own,
         embedding.astype(jnp.bfloat16),
         ids_own,
-    )
+        gate_up_own,
+        down_own,
+    )
+    gate_up_w = gate_up_w.reshape(2048, PAD_FF // 2)
+    down_w = down_w.reshape(PAD_FF // 4, 2048)
     qkvo = qkvo.reshape(2048, 4608)
     w_qkv, w_out = qkvo[:, :2560], qkvo[:, 2560:]
     head_own, ids = lax.optimization_barrier((frozen_output_table, ids))

time: 960 us -> 755 us (0.79)
  waiting for transfers between devices: 251 us -> 3.87 us
  Pallas kernels: 572 us -> 613 us
    all_gather x2 -> x0, waiting for transfers between devices: 166 us -> none  [the longest x1 166 us: per_device(): lax.all_gather(spread_gate_up(gate_up_own, 14).reshape(128, PAD_FF // 2),...]
    all_gather x1, waiting for transfers between devices: 84.9 us -> 3.85 us  [per_device(): head = lax.all_gather(head_own, SEQ, axis=1, tiled=True)]
    pallas_call x2 -> x1, Pallas kernels: 244 us -> 280 us  [gather_weights(): remote_call(body, out_shape, [ANY] * 6, [ANY] * 6, [DMA((sem_count,))], 1...]
  transfers between devices with their start and end apart: 3 -> 1, of which waited for: 2 -> 1; matrix products, arithmetic and copies ran while one was open for 5% -> 5% of each run, Pallas kernels for 35% -> 13%
where the time goes in v4:
time: 755 us; the launch traced here: 745 us
  Pallas kernels  613 us (81%)
  matrix products  44.9 us (6%)
  other arithmetic  35.4 us (5%)
  local copies, waits for them, and re-layouts  28.6 us (4%)
  between operations  19.6 us (3%)
    pallas_call x1, Pallas kernels, gather_weights(): remote_call(body, out_shape, [ANY] * 6, [ANY] * 6, [DMA((sem_count,))], 1...  280 us
    pallas_call x1, Pallas kernels, token_gradients(): remote_call(body, [jax.ShapeDtypeStruct((vocab, width), jnp.float32), jax...  76.3 us
    pallas_call x1, Pallas kernels, head_step(): remote_call(body, [jax.ShapeDtypeStruct((64, width), jnp.float32), jax.Sh...  74.8 us
    pallas_call x1, Pallas kernels, feed_forward(): remote_call(body, total, [VMEM, ANY, ANY, ANY], VMEM, scratch, collective...  38.7 us
    pallas_call x1, Pallas kernels, feed_forward(): remote_call(body, [total, products], [VMEM, ANY, ANY], [VMEM, ANY], scrat...  36.7 us
    pallas_call x1, Pallas kernels, rows_of_tokens(): remote_call(body, jax.ShapeDtypeStruct((128, SEQ_N * width), jnp.bfloat16...  28.2 us
    pallas_call x1, Pallas kernels, key_value_window(): remote_call(body, jax.ShapeDtypeStruct((2, 5 * TOK, 512), jnp.bfloat16),...  26.3 us
    dot_general x6, matrix products, nt(): lax.dot_general(left, right, (((1,), (1,)), ((), ())), preferred_element_...  18.3 us
  transfers between devices with their start and end apart: 1, of which 1 were waited for; matrix products, arithmetic and copies ran while one was open for 5% of the time, Pallas kernels for 13%

profile of v4, /device:TPU:1, one launch (start us, length us, event | category | flops | bytes accessed | tf_op | source)
XLA Modules:
  0.0 745.4 jit_solution(2847761317163793135)
XLA Ops:
  7.2 3.9 reshape.404
  12.2 1.4 pad.23
  13.6 2.8 reshape.405.refs_4_
  20.5 279.5 %gather_weights.1 = (bf16[2,4,2,4,2,16,4608]{6,5,4,3,2,1,0:T(8,128)(2,1)}, f32[2,4,2,4,2,8,128]{6,5,4,3,2,1,0:T(8,128)}, bf16[8,4000,128]{2,1,0:T(8,128)(2,1)}, ...) custom-call(bf16[16,4608]{1,0:T(8,128)(2,1)} %pad_maximum_fusion.4.ref, ...), custom_call_target="tpu_custom_call" | custom-call | tf_op jit(solution)/shard_map/gather_weights/pallas_call | solution.py:487
  304.8 28.2 %rows_of_tokens.1 = bf16[128,2048]{1,0:T(8,128)(2,1)} custom-call(s32[16,128]{1,0:T(8,128)} %reshape.407.ids_ref, bf16[32000,128]{1,0:T(8,128)(2,1)} %bitcast.167), custom_call_target="tpu_custom_call" | custom-call | tf_op jit(solution)/shard_map/rows_of_tokens/pallas_call | solution.py:522
  334.8 1.4 convolution_convert_fusion.1
  336.2 5.2 fusion.2
  349.8 26.3 %key_value_window.1.kv_ref = bf16[2,320,512]{2,1,0:T(8,128)(2,1)} custom-call(f32[128,512]{1,0:T(8,128)} %slice.161.kv_ref, f32[64,512]{1,0:T(8,128)} %copy.123.cos_ref, f32[64,512]{1,0:T(8,128)} %tile.21.sin_ref), custom_call_target="tpu_custom_call" | custom-call | tf_op jit(solution)/shard_map/key_value_window/pallas_call | solution.py:976
  376.2 7.9 %attend.1 = (bf16[128,2048]{1,0:T(8,128)(2,1)}, bf16[128,2048]{1,0:T(8,128)(2,1)}) custom-call(s32[1]{0:T(128)} %bitcast.5.start_ref, s32[4]{0:T(128)} %shift_ref.3, f32[128,2560]{1,0:T(8,128)} %copy-done.5, bf16[2,320,512]{2,1,0:T(8,128)(2,1)} %key_value_window.1.kv_ref, f32[64,512]{1,0:T(8,128)} %copy.123.cos_ref, f32[64,512]{1,0:T(8,128)} %tile.21.sin_ref, ...), custom_call_target="tpu_custom_call" | custom-call | tf_op jit(solution)/shard_map/attend/pallas_call | solution.py:1071
  385.4 4.8 fusion.10
  392.1 36.7 %feed_forward.1 = (f32[128,2048]{1,0:T(8,128)}, f32[512,3072]{1,0:T(8,128)}) custom-call(bf16[128,2048]{1,0:T(8,128)(2,1)} %multiply_convert_fusion.1.refs_0_, bf16[2048,3072]{1,0:T(8,128)(2,1)} %bitcast.163, bf16[1536,2048]{1,0:T(8,128)(2,1)} %bitcast.165), custom_call_target="tpu_custom_call" | custom-call | tf_op jit(solution)/shard_map/feed_forward/pallas_call | solution.py:938
  430.1 1.4 multiply_reduce_fusion.5
  433.5 1.4 broadcast_divide_fusion.scaled_ref
  435.9 3.9 all-gather.2.cloned.1.call-done.head_hbm
  439.7 74.8 %head_step.1 = (f32[64,2048]{1,0:T(8,128)}, f32[8,128]{1,0:T(8,128)}) custom-call(bf16[64,2048]{1,0:T(8,128)(2,1)} %convolution_convert_fusion.chosen_ref, bf16[4000,2048]{1,0:T(8,128)(2,1)} %all-gather.2.cloned.1.call-done.head_hbm, s32[512,1]{1,0:T(8,128)} %compare_select_fusion.target_ref, f32[512,1]{1,0:T(8,128)} %copy-done.6, ...), custom_call_target="tpu_custom_call" | custom-call | tf_op jit(solution)/shard_map/head_step/pallas_call | solution.py:639
  514.5 2.6 multiply_reduce_fusion.1
  518.1 38.7 %feed_forward_back.1 = f32[128,2048]{1,0:T(8,128)} custom-call(bf16[128,2048]{1,0:T(8,128)(2,1)} %fusion.161.refs_0_, bf16[2048,3072]{1,0:T(8,128)(2,1)} %bitcast.164, bf16[1536,2048]{1,0:T(8,128)(2,1)} %bitcast.166, f32[512,3072]{1,0:T(8,128)} %get-tuple-element.46.refs_3_), custom_call_target="tpu_custom_call" | custom-call | tf_op jit(solution)/shard_map/feed_forward_back/pallas_call | solution.py:941
  556.9 2.2 multiply_reduce_fusion.2
  560.6 6.3 fusion.4
  568.2 11.1 %attend_back.1 = (bf16[128,2048]{1,0:T(8,128)(2,1)}, bf16[2,256,512]{2,1,0:T(8,128)(2,1)}, f32[2,64,512]{2,1,0:T(8,128)}) custom-call(s32[1]{0:T(128)} %bitcast.5.start_ref, s32[4]{0:T(128)} %shift_ref.3, bf16[128,2048]{1,0:T(8,128)(2,1)} %get-tuple-element.47.q_ref, bf16[2,320,512]{2,1,0:T(8,128)(2,1)} %key_value_window.1.kv_ref, ...), custom_call_target="tpu_custom_call" | custom-call | tf_op jit(solution)/shard_map/attend_back/pallas_call | solution.py:1116
  579.3 16.5 %key_value_back.1 = bf16[128,512]{1,0:T(8,128)(2,1)} custom-call(bf16[2,256,512]{2,1,0:T(8,128)(2,1)} %get-tuple-element.49.far_ref, f32[2,64,512]{2,1,0:T(8,128)} %get-tuple-element.50.own_ref, f32[64,512]{1,0:T(8,128)} %copy.123.cos_ref, f32[64,512]{1,0:T(8,128)} %tile.21.sin_ref), custom_call_target="tpu_custom_call" | custom-call | tf_op jit(solution)/shard_map/key_value_back/pallas_call | solution.py:1007
  595.9 1.4 fusion.23
  597.4 7.7 %fusion = f32[128,2048]{1,0:T(8,128)S(1)} fusion(bf16[2048,4608]{1,0:T(8,128)(2,1)} %bitcast.190, bf16[128,512]{1,0:T(8,128)(2,1)} %key_value_back.1, bf16[128,2048]{1,0:T(8,128)(2,1)S(1)} %copy-done.9), kind=kOutput, calls=%fused_computation | convolution fusion | flops 1343488000 | bytes 12189696 | tf_op jit(solution)/shard_map/dot_general | solution.py:1040
  610.8 76.3 %token_gradients.1 = (f32[4000,128]{1,0:T(8,128)}, f32[64,128]{1,0:T(8,128)}) custom-call(bf16[128,2048]{1,0:T(8,128)(2,1)} %fusion.34.src, f32[16,64,128]{2,1,0:T(8,128)} %pad_maximum_fusion.1.small_ref, s32[16,1024]{1,0:T(8,128)} %sub.146.ids_ref), custom_call_target="tpu_custom_call" | custom-call | tf_op jit(solution)/shard_map/token_gradients/pallas_call | solution.py:752
  688.7 1.3 multiply_reduce_fusion.8
  693.0 2.7 multiply_reduce_fusion
  695.7 1.3 slice.145
  697.7 1.3 maximum_bitcast_fusion.src
  699.1 9.7 %totals_seq.1.src = f32[8,128]{1,0:T(8,128)} custom-call(f32[8,128]{1,0:T(8,128)} %maximum_bitcast_fusion.src), custom_call_target="tpu_custom_call" | custom-call | tf_op jit(solution)/shard_map/totals_seq/pallas_call | solution.py:140
  708.8 7.2 totals_fsdp.1
  716.0 1.3 fusion.169
  729.4 6.1 fusion.19
  (300 shorter events, 52.4 us)
Async XLA Ops:
  7.2 432.6 %all-gather.2.cloned.1.call-start = ((), (), s32[]{:S(2)}) async-start(), calls=%async_computation | async-start | bytes 17408000 | tf_op jit(solution)/shard_map/all_gather | solution.py:1281
  304.2 30.6 %copy-start.11 = (bf16[24,2048]{1,0:T(8,128)(2,1)}, bf16[24,2048]{1,0:T(8,128)(2,1)S(1)}, u32[]{:S(2)}) copy-start(bf16[24,2048]{1,0:T(8,128)(2,1)S(1)} %slice.124) | copy-start | bytes 294916
  304.8 36.6 %copy-start.14 = (bf16[8,2560]{1,0:T(8,128)(2,1)}, bf16[8,2560]{1,0:T(8,128)(2,1)S(1)}, u32[]{:S(2)}) copy-start(bf16[8,2560]{1,0:T(8,128)(2,1)S(1)} %slice.160) | copy-start | bytes 122884
  333.0 8.4 %copy-start.53 = (s32[24]{0:T(128)}, s32[24]{0:T(128)S(1)}, u32[]{:S(2)}) copy-start(s32[24]{0:T(128)S(1)} %and_select_fusion) | copy-start | bytes 292
  334.8 6.6 copy-start.44
  344.6 31.6 %copy-start.19 = (s32[2,1,320]{2,1,0:T(1,128)}, s32[2,1,320]{2,1,0:T(1,128)S(1)}, u32[]{:S(2)}) copy-start(s32[2,1,320]{2,1,0:T(1,128)S(1)} %broadcast_in_dim.30.ks_ref) | copy-start | bytes 7684
  348.6 84.8 %copy-start.6 = (f32[512,1]{1,0:T(8,128)}, f32[512,1]{1,0:T(8,128)S(1)}, u32[]{:S(2)}) copy-start(f32[512,1]{1,0:T(8,128)S(1)} %reshape_reshape.4.weight_ref) | copy-start | bytes 6148
  349.8 35.5 %copy-start.1 = (bf16[128,2048]{1,0:T(8,128)(2,1)S(1)}, bf16[128,2048]{1,0:T(8,128)(2,1)}, u32[]{:S(2)}) copy-start(bf16[128,2048]{1,0:T(8,128)(2,1)} %rows_of_tokens.1) | copy-start | bytes 1572868
  391.2 165.6 %copy-start.42 = (f32[128]{0:T(128)}, f32[128]{0:T(128)S(1)}, u32[]{:S(2)}) copy-start(f32[128]{0:T(128)S(1)} %get-tuple-element.160) | copy-start | bytes 1540
  431.5 85.5 %copy-start.40 = (f32[128]{0:T(128)}, f32[128]{0:T(128)S(1)}, u32[]{:S(2)}) copy-start(f32[128]{0:T(128)S(1)} %get-tuple-element.162) | copy-start | bytes 1540
  431.5 85.5 %copy-start.49 = (f32[128]{0:T(128)}, f32[128]{0:T(128)S(1)}, u32[]{:S(2)}) copy-start(f32[128]{0:T(128)S(1)} %get-tuple-element.161) | copy-start | bytes 1540
  560.6 6.3 copy-start.7
  567.1 28.7 %copy-start.15 = (bf16[8,2560]{1,0:T(8,128)(2,1)S(1)}, bf16[8,2560]{1,0:T(8,128)(2,1)}, u32[]{:S(2)}) copy-start(bf16[8,2560]{1,0:T(8,128)(2,1)} %copy-done.14) | copy-start | bytes 122884
  567.1 28.7 %copy-start.54 = (s32[24]{0:T(128)S(1)}, s32[24]{0:T(128)}, u32[]{:S(2)}) copy-start(s32[24]{0:T(128)} %copy-done.53) | copy-start | bytes 292
  579.3 18.0 %copy-start.9 = (bf16[128,2048]{1,0:T(8,128)(2,1)S(1)}, bf16[128,2048]{1,0:T(8,128)(2,1)}, u32[]{:S(2)}) copy-start(bf16[128,2048]{1,0:T(8,128)(2,1)} %get-tuple-element.48) | copy-start | bytes 1572868
  597.3 7.8 %copy-start.28 = (bf16[128,24]{0,1:T(8,128)(2,1)S(1)}, bf16[128,24]{0,1:T(8,128)(2,1)}, u32[]{:S(2)}) copy-start(bf16[128,24]{0,1:T(8,128)(2,1)} %copy-done.27) | copy-start | bytes 18436
  597.3 8.0 %copy-start.8 = (bf16[128,512]{1,0:T(8,128)(2,1)S(1)}, bf16[128,512]{1,0:T(8,128)(2,1)}, u32[]{:S(2)}) copy-start(bf16[128,512]{1,0:T(8,128)(2,1)} %key_value_back.1) | copy-start | bytes 393220
  597.3 8.2 %copy-start.31 = (bf16[128,8]{0,1:T(8,128)(2,1)S(1)}, bf16[128,8]{0,1:T(8,128)(2,1)}, u32[]{:S(2)}) copy-start(bf16[128,8]{0,1:T(8,128)(2,1)} %copy-done.30) | copy-start | bytes 6148
  597.3 8.4 %copy-start.2 = (bf16[128,2048]{1,0:T(8,128)(2,1)S(1)}, bf16[128,2048]{1,0:T(8,128)(2,1)}, u32[]{:S(2)}) copy-start(bf16[128,2048]{1,0:T(8,128)(2,1)} %rows_of_tokens.1) | copy-start | bytes 1572868
  597.4 8.4 %copy-start.45 = (f32[128]{0:T(128)S(1)}, f32[128]{0:T(128)}, u32[]{:S(2)}) copy-start(f32[128]{0:T(128)} %copy-done.44) | copy-start | bytes 1540
  609.6 81.9 %copy-start.29 = (f32[288,4]{0,1:T(4,128)S(1)}, f32[288,4]{0,1:T(4,128)}, u32[]{:S(2)}) copy-start(f32[288,4]{0,1:T(4,128)} %convert_bitcast_fusion) | copy-start | bytes 13828
  610.8 108.0 %copy-start.23 = (f32[8,8,8]{2,1,0:T(8,128)S(1)}, f32[8,8,8]{2,1,0:T(8,128)}, u32[]{:S(2)}) copy-start(f32[8,8,8]{2,1,0:T(8,128)} %param.41) | copy-start | bytes 6148
  693.0 31.4 %copy-start.43 = (f32[8,8]{1,0:T(8,128)S(1)}, f32[8,8]{1,0:T(8,128)}, u32[]{:S(2)}) copy-start(f32[8,8]{1,0:T(8,128)} %fusion.125) | copy-start | bytes 772
  695.7 31.5 %copy-start.46 = (f32[4,16]{1,0:T(4,128)S(1)}, f32[4,16]{1,0:T(4,128)}, u32[]{:S(2)}) copy-start(f32[4,16]{1,0:T(4,128)} %param.42) | copy-start | bytes 772
  695.7 32.3 %copy-start.26 = (f32[32,16]{0,1:T(8,128)S(1)}, f32[32,16]{0,1:T(8,128)}, u32[]{:S(2)}) copy-start(f32[32,16]{0,1:T(8,128)} %param.39) | copy-start | bytes 6148
  695.7 33.1 %copy-start.55 = (f32[36]{0:T(128)S(1)}, f32[36]{0:T(128)}, u32[]{:S(2)}) copy-start(f32[36]{0:T(128)} %param.43) | copy-start | bytes 436
  695.7 33.6 %copy-start.4 = (f32[4000,128]{1,0:T(8,128)S(1)}, f32[4000,128]{1,0:T(8,128)}, u32[]{:S(2)}) copy-start(f32[4000,128]{1,0:T(8,128)} %param.28) | copy-start | bytes 6144004
  719.0 16.4 %copy-start.24 = (f32[8,8,8]{2,1,0:T(8,128)}, f32[8,8,8]{2,1,0:T(8,128)S(1)}, u32[]{:S(2)}) copy-start(f32[8,8,8]{2,1,0:T(8,128)S(1)} %get-tuple-element.129) | copy-start | bytes 6148
  728.8 6.6 copy-start.34
  729.3 7.0 copy-start.39
  729.3 7.0 copy-start.47
  729.3 6.9 copy-start.48
  (26 other events, 82.5 us)
Sparse Core Ops, SparseCore 0:
  300.2 139.5 all-gather.1

commit v5 on v3

--- a/solution.py
+++ b/solution.py
@@ -62,39 +62,6 @@
     return {**z_at(i // 2), "fsdp_2": i % 2}
 
 
-RINGS = {"seq": (SEQ_N, seq_me, seq_at), "fsdp": (FSDP_N, fsdp_me, fsdp_at)}
-
-
-def greet(kind, offsets):
-    count, where, at = RINGS[kind]
-    me = where()
-    barrier = pltpu.get_barrier_semaphore()
-    for k in offsets:
-        pl.semaphore_signal(
-            barrier, inc=1, device_id=at((me + count - k) % count), device_id_type=MESH_ID
-        )
-    pl.semaphore_wait(barrier, len(offsets))
-    return me
-
-
-def send_each(kind, me, offsets, src_of, dst_of, send_sem, recv_sem):
-    count, _, at = RINGS[kind]
-    copies = []
-    for n, k in enumerate(offsets):
-        peer = (me + k) % count
-        copy = pltpu.make_async_remote_copy(
-            src_ref=src_of(k, peer),
-            dst_ref=dst_of(k, peer),
-            send_sem=send_sem.at[n],
-            recv_sem=recv_sem.at[n],
-            device_id=at(peer),
-            device_id_type=MESH_ID,
-        )
-        copy.start()
-        copies.append(copy)
-    return copies
-
-
 def remote_call(body, out_shape, in_specs, out_specs, scratch, collective_id, name):
     return pl.pallas_call(
         body,
@@ -109,51 +76,20 @@
     )
 
 
-def sems(n):
-    return [DMA((n,)), DMA((n,))]
-
-
 ALL16 = range(1, SEQ_N)
 ALL8 = range(1, FSDP_N)
 
 
-def sum_over(kind, block, collective_id, name, scatter):
-    count = RINGS[kind][0]
-    offsets = ALL16 if kind == "seq" else ALL8
-    part = block.shape[1:] if scatter else block.shape
-
-    def body(src, out, held, ssem, rsem):
-        me = greet(kind, offsets)
-        copies = send_each(
-            kind, me, offsets,
-            (lambda k, p: src.at[p]) if scatter else (lambda k, p: src),
-            lambda k, p: held.at[k - 1], ssem, rsem,
-        )
-        total = (src[me] if scatter else src[...]).astype(jnp.float32)
-        for n, copy in enumerate(copies):
-            copy.wait_recv()
-            total = total + held[n].astype(jnp.float32)
-        out[...] = total
-        for copy in copies:
-            copy.wait_send()
-
-    return remote_call(
-        body,
-        jax.ShapeDtypeStruct(part, jnp.float32),
-        [VMEM],
-        VMEM,
-        [pltpu.VMEM((count - 1, *part), block.dtype)] + sems(count - 1),
-        collective_id,
-        name,
-    )(block)
-
-
 ORDER = (
-    "s", "t", "q0", "q1", "q2", "s", "s", "q0", "q0", "s", "q1", "q2",
-    "q1", "q2", "s", "s", "q0", "s", "q1", "q2", "s", "s", "q2", "q2",
-    "q1", "q1", "q2", "q0", "q0", "s", "q1", "t", "q0", "q2", "q2", "t",
-    "t", "t", "t", "q2", "q1", "q1", "q0", "q0", "t", "q1", "t", "q0",
+    "q2", "s", "q0", "d0", "t0", "q1", "q0", "q2", "d1", "d0", "s", "q2",
+    "q1", "g0", "q1", "q0", "q2", "d1", "g1", "q0", "s", "q2", "q2", "g0",
+    "t0", "t1", "g1", "q2", "t1", "q1", "g1", "d0", "q2", "g0", "s", "g1",
+    "q0", "d0", "g0", "s", "d1", "d1", "s", "q1", "q2", "q1", "q1", "s",
+    "q0", "t0", "d1", "g1", "d0", "q0", "g0", "t0", "q1", "g0", "q1", "d1",
+    "d1", "t0", "g1", "g0", "q2", "q0", "g1", "d0", "q0", "s", "s", "d1",
+    "t1", "d0", "q1", "t1", "q0", "g0", "s", "d0", "t1", "g1",
 )
+EVERY = slice(None)
 
 
 class Post:
@@ -246,144 +182,228 @@
         copy.wait_recv()
 
 
-def spread_gate_up(gate_up, collective_id):
-    rows = gate_up.shape[0]
+def no_hand(view):
+    return None
+
+
+class Ways:
+    def __init__(self, post):
+        self.post = post
+        self.yh, self.x, self.c = (lax.axis_index(a) for a in SEQ)
+        self.z, self.yl = z_me(), lax.axis_index("fsdp_2")
+        self.where = {"x": self.x, "y": 2 * self.yh + self.yl, "z": self.z}
+        z, c = self.z, self.c
+        self.column = [
+            ((z + dz) % 4, (c + dc) % 2, dz, dc) for dz in range(4) for dc in range(2) if dz or dc
+        ]
+
+    def beside(self, axis, step):
+        at = (self.where[axis] + step + 4) % 4
+        if axis == "x":
+            return {"seq_1": at}
+        if axis == "z":
+            return z_at(at)
+        return {"seq_0": at // 2, "fsdp_2": at % 2}
+
+    def all_devices(self):
+        return (
+            [self.beside("y", 1), self.beside("y", -1)]
+            + [{**z_at(zz), "seq_2": cc} for zz, cc, dz, dc in self.column if dz]
+            + seq_peers()
+        )
+
+    def arrived(self, ref, rsem):
+        pltpu.make_async_copy(ref, ref, rsem).wait()
+
+    def rings(self, block, order, sizes, halves, across):
+        post = self.post
+        for n, axis in enumerate(order):
+            done = order[:n]
+            at = self.where[axis]
+            before, after, far = (at + 3) % 4, (at + 1) % 4, (at + 2) % 4
+            send, from_before, from_after, far_first = (post.fresh() for _ in range(4))
+            post.late.append((send, sizes[axis, n]))
+            own = block(done, axis, at, None)
+            post.start(own, own, send, from_before, self.beside(axis, 1))
+            post.start(own, own, send, from_after, self.beside(axis, -1))
+            yield
+            got = block(done, axis, before, None)
+            self.arrived(got, from_before)
+            half = block(done, axis, before, 0)
+            post.start(half, half, send, far_first, self.beside(axis, 1))
+            across(got)
+            yield
+            got = block(done, axis, after, None)
+            self.arrived(got, from_after)
+            if halves:
+                far_second = post.fresh()
+                half = block(done, axis, after, 1)
+                post.start(half, half, send, far_second, self.beside(axis, -1))
+            across(got)
+            yield
+            self.arrived(block(done, axis, far, 0), far_first)
+            if halves:
+                self.arrived(block(done, axis, far, 1), far_second)
+            across(block(done, axis, far, None))
+
+    def place(self, done, axis, at):
+        spot = {"yh": self.yh, "x": self.x, "z": self.z, "yl": self.yl}
+        for a in done:
+            if a == "y":
+                spot["yh"] = spot["yl"] = EVERY
+            else:
+                spot[a] = EVERY
+        if axis == "y":
+            spot["yh"], spot["yl"] = at // 2, at % 2
+        elif axis is not None:
+            spot[axis] = at
+        return spot
+
+    def everything(self, ref, order, tails, halves=True):
+        post, c = self.post, self.c
+
+        def block(done, axis, at, half):
+            spot = self.place(done, axis, at)
+            tail = tails[0 if half is None else half + 1]
+            return ref.at[(spot["yh"], spot["x"], c, spot["z"], spot["yl"]) + tail]
+
+        across_s, across_r = post.fresh(), post.fresh()
+        post.late.append((across_s, ref.at[(EVERY, EVERY, c, EVERY, EVERY) + tails[0]]))
+        post.late.append((across_r, ref.at[(EVERY, EVERY, 1 - c, EVERY, EVERY) + tails[0]]))
+
+        def across(view):
+            post.start(view, view, across_s, across_r, {"seq_2": 1 - c})
+
+        three = pl.ds(0, 3)
+        sizes = {}
+        for axis in "xyz":
+            sizes[axis, 0] = ref.at[(0, 0, 0, three, 0) + tails[0]]
+            sizes[axis, 1] = ref.at[(0, pl.ds(0, 2), 0, three, EVERY) + tails[0]]
+            sizes[axis, 2] = ref.at[(EVERY, EVERY, 0, three, EVERY) + tails[0]]
+        across(block([], None, None, None))
+        yield from self.rings(block, order, sizes, halves, across)
+
+    def gate_up(self, src, ref, order, start, width):
+        post = self.post
+        quarter = src.shape[1] // 4
+        yh, x, c, z, yl = self.yh, self.x, self.c, self.z, self.yl
+        tails = [
+            (EVERY, pl.ds(start, width)),
+            (EVERY, pl.ds(start, width // 2)),
+            (EVERY, pl.ds(start + width // 2, width // 2)),
+        ]
+
+        def block(done, axis, at, half):
+            spot = self.place(done, axis, at)
+            tail = tails[0 if half is None else half + 1]
+            return ref.at[(spot["yh"], spot["x"], EVERY, EVERY, spot["yl"]) + tail]
+
+        marks = []
+        for zz, cc, dz, dc in self.column:
+            send, recv = post.fresh(), post.fresh()
+            first = pl.multiple_of((2 * (zz % 2) + cc) * quarter + start, 128)
+            here = ref.at[(yh, x, c, z, yl) + tails[0]]
+            post.start(src.at[:, pl.ds(first, width)], here, send, recv, {**z_at(zz), "seq_2": cc})
+            post.late.append((send, here))
+            marks.append((ref.at[(yh, x, (c + dc) % 2, (z + 4 - dz) % 4, yl) + tails[0]], recv))
+        yield
+        for view, recv in marks:
+            self.arrived(view, recv)
+        three = pl.ds(0, 3)
+        sizes = {}
+        for axis in "xy":
+            sizes[axis, 0] = ref.at[(0, three, EVERY, EVERY, 0) + tails[0]]
+            sizes[axis, 1] = ref.at[(EVERY, three, EVERY, EVERY, EVERY) + tails[0]]
+        yield from self.rings(block, order, sizes, True, no_hand)
+
+    def down(self, ref, order, start, width):
+        post = self.post
+        yh, x, z, yl = self.yh, self.x, self.z, self.yl
+        tails = [
+            (EVERY, pl.ds(start, width)),
+            (EVERY, pl.ds(start, width // 2)),
+            (EVERY, pl.ds(start + width // 2, width // 2)),
+        ]
+        zh = z // 2
+
+        def block(done, axis, at, half):
+            spot = self.place(done, axis, at)
+            tail = tails[0 if half is None else half + 1]
+            return ref.at[(spot["yh"], spot["x"], EVERY, spot["yl"]) + tail]
+
+        send, recv = post.fresh(), post.fresh()
+        here = ref.at[(yh, x, zh, yl) + tails[0]]
+        post.start(here, here, send, recv, z_at((z + 2) % 4))
+        post.late.append((send, here))
+        yield
+        self.arrived(ref.at[(yh, x, 1 - zh, yl) + tails[0]], recv)
+        three = pl.ds(0, 3)
+        sizes = {}
+        for axis in "xy":
+            sizes[axis, 0] = ref.at[(0, three, EVERY, 0) + tails[0]]
+            sizes[axis, 1] = ref.at[(EVERY, three, EVERY, EVERY) + tails[0]]
+        yield from self.rings(block, order, sizes, True, no_hand)
+
+    def table(self, ref, low, high):
+        post, z, yl = self.post, self.z, self.yl
+        middle = (low + high) // 32 * 16
+        part = (pl.ds(low, high - low), pl.ds(low, middle - low), pl.ds(middle, high - middle))
+        send_y, recv_y = post.fresh(), post.fresh()
+        post.late.append((send_y, ref.at[0, part[0]]))
+        own = ref.at[2 * z + yl, part[0]]
+        post.start(own, own, send_y, recv_y, {"fsdp_2": 1 - yl})
+        yield
+        self.arrived(ref.at[2 * z + 1 - yl, part[0]], recv_y)
+
+        def block(done, axis, at, half):
+            return ref.at[pl.ds(2 * at, 2), part[0 if half is None else half + 1]]
+
+        sizes = {("z", 0): ref.at[pl.ds(0, 6), part[0]]}
+        yield from self.rings(block, ("z",), sizes, True, no_hand)
+
+    def own_gate_up(self, src, ref):
+        quarter = ref.shape[-1]
+        first = pl.multiple_of((2 * (self.z % 2) + self.c) * quarter, 128)
+        return src.at[:, pl.ds(first, quarter)], ref.at[self.yh, self.x, self.c, self.z, self.yl]
+
+
+def local_copies(pairs, post):
+    copies = [pltpu.make_async_copy(src, dst, post.fresh()) for src, dst in pairs]
+    for copy in copies:
+        copy.start()
+    return copies
+
+
+def gather_weights(qkvo, small, table, ids, gate_up, down):
     quarter = gate_up.shape[1] // 4
-
-    def body(src, out, sem, lsem):
-        post = Post(sem, 14)
-        z, c = z_me(), lax.axis_index("seq_2")
-        column = [((z + dz) % 4, (c + dc) % 2) for dz in range(4) for dc in range(2) if dz or dc]
-        greet_devices([{**z_at(zz), "seq_2": cc} for zz, cc in column])
-
-        def part(zz, cc):
-            first = pl.multiple_of((2 * (zz % 2) + cc) * quarter, 128)
-            return src.at[:, pl.ds(first, quarter)]
-
-        for zz, cc in column:
-            post.send(part(zz, cc), out.at[c, z], {**z_at(zz), "seq_2": cc})
-        own = pltpu.make_async_copy(part(z, c), out.at[c, z], lsem)
-        own.start()
-        for copy in post.sent:
-            copy.wait_recv()
-        post.finish()
-        own.wait()
-
-    return remote_call(
-        body,
-        jax.ShapeDtypeStruct((2, 4, rows, quarter), gate_up.dtype),
-        [ANY], ANY, [DMA((14,)), DMA], collective_id, "spread_gate_up",
-    )(gate_up)
-
-
-def gather_weights(qkvo, small, table, ids):
     out_shape = [
         jax.ShapeDtypeStruct((2, 4, 2, 4, 2, *qkvo.shape), qkvo.dtype),
         jax.ShapeDtypeStruct((2, 4, 2, 4, 2, *small.shape), small.dtype),
         jax.ShapeDtypeStruct((FSDP_N, *table.shape), table.dtype),
         jax.ShapeDtypeStruct((SEQ_N, *ids.shape), ids.dtype),
+        jax.ShapeDtypeStruct((2, 4, 2, 4, 2, gate_up.shape[0], quarter), gate_up.dtype),
+        jax.ShapeDtypeStruct((2, 4, 2, 2, *down.shape), down.dtype),
     ]
-    sem_count = 160
-    every = slice(None)
+    sem_count = 320
 
     def body(*refs):
-        ins, outs, sem = refs[:4], refs[4:8], refs[8]
+        ins, outs, sem = refs[:6], refs[6:12], refs[12]
         post = Post(sem, sem_count)
-        yh, x, c, z, yl = (
-            lax.axis_index("seq_0"), lax.axis_index("seq_1"), lax.axis_index("seq_2"), z_me(),
-            lax.axis_index("fsdp_2"),
+        ways = Ways(post)
+        yh, x, c, z, yl = ways.yh, ways.x, ways.c, ways.z, ways.yl
+        seq = seq_me()
+        local = local_copies(
+            [
+                (ins[0], outs[0].at[yh, x, c, z, yl]),
+                (ins[1], outs[1].at[yh, x, c, z, yl]),
+                (ins[2], outs[2].at[z * 2 + yl]),
+                (ins[3], outs[3].at[seq]),
+                ways.own_gate_up(ins[4], outs[4]),
+                (ins[5], outs[5].at[yh, x, z // 2, yl]),
+            ],
+            post,
         )
-        where = {"x": x, "y": 2 * yh + yl, "z": z}
-        seq = seq_me()
-
-        def beside(axis, step):
-            at = (where[axis] + step + 4) % 4
-            if axis == "x":
-                return {"seq_1": at}
-            if axis == "z":
-                return z_at(at)
-            return {"seq_0": at // 2, "fsdp_2": at % 2}
-
-        other = {"seq_2": 1 - c}
-
-        def arrived(ref, rsem):
-            pltpu.make_async_copy(ref, ref, rsem).wait()
-
-        def rings(block, order, sizes, halves, across):
-            for n, axis in enumerate(order):
-                done = order[:n]
-                at = where[axis]
-                before, after, far = (at + 3) % 4, (at + 1) % 4, (at + 2) % 4
-                send, from_before, from_after, far_first = (post.fresh() for _ in range(4))
-                post.late.append((send, sizes[axis, n]))
-                own = block(done, axis, at, None)
-                post.start(own, own, send, from_before, beside(axis, 1))
-                post.start(own, own, send, from_after, beside(axis, -1))
-                yield
-                got = block(done, axis, before, None)
-                arrived(got, from_before)
-                half = block(done, axis, before, 0)
-                post.start(half, half, send, far_first, beside(axis, 1))
-                across(got)
-                yield
-                got = block(done, axis, after, None)
-                arrived(got, from_after)
-                if halves:
-                    far_second = post.fresh()
-                    half = block(done, axis, after, 1)
-                    post.start(half, half, send, far_second, beside(axis, -1))
-                across(got)
-                yield
-                arrived(block(done, axis, far, 0), far_first)
-                if halves:
-                    arrived(block(done, axis, far, 1), far_second)
-                across(block(done, axis, far, None))
-
-        def all_stream(ref, order, tails, halves=True):
-            def block(done, axis, at, half):
-                spot = {"yh": yh, "x": x, "z": z, "yl": yl}
-                for a in done:
-                    if a == "y":
-                        spot["yh"] = spot["yl"] = every
-                    else:
-                        spot[a] = every
-                if axis == "y":
-                    spot["yh"], spot["yl"] = at // 2, at % 2
-                elif axis is not None:
-                    spot[axis] = at
-                tail = tails[0 if half is None else half + 1]
-                return ref.at[(spot["yh"], spot["x"], c, spot["z"], spot["yl"]) + tail]
-
-            across_s, across_r = post.fresh(), post.fresh()
-            post.late.append((across_s, ref.at[(every, every, c, every, every) + tails[0]]))
-            post.late.append((across_r, ref.at[(every, every, 1 - c, every, every) + tails[0]]))
-
-            def across(view):
-                post.start(view, view, across_s, across_r, other)
-
-            three = pl.ds(0, 3)
-            sizes = {}
-            for axis in "xyz":
-                sizes[axis, 0] = ref.at[(0, 0, 0, three, 0) + tails[0]]
-                sizes[axis, 1] = ref.at[(0, pl.ds(0, 2), 0, three, every) + tails[0]]
-                sizes[axis, 2] = ref.at[(every, every, 0, three, every) + tails[0]]
-            across(block([], None, None, None))
-            yield from rings(block, order, sizes, halves, across)
-
-        own_views = [
-            (ins[0], outs[0].at[yh, x, c, z, yl]),
-            (ins[1], outs[1].at[yh, x, c, z, yl]),
-            (ins[2], outs[2].at[z * 2 + yl]),
-            (ins[3], outs[3].at[seq]),
-        ]
-        local = []
-        for src, dst in own_views:
-            copy = pltpu.make_async_copy(src, dst, post.fresh())
-            copy.start()
-            local.append(copy)
-        greet_devices(
-            [beside(axis, step) for axis in "yz" for step in (1, -1)] + seq_peers()
-        )
+        greet_devices(ways.all_devices())
         for copy in local:
             copy.wait()
 
@@ -395,19 +415,23 @@
 
         third = qkvo.shape[1] // 3
         streams = {
-            "s": all_stream(outs[1], "xyz", [(every, every)] * 2, False),
-            "t": relay(
-                post, outs[2], (pl.ds(0, 2000),), (pl.ds(2000, 2000),), (pl.ds(0, 1008),),
-                (pl.ds(1008, 992),),
-            ),
+            "s": ways.everything(outs[1], "xyz", [(EVERY, EVERY)] * 2, False),
         }
-        for n, order in enumerate(("yzx", "zyx", "zxy")):
-            streams["q%d" % n] = all_stream(
+        rows = table.shape[0]
+        cuts = (0, 1984, rows)
+        for n in range(len(cuts) - 1):
+            streams["t%d" % n] = ways.table(outs[2], cuts[n], cuts[n + 1])
+        half, wide = quarter // 2, down.shape[1] // 2
+        for n, order in enumerate(("xy", "yx")):
+            streams["g%d" % n] = ways.gate_up(ins[4], outs[4], order, n * half, half)
+            streams["d%d" % n] = ways.down(outs[5], order, n * wide, wide)
+        for n, order in enumerate(('yxz', 'xyz', 'zyx')):
+            streams["q%d" % n] = ways.everything(
                 outs[0], order,
                 [
-                    (every, pl.ds(n * third, third)),
-                    (every, pl.ds(n * third, third // 2)),
-                    (every, pl.ds(n * third + third // 2, third // 2)),
+                    (EVERY, pl.ds(n * third, third)),
+                    (EVERY, pl.ds(n * third, third // 2)),
+                    (EVERY, pl.ds(n * third + third // 2, third // 2)),
                 ],
             )
         for name in ORDER:
@@ -417,55 +441,176 @@
         post.finish()
 
     return remote_call(
-        body, out_shape, [ANY] * 4, [ANY] * 4, [DMA((sem_count,))], 1, "gather_weights"
-    )(qkvo, small, table, ids)
-
-
-def rows_of_tokens(table, ids, collective_id):
-    vocab, width = table.shape
-
-    def body(ids_ref, table_ref, out, wide, rows, block, sem, lsem):
-        post = Post(sem, 30)
+        body, out_shape, [ANY] * 6, [ANY] * 6, [DMA((sem_count,))], 1, "gather_weights"
+    )(qkvo, small, table, ids, gate_up, down)
+
+
+def attention_block(
+    table, ids, qkvo, a_low, b_in, b_out, gain, cosine, sine, query_seg, key_seg, shifts, collective_id
+):
+    vocab, width = table.shape[1:]
+    rows_n = 2 * TOK
+    sem_count = 64
+
+    def body(
+        table_hbm, ids_ref, qkvo_hbm, a_ref, bi_ref, bo_ref, gain_ref, cos_ref, sin_ref, qs_ref, ks_ref,
+        shift_ref,
+        x_out, n_out, u_out, q_out, kv_out, a_out, v_out, mid_out, two_out,
+        stage, wide, rows, block, low, packed, own_kv, w_qkv, w_out, sem,
+    ):
+        post = Post(sem, sem_count)
         me = seq_me()
-        wide[...] = table_ref[...].astype(jnp.float32)
+        loads = [post.fresh() for _ in range(2)]
+
+        def staged(n):
+            return pltpu.make_async_copy(table_hbm.at[n], stage.at[n % 2], loads[n % 2])
+
+        staged(0).start()
+        weights = local_copies(
+            [
+                (qkvo_hbm.at[:, pl.ds(0, 2560)], w_qkv),
+                (qkvo_hbm.at[:, pl.ds(2560, 2048)], w_out),
+            ],
+            post,
+        )
+        greet_devices(seq_peers())
+        for n in range(FSDP_N):
+            if n + 1 < FSDP_N:
+                staged(n + 1).start()
+            staged(n).wait()
+            wide[pl.ds(n * vocab, vocab), :] = stage[n % 2].astype(jnp.float32)
+
         spot = pl.ds(pl.multiple_of(me * width, width), width)
-        greet_devices(seq_peers())
 
         def fetch(s):
             def step(t, carry):
                 rows[pl.ds(t, 1), :] = wide[pl.ds(ids_ref[s, t], 1), :]
                 return carry
 
-            lax.fori_loop(0, 128, step, 0, unroll=16)
-
+            lax.fori_loop(0, rows_n, step, 0, unroll=16)
+
+        moved = []
         for k in list(ALL16) + [0]:
             peer = (me + k) % SEQ_N
             fetch(peer)
             block[k] = rows[...].astype(jnp.bfloat16)
             if k:
-                post.send(block.at[k], out.at[:, spot], seq_at(peer))
-        own = pltpu.make_async_copy(block.at[0], out.at[:, spot], lsem)
+                moved.append(post.send(block.at[k], low.at[:, spot], seq_at(peer)))
+        own = pltpu.make_async_copy(block.at[0], low.at[:, spot], post.fresh())
         own.start()
-        for copy in post.sent:
+        for copy in moved:
             copy.wait_recv()
+        own.wait()
+
+        start = low[...].astype(jnp.float32)
+        x_out[...] = start
+        scale = lax.rsqrt(jnp.mean(start * start, axis=-1, keepdims=True) + NORM_EPS)
+        n_out[...] = (start * scale * gain_ref[0:1, :]).astype(jnp.bfloat16)
+        inner = nt(n_out[...], a_ref[0:24, :]).astype(jnp.bfloat16)
+        u_out[...] = inner
+        weights[0].wait()
+
+        def project(at):
+            packed[:, at] = jnp.dot(
+                n_out[...], w_qkv[:, at], preferred_element_type=jnp.float32
+            ) + ADAPTER_SCALE * jnp.dot(u_out[...], bi_ref[:, at], preferred_element_type=jnp.float32)
+
+        project(pl.ds(2048, 512))
+        for n in range(2):
+            some = slice(n * TOK, n * TOK + TOK)
+            own_kv[n, :, 0:256] = turn(
+                packed[some, 2048:2304], cos_ref[:, 0:256], sin_ref[:, 0:256]
+            ).astype(jnp.bfloat16)
+            own_kv[n, :, 256:512] = packed[some, 2304:2560].astype(jnp.bfloat16)
+        keys = [
+            post.send(
+                own_kv, kv_out.at[:, pl.ds((4 - k) * TOK, TOK), :], seq_at((me + k) % SEQ_N)
+            )
+            for k in range(1, 5)
+        ]
+        kv_out[:, 4 * TOK :, :] = own_kv[...]
+
+        def project_some(n, carry):
+            project(pl.ds(pl.multiple_of(n * 512, 512), 512))
+            return carry
+
+        lax.fori_loop(0, 4, project_some, 0)
+        for copy in keys:
+            copy.wait_recv()
+
+        first = me * TOK
+
+        def attend_one(n, carry):
+            some = pl.ds(pl.multiple_of(n * TOK, TOK), TOK)
+            for h in range(4):
+                cols = slice(512 * h, 512 * h + 512)
+                turned = turn(packed[some, cols], cos_ref[...], sin_ref[...]).astype(jnp.bfloat16)
+                q_out[some, cols] = turned
+                mask = window_mask(first, qs_ref[n], ks_ref[n], shift_ref[h])
+                probs = probabilities(
+                    spread_heads(turned), kv_out[n, :, 64 * h : 64 * h + 64], mask
+                )
+                values = kv_out[n, :, 256 + 64 * h : 256 + 64 * h + 64]
+                mixed = jnp.dot(
+                    probs.astype(jnp.bfloat16), values, preferred_element_type=jnp.float32
+                )
+                a_out[some, cols] = join_heads(mixed).astype(jnp.bfloat16)
+            return carry
+
+        lax.fori_loop(0, 2, attend_one, 0)
+        middle = nt(a_out[...], a_ref[24:32, :]).astype(jnp.bfloat16)
+        v_out[...] = middle
+        weights[1].wait()
+
+        def project_out(n, carry):
+            at = pl.ds(pl.multiple_of(n * 512, 512), 512)
+            mid_out[:, at] = (
+                x_out[:, at]
+                + jnp.dot(a_out[...], w_out[:, at], preferred_element_type=jnp.float32)
+                + ADAPTER_SCALE
+                * jnp.dot(v_out[...], bo_ref[:, at], preferred_element_type=jnp.float32)
+            )
+            return carry
+
+        lax.fori_loop(0, 4, project_out, 0)
+        middle_rows = mid_out[...]
+        scale = lax.rsqrt(jnp.mean(middle_rows * middle_rows, axis=-1, keepdims=True) + NORM_EPS)
+        two_out[...] = (middle_rows * scale * gain_ref[1:2, :]).astype(jnp.bfloat16)
         post.finish()
-        own.wait()
+
+    def shape(*dims, dtype=jnp.bfloat16):
+        return jax.ShapeDtypeStruct(dims, dtype)
 
     return remote_call(
         body,
-        jax.ShapeDtypeStruct((128, SEQ_N * width), jnp.bfloat16),
-        [SMEM, VMEM],
-        VMEM,
         [
-            pltpu.VMEM((vocab, width), jnp.float32),
-            pltpu.VMEM((128, width), jnp.float32),
-            pltpu.VMEM((SEQ_N, 128, width), jnp.bfloat16),
-            DMA((30,)),
-            DMA,
+            shape(rows_n, 2048, dtype=jnp.float32),
+            shape(rows_n, 2048),
+            shape(rows_n, 24),
+            shape(rows_n, 2048),
+            shape(2, 5 * TOK, 512),
+            shape(rows_n, 2048),
+            shape(rows_n, 8),
+            shape(rows_n, 2048, dtype=jnp.float32),
+            shape(rows_n, 2048),
+        ],
+        [ANY, SMEM, ANY] + [VMEM] * 8 + [SMEM],
+        [VMEM] * 9,
+        [
+            pltpu.VMEM((2, vocab, width), jnp.bfloat16),
+            pltpu.VMEM((FSDP_N * vocab, width), jnp.float32),
+            pltpu.VMEM((rows_n, width), jnp.float32),
+            pltpu.VMEM((SEQ_N, rows_n, width), jnp.bfloat16),
+            pltpu.VMEM((rows_n, 2048), jnp.bfloat16),
+            pltpu.VMEM((rows_n, 2560), jnp.float32),
+            pltpu.VMEM((2, TOK, 512), jnp.bfloat16),
+            pltpu.VMEM((2048, 2560), jnp.bfloat16),
+            pltpu.VMEM((2048, 2048), jnp.bfloat16),
+            DMA((sem_count,)),
         ],
         collective_id,
-        "rows_of_tokens",
-    )(ids, table)
+        "attention_block",
+    )(table, ids, qkvo, a_low, b_in, b_out, gain, cosine, sine, query_seg, key_seg, shifts)
 
 
 def head_step(chosen, head, target, weight, scaled, collective_id):
@@ -593,13 +738,16 @@
     )(chosen, head, target, weight, scaled)
 
 
-def token_gradients(d_start, small, ids, vocab, collective_id):
+def token_gradients(d_start, left, right, ids, loss, vocab, collective_id):
     width = 128
     low_n, tile = 1024, 1024
-    rows = small.shape[1]
-
-    def body(src, small_ref, ids_ref, out, small_out, held, parts, mid, parts_b, total, spread, sem, lsem):
-        post = Post(sem, 120)
+
+    def body(
+        src, left_ref, right_ref, ids_ref, loss_ref, out, left_out, right_out, totals_out, held, left_parts,
+        right_parts, left_mid, right_mid, left_more, right_more, total, spread, sums_a, parts_a, sums_b,
+        parts_b, sem, lsem,
+    ):
+        post = Post(sem, 220)
         f, s = fsdp_me(), seq_me()
         z, yl = z_me(), lax.axis_index("fsdp_2")
         greet_devices(seq_peers() + fsdp_peers())
@@ -607,20 +755,30 @@
         def cols(p):
             return pl.ds(pl.multiple_of(p * width, width), width)
 
+        def window(p):
+            return pl.ds(pl.multiple_of((9 * p) // 4 * 128, 128), 384)
+
         moves, sums = [], []
         for k in ALL16:
             peer = (s + k) % SEQ_N
-            sums.append(post.send(small_ref.at[peer], parts.at[k - 1], seq_at(peer)))
+            sums.append(post.send(left_ref.at[:, cols(peer)], left_parts.at[k - 1], seq_at(peer)))
+            sums.append(post.send(right_ref.at[:, window(peer)], right_parts.at[k - 1], seq_at(peer)))
             moves.append(post.send(src.at[:, cols(peer)], held.at[f, s], seq_at(peer)))
         own = pltpu.make_async_copy(src.at[:, cols(s)], held.at[f, s], lsem)
         own.start()
         total[...] = jnp.zeros_like(total)
-        amount = small_ref[s]
-        for n, copy in enumerate(sums):
+        left_sum, right_sum = left_ref[:, cols(s)], right_ref[:, window(s)]
+        for copy in sums:
             copy.wait_recv()
-            amount = amount + parts[n]
-        mid[...] = amount
-        shares = [post.send(mid, parts_b.at[k - 1], fsdp_at((f + k) % FSDP_N)) for k in ALL8]
+        for n in range(15):
+            left_sum, right_sum = left_sum + left_parts[n], right_sum + right_parts[n]
+        left_mid[...] = left_sum
+        right_mid[...] = right_sum
+        shares = []
+        for k in ALL8:
+            device = fsdp_at((f + k) % FSDP_N)
+            shares.append(post.send(left_mid, left_more.at[k - 1], device))
+            shares.append(post.send(right_mid, right_more.at[k - 1], device))
         for copy in moves:
             copy.wait_recv()
         own.wait()
@@ -671,52 +829,115 @@
         assert next(steps, "end") == "end"
         for zz in (before, after, far):
             add(zz * 2 + 1 - yl)
-        for n, copy in enumerate(shares):
-            copy.wait_recv()
-            mid_part = parts_b[n]
-            amount = amount + mid_part
-        small_out[...] = amount
+        squares = jnp.zeros((1, width), jnp.float32)
         for h in range(4):
             count = min(low_n, vocab - h * low_n)
-            out[h * low_n : h * low_n + count, :] = total[0:count, h * width : (h + 1) * width]
+            rows = total[0:count, h * width : (h + 1) * width]
+            out[h * low_n : h * low_n + count, :] = rows
+            squares = squares + jnp.sum(rows * rows, axis=0, keepdims=True)
+        for copy in shares:
+            copy.wait_recv()
+        for n in range(7):
+            left_sum, right_sum = left_sum + left_more[n], right_sum + right_more[n]
+        left_out[...] = left_sum
+        base = (9 * s) // 4 * 128
+        column = lax.broadcasted_iota(jnp.int32, (8, 384), 1) + base
+        right_own = jnp.where((column >= 288 * s) & (column < 288 * s + 288), right_sum, 0.0)
+        right_out[...] = right_sum
+        factor = (column >= 2048).astype(jnp.int32) + (column >= 2304) + (column >= 2560)
+        blank = jnp.zeros((32, width), jnp.float32)
+
+        def products(a, b):
+            return lax.dot_general(
+                a, b, (((1,), (1,)), ((), ())), preferred_element_type=jnp.float32, precision=HIGHEST
+            )
+
+        lane = lax.broadcasted_iota(jnp.int32, (8, width), 1)
+        row = lax.broadcasted_iota(jnp.int32, (8, width), 0)
+        factors = jnp.concatenate([left_sum[0:32], blank, blank, blank], axis=0)
+        result = jnp.zeros((8, width), jnp.float32)
+        for k in range(4):
+            one = products(left_sum[8 * k : 8 * k + 8], factors)
+            result = result + jnp.where(lane >> 3 == k, one, 0.0)
+        for n in range(3):
+            part = right_own[:, n * width : (n + 1) * width]
+            which = factor[:, n * width : (n + 1) * width]
+            spread_rows = [jnp.where(which == k, part, 0.0) for k in range(4)]
+            result = result + products(
+                part, jnp.concatenate([blank] + spread_rows + [blank, blank], axis=0)
+            )
+        small_squares = jnp.sum(
+            jnp.sum(left_sum * left_sum, axis=0, keepdims=True), axis=1, keepdims=True
+        ) + jnp.sum(jnp.sum(right_own * right_own, axis=0, keepdims=True), axis=1, keepdims=True)
+        result = jnp.where((lane == 64) & (row == 0), small_squares, result)
+        result = jnp.where(f == 0, result, 0.0)
+        result = result + jnp.where(
+            (lane == 64) & (row == 0), jnp.sum(squares, axis=1, keepdims=True), 0.0
+        )
+        result = result + jnp.where((lane == 65) & (row == 0), loss_ref[...], 0.0)
+        sums_a[...] = result
+        copies = [post.send(sums_a, parts_a.at[k - 1], seq_at((s + k) % SEQ_N)) for k in ALL16]
+        for copy in copies:
+            copy.wait_recv()
+        for n in range(15):
+            result = result + parts_a[n]
+        sums_b[...] = result
+        copies = [post.send(sums_b, parts_b.at[k - 1], fsdp_at((f + k) % FSDP_N)) for k in ALL8]
+        for copy in copies:
+            copy.wait_recv()
+        for n in range(7):
+            result = result + parts_b[n]
+        totals_out[...] = result
         post.finish()
 
     return remote_call(
         body,
         [
             jax.ShapeDtypeStruct((vocab, width), jnp.float32),
-            jax.ShapeDtypeStruct((rows, width), jnp.float32),
+            jax.ShapeDtypeStruct((40, width), jnp.float32),
+            jax.ShapeDtypeStruct((8, 384), jnp.float32),
+            jax.ShapeDtypeStruct((8, width), jnp.float32),
         ],
-        [VMEM, VMEM, VMEM],
-        [VMEM, VMEM],
+        [VMEM] * 5,
+        [VMEM] * 4,
         [
             pltpu.VMEM((FSDP_N, SEQ_N, 128, width), jnp.bfloat16),
-            pltpu.VMEM((15, rows, width), jnp.float32),
-            pltpu.VMEM((rows, width), jnp.float32),
-            pltpu.VMEM((7, rows, width), jnp.float32),
+            pltpu.VMEM((15, 40, width), jnp.float32),
+            pltpu.VMEM((15, 8, 384), jnp.float32),
+            pltpu.VMEM((40, width), jnp.float32),
+            pltpu.VMEM((8, 384), jnp.float32),
+            pltpu.VMEM((7, 40, width), jnp.float32),
+            pltpu.VMEM((7, 8, 384), jnp.float32),
             pltpu.VMEM((low_n, 4 * width), jnp.float32),
             pltpu.VMEM((tile, 4 * width), jnp.bfloat16),
-            DMA((120,)),
+            pltpu.VMEM((8, width), jnp.float32),
+            pltpu.VMEM((15, 8, width), jnp.float32),
+            pltpu.VMEM((8, width), jnp.float32),
+            pltpu.VMEM((7, 8, width), jnp.float32),
+            DMA((220,)),
             DMA,
         ],
         collective_id,
         "token_gradients",
-    )(d_start, small, ids)
-
-
-def feed_forward(rows, gate_up_w, down_w, saved, collective_id, name):
+    )(d_start, left, right, ids, loss)
+
+
+def feed_forward(rows, gate_up_parts, down_parts, saved, collective_id, name):
     forward = saved is None
     count, width = rows.shape
-    quarter = gate_up_w.shape[-1]
+    quarter = sum(part.shape[1] for part in gate_up_parts)
     units = quarter // 2
+    parts_n = len(gate_up_parts)
     chunk = count // 2
     tile = 512
 
     def body(*refs):
         if forward:
-            (src, gu_hbm, dn_hbm, out, gu_out, held, gu_blocks, dn, saved_v, mid, part, give, got, sem) = refs
+            src, gu_hbm, dn_hbm = refs[0], refs[1 : 1 + parts_n], refs[1 + parts_n : 1 + 2 * parts_n]
+            out, gu_out, held, gu, dn, saved_v, mid, part, give, got, sem = refs[1 + 2 * parts_n :]
         else:
-            (src, gu_hbm, dn_hbm, gu_in, out, held, gu_blocks, dn, saved_v, mid, part, give, got, sem) = refs
+            src, gu_hbm, dn_hbm = refs[0], refs[1 : 1 + parts_n], refs[1 + parts_n : 1 + 2 * parts_n]
+            gu_in, out, held, gu, dn, saved_v, mid, part, give, got, sem = refs[1 + 2 * parts_n :]
         c = lax.axis_index("seq_2")
         sibling = {"seq_2": 1 - c}
         partner = {"fsdp_1": 1 - lax.axis_index("fsdp_1")}
@@ -726,11 +947,13 @@
             used[0] += 1
             return sem.at[used[0] - 1]
 
-        gu = gu_blocks.reshape(width, quarter)
-        load_gu = [
-            pltpu.make_async_copy(gu_hbm.at[:, k], gu_blocks.at[:, :, k], fresh()) for k in range(2)
-        ]
-        load_dn = [pltpu.make_async_copy(dn_hbm, dn, fresh())]
+        load_gu, load_dn = [], []
+        for copies, hbm, whole in ((load_gu, gu_hbm, gu), (load_dn, dn_hbm, dn)):
+            at = 0
+            for piece in hbm:
+                view = whole.at[:, pl.ds(at, piece.shape[1])]
+                copies.append(pltpu.make_async_copy(piece, view, fresh()))
+                at += piece.shape[1]
         loads = [load_gu, load_dn]
         if not forward:
             load_dn.append(pltpu.make_async_copy(gu_in, saved_v, fresh()))
@@ -858,8 +1081,8 @@
 
     scratch = [
         pltpu.VMEM((4 * count, width), jnp.bfloat16),
-        pltpu.VMEM((8, 8, 2, 16, quarter), jnp.bfloat16),
-        pltpu.VMEM(down_w.shape, jnp.bfloat16),
+        pltpu.VMEM((width, quarter), jnp.bfloat16),
+        pltpu.VMEM((units, width), jnp.bfloat16),
         pltpu.VMEM((4 * count, quarter), jnp.float32),
         pltpu.VMEM((2 * count, units if forward else quarter), jnp.bfloat16),
         pltpu.VMEM((2, 2 * count, width), jnp.float32),
@@ -871,11 +1094,12 @@
     if forward:
         products = jax.ShapeDtypeStruct((4 * count, quarter), jnp.float32)
         return remote_call(
-            body, [total, products], [VMEM, ANY, ANY], [VMEM, ANY], scratch, collective_id, name
-        )(rows, gate_up_w, down_w)
+            body, [total, products], [VMEM] + [ANY] * (2 * parts_n), [VMEM, ANY], scratch,
+            collective_id, name,
+        )(rows, *gate_up_parts, *down_parts)
     return remote_call(
-        body, total, [VMEM, ANY, ANY, ANY], VMEM, scratch, collective_id, name
-    )(rows, gate_up_w, down_w, saved)
+        body, total, [VMEM] + [ANY] * (2 * parts_n + 1), VMEM, scratch, collective_id, name
+    )(rows, *gate_up_parts, *down_parts, saved)
 
 
 def turn(values, cosine, sine):
@@ -889,44 +1113,23 @@
     return values * cosine + swapped * sine
 
 
-def key_value_window(key_value, cosine, sine, collective_id):
-    def body(kv_ref, cos_ref, sin_ref, out, held, ssem, rsem, lsem):
-        me = greet("seq", range(1, 5))
-        for m in range(2):
-            rows = kv_ref[pl.ds(m * TOK, TOK), :]
-            held[m, :, 0:256] = turn(rows[:, 0:256], cos_ref[:, 0:256], sin_ref[:, 0:256]).astype(
-                jnp.bfloat16
+def key_value_back(far, own, cosine, sine, collective_id):
+    def body(far_ref, own_ref, cos_ref, sin_ref, out, held, sem):
+        me = seq_me()
+        post = Post(sem, 8)
+        barrier = pltpu.get_barrier_semaphore()
+        for k in range(1, 5):
+            pl.semaphore_signal(
+                barrier, inc=1, device_id=seq_at((me + k) % SEQ_N), device_id_type=MESH_ID
             )
-            held[m, :, 256:512] = rows[:, 256:512].astype(jnp.bfloat16)
-        copies = send_each(
-            "seq", me, range(1, 5), lambda k, p: held,
-            lambda k, p: out.at[:, pl.ds((4 - k) * TOK, TOK), :], ssem, rsem,
-        )
-        own = pltpu.make_async_copy(held, out.at[:, pl.ds(4 * TOK, TOK), :], lsem)
-        own.start()
-        for copy in copies:
-            copy.wait()
-        own.wait()
-
-    return remote_call(
-        body,
-        jax.ShapeDtypeStruct((2, 5 * TOK, 512), jnp.bfloat16),
-        [VMEM] * 3,
-        VMEM,
-        [pltpu.VMEM((2, TOK, 512), jnp.bfloat16)] + sems(4) + [DMA],
-        collective_id,
-        "key_value_window",
-    )(key_value, cosine, sine)
-
-
-def key_value_back(far, own, cosine, sine, collective_id):
-    def body(far_ref, own_ref, cos_ref, sin_ref, out, held, ssem, rsem):
-        me = greet("seq", range(12, 16))
-        copies = send_each(
-            "seq", me, range(12, 16),
-            lambda k, p: far_ref.at[:, pl.ds((k - 12) * TOK, TOK), :],
-            lambda k, p: held.at[k - 12], ssem, rsem,
-        )
+        pl.semaphore_wait(barrier, 4)
+        copies = [
+            post.send(
+                far_ref.at[:, pl.ds((4 - k) * TOK, TOK), :], held.at[4 - k],
+                seq_at((me + SEQ_N - k) % SEQ_N),
+            )
+            for k in range(1, 5)
+        ]
         for copy in copies:
             copy.wait_recv()
         for m in range(2):
@@ -936,15 +1139,14 @@
             keys = turn(total[:, 0:256], cos_ref[:, 0:256], -sin_ref[:, 0:256])
             out[pl.ds(m * TOK, TOK), 0:256] = keys.astype(jnp.bfloat16)
             out[pl.ds(m * TOK, TOK), 256:512] = total[:, 256:512].astype(jnp.bfloat16)
-        for copy in copies:
-            copy.wait_send()
+        post.finish()
 
     return remote_call(
         body,
         jax.ShapeDtypeStruct((2 * TOK, 512), jnp.bfloat16),
         [VMEM] * 4,
         VMEM,
-        [pltpu.VMEM((4, 2, TOK, 512), jnp.bfloat16)] + sems(4),
+        [pltpu.VMEM((4, 2, TOK, 512), jnp.bfloat16), DMA((8,))],
         collective_id,
         "key_value_back",
     )(far, own, cosine, sine)
@@ -958,8 +1160,7 @@
     return jnp.concatenate([block[64 * g : 64 * g + 64, :] for g in range(8)], axis=1)
 
 
-def window_mask(start_ref, query_seg, key_seg, shift):
-    start = start_ref[0]
+def window_mask(start, query_seg, key_seg, shift):
     query = start + lax.broadcasted_iota(jnp.int32, (TOK, 5 * TOK), 0)
     key = start - 4 * TOK + lax.broadcasted_iota(jnp.int32, (TOK, 5 * TOK), 1)
     allowed = (
@@ -990,39 +1191,6 @@
     return raised / jnp.sum(raised, axis=-1, keepdims=True)
 
 
-def attend(queries, window, cosine, sine, query_seg, key_seg, start, shifts):
-    def body(start_ref, shift_ref, q_ref, kv_ref, cos_ref, sin_ref, qs_ref, ks_ref, q_out, a_out):
-        for h in range(4):
-            cols = slice(512 * h, 512 * h + 512)
-            turned = turn(q_ref[:, cols], cos_ref[...], sin_ref[...]).astype(jnp.bfloat16)
-            q_out[:, cols] = turned
-            mask = window_mask(start_ref, qs_ref[0], ks_ref[0], shift_ref[h])
-            probs = probabilities(spread_heads(turned), kv_ref[0, :, 64 * h : 64 * h + 64], mask)
-            values = kv_ref[0, :, 256 + 64 * h : 256 + 64 * h + 64]
-            mixed = jnp.dot(probs.astype(jnp.bfloat16), values, preferred_element_type=jnp.float32)
-            a_out[:, cols] = join_heads(mixed).astype(jnp.bfloat16)
-
-    wide = pl.BlockSpec((TOK, 2048), lambda m: (m, 0))
-    return pl.pallas_call(
-        body,
-        out_shape=[jax.ShapeDtypeStruct((2 * TOK, 2048), jnp.bfloat16)] * 2,
-        grid=(2,),
-        in_specs=[
-            SMEM,
-            SMEM,
-            wide,
-            pl.BlockSpec((1, 5 * TOK, 512), lambda m: (m, 0, 0)),
-            pl.BlockSpec((TOK, 512), lambda m: (0, 0)),
-            pl.BlockSpec((TOK, 512), lambda m: (0, 0)),
-            pl.BlockSpec((1, TOK, 1), lambda m: (m, 0, 0)),
-            pl.BlockSpec((1, 1, 5 * TOK), lambda m: (m, 0, 0)),
-        ],
-        out_specs=[wide, wide],
-        compiler_params=pltpu.CompilerParams(vmem_limit_bytes=VMEM_LIMIT),
-        name="attend",
-    )(start, shifts, queries, window, cosine, sine, query_seg, key_seg)
-
-
 def attend_back(queries, window, upstream, cosine, sine, query_seg, key_seg, start, shifts):
     def body(
         start_ref, shift_ref, q_ref, kv_ref, g_ref, cos_ref, sin_ref, qs_ref, ks_ref,
@@ -1030,7 +1198,7 @@
     ):
         for h in range(4):
             cols = slice(512 * h, 512 * h + 512)
-            mask = window_mask(start_ref, qs_ref[0], ks_ref[0], shift_ref[h])
+            mask = window_mask(start_ref[0], qs_ref[0], ks_ref[0], shift_ref[h])
             spread = spread_heads(q_ref[:, cols])
             keys = kv_ref[0, :, 64 * h : 64 * h + 64]
             values = kv_ref[0, :, 256 + 64 * h : 256 + 64 * h + 64]
@@ -1116,15 +1284,6 @@
     return (factor_id[None, :] == jnp.arange(4)[:, None]).astype(jnp.float32)
 
 
-def shampoo_parts(down_factor_gradient, up_factor_gradient, onehot):
-    left_three = down_factor_gradient.reshape(4, up_factor_gradient.shape[0], -1)
-    stats_left = jnp.einsum("krd,ksd->krs", left_three, left_three, precision=HIGHEST)
-    stats_right = jnp.einsum(
-        "rc,sc,kc->krs", up_factor_gradient, up_factor_gradient, onehot, precision=HIGHEST
-    )
-    return jnp.concatenate([stats_left, stats_right], 0)
-
-
 def inverse_root(stats):
     unit_mat = jnp.eye(stats.shape[-1], dtype=stats.dtype)[None]
     norm_of = jnp.sqrt(jnp.sum(stats * stats, axis=(1, 2), keepdims=True))
@@ -1200,20 +1359,13 @@
         (0, 1024 - 848),
     ).reshape(8, 128)
     ids_own = jnp.pad(input_token_index.reshape(16, TOK), ((0, 0), (0, 64)))
-    gate_up_w = lax.all_gather(
-        spread_gate_up(gate_up_own, 14).reshape(128, PAD_FF // 2),
-        ("seq_0", "seq_1", "fsdp_2"),
-        axis=0,
-        tiled=True,
-    ).reshape(8, 2, 8, 16, PAD_FF // 2)
-    down_w = lax.all_gather(
-        down_own, ("seq_0", "seq_1", "fsdp_0", "fsdp_2"), axis=0, tiled=True
-    )
-    qkvo, small, table, ids = gather_weights(
+    qkvo, small, table, ids, gate_up_w, down_w = gather_weights(
         qkvo_own,
         small_own,
         embedding.astype(jnp.bfloat16),
         ids_own,
+        gate_up_own,
+        down_own,
     )
     qkvo = qkvo.reshape(2048, 4608)
     w_qkv, w_out = qkvo[:, :2560], qkvo[:, 2560:]
@@ -1260,8 +1412,6 @@
 
     ids = ids[:, :, :TOK].reshape(SEQ_N, 2, 8, TOK)
     row_ids = lax.dynamic_index_in_dim(ids, fsdp_here, 2, keepdims=False).reshape(SEQ_N, 128)
-    x_start = rows_of_tokens(table.reshape(8 * vocab_dev, 128), row_ids, 2).astype(jnp.float32)
-
     half = 32
     freqs = ROPE_BASE ** (-2.0 * jnp.arange(half).astype(jnp.float32) / 64)
     angles = (seq_here * TOK + jnp.arange(TOK)).astype(jnp.float32)[:, None] * freqs[None, :]
@@ -1273,17 +1423,15 @@
     key_seg = lax.dynamic_slice_in_dim(padded, seq_here * TOK, 5 * TOK, 1)[:, None, :]
     query_seg = key_seg[:, 0, 4 * TOK :][:, :, None]
     start = (seq_here * TOK).reshape(1)
-    normed_one = (x_start * norm_scale(x_start) * gain[0]).astype(jnp.bfloat16)
-    adapter_in = nt(normed_one, a_in).astype(jnp.bfloat16)
-    packed = dot(normed_one, w_qkv) + ADAPTER_SCALE * dot(adapter_in, b_in)
-    window = key_value_window(packed[:, 2048:], cosine, sine, 3)
-    queries, attended = attend(
-        packed, window, cosine, sine, query_seg, key_seg, start, head_group_offsets
-    )
-    adapter_mid = nt(attended, a_out).astype(jnp.bfloat16)
-    x_mid = x_start + dot(attended, w_out) + ADAPTER_SCALE * dot(adapter_mid, b_out)
-
-    normed_two = (x_mid * norm_scale(x_mid) * gain[1]).astype(jnp.bfloat16)
+    (
+        x_start, normed_one, adapter_in, queries, window, attended, adapter_mid, x_mid, normed_two,
+    ) = attention_block(
+        table, row_ids, qkvo, a_low, b_in, b_out, gain, cosine, sine, query_seg, key_seg,
+        head_group_offsets, 2,
+    )
+    gate_up_w = [gate_up_w.reshape(2048, -1)]
+    down_w = [down_w.reshape(PAD_FF // 4, -1)]
+
     hidden_sum, gate_up = feed_forward(normed_two, gate_up_w, down_w, None, 12, "feed_forward")
     x_end = x_mid + hidden_sum
     normed_end = (x_end * norm_scale(x_end) * gain[2]).astype(jnp.bfloat16)
@@ -1295,7 +1443,6 @@
     d_chosen, loss_tile = head_step(
         chosen, head, local_target, weight_column, weight_column / document_total, 4
     )
-    loss_part = loss_tile[0, 0]
 
     upstream = lax.dot_general(pick, d_chosen, (((0,), (0,)), ((), ())), precision=HIGHEST)
     d_end, gain_end = norm_back(x_end, gain[2], upstream)
@@ -1339,41 +1486,21 @@
         ],
         0,
     )
-    left = left.reshape(40, 16, 128).transpose(1, 0, 2)
-    right = jnp.concatenate([up_gradient_in, up_gradient_out], 1).reshape(8, 16, 288)
-    right = jnp.pad(right, ((0, 0), (0, 0), (0, 96))).transpose(1, 0, 2).reshape(16, 24, 128)
+    right = jnp.concatenate([up_gradient_in, up_gradient_out], 1)
     all_ids = ids.transpose(2, 0, 1, 3).reshape(16, 1024) - fsdp_here * vocab_dev
-    grad_embed, small_sum = token_gradients(
-        d_start, jnp.concatenate([left, right], 1), all_ids, vocab_dev, 8
-    )
-    left_sum = small_sum[:40]
-    right_sum = small_sum[40:].reshape(8, 384)[:, :288]
-    group_onehot = factor_onehot(seq_here * 288 + jnp.arange(288))
-    stats_part = shampoo_parts(left_sum[:32], right_sum, group_onehot)
-    first = (fsdp_here == 0).astype(jnp.float32)
-    squares = jnp.sum(grad_embed * grad_embed) + first * (
-        jnp.sum(left_sum[:35] * left_sum[:35]) + jnp.sum(right_sum * right_sum)
-    )
-    totals = jnp.concatenate(
-        [
-            (first * stats_part).reshape(-1),
-            squares.reshape(1),
-            loss_part.reshape(1),
-            jnp.zeros((510,), jnp.float32),
-        ]
-    ).reshape(8, 128)
-    totals = sum_over("seq", totals, 10, "totals_seq", False)
-    totals = sum_over("fsdp", totals, 11, "totals_fsdp", False)
-    stats_all = totals[:4].reshape(8, 8, 8)
-    document_loss_sum = totals[4, 1]
-    global_gradient_norm = jnp.sqrt(totals[4, 0])
+    grad_embed, left_sum, right_sum, totals = token_gradients(
+        d_start, left, right, all_ids, loss_tile, vocab_dev, 8
+    )
+    stats_all = totals[:, :64].reshape(8, 8, 8).transpose(1, 0, 2)
+    document_loss_sum = totals[0, 65]
+    global_gradient_norm = jnp.sqrt(totals[0, 64])
     clip_factor = CLIP_MAX / jnp.maximum(global_gradient_norm, CLIP_MAX)
 
     own_left = lax.dynamic_slice_in_dim(left_sum, fsdp_here * 16, 16, 1)
     down_factor_gradient = own_left[:32] * clip_factor
     grad_gain = own_left[32:35] * clip_factor
     up_factor_gradient = (
-        lax.dynamic_slice_in_dim(right_sum, fsdp_here * 36, 36, 1) * clip_factor
+        lax.dynamic_slice_in_dim(right_sum, 32 * ((9 * seq_here) % 4) + fsdp_here * 36, 36, 1) * clip_factor
     )
     grad_embed = grad_embed * clip_factor
     unused_first, updated_embedding_second_moment, updated_embedding_table = adam_update(

time: 960 us -> 643 us (0.67)
  waiting for transfers between devices: 251 us -> 15.3 us
  Pallas kernels: 572 us -> 517 us
  matrix products: 46.9 us -> 31.1 us
  other arithmetic: 34.9 us -> 24.7 us
    all_gather x2 -> x0, waiting for transfers between devices: 166 us -> none  [the longest x1 166 us: per_device(): lax.all_gather(spread_gate_up(gate_up_own, 14).reshape(128, PAD_FF // 2),...]
    all_gather x1, waiting for transfers between devices: 84.9 us -> 15.3 us  [per_device(): head = lax.all_gather(head_own, SEQ, axis=1, tiled=True)]
    pallas_call x9 -> x4, Pallas kernels: 394 us -> 325 us  [the longest x1 192 us: gather_weights(): remote_call(body, out_shape, [ANY] * 6, [ANY] * 6, [DMA((sem_count,))], 1...]
    pallas_call x1, Pallas kernels: 76.6 us -> 93.7 us  [token_gradients(): remote_call(body, [jax.ShapeDtypeStruct((vocab, width), jnp.float32), jax...]
    dot_general x7 -> x3, matrix products: 14.9 us -> 2.71 us  [dot(): return jnp.dot(left, right, preferred_element_type=jnp.float32)]
  transfers between devices with their start and end apart: 3 -> 1, of which waited for: 2 -> 1; matrix products, arithmetic and copies ran while one was open for 5% -> 3% of each run, Pallas kernels for 35% -> 15%
where the time goes in v5:
time: 643 us; the launch traced here: 634 us
  Pallas kernels  517 us (80%)
  matrix products  31.1 us (5%)
  local copies, waits for them, and re-layouts  27.8 us (4%)
  other arithmetic  24.7 us (4%)
  between operations  17.4 us (3%)
  waiting for transfers between devices  15.3 us (2%)
    pallas_call x1, Pallas kernels, gather_weights(): remote_call(body, out_shape, [ANY] * 6, [ANY] * 6, [DMA((sem_count,))], 1...  192 us
    pallas_call x1, Pallas kernels, token_gradients(): remote_call(body, [jax.ShapeDtypeStruct((vocab, width), jnp.float32), jax...  93.7 us
    pallas_call x1, Pallas kernels, head_step(): remote_call(body, [jax.ShapeDtypeStruct((64, width), jnp.float32), jax.Sh...  74.5 us
    pallas_call x1, Pallas kernels, attention_block(): remote_call(body, [shape(rows_n, 2048, dtype=jnp.float32), shape(rows_n,...  58.3 us
    pallas_call x1, Pallas kernels, feed_forward(): remote_call(body, total, [VMEM] + [ANY] * (2 * parts_n + 1), VMEM, scratc...  38.5 us
    pallas_call x1, Pallas kernels, feed_forward(): remote_call(body, [total, products], [VMEM] + [ANY] * (2 * parts_n), [VME...  36.4 us
    all_gather x1, waiting for transfers between devices, per_device(): head = lax.all_gather(head_own, SEQ, axis=1, tiled=True)  15.3 us
    dot_general x4, matrix products, nt(): lax.dot_general(left, right, (((1,), (1,)), ((), ())), preferred_element_...  14.2 us
  transfers between devices with their start and end apart: 1, of which 1 were waited for; matrix products, arithmetic and copies ran while one was open for 3% of the time, Pallas kernels for 15%

profile of v5, /device:TPU:1, one launch (start us, length us, event | category | flops | bytes accessed | tf_op | source)
XLA Modules:
  0.0 633.6 jit_solution(7418503547790579521)
XLA Ops:
  7.2 3.9 reshape.359
  12.2 1.4 pad.19
  13.6 2.8 reshape.360.refs_4_
  16.5 1.1 convert_element_type.129.refs_2_
  20.5 192.2 %gather_weights.1 = (bf16[2,4,2,4,2,16,4608]{6,5,4,3,2,1,0:T(8,128)(2,1)}, f32[2,4,2,4,2,8,128]{6,5,4,3,2,1,0:T(8,128)}, bf16[8,4000,128]{2,1,0:T(8,128)(2,1)}, ...) custom-call(bf16[16,4608]{1,0:T(8,128)(2,1)} %pad_maximum_fusion.3.ref, ...), custom_call_target="tpu_custom_call" | custom-call | tf_op jit(solution)/shard_map/gather_weights/pallas_call | solution.py:443
  212.8 1.1 copy.167
  222.4 1.3 convert_reduce_fusion
  225.7 1.2 slice.105
  228.6 58.3 %attention_block.1 = (f32[128,2048]{1,0:T(8,128)}, bf16[128,2048]{1,0:T(8,128)(2,1)}, bf16[128,24]{1,0:T(8,128)(2,1)}, bf16[128,2048]{1,0:T(8,128)(2,1)}, bf16[2...) custom-call(bf16[8,4000,128]{2,1,0:T(8,128)(2,1)} %get-tuple-element, ...), custom_call_target="tpu_custom_call" | custom-call | tf_op jit(solution)/shard_map/attention_block/pallas_call | solution.py:584
  286.9 36.4 %feed_forward.1 = (f32[128,2048]{1,0:T(8,128)}, f32[512,3072]{1,0:T(8,128)}) custom-call(bf16[128,2048]{1,0:T(8,128)(2,1)} %get-tuple-element.50.refs_0_, bf16[2048,3072]{1,0:T(8,128)(2,1)} %bitcast.134, bf16[1536,2048]{1,0:T(8,128)(2,1)} %bitcast.136), custom_call_target="tpu_custom_call" | custom-call | tf_op jit(solution)/shard_map/feed_forward/pallas_call | solution.py:1096
  324.0 1.5 multiply_reduce_fusion.8
  326.2 1.4 broadcast_divide_fusion.scaled_ref
  328.6 15.3 %all-gather.2.cloned.1.call-done.head_hbm = bf16[4000,2048]{1,0:T(8,128)(2,1)} async-done(((bf16[4000,128]{1,0:T(8,128)(2,1)}), bf16[4000,2048]{1,0:T(8,128)(2,1)}) %all-gather.2.cloned.1.call-update) | async-done | bytes 16384016 | tf_op jit(solution)/shard_map/all_gather | solution.py:1373
  344.0 74.5 %head_step.1 = (f32[64,2048]{1,0:T(8,128)}, f32[8,128]{1,0:T(8,128)}) custom-call(bf16[64,2048]{1,0:T(8,128)(2,1)} %convolution_convert_fusion.chosen_ref, bf16[4000,2048]{1,0:T(8,128)(2,1)} %all-gather.2.cloned.1.call-done.head_hbm, s32[512,1]{1,0:T(8,128)} %compare_select_fusion.target_ref, f32[512,1]{1,0:T(8,128)} %copy-done.5, ...), custom_call_target="tpu_custom_call" | custom-call | tf_op jit(solution)/shard_map/head_step/pallas_call | solution.py:716
  418.5 2.0 multiply_reduce_fusion
  420.5 1.1 fusion.128.refs_0_
  421.6 38.5 %feed_forward_back.1 = f32[128,2048]{1,0:T(8,128)} custom-call(bf16[128,2048]{1,0:T(8,128)(2,1)} %fusion.128.refs_0_, bf16[2048,3072]{1,0:T(8,128)(2,1)} %bitcast.135, bf16[1536,2048]{1,0:T(8,128)(2,1)} %bitcast.137, f32[512,3072]{1,0:T(8,128)} %get-tuple-element.56.refs_3_), custom_call_target="tpu_custom_call" | custom-call | tf_op jit(solution)/shard_map/feed_forward_back/pallas_call | solution.py:1100
  460.1 1.6 multiply_reduce_fusion.1
  462.6 6.3 fusion.2
  468.9 1.1 fusion.4.g_ref
  470.0 11.3 %attend_back.1 = (bf16[128,2048]{1,0:T(8,128)(2,1)}, bf16[2,256,512]{2,1,0:T(8,128)(2,1)}, f32[2,64,512]{2,1,0:T(8,128)}) custom-call(s32[1]{0:T(128)} %bitcast.20.start_ref, s32[4]{0:T(128)} %shift_ref.3, bf16[128,2048]{1,0:T(8,128)(2,1)} %get-tuple-element.58.q_ref, bf16[2,320,512]{2,1,0:T(8,128)(2,1)} %get-tuple-element.59.kv_ref, ...), custom_call_target="tpu_custom_call" | custom-call | tf_op jit(solution)/shard_map/attend_back/pallas_call | solution.py:1219
  481.3 12.3 %key_value_back.1 = bf16[128,512]{1,0:T(8,128)(2,1)} custom-call(bf16[2,256,512]{2,1,0:T(8,128)(2,1)} %get-tuple-element.61.far_ref, f32[2,64,512]{2,1,0:T(8,128)} %get-tuple-element.62.own_ref, f32[64,512]{1,0:T(8,128)} %copy.126.cos_ref, f32[64,512]{1,0:T(8,128)} %tile.21.sin_ref), custom_call_target="tpu_custom_call" | custom-call | tf_op jit(solution)/shard_map/key_value_back/pallas_call | solution.py:1144
  493.6 1.1 fusion.24
  494.7 1.1 fusion.22
  495.8 1.3 fusion.30
  497.1 1.4 fusion.14
  498.6 6.2 fusion
  506.7 1.1 add_convert_fusion.src
  507.9 2.0 concatenate.33.left_ref
  509.9 93.7 %token_gradients.1 = (f32[4000,128]{1,0:T(8,128)}, f32[40,128]{1,0:T(8,128)}, f32[8,384]{1,0:T(8,128)}, f32[8,128]{1,0:T(8,128)}) custom-call(bf16[128,2048]{1,0:T(8,128)(2,1)} %add_convert_fusion.src, f32[40,2048]{1,0:T(8,128)} %concatenate.33.left_ref, f32[8,4608]{1,0:T(8,128)} %pad_maximum_fusion.4.right_ref, s32[16,1024]{1,0:T(8,128)} %sub.146.ids_ref, ...), custom_call_target="tpu_custom_call" | custom-call | tf_op jit(solution)/shard_map/token_gradients/pallas_call | solution.py:893
  603.6 1.4 fusion.132
  619.2 6.0 fusion.10
  (224 shorter events, 34.1 us)
Async XLA Ops:
  7.2 336.8 %all-gather.2.cloned.1.call-start = ((), (), s32[]{:S(2)}) async-start(), calls=%async_computation | async-start | bytes 17408000 | tf_op jit(solution)/shard_map/all_gather | solution.py:1373
  12.2 4.2 copy-start.3
  13.6 3.9 copy-start.12
  16.4 2.0 copy-start.23
  16.4 2.0 copy-start.27
  16.4 2.1 copy-start.14
  16.4 2.1 copy-start.15
  16.4 2.8 copy-start.25
  213.9 2.1 copy-start.13
  213.9 2.9 copy-start.9
  215.4 5.8 copy-start.17
  215.9 5.8 copy-start.31
  216.1 6.2 copy-start.16
  217.9 6.3 copy-start.26
  224.1 102.1 %copy-start.5 = (f32[512,1]{1,0:T(8,128)}, f32[512,1]{1,0:T(8,128)S(1)}, u32[]{:S(2)}) copy-start(f32[512,1]{1,0:T(8,128)S(1)} %reshape_reshape.4.weight_ref) | copy-start | bytes 6148
  286.9 37.1 %copy-start.2 = (f32[128,2048]{1,0:T(8,128)S(1)}, f32[128,2048]{1,0:T(8,128)}, u32[]{:S(2)}) copy-start(f32[128,2048]{1,0:T(8,128)} %get-tuple-element.49) | copy-start | bytes 3145732
  421.6 38.6 %copy-start = (f32[128,2048]{1,0:T(8,128)S(1)}, f32[128,2048]{1,0:T(8,128)}, u32[]{:S(2)}) copy-start(f32[128,2048]{1,0:T(8,128)} %get-tuple-element.57) | copy-start | bytes 3145732
  468.9 24.7 %copy-start.11 = (bf16[128,24]{1,0:T(8,128)(2,1)S(1)}, bf16[128,24]{1,0:T(8,128)(2,1)}, u32[]{:S(2)}) copy-start(bf16[128,24]{1,0:T(8,128)(2,1)} %get-tuple-element.65) | copy-start | bytes 18436
  481.3 17.3 %copy-start.7 = (bf16[128,2048]{1,0:T(8,128)(2,1)S(1)}, bf16[128,2048]{1,0:T(8,128)(2,1)}, u32[]{:S(2)}) copy-start(bf16[128,2048]{1,0:T(8,128)(2,1)} %get-tuple-element.60) | copy-start | bytes 1572868
  493.6 5.0 copy-start.10
  498.6 6.3 copy-start.20
  498.6 6.5 %copy-start.6 = (bf16[128,2048]{1,0:T(8,128)(2,1)S(1)}, bf16[128,2048]{1,0:T(8,128)(2,1)}, u32[]{:S(2)}) copy-start(bf16[128,2048]{1,0:T(8,128)(2,1)} %get-tuple-element.64) | copy-start | bytes 1572868
  498.6 6.7 %copy-start.8 = (bf16[128,2048]{1,0:T(8,128)(2,1)S(1)}, bf16[128,2048]{1,0:T(8,128)(2,1)}, u32[]{:S(2)}) copy-start(bf16[128,2048]{1,0:T(8,128)(2,1)} %get-tuple-element.63) | copy-start | bytes 1572868
  506.7 99.8 %copy-start.18 = (f32[8,8,8]{2,1,0:T(8,128)S(1)}, f32[8,8,8]{2,1,0:T(8,128)}, u32[]{:S(2)}) copy-start(f32[8,8,8]{2,1,0:T(8,128)} %param.41) | copy-start | bytes 6148
  603.5 10.4 %copy-start.22 = (f32[40,128]{1,0:T(8,128)S(1)}, f32[40,128]{1,0:T(8,128)}, u32[]{:S(2)}) copy-start(f32[40,128]{1,0:T(8,128)} %get-tuple-element.70) | copy-start | bytes 61444
  603.5 11.4 %copy-start.28 = (f32[4,16]{1,0:T(4,128)S(1)}, f32[4,16]{1,0:T(4,128)}, u32[]{:S(2)}) copy-start(f32[4,16]{1,0:T(4,128)} %param.42) | copy-start | bytes 772
  603.6 13.6 %copy-start.32 = (f32[36]{0:T(128)S(1)}, f32[36]{0:T(128)}, u32[]{:S(2)}) copy-start(f32[36]{0:T(128)} %param.43) | copy-start | bytes 436
  603.6 14.9 %copy-start.29 = (f32[3,16]{1,0:T(4,128)S(1)}, f32[3,16]{1,0:T(4,128)}, u32[]{:S(2)}) copy-start(f32[3,16]{1,0:T(4,128)} %param.38) | copy-start | bytes 580
  603.6 14.9 %copy-start.30 = (f32[3,16]{1,0:T(4,128)S(1)}, f32[3,16]{1,0:T(4,128)}, u32[]{:S(2)}) copy-start(f32[3,16]{1,0:T(4,128)} %param.37) | copy-start | bytes 580
  603.6 15.6 %copy-start.4 = (f32[4000,128]{1,0:T(8,128)S(1)}, f32[4000,128]{1,0:T(8,128)}, u32[]{:S(2)}) copy-start(f32[4000,128]{1,0:T(8,128)} %param.28) | copy-start | bytes 6144004
  606.6 18.5 %copy-start.19 = (f32[8,8,8]{2,1,0:T(8,128)}, f32[8,8,8]{2,1,0:T(8,128)S(1)}, u32[]{:S(2)}) copy-start(f32[8,8,8]{2,1,0:T(8,128)S(1)} %get-tuple-element.147) | copy-start | bytes 6148
  617.1 8.1 %copy-start.24 = (f32[8,36]{1,0:T(8,128)}, f32[8,36]{1,0:T(8,128)S(1)}, u32[]{:S(2)}) copy-start(f32[8,36]{1,0:T(8,128)S(1)} %get-tuple-element.149) | copy-start | bytes 3460
  (2 other events, 3.5 us)
Sparse Core Ops, SparseCore 0:
  212.9 131.0 all-gather.1

commit v6 on v5

--- a/solution.py
+++ b/solution.py
@@ -375,7 +375,9 @@
 
 
 def gather_weights(qkvo, small, table, ids, gate_up, down):
-    quarter = gate_up.shape[1] // 4
+    groups, units = 8, gate_up.shape[1] // 8
+    spread = units // 44 * 48
+    quarter = groups * spread // 4
     out_shape = [
         jax.ShapeDtypeStruct((2, 4, 2, 4, 2, *qkvo.shape), qkvo.dtype),
         jax.ShapeDtypeStruct((2, 4, 2, 4, 2, *small.shape), small.dtype),
@@ -387,7 +389,7 @@
     sem_count = 320
 
     def body(*refs):
-        ins, outs, sem = refs[:6], refs[6:12], refs[12]
+        ins, outs, ordered, picks, sem = refs[:6], refs[6:12], refs[12], refs[13], refs[14]
         post = Post(sem, sem_count)
         ways = Ways(post)
         yh, x, c, z, yl = ways.yh, ways.x, ways.c, ways.z, ways.yl
@@ -398,11 +400,36 @@
                 (ins[1], outs[1].at[yh, x, c, z, yl]),
                 (ins[2], outs[2].at[z * 2 + yl]),
                 (ins[3], outs[3].at[seq]),
-                ways.own_gate_up(ins[4], outs[4]),
                 (ins[5], outs[5].at[yh, x, z // 2, yl]),
             ],
             post,
         )
+        at = lax.broadcasted_iota(jnp.int32, (1, spread), 1)
+        part, rest = at // (spread // 4), at % (spread // 4)
+        unit = rest % 48
+        here = rest // 48
+        source = (
+            (here // 4) * 16 + (part % 2) * 8 + ((here // 2) % 2) * 4 + (part // 2) * 2 + here % 2
+        ) * 44 + unit
+        source = jnp.where(unit < 44, source, -1)
+
+        def pick(n, carry):
+            start = pl.multiple_of(n * 128, 128)
+            row = lax.broadcasted_iota(jnp.int32, (128, spread), 0) + start
+            picks[pl.ds(start, 128), :] = (row == source).astype(jnp.float32).astype(jnp.bfloat16)
+            return carry
+
+        lax.fori_loop(0, units // 128, pick, 0)
+        for n in range(groups):
+            moved = jnp.dot(
+                ins[4][:, n * units : (n + 1) * units], picks[...], preferred_element_type=jnp.float32
+            ).astype(jnp.bfloat16)
+            width = spread // 4
+            for k in range(4):
+                first = k * quarter + n * width
+                ordered[:, first : first + width] = moved[:, k * width : (k + 1) * width]
+        mine = ways.own_gate_up(ordered, outs[4])
+        local += local_copies([mine], post)
         greet_devices(ways.all_devices())
         for copy in local:
             copy.wait()
@@ -423,7 +450,7 @@
             streams["t%d" % n] = ways.table(outs[2], cuts[n], cuts[n + 1])
         half, wide = quarter // 2, down.shape[1] // 2
         for n, order in enumerate(("xy", "yx")):
-            streams["g%d" % n] = ways.gate_up(ins[4], outs[4], order, n * half, half)
+            streams["g%d" % n] = ways.gate_up(ordered, outs[4], order, n * half, half)
             streams["d%d" % n] = ways.down(outs[5], order, n * wide, wide)
         for n, order in enumerate(('yxz', 'xyz', 'zyx')):
             streams["q%d" % n] = ways.everything(
@@ -441,7 +468,13 @@
         post.finish()
 
     return remote_call(
-        body, out_shape, [ANY] * 6, [ANY] * 6, [DMA((sem_count,))], 1, "gather_weights"
+        body, out_shape, [ANY] * 4 + [VMEM, ANY], [ANY] * 6,
+        [
+            pltpu.VMEM((gate_up.shape[0], 4 * quarter), gate_up.dtype),
+            pltpu.VMEM((units, spread), gate_up.dtype),
+            DMA((sem_count,)),
+        ],
+        1, "gather_weights",
     )(qkvo, small, table, ids, gate_up, down)
 
 
@@ -761,12 +794,52 @@
         moves, sums = [], []
         for k in ALL16:
             peer = (s + k) % SEQ_N
-            sums.append(post.send(left_ref.at[:, cols(peer)], left_parts.at[k - 1], seq_at(peer)))
-            sums.append(post.send(right_ref.at[:, window(peer)], right_parts.at[k - 1], seq_at(peer)))
             moves.append(post.send(src.at[:, cols(peer)], held.at[f, s], seq_at(peer)))
         own = pltpu.make_async_copy(src.at[:, cols(s)], held.at[f, s], lsem)
         own.start()
+        for k in ALL16:
+            peer = (s + k) % SEQ_N
+            sums.append(post.send(left_ref.at[:, cols(peer)], left_parts.at[k - 1], seq_at(peer)))
+            sums.append(post.send(right_ref.at[:, window(peer)], right_parts.at[k - 1], seq_at(peer)))
         total[...] = jnp.zeros_like(total)
+        for copy in moves:
+            copy.wait_recv()
+        own.wait()
+
+        def add(block):
+            def one(t, carry):
+                ids_row = ids_ref[pl.ds(block * 2 + t, 1), :]
+                high, low = ids_row >> 10, ids_row & 1023
+                part = lax.broadcasted_iota(jnp.int32, (8, tile), 0)
+                which = jnp.transpose((part == high).astype(jnp.float32))
+                grad = held[block, pl.ds(t * 8, 8)].reshape(tile, width).astype(jnp.float32)
+                for h in range(4):
+                    spread[:, h * width : (h + 1) * width] = jnp.where(
+                        which[:, h : h + 1] > 0.5, grad, 0.0
+                    ).astype(jnp.bfloat16)
+
+                def step(n, inner):
+                    start = pl.multiple_of(n * 256, 256)
+                    row = lax.broadcasted_iota(jnp.int32, (256, tile), 0) + start
+                    hot = (row == low).astype(jnp.float32).astype(jnp.bfloat16)
+                    total[pl.ds(start, 256), :] += jnp.dot(
+                        hot, spread[...], preferred_element_type=jnp.float32
+                    )
+                    return inner
+
+                lax.fori_loop(0, low_n // 256, step, 0)
+                return carry
+
+            lax.fori_loop(0, 2, one, 0)
+
+        every = slice(None)
+        steps = relay(
+            post, held, (pl.ds(0, 8),), (pl.ds(8, 8),), (pl.ds(0, 4),), (pl.ds(4, 4),)
+        )
+        before, after, far = (z + 3) % 4, (z + 1) % 4, (z + 2) % 4
+        next(steps)
+        add(f)
+        next(steps)
         left_sum, right_sum = left_ref[:, cols(s)], right_ref[:, window(s)]
         for copy in sums:
             copy.wait_recv()
@@ -779,44 +852,6 @@
             device = fsdp_at((f + k) % FSDP_N)
             shares.append(post.send(left_mid, left_more.at[k - 1], device))
             shares.append(post.send(right_mid, right_more.at[k - 1], device))
-        for copy in moves:
-            copy.wait_recv()
-        own.wait()
-
-        def add(block):
-            def one(t, carry):
-                ids_row = ids_ref[pl.ds(block * 2 + t, 1), :]
-                high, low = ids_row >> 10, ids_row & 1023
-                part = lax.broadcasted_iota(jnp.int32, (8, tile), 0)
-                which = jnp.transpose((part == high).astype(jnp.float32))
-                grad = held[block, pl.ds(t * 8, 8)].reshape(tile, width).astype(jnp.float32)
-                for h in range(4):
-                    spread[:, h * width : (h + 1) * width] = jnp.where(
-                        which[:, h : h + 1] > 0.5, grad, 0.0
-                    ).astype(jnp.bfloat16)
-
-                def step(n, inner):
-                    start = pl.multiple_of(n * 256, 256)
-                    row = lax.broadcasted_iota(jnp.int32, (256, tile), 0) + start
-                    hot = (row == low).astype(jnp.float32).astype(jnp.bfloat16)
-                    total[pl.ds(start, 256), :] += jnp.dot(
-                        hot, spread[...], preferred_element_type=jnp.float32
-                    )
-                    return inner
-
-                lax.fori_loop(0, low_n // 256, step, 0)
-                return carry
-
-            lax.fori_loop(0, 2, one, 0)
-
-        every = slice(None)
-        steps = relay(
-            post, held, (pl.ds(0, 8),), (pl.ds(8, 8),), (pl.ds(0, 4),), (pl.ds(4, 4),)
-        )
-        before, after, far = (z + 3) % 4, (z + 1) % 4, (z + 2) % 4
-        next(steps)
-        add(f)
-        next(steps)
         next(steps)
         next(steps)
         add(z * 2 + 1 - yl)
@@ -1245,6 +1280,106 @@
     )(start, shifts, queries, window, upstream, cosine, sine, query_seg, key_seg)
 
 
+def small_updates(
+    totals, left, right, rank, a_old, b_old, width_a, width_b, gain, gain_first, gain_second, columns
+):
+    def body(
+        t_ref, l_ref, r_ref, k_ref, a_ref, b_ref, wa_ref, wb_ref, g_ref, gf_ref, gs_ref, c_ref,
+        scalars, ga_out, gb_out, gf_out, gs_out, g_out, k_out, wa_out, wb_out, a_out, b_out,
+    ):
+        totals_now = t_ref[...]
+        norm = jnp.sqrt(totals_now[0:1, 64:65])
+        clip = CLIP_MAX / jnp.maximum(norm, CLIP_MAX)
+        lane = lax.broadcasted_iota(jnp.int32, (8, 128), 1)
+        scalars[...] = jnp.where(lane == 0, norm, jnp.where(lane == 1, clip, 0.0))
+        parts = [totals_now[:, 8 * k : 8 * k + 8] for k in range(8)]
+        square = (clip * clip)[0:1, 0:1].reshape(1, 1, 1)
+        stats = SECOND_DECAY * k_ref[...] + (1.0 - SECOND_DECAY) * square * jnp.stack(parts)
+        k_out[...] = stats
+
+        def times(x, y):
+            total = x[:, :, 0:1] * y[:, 0:1, :]
+            for n in range(1, 8):
+                total = total + x[:, :, n : n + 1] * y[:, n : n + 1, :]
+            return total
+
+        size = jnp.sqrt(jnp.sum(jnp.sum(stats * stats, axis=2, keepdims=True), axis=1, keepdims=True))
+        unit = (
+            lax.broadcasted_iota(jnp.int32, (8, 8, 8), 1) == lax.broadcasted_iota(jnp.int32, (8, 8, 8), 2)
+        ).astype(jnp.float32)
+
+        def newton(n, carry):
+            root, matrix = carry
+            factor = (5.0 * unit - matrix) * 0.25
+            square_of = times(factor, factor)
+            return times(root, factor), times(times(square_of, square_of), matrix)
+
+        roots, _ = lax.fori_loop(
+            0, 10, newton, (unit * lax.rsqrt(jnp.sqrt(size)), stats / size)
+        )
+
+        gradient = l_ref[...] * clip
+        down = gradient[0:32]
+        ga_out[...] = down
+        up = r_ref[...] * clip
+        gb_out[...] = up
+
+        first = FIRST_DECAY * gf_ref[...] + (1.0 - FIRST_DECAY) * gradient[32:35]
+        second = SECOND_DECAY * gs_ref[...] + (1.0 - SECOND_DECAY) * gradient[32:35] * gradient[32:35]
+        gf_out[...] = first
+        gs_out[...] = second
+        first_hat = first / (1.0 - FIRST_DECAY**STEP)
+        second_hat = second / (1.0 - SECOND_DECAY**STEP)
+        gains = g_ref[...]
+        g_out[...] = gains - RATE_GAIN * (
+            first_hat / (jnp.sqrt(second_hat) + ADAM_EPS) + WEIGHT_DECAY * gains
+        )
+
+        def apply(root, gradients):
+            total = root[:, 0:1] * gradients[0:1, :]
+            for n in range(1, 8):
+                total = total + root[:, n : n + 1] * gradients[n : n + 1, :]
+            return total
+
+        for k in range(4):
+            rows = slice(8 * k, 8 * k + 8)
+            mine = down[rows]
+            wide = SECOND_DECAY * wa_ref[k : k + 1, :] + (1.0 - SECOND_DECAY) * jnp.sum(
+                mine * mine, axis=0, keepdims=True
+            )
+            wa_out[k : k + 1, :] = wide
+            a_out[rows, :] = a_ref[rows, :] - LEARN_RATE_DOWN * (
+                apply(roots[k], mine) * lax.rsqrt(jnp.sqrt(wide))
+            )
+        wide = SECOND_DECAY * wb_ref[...] + (1.0 - SECOND_DECAY) * jnp.sum(
+            up * up, axis=0, keepdims=True
+        )
+        wb_out[...] = wide
+        column = c_ref[...]
+        factor = (column >= 2048).astype(jnp.int32) + (column >= 2304) + (column >= 2560)
+        step = jnp.zeros(up.shape, jnp.float32)
+        for k in range(4):
+            step = step + jnp.where(factor == k, apply(roots[4 + k], up), 0.0)
+        b_out[...] = b_ref[...] - LEARN_RATE_UP * (step * lax.rsqrt(jnp.sqrt(wide)))
+
+    def like(array):
+        return jax.ShapeDtypeStruct(array.shape, jnp.float32)
+
+    return pl.pallas_call(
+        body,
+        out_shape=[
+            jax.ShapeDtypeStruct((8, 128), jnp.float32), like(a_old), like(right), like(gain), like(gain),
+            like(gain), like(rank), like(width_a), like(width_b), like(a_old), like(b_old),
+        ],
+        in_specs=[VMEM] * 12,
+        out_specs=[VMEM] * 11,
+        compiler_params=pltpu.CompilerParams(vmem_limit_bytes=VMEM_LIMIT),
+        name="small_updates",
+    )(
+        totals, left, right, rank, a_old, b_old, width_a, width_b, gain, gain_first, gain_second, columns
+    )
+
+
 def dot(left, right):
     return jnp.dot(left, right, preferred_element_type=jnp.float32)
 
@@ -1273,45 +1408,6 @@
     second_hat = second_new / (1.0 - SECOND_DECAY**STEP)
     step_vals = first_hat / (jnp.sqrt(second_hat) + ADAM_EPS) + WEIGHT_DECAY * weight_vals
     return (first_new, second_new, weight_vals - rate * step_vals)
-
-
-def factor_onehot(columns):
-    factor_id = (
-        (columns >= 2048).astype(jnp.int32)
-        + (columns >= 2048 + 256).astype(jnp.int32)
-        + (columns >= 2048 + 512).astype(jnp.int32)
-    )
-    return (factor_id[None, :] == jnp.arange(4)[:, None]).astype(jnp.float32)
-
-
-def inverse_root(stats):
-    unit_mat = jnp.eye(stats.shape[-1], dtype=stats.dtype)[None]
-    norm_of = jnp.sqrt(jnp.sum(stats * stats, axis=(1, 2), keepdims=True))
-    matrix = stats / norm_of
-    root_mat = unit_mat * lax.rsqrt(jnp.sqrt(norm_of))
-    for iteration in range(10):
-        factor = (5.0 * unit_mat - matrix) * 0.25
-        root_mat = jnp.einsum("kab,kbc->kac", root_mat, factor, precision=HIGHEST)
-        square = jnp.einsum("kab,kbc->kac", factor, factor, precision=HIGHEST)
-        fourth = jnp.einsum("kab,kbc->kac", square, square, precision=HIGHEST)
-        matrix = jnp.einsum("kab,kbc->kac", fourth, matrix, precision=HIGHEST)
-    return root_mat
-
-
-def shampoo_apply(
-    stats_new, width_left, width_right, down_factor_gradient, up_factor_gradient, onehot
-):
-    roots = inverse_root(stats_new)
-    left_three = down_factor_gradient.reshape(4, up_factor_gradient.shape[0], -1)
-    down_factor_step = (
-        jnp.einsum("krs,ksd->krd", roots[:4], left_three, precision=HIGHEST)
-        * lax.rsqrt(jnp.sqrt(width_left))[:, None, :]
-    )
-    up_factor_step = (
-        jnp.einsum("krs,sc,kc->rc", roots[4:], up_factor_gradient, onehot, precision=HIGHEST)
-        * lax.rsqrt(jnp.sqrt(width_right))[None, :]
-    )
-    return (down_factor_step.reshape(down_factor_gradient.shape), up_factor_step)
 
 
 def per_device(
@@ -1343,10 +1439,6 @@
     vocab_dev = embedding.shape[0]
 
     qkvo_own = jnp.concatenate([frozen_query_key_value_weight, frozen_attention_output_weight], 1)
-    gate_up_own = frozen_gate_up_weight.reshape(16, 2, 8, 2, 2, 2, 2, 44).transpose(
-        0, 5, 3, 1, 2, 4, 6, 7
-    )
-    gate_up_own = jnp.pad(gate_up_own, [(0, 0)] * 7 + [(0, 4)]).reshape(16, 2 * PAD_FF)
     down_own = jnp.pad(frozen_down_weight, ((0, 4), (0, 0)))
     small_own = jnp.pad(
         jnp.concatenate(
@@ -1364,7 +1456,7 @@
         small_own,
         embedding.astype(jnp.bfloat16),
         ids_own,
-        gate_up_own,
+        frozen_gate_up_weight,
         down_own,
     )
     qkvo = qkvo.reshape(2048, 4608)
@@ -1491,45 +1583,45 @@
     grad_embed, left_sum, right_sum, totals = token_gradients(
         d_start, left, right, all_ids, loss_tile, vocab_dev, 8
     )
-    stats_all = totals[:, :64].reshape(8, 8, 8).transpose(1, 0, 2)
     document_loss_sum = totals[0, 65]
-    global_gradient_norm = jnp.sqrt(totals[0, 64])
-    clip_factor = CLIP_MAX / jnp.maximum(global_gradient_norm, CLIP_MAX)
 
     own_left = lax.dynamic_slice_in_dim(left_sum, fsdp_here * 16, 16, 1)
-    down_factor_gradient = own_left[:32] * clip_factor
-    grad_gain = own_left[32:35] * clip_factor
-    up_factor_gradient = (
-        lax.dynamic_slice_in_dim(right_sum, 32 * ((9 * seq_here) % 4) + fsdp_here * 36, 36, 1) * clip_factor
-    )
-    grad_embed = grad_embed * clip_factor
-    unused_first, updated_embedding_second_moment, updated_embedding_table = adam_update(
-        embedding, embedding_first_moment, embedding_second_moment, grad_embed, RATE_EMBED
-    )
-    updated_gain_first_moment, updated_gain_second_moment, updated_norm_gains = adam_update(
-        norm_gain_vectors, norm_gain_first_moment, norm_gain_second_moment, grad_gain, RATE_GAIN
-    )
-    updated_rank_statistics = (
-        SECOND_DECAY * rank_side_statistics
-        + (1.0 - SECOND_DECAY) * (clip_factor * clip_factor) * stats_all
-    )
-    updated_down_width_statistics = SECOND_DECAY * down_width_statistics + (
-        1.0 - SECOND_DECAY
-    ) * jnp.sum(down_factor_gradient.reshape(4, 8, -1) ** 2, axis=1)
-    updated_up_width_statistics = SECOND_DECAY * up_width_statistics + (
-        1.0 - SECOND_DECAY
-    ) * jnp.sum(up_factor_gradient * up_factor_gradient, axis=0)
-    onehot = factor_onehot((seq_here * 8 + fsdp_here) * 36 + jnp.arange(36))
-    down_factor_step, up_factor_step = shampoo_apply(
+    own_right = lax.dynamic_slice_in_dim(
+        right_sum, 32 * ((9 * seq_here) % 4) + fsdp_here * 36, 36, 1
+    )
+    columns = ((seq_here * 8 + fsdp_here) * 36 + jnp.arange(36)).reshape(1, 36)
+    (
+        scalars,
+        down_factor_gradient,
+        up_factor_gradient,
+        updated_gain_first_moment,
+        updated_gain_second_moment,
+        updated_norm_gains,
         updated_rank_statistics,
         updated_down_width_statistics,
         updated_up_width_statistics,
-        down_factor_gradient,
-        up_factor_gradient,
-        onehot,
-    )
-    updated_down_factors = adapter_down_factors - LEARN_RATE_DOWN * down_factor_step
-    updated_up_factors = adapter_up_factors - LEARN_RATE_UP * up_factor_step
+        updated_down_factors,
+        updated_up_factors,
+    ) = small_updates(
+        totals,
+        own_left,
+        own_right,
+        rank_side_statistics,
+        adapter_down_factors,
+        adapter_up_factors,
+        down_width_statistics,
+        up_width_statistics.reshape(1, 36),
+        norm_gain_vectors,
+        norm_gain_first_moment,
+        norm_gain_second_moment,
+        columns,
+    )
+    updated_up_width_statistics = updated_up_width_statistics.reshape(36)
+    global_gradient_norm = scalars[0, 0]
+    grad_embed = grad_embed * scalars[0, 1]
+    unused_first, updated_embedding_second_moment, updated_embedding_table = adam_update(
+        embedding, embedding_first_moment, embedding_second_moment, grad_embed, RATE_EMBED
+    )
     return (
         document_loss_sum,
         document_total,

time: 643 us -> 633 us (0.984)
  matrix products: 31.1 us -> 23 us
    dot_general x39 -> x0, matrix products: 8.17 us -> none  [the longest x10 1.95 us: inverse_root(): root_mat = jnp.einsum('kab,kbc->kac', root_mat, factor, precision=HIGHEST)]
    reshape x3 -> x0, local copies, waits for them, and re-layouts: 7.77 us -> none  [the longest x2 4.99 us: per_device(): frozen_gate_up_weight.reshape(16, 2, 8, 2, 2, 2, 2, 44)]
    pallas_call x1 -> x2, Pallas kernels: 192 us -> 198 us  [the longest x1 190 us: gather_weights(): remote_call(body, out_shape, [ANY] * 4 + [VMEM, ANY], [ANY] * 6, [pltpu.V...]
where the time goes in v6:
time: 633 us; the launch traced here: 623 us
  Pallas kernels  521 us (82%)
  local copies, waits for them, and re-layouts  26.7 us (4%)
  matrix products  23 us (4%)
  other arithmetic  22.9 us (4%)
  between operations  15.1 us (2%)
  waiting for transfers between devices  14.8 us (2%)
    pallas_call x1, Pallas kernels, gather_weights(): remote_call(body, out_shape, [ANY] * 4 + [VMEM, ANY], [ANY] * 6, [pltpu.V...  190 us
    pallas_call x1, Pallas kernels, token_gradients(): remote_call(body, [jax.ShapeDtypeStruct((vocab, width), jnp.float32), jax...  90.8 us
    pallas_call x1, Pallas kernels, head_step(): remote_call(body, [jax.ShapeDtypeStruct((64, width), jnp.float32), jax.Sh...  74.2 us
    pallas_call x1, Pallas kernels, attention_block(): remote_call(body, [shape(rows_n, 2048, dtype=jnp.float32), shape(rows_n,...  58.6 us
    pallas_call x1, Pallas kernels, feed_forward(): remote_call(body, total, [VMEM] + [ANY] * (2 * parts_n + 1), VMEM, scratc...  38.7 us
    pallas_call x1, Pallas kernels, feed_forward(): remote_call(body, [total, products], [VMEM] + [ANY] * (2 * parts_n), [VME...  36.4 us
    all_gather x1, waiting for transfers between devices, per_device(): head = lax.all_gather(head_own, SEQ, axis=1, tiled=True)  14.8 us
    dot_general x4, matrix products, nt(): lax.dot_general(left, right, (((1,), (1,)), ((), ())), preferred_element_...  14.2 us
  transfers between devices with their start and end apart: 1, of which 1 were waited for; matrix products, arithmetic and copies ran while one was open for 3% of the time, Pallas kernels for 15%

profile of v6, /device:TPU:1, one launch (start us, length us, event | category | flops | bytes accessed | tf_op | source)
XLA Modules:
  0.0 623.3 jit_solution(17324626706916930219)
XLA Ops:
  9.7 2.6 convert_element_type.97.refs_2_
  15.0 190.3 %gather_weights.1 = (bf16[2,4,2,4,2,16,4608]{6,5,4,3,2,1,0:T(8,128)(2,1)}, f32[2,4,2,4,2,8,128]{6,5,4,3,2,1,0:T(8,128)}, bf16[8,4000,128]{2,1,0:T(8,128)(2,1)}, ...) custom-call(bf16[16,4608]{1,0:T(8,128)(2,1)} %pad_maximum_fusion.3.ref, ...), custom_call_target="tpu_custom_call" | custom-call | tf_op jit(solution)/shard_map/gather_weights/pallas_call | solution.py:470
  205.3 1.1 copy.159
  218.0 1.2 slice.93
  220.8 58.6 %attention_block.1 = (f32[128,2048]{1,0:T(8,128)}, bf16[128,2048]{1,0:T(8,128)(2,1)}, bf16[128,24]{1,0:T(8,128)(2,1)}, bf16[128,2048]{1,0:T(8,128)(2,1)}, bf16[2...) custom-call(bf16[8,4000,128]{2,1,0:T(8,128)(2,1)} %get-tuple-element, ...), custom_call_target="tpu_custom_call" | custom-call | tf_op jit(solution)/shard_map/attention_block/pallas_call | solution.py:617
  279.5 36.4 %feed_forward.1 = (f32[128,2048]{1,0:T(8,128)}, f32[512,3072]{1,0:T(8,128)}) custom-call(bf16[128,2048]{1,0:T(8,128)(2,1)} %get-tuple-element.61.refs_0_, bf16[2048,3072]{1,0:T(8,128)(2,1)} %bitcast.62, bf16[1536,2048]{1,0:T(8,128)(2,1)} %bitcast.64), custom_call_target="tpu_custom_call" | custom-call | tf_op jit(solution)/shard_map/feed_forward/pallas_call | solution.py:1131
  317.1 1.5 multiply_reduce_fusion.8
  319.3 1.4 broadcast_divide_fusion.scaled_ref
  321.8 14.8 %all-gather.2.cloned.1.call-done.head_hbm = bf16[4000,2048]{1,0:T(8,128)(2,1)} async-done(((bf16[4000,128]{1,0:T(8,128)(2,1)}), bf16[4000,2048]{1,0:T(8,128)(2,1)}) %all-gather.2.cloned.1.call-update) | async-done | bytes 16384016 | tf_op jit(solution)/shard_map/all_gather | solution.py:1465
  336.6 74.2 %head_step.1 = (f32[64,2048]{1,0:T(8,128)}, f32[8,128]{1,0:T(8,128)}) custom-call(bf16[64,2048]{1,0:T(8,128)(2,1)} %convolution_convert_fusion.chosen_ref, bf16[4000,2048]{1,0:T(8,128)(2,1)} %all-gather.2.cloned.1.call-done.head_hbm, s32[512,1]{1,0:T(8,128)} %compare_select_fusion.target_ref, f32[512,1]{1,0:T(8,128)} %copy-done.4, ...), custom_call_target="tpu_custom_call" | custom-call | tf_op jit(solution)/shard_map/head_step/pallas_call | solution.py:749
  410.8 2.0 multiply_reduce_fusion
  413.8 38.7 %feed_forward_back.1 = f32[128,2048]{1,0:T(8,128)} custom-call(bf16[128,2048]{1,0:T(8,128)(2,1)} %fusion.35.refs_0_, bf16[2048,3072]{1,0:T(8,128)(2,1)} %bitcast.63, bf16[1536,2048]{1,0:T(8,128)(2,1)} %bitcast.65, f32[512,3072]{1,0:T(8,128)} %get-tuple-element.67.refs_3_), custom_call_target="tpu_custom_call" | custom-call | tf_op jit(solution)/shard_map/feed_forward_back/pallas_call | solution.py:1135
  452.5 1.6 multiply_reduce_fusion.1
  454.9 6.3 %fusion.2 = f32[128,2048]{1,0:T(8,128)S(1)} fusion(bf16[2048,4608]{1,0:T(8,128)(2,1)} %bitcast.67, f32[128,2048]{1,0:T(8,128)S(1)} %subtract_add_fusion), kind=kOutput, calls=%fused_computation.2 | convolution fusion | flops 1074003968 | bytes 10485760 | tf_op jit(solution)/shard_map/dot_general | solution.py:1211
  461.2 1.1 fusion.4.g_ref
  462.4 11.3 %attend_back.1 = (bf16[128,2048]{1,0:T(8,128)(2,1)}, bf16[2,256,512]{2,1,0:T(8,128)(2,1)}, f32[2,64,512]{2,1,0:T(8,128)}) custom-call(s32[1]{0:T(128)} %bitcast.19.start_ref, s32[4]{0:T(128)} %shift_ref.3, bf16[128,2048]{1,0:T(8,128)(2,1)} %get-tuple-element.69.q_ref, bf16[2,320,512]{2,1,0:T(8,128)(2,1)} %get-tuple-element.70.kv_ref, ...), custom_call_target="tpu_custom_call" | custom-call | tf_op jit(solution)/shard_map/attend_back/pallas_call | solution.py:1254
  473.6 12.7 %key_value_back.1 = bf16[128,512]{1,0:T(8,128)(2,1)} custom-call(bf16[2,256,512]{2,1,0:T(8,128)(2,1)} %get-tuple-element.72.far_ref, f32[2,64,512]{2,1,0:T(8,128)} %get-tuple-element.73.own_ref, f32[64,512]{1,0:T(8,128)} %copy.122.cos_ref, f32[64,512]{1,0:T(8,128)} %tile.21.sin_ref), custom_call_target="tpu_custom_call" | custom-call | tf_op jit(solution)/shard_map/key_value_back/pallas_call | solution.py:1179
  486.4 1.1 fusion.18
  488.6 1.3 fusion.22
  489.9 1.4 fusion.11
  491.4 6.2 %fusion = f32[128,2048]{1,0:T(8,128)S(1)} fusion(bf16[2048,4608]{1,0:T(8,128)(2,1)} %bitcast.68, bf16[128,512]{1,0:T(8,128)(2,1)S(1)} %copy-done.9, bf16[128,2048]{1,0:T(8,128)(2,1)S(1)} %copy-done.6), kind=kOutput, calls=%fused_computation | convolution fusion | flops 1343488000 | bytes 12189696 | tf_op jit(solution)/shard_map/dot_general | solution.py:1211
  499.5 1.1 add_convert_fusion.src
  500.7 2.0 concatenate.33.left_ref
  502.7 90.8 %token_gradients.1 = (f32[4000,128]{1,0:T(8,128)}, f32[40,128]{1,0:T(8,128)}, f32[8,384]{1,0:T(8,128)}, f32[8,128]{1,0:T(8,128)}) custom-call(bf16[128,2048]{1,0:T(8,128)(2,1)} %add_convert_fusion.src, f32[40,2048]{1,0:T(8,128)} %concatenate.33.left_ref, f32[8,4608]{1,0:T(8,128)} %pad_maximum_fusion.4.right_ref, s32[16,1024]{1,0:T(8,128)} %sub.57.ids_ref, ...), custom_call_target="tpu_custom_call" | custom-call | tf_op jit(solution)/shard_map/token_gradients/pallas_call | solution.py:928
  593.5 1.3 slice.99
  594.7 1.4 constant_dynamic-slice_fusion.r_ref
  596.1 1.4 constant_dynamic-slice_fusion.1.l_ref
  597.5 7.9 %small_updates.1 = (f32[8,128]{1,0:T(8,128)}, f32[32,16]{1,0:T(8,128)}, f32[8,36]{1,0:T(8,128)}, f32[3,16]{1,0:T(4,128)}, f32[3,16]{1,0:T(4,128)}, /*index=5*/f3...) custom-call(f32[8,128]{1,0:T(8,128)} %get-tuple-element.79.t_ref, ...), custom_call_target="tpu_custom_call" | custom-call | tf_op jit(solution)/shard_map/small_updates/pallas_call | solution.py:1368
  605.4 1.3 fusion.38
  606.7 1.4 copy.148
  608.1 1.4 copy.149
  609.5 6.6 %fusion.10 = (f32[4000,128]{1,0:T(8,128)}, f32[4000,128]{1,0:T(8,128)}, f32[4000,128]{1,0:T(8,128)}) fusion(f32[4000,128]{1,0:T(8,128)S(1)} %copy-done.3, f32[4000,128]{1,0:T(8,128)} %param.29, f32[4000,128]{1,0:T(8,128)} %param.30, f32[4000,128]{1,0:T(8,128)} %get-tuple-element.83, f32[]{:T(128)} %bitcast.28), kind=kLoop, calls=%fused_computation.16 | loop fusion | flops 7680000 | bytes 14336004 | tf_op jit(solution)/shard_map/sub | solution.py:1410
  (150 shorter events, 25.8 us)
Async XLA Ops:
  7.2 5.2 copy-start.11
  7.2 5.9 copy-start.14
  7.2 5.9 copy-start.15
  7.2 6.5 %copy-start.19 = (s32[2,8,64]{2,1,0:T(8,128)S(1)}, s32[2,8,64]{2,1,0:T(8,128)}, u32[]{:S(2)}) copy-start(s32[2,8,64]{2,1,0:T(8,128)} %param.22) | copy-start | bytes 12292
  7.2 329.4 %all-gather.2.cloned.1.call-start = ((), (), s32[]{:S(2)}) async-start(), calls=%async_computation | async-start | bytes 17408000 | tf_op jit(solution)/shard_map/all_gather | solution.py:1465
  8.1 197.2 %copy-start.12 = (f32[32,16]{1,0:T(8,128)}, f32[32,16]{1,0:T(8,128)S(1)}, u32[]{:S(2)}) copy-start(f32[32,16]{1,0:T(8,128)S(1)} %copy.114.a_ref) | copy-start | bytes 6148
  206.5 2.1 copy-start.13
  206.5 2.9 copy-start.8
  208.0 5.8 copy-start.17
  208.5 5.8 copy-start.21
  208.7 6.2 copy-start.16
  210.5 5.9 copy-start.20
  216.4 103.0 %copy-start.4 = (f32[512,1]{1,0:T(8,128)}, f32[512,1]{1,0:T(8,128)S(1)}, u32[]{:S(2)}) copy-start(f32[512,1]{1,0:T(8,128)S(1)} %reshape_reshape.4.weight_ref) | copy-start | bytes 6148
  279.5 37.6 %copy-start.2 = (f32[128,2048]{1,0:T(8,128)S(1)}, f32[128,2048]{1,0:T(8,128)}, u32[]{:S(2)}) copy-start(f32[128,2048]{1,0:T(8,128)} %get-tuple-element.60) | copy-start | bytes 3145732
  413.8 38.7 %copy-start = (f32[128,2048]{1,0:T(8,128)S(1)}, f32[128,2048]{1,0:T(8,128)}, u32[]{:S(2)}) copy-start(f32[128,2048]{1,0:T(8,128)} %get-tuple-element.68) | copy-start | bytes 3145732
  452.5 1.7 copy-start.1
  461.2 25.2 %copy-start.10 = (bf16[128,24]{1,0:T(8,128)(2,1)S(1)}, bf16[128,24]{1,0:T(8,128)(2,1)}, u32[]{:S(2)}) copy-start(bf16[128,24]{1,0:T(8,128)(2,1)} %get-tuple-element.76) | copy-start | bytes 18436
  473.6 17.7 %copy-start.6 = (bf16[128,2048]{1,0:T(8,128)(2,1)S(1)}, bf16[128,2048]{1,0:T(8,128)(2,1)}, u32[]{:S(2)}) copy-start(bf16[128,2048]{1,0:T(8,128)(2,1)} %get-tuple-element.71) | copy-start | bytes 1572868
  486.4 5.0 copy-start.9
  491.4 6.3 %copy-start.18 = (bf16[128,8]{1,0:T(8,128)(2,1)S(1)}, bf16[128,8]{1,0:T(8,128)(2,1)}, u32[]{:S(2)}) copy-start(bf16[128,8]{1,0:T(8,128)(2,1)} %get-tuple-element.77) | copy-start | bytes 6148
  491.4 6.5 %copy-start.5 = (bf16[128,2048]{1,0:T(8,128)(2,1)S(1)}, bf16[128,2048]{1,0:T(8,128)(2,1)}, u32[]{:S(2)}) copy-start(bf16[128,2048]{1,0:T(8,128)(2,1)} %get-tuple-element.75) | copy-start | bytes 1572868
  491.4 6.7 %copy-start.7 = (bf16[128,2048]{1,0:T(8,128)(2,1)S(1)}, bf16[128,2048]{1,0:T(8,128)(2,1)}, u32[]{:S(2)}) copy-start(bf16[128,2048]{1,0:T(8,128)(2,1)} %get-tuple-element.74) | copy-start | bytes 1572868
  499.5 109.9 %copy-start.3 = (f32[4000,128]{1,0:T(8,128)S(1)}, f32[4000,128]{1,0:T(8,128)}, u32[]{:S(2)}) copy-start(f32[4000,128]{1,0:T(8,128)} %param.28) | copy-start | bytes 6144004
Sparse Core Ops, SparseCore 0:
  205.5 131.0 all-gather.1

commit v7 on v6

--- a/solution.py
+++ b/solution.py
@@ -646,34 +646,46 @@
     )(table, ids, qkvo, a_low, b_in, b_out, gain, cosine, sine, query_seg, key_seg, shifts)
 
 
-def head_step(chosen, head, target, weight, scaled, collective_id):
+def chosen_rows(chosen, collective_id):
+    def body(src, out, sem):
+        post = Post(sem, 24)
+        out[fsdp_me()] = src[...]
+        greet_devices(fsdp_peers())
+        for _ in relay(
+            post, out, (pl.ds(0, 32),), (pl.ds(32, 32),), (pl.ds(0, 16),), (pl.ds(16, 16),)
+        ):
+            pass
+        post.finish()
+
+    return remote_call(
+        body,
+        jax.ShapeDtypeStruct((FSDP_N, *chosen.shape), chosen.dtype),
+        [VMEM], VMEM, [DMA((24,))], collective_id, "chosen_rows",
+    )(chosen)
+
+
+def head_step(rows, head, target, weight, scaled, collective_id):
     vocab, width = head.shape
     padded = -(-vocab // 512) * 512
     tiles = padded // 512
 
     def body(
-        chosen_ref, head_hbm, target_ref, weight_ref, scaled_ref, out, loss, hd, held, raised, d_logits,
-        prod, got, stat, stats, sem, lsem,
+        rows_ref, head_hbm, target_ref, weight_ref, scaled_ref, out, loss, hd, raised, d_logits, prod,
+        got, stat, stats, sem, lsem,
     ):
         post = Post(sem, 60)
         me = fsdp_me()
         load = pltpu.make_async_copy(head_hbm, hd.at[pl.ds(0, vocab)], lsem)
         load.start()
-        held[me] = chosen_ref[...]
         greet_devices(fsdp_peers())
-        for _ in relay(
-            post, held, (pl.ds(0, 32),), (pl.ds(32, 32),), (pl.ds(0, 16),), (pl.ds(16, 16),)
-        ):
-            pass
         hd[vocab:, :] = jnp.zeros((padded - vocab, width), jnp.bfloat16)
         load.wait()
-        rows = held[...].reshape(512, width)
         target_at = target_ref[...]
 
         def logits(n, carry):
             top, picked = carry
             at = pl.multiple_of(n * 512, 512)
-            tile = nt(held[...].reshape(512, width), hd[pl.ds(at, 512), :])
+            tile = nt(rows_ref[...], hd[pl.ds(at, 512), :])
             column = lax.broadcasted_iota(jnp.int32, (512, 512), 1) + at
             tile = jnp.where(column < vocab, tile, -1e30)
             raised[:, pl.ds(at, 512)] = tile
@@ -756,7 +768,6 @@
         [VMEM, VMEM],
         [
             pltpu.VMEM((padded, width), jnp.bfloat16),
-            pltpu.VMEM((8, 64, width), jnp.bfloat16),
             pltpu.VMEM((512, padded), jnp.float32),
             pltpu.VMEM((512, padded), jnp.bfloat16),
             pltpu.VMEM((8, 64, width), jnp.bfloat16),
@@ -768,7 +779,7 @@
         ],
         collective_id,
         "head_step",
-    )(chosen, head, target, weight, scaled)
+    )(rows, head, target, weight, scaled)
 
 
 def token_gradients(d_start, left, right, ids, loss, vocab, collective_id):
@@ -806,7 +817,7 @@
             copy.wait_recv()
         own.wait()
 
-        def add(block):
+        def add(block, halves=(0, 2)):
             def one(t, carry):
                 ids_row = ids_ref[pl.ds(block * 2 + t, 1), :]
                 high, low = ids_row >> 10, ids_row & 1023
@@ -830,7 +841,7 @@
                 lax.fori_loop(0, low_n // 256, step, 0)
                 return carry
 
-            lax.fori_loop(0, 2, one, 0)
+            lax.fori_loop(*halves, one, 0)
 
         every = slice(None)
         steps = relay(
@@ -858,12 +869,15 @@
         next(steps)
         next(steps)
         add(before * 2 + yl)
+        add(after * 2 + yl)
         next(steps)
-        add(after * 2 + yl)
+        for zz in (before, after):
+            add(zz * 2 + 1 - yl, (0, 1))
         add(far * 2 + yl)
         assert next(steps, "end") == "end"
-        for zz in (before, after, far):
-            add(zz * 2 + 1 - yl)
+        for zz in (before, after):
+            add(zz * 2 + 1 - yl, (1, 2))
+        add(far * 2 + 1 - yl)
         squares = jnp.zeros((1, width), jnp.float32)
         for h in range(4):
             count = min(low_n, vocab - h * low_n)
@@ -1015,7 +1029,7 @@
         def lines(block, k=None):
             if k is None:
                 return pl.ds(block * count, count)
-            return pl.ds(block * count + k * chunk, chunk)
+            return pl.ds(2 * count + (2 * k + block - 2) * chunk, chunk)
 
         along = [
             remote(src.at[pl.ds(k * chunk, chunk)], held.at[lines(2, k)], partner) for k in range(2)
@@ -1023,8 +1037,8 @@
         beside = remote(src, held.at[lines(1)], sibling)
         held[lines(0), :] = src[...]
 
-        def first_product(pair):
-            mine = pl.ds(pair * 2 * count, 2 * count)
+        def first_product(first, size):
+            mine, low_rows = pl.ds(first, size), pl.ds(0, size)
 
             def step(n, carry):
                 at = pl.multiple_of(n * tile, tile)
@@ -1035,28 +1049,30 @@
                     up = jnp.dot(block, gu[:, high], preferred_element_type=jnp.float32)
                     saved_v[mine, low] = gate
                     saved_v[mine, high] = up
-                    mid[:, low] = (gate * jax.nn.sigmoid(gate) * up).astype(jnp.bfloat16)
+                    mid[low_rows, low] = (gate * jax.nn.sigmoid(gate) * up).astype(jnp.bfloat16)
                 else:
                     d_hidden = nt(block, dn[low, :])
                     gate, up = saved_v[mine, low], saved_v[mine, high]
                     sigmoid_of = jax.nn.sigmoid(gate)
-                    mid[:, low] = (
+                    mid[low_rows, low] = (
                         d_hidden * up * sigmoid_of * (1.0 + gate * (1.0 - sigmoid_of))
                     ).astype(jnp.bfloat16)
-                    mid[:, high] = (d_hidden * gate * sigmoid_of).astype(jnp.bfloat16)
+                    mid[low_rows, high] = (d_hidden * gate * sigmoid_of).astype(jnp.bfloat16)
                 return carry
 
             lax.fori_loop(0, units // tile, step, 0)
 
-        def second_product(pair):
+        def second_product(first, size):
+            mine, low_rows = pl.ds(first, size), pl.ds(0, size)
+
             def step(n, carry):
                 at = pl.ds(pl.multiple_of(n * tile, tile), tile)
                 if forward:
-                    part[pair, :, at] = jnp.dot(
-                        mid[...], dn[:, at], preferred_element_type=jnp.float32
+                    part[mine, at] = jnp.dot(
+                        mid[low_rows, :], dn[:, at], preferred_element_type=jnp.float32
                     )
                 else:
-                    part[pair, :, at] = nt(mid[...], gu[at, :])
+                    part[mine, at] = nt(mid[low_rows, :], gu[at, :])
                 return carry
 
             lax.fori_loop(0, width // tile, step, 0)
@@ -1064,46 +1080,56 @@
         for load in loads[0]:
             load.wait()
         beside.wait_recv()
-        first_product(0)
+        first_product(0, 2 * count)
         along[0].wait_recv()
         passed = [remote(held.at[lines(2, 0)], held.at[lines(3, 0)], sibling)]
         for load in loads[1]:
             load.wait()
-        second_product(0)
-        along[1].wait_recv()
-        passed.append(remote(held.at[lines(2, 1)], held.at[lines(3, 1)], sibling))
-        give[0] = part[0, count:, :].astype(jnp.bfloat16)
+        second_product(0, 2 * count)
+        give[0] = part[lines(1), :].astype(jnp.bfloat16)
         home = remote(give.at[0], got.at[0], sibling)
-        if forward:
-            stores = [
-                pltpu.make_async_copy(
-                    saved_v.at[pl.ds(0, 2 * count)], gu_out.at[pl.ds(0, 2 * count)], fresh()
+        stores = []
+
+        def store(first, size):
+            if forward:
+                copy = pltpu.make_async_copy(
+                    saved_v.at[pl.ds(first, size)], gu_out.at[pl.ds(first, size)], fresh()
                 )
-            ]
-            stores[0].start()
-        for copy in passed:
-            copy.wait_recv()
-        first_product(1)
-        if forward:
-            stores.append(
-                pltpu.make_async_copy(
-                    saved_v.at[pl.ds(2 * count, 2 * count)], gu_out.at[pl.ds(2 * count, 2 * count)], fresh()
-                )
-            )
-            stores[1].start()
-        second_product(1)
-        give[1] = part[1, count:, :].astype(jnp.bfloat16)
-        over = remote(give.at[1], got.at[1], sibling)
-        over.wait_recv()
-        back = []
-        for k in range(2):
+                copy.start()
+                stores.append(copy)
+
+        store(0, 2 * count)
+        over, back = [], []
+
+        def hand_over(k):
             some = pl.ds(k * chunk, chunk)
-            give[2, some, :] = (part[1, some, :] + got[1, some, :].astype(jnp.float32)).astype(
+            give[1, some, :] = part[lines(3, k), :].astype(jnp.bfloat16)
+            over.append(remote(give.at[1, some], got.at[1, some], sibling))
+
+        def send_back(k):
+            some = pl.ds(k * chunk, chunk)
+            over[k].wait_recv()
+            give[2, some, :] = (part[lines(2, k), :] + got[1, some, :].astype(jnp.float32)).astype(
                 jnp.bfloat16
             )
             back.append(remote(give.at[2, some], got.at[2, some], partner))
+
+        first, second = 2 * count, 2 * count + 2 * chunk
+        passed[0].wait_recv()
+        first_product(first, 2 * chunk)
+        along[1].wait_recv()
+        passed.append(remote(held.at[lines(2, 1)], held.at[lines(3, 1)], sibling))
+        second_product(first, 2 * chunk)
+        hand_over(0)
+        passed[1].wait_recv()
+        first_product(second, 2 * chunk)
+        send_back(0)
+        store(first, 4 * chunk)
+        second_product(second, 2 * chunk)
+        hand_over(1)
+        send_back(1)
         home.wait_recv()
-        out[...] = part[0, 0:count, :] + got[0].astype(jnp.float32)
+        out[...] = part[lines(0), :] + got[0].astype(jnp.float32)
         for k in range(2):
             some = pl.ds(k * chunk, chunk)
             back[k].wait_recv()
@@ -1120,10 +1146,10 @@
         pltpu.VMEM((units, width), jnp.bfloat16),
         pltpu.VMEM((4 * count, quarter), jnp.float32),
         pltpu.VMEM((2 * count, units if forward else quarter), jnp.bfloat16),
-        pltpu.VMEM((2, 2 * count, width), jnp.float32),
+        pltpu.VMEM((4 * count, width), jnp.float32),
         pltpu.VMEM((3, count, width), jnp.bfloat16),
         pltpu.VMEM((3, count, width), jnp.bfloat16),
-        DMA((24,)),
+        DMA((32,)),
     ]
     total = jax.ShapeDtypeStruct((count, width), jnp.float32)
     if forward:
@@ -1469,6 +1495,7 @@
     up_full = small[:, 560:848].reshape(128, 8, 36).transpose(1, 0, 2).reshape(8, 4608)
     a_low = down_full.astype(jnp.bfloat16)
     b_low = up_full.astype(jnp.bfloat16)
+    a_low, b_low, gain = lax.optimization_barrier((a_low, b_low, gain))
     a_in, a_out = a_low[:24], a_low[24:]
     factor_of = (jnp.arange(2560) >= 2048).astype(jnp.int32) + (jnp.arange(2560) >= 2304)
     b_in = jnp.where(
@@ -1532,8 +1559,10 @@
     local_target = target_token_index.transpose(1, 0, 2).reshape(512, 1) - fsdp_here * vocab_dev
     local_target = jnp.where(local_target < vocab_dev, local_target, -1)
     weight_column = weight_flat.reshape(512, 1)
+    rows = chosen_rows(chosen, 5).reshape(512, 2048)
+    head, rows = lax.optimization_barrier((head, rows))
     d_chosen, loss_tile = head_step(
-        chosen, head, local_target, weight_column, weight_column / document_total, 4
+        rows, head, local_target, weight_column, weight_column / document_total, 4
     )
 
     upstream = lax.dot_general(pick, d_chosen, (((0,), (0,)), ((), ())), precision=HIGHEST)

time: 633 us -> 627 us (level)
  waiting for transfers between devices: 14.8 us -> 4.5 us
    pallas_call x0 -> x1, Pallas kernels: none -> 22.4 us  [chosen_rows(): remote_call(body, jax.ShapeDtypeStruct((FSDP_N, *chosen.shape), chosen.dt...]
    all_gather x1, waiting for transfers between devices: 14.8 us -> 4.48 us  [per_device(): head = lax.all_gather(head_own, SEQ, axis=1, tiled=True)]
    pallas_call x1, Pallas kernels: 74.2 us -> 64.3 us  [head_step(): remote_call(body, [jax.ShapeDtypeStruct((64, width), jnp.float32), jax.Sh...]
  transfers between devices with their start and end apart: 1 -> 1, of which waited for: 1 -> 1; matrix products, arithmetic and copies ran while one was open for 3% -> 3% of each run, Pallas kernels for 15% -> 18%
where the time goes in v7:
time: 627 us; the launch traced here: 617 us
  Pallas kernels  527 us (84%)
  local copies, waits for them, and re-layouts  24 us (4%)
  matrix products  23.1 us (4%)
  other arithmetic  22.8 us (4%)
  between operations  15.1 us (2%)
    pallas_call x1, Pallas kernels, gather_weights(): remote_call(body, out_shape, [ANY] * 4 + [VMEM, ANY], [ANY] * 6, [pltpu.V...  190 us
    pallas_call x1, Pallas kernels, token_gradients(): remote_call(body, [jax.ShapeDtypeStruct((vocab, width), jnp.float32), jax...  90.8 us
    pallas_call x1, Pallas kernels, head_step(): remote_call(body, [jax.ShapeDtypeStruct((64, width), jnp.float32), jax.Sh...  64.3 us
    pallas_call x1, Pallas kernels, attention_block(): remote_call(body, [shape(rows_n, 2048, dtype=jnp.float32), shape(rows_n,...  56.5 us
    pallas_call x1, Pallas kernels, feed_forward(): remote_call(body, total, [VMEM] + [ANY] * (2 * parts_n + 1), VMEM, scratc...  40.9 us
    pallas_call x1, Pallas kernels, feed_forward(): remote_call(body, [total, products], [VMEM] + [ANY] * (2 * parts_n), [VME...  32.3 us
    pallas_call x1, Pallas kernels, chosen_rows(): remote_call(body, jax.ShapeDtypeStruct((FSDP_N, *chosen.shape), chosen.dt...  22.4 us
    dot_general x4, matrix products, nt(): lax.dot_general(left, right, (((1,), (1,)), ((), ())), preferred_element_...  14.2 us
  transfers between devices with their start and end apart: 1, of which 1 were waited for; matrix products, arithmetic and copies ran while one was open for 3% of the time, Pallas kernels for 18%

profile of v7, /device:TPU:1, one launch (start us, length us, event | category | flops | bytes accessed | tf_op | source)
XLA Modules:
  0.0 616.9 jit_solution(13411434132366249376)
XLA Ops:
  9.7 2.6 convert_element_type.100.refs_2_
  15.0 190.3 %gather_weights.1 = (bf16[2,4,2,4,2,16,4608]{6,5,4,3,2,1,0:T(8,128)(2,1)}, f32[2,4,2,4,2,8,128]{6,5,4,3,2,1,0:T(8,128)}, bf16[8,4000,128]{2,1,0:T(8,128)(2,1)}, ...) custom-call(bf16[16,4608]{1,0:T(8,128)(2,1)} %pad_maximum_fusion.3.ref, ...), custom_call_target="tpu_custom_call" | custom-call | tf_op jit(solution)/shard_map/gather_weights/pallas_call | solution.py:470
  205.3 1.1 copy.144
  214.8 56.5 %attention_block.1 = (f32[128,2048]{1,0:T(8,128)}, bf16[128,2048]{1,0:T(8,128)(2,1)}, bf16[128,24]{1,0:T(8,128)(2,1)}, bf16[128,2048]{1,0:T(8,128)(2,1)}, bf16[2...) custom-call(bf16[8,4000,128]{2,1,0:T(8,128)(2,1)} %get-tuple-element, ...), custom_call_target="tpu_custom_call" | custom-call | tf_op jit(solution)/shard_map/attention_block/pallas_call | solution.py:617
  271.4 32.3 %feed_forward.1 = (f32[128,2048]{1,0:T(8,128)}, f32[512,3072]{1,0:T(8,128)}) custom-call(bf16[128,2048]{1,0:T(8,128)(2,1)} %get-tuple-element.69.refs_0_, bf16[2048,3072]{1,0:T(8,128)(2,1)} %bitcast.64, bf16[1536,2048]{1,0:T(8,128)(2,1)} %bitcast.66), custom_call_target="tpu_custom_call" | custom-call | tf_op jit(solution)/shard_map/feed_forward/pallas_call | solution.py:1157
  303.7 1.5 multiply_reduce_fusion.8
  306.3 22.4 %chosen_rows.1 = bf16[8,64,2048]{2,1,0:T(8,128)(2,1)} custom-call(bf16[64,2048]{1,0:T(8,128)(2,1)} %convolution_convert_fusion.src), custom_call_target="tpu_custom_call" | custom-call | tf_op jit(solution)/shard_map/chosen_rows/pallas_call | solution.py:660
  333.8 1.4 broadcast_divide_fusion.scaled_ref
  335.2 4.5 all-gather.2.cloned.1.call-done.head_hbm
  339.7 64.3 %head_step.1 = (f32[64,2048]{1,0:T(8,128)}, f32[8,128]{1,0:T(8,128)}) custom-call(bf16[512,2048]{1,0:T(8,128)(2,1)} %bitcast.71, bf16[4000,2048]{1,0:T(8,128)(2,1)} %all-gather.2.cloned.1.call-done.head_hbm, s32[512,1]{1,0:T(8,128)} %compare_select_fusion.target_ref, f32[512,1]{1,0:T(8,128)} %copy-done.4, f32[512,1]{1,0:T(8,128)} %broadcast_divide_fusion.scaled_ref), custom_call_target="tpu_custom_call" | custom-call | tf_op jit(solution)/shard_map/head_step/pallas_call | solution.py:761
  403.9 2.0 multiply_reduce_fusion
  407.0 40.9 %feed_forward_back.1 = f32[128,2048]{1,0:T(8,128)} custom-call(bf16[128,2048]{1,0:T(8,128)(2,1)} %fusion.37.refs_0_, bf16[2048,3072]{1,0:T(8,128)(2,1)} %bitcast.65, bf16[1536,2048]{1,0:T(8,128)(2,1)} %bitcast.67, f32[512,3072]{1,0:T(8,128)} %get-tuple-element.77.refs_3_), custom_call_target="tpu_custom_call" | custom-call | tf_op jit(solution)/shard_map/feed_forward_back/pallas_call | solution.py:1161
  447.9 1.6 multiply_reduce_fusion.1
  450.3 6.3 %fusion.2 = f32[128,2048]{1,0:T(8,128)S(1)} fusion(bf16[2048,4608]{1,0:T(8,128)(2,1)} %bitcast.69, f32[128,2048]{1,0:T(8,128)S(1)} %subtract_add_fusion), kind=kOutput, calls=%fused_computation.2 | convolution fusion | flops 1074003968 | bytes 10485760 | tf_op jit(solution)/shard_map/dot_general | solution.py:1237
  456.6 1.3 fusion.4.g_ref
  457.9 11.3 %attend_back.1 = (bf16[128,2048]{1,0:T(8,128)(2,1)}, bf16[2,256,512]{2,1,0:T(8,128)(2,1)}, f32[2,64,512]{2,1,0:T(8,128)}) custom-call(s32[1]{0:T(128)} %bitcast.22.start_ref, s32[4]{0:T(128)} %shift_ref.3, bf16[128,2048]{1,0:T(8,128)(2,1)} %get-tuple-element.79.q_ref, bf16[2,320,512]{2,1,0:T(8,128)(2,1)} %get-tuple-element.80.kv_ref, ...), custom_call_target="tpu_custom_call" | custom-call | tf_op jit(solution)/shard_map/attend_back/pallas_call | solution.py:1280
  469.2 10.7 %key_value_back.1 = bf16[128,512]{1,0:T(8,128)(2,1)} custom-call(bf16[2,256,512]{2,1,0:T(8,128)(2,1)} %get-tuple-element.82.far_ref, f32[2,64,512]{2,1,0:T(8,128)} %get-tuple-element.83.own_ref, f32[64,512]{1,0:T(8,128)} %copy.112.cos_ref, f32[64,512]{1,0:T(8,128)} %tile.21.sin_ref), custom_call_target="tpu_custom_call" | custom-call | tf_op jit(solution)/shard_map/key_value_back/pallas_call | solution.py:1205
  479.9 1.1 fusion.20
  482.1 1.3 fusion.24
  483.4 1.4 fusion.11
  484.9 6.2 %fusion = f32[128,2048]{1,0:T(8,128)S(1)} fusion(bf16[2048,4608]{1,0:T(8,128)(2,1)} %bitcast.70, bf16[128,512]{1,0:T(8,128)(2,1)S(1)} %copy-done.9, bf16[128,2048]{1,0:T(8,128)(2,1)S(1)} %copy-done.6), kind=kOutput, calls=%fused_computation | convolution fusion | flops 1343488000 | bytes 12189696 | tf_op jit(solution)/shard_map/dot_general | solution.py:1237
  493.1 1.1 add_convert_fusion.src
  494.2 2.0 concatenate.33.left_ref
  496.2 90.8 %token_gradients.1 = (f32[4000,128]{1,0:T(8,128)}, f32[40,128]{1,0:T(8,128)}, f32[8,384]{1,0:T(8,128)}, f32[8,128]{1,0:T(8,128)}) custom-call(bf16[128,2048]{1,0:T(8,128)(2,1)} %add_convert_fusion.src, f32[40,2048]{1,0:T(8,128)} %concatenate.33.left_ref, f32[8,4608]{1,0:T(8,128)} %pad_maximum_fusion.4.right_ref, s32[16,1024]{1,0:T(8,128)} %sub.57.ids_ref, ...), custom_call_target="tpu_custom_call" | custom-call | tf_op jit(solution)/shard_map/token_gradients/pallas_call | solution.py:942
  587.0 1.3 slice.88
  588.3 1.4 constant_dynamic-slice_fusion.r_ref
  589.6 1.4 constant_dynamic-slice_fusion.1.l_ref
  591.0 7.9 %small_updates.1 = (f32[8,128]{1,0:T(8,128)}, f32[32,16]{1,0:T(8,128)}, f32[8,36]{1,0:T(8,128)}, f32[3,16]{1,0:T(4,128)}, f32[3,16]{1,0:T(4,128)}, /*index=5*/f3...) custom-call(f32[8,128]{1,0:T(8,128)} %get-tuple-element.89.t_ref, ...), custom_call_target="tpu_custom_call" | custom-call | tf_op jit(solution)/shard_map/small_updates/pallas_call | solution.py:1394
  598.9 1.3 fusion.40
  600.2 1.4 copy.133
  601.6 1.4 copy.134
  603.0 6.6 %fusion.10 = (f32[4000,128]{1,0:T(8,128)}, f32[4000,128]{1,0:T(8,128)}, f32[4000,128]{1,0:T(8,128)}) fusion(f32[4000,128]{1,0:T(8,128)S(1)} %copy-done.3, f32[4000,128]{1,0:T(8,128)} %param.29, f32[4000,128]{1,0:T(8,128)} %param.30, f32[4000,128]{1,0:T(8,128)} %get-tuple-element.93, f32[]{:T(128)} %bitcast.30), kind=kLoop, calls=%fused_computation.16 | loop fusion | flops 7680000 | bytes 14336004 | tf_op jit(solution)/shard_map/sub | solution.py:1436
  (141 shorter events, 24.3 us)
Async XLA Ops:
  7.2 5.2 copy-start.12
  7.2 5.9 copy-start.15
  7.2 5.9 copy-start.16
  7.2 6.5 %copy-start.20 = (s32[2,8,64]{2,1,0:T(8,128)S(1)}, s32[2,8,64]{2,1,0:T(8,128)}, u32[]{:S(2)}) copy-start(s32[2,8,64]{2,1,0:T(8,128)} %param.22) | copy-start | bytes 12292
  7.2 332.4 %all-gather.2.cloned.1.call-start = ((), (), s32[]{:S(2)}) async-start(), calls=%async_computation | async-start | bytes 17408000 | tf_op jit(solution)/shard_map/all_gather | solution.py:1491
  8.1 197.2 %copy-start.13 = (f32[32,16]{1,0:T(8,128)}, f32[32,16]{1,0:T(8,128)S(1)}, u32[]{:S(2)}) copy-start(f32[32,16]{1,0:T(8,128)S(1)} %copy.104.a_ref) | copy-start | bytes 6148
  206.5 2.9 copy-start.14
  206.5 3.8 copy-start.8
  207.3 6.4 %copy-start.18 = (s32[2,8,512]{2,1,0:T(8,128)S(1)}, s32[2,8,512]{2,1,0:T(8,128)}, u32[]{:S(2)}) copy-start(s32[2,8,512]{2,1,0:T(8,128)} %param.24) | copy-start | bytes 98308
  209.5 5.3 copy-start.17
  271.3 32.4 %copy-start.2 = (f32[128,2048]{1,0:T(8,128)S(1)}, f32[128,2048]{1,0:T(8,128)}, u32[]{:S(2)}) copy-start(f32[128,2048]{1,0:T(8,128)} %get-tuple-element.68) | copy-start | bytes 3145732
  303.7 1.5 copy-start.11
  305.2 23.5 %copy-start.22 = (s32[2,8]{1,0:T(2,128)S(1)}, s32[2,8]{1,0:T(2,128)}, u32[]{:S(2)}) copy-start(s32[2,8]{1,0:T(2,128)} %param.26) | copy-start | bytes 196
  306.3 24.5 %copy-start.21 = (s32[2,8,32]{2,1,0:T(8,128)S(1)}, s32[2,8,32]{2,1,0:T(8,128)}, u32[]{:S(2)}) copy-start(s32[2,8,32]{2,1,0:T(8,128)} %param.23) | copy-start | bytes 6148
  330.7 8.9 %copy-start.4 = (f32[512,1]{1,0:T(8,128)}, f32[512,1]{1,0:T(8,128)S(1)}, u32[]{:S(2)}) copy-start(f32[512,1]{1,0:T(8,128)S(1)} %reshape_reshape.4.weight_ref) | copy-start | bytes 6148
  407.0 40.9 %copy-start = (f32[128,2048]{1,0:T(8,128)S(1)}, f32[128,2048]{1,0:T(8,128)}, u32[]{:S(2)}) copy-start(f32[128,2048]{1,0:T(8,128)} %get-tuple-element.78) | copy-start | bytes 3145732
  447.9 1.7 copy-start.1
  457.9 22.0 %copy-start.10 = (bf16[128,24]{1,0:T(8,128)(2,1)S(1)}, bf16[128,24]{1,0:T(8,128)(2,1)}, u32[]{:S(2)}) copy-start(bf16[128,24]{1,0:T(8,128)(2,1)} %get-tuple-element.86) | copy-start | bytes 18436
  469.2 15.7 %copy-start.6 = (bf16[128,2048]{1,0:T(8,128)(2,1)S(1)}, bf16[128,2048]{1,0:T(8,128)(2,1)}, u32[]{:S(2)}) copy-start(bf16[128,2048]{1,0:T(8,128)(2,1)} %get-tuple-element.81) | copy-start | bytes 1572868
  479.9 5.0 copy-start.9
  484.9 6.3 %copy-start.19 = (bf16[128,8]{1,0:T(8,128)(2,1)S(1)}, bf16[128,8]{1,0:T(8,128)(2,1)}, u32[]{:S(2)}) copy-start(bf16[128,8]{1,0:T(8,128)(2,1)} %get-tuple-element.87) | copy-start | bytes 6148
  484.9 6.5 %copy-start.5 = (bf16[128,2048]{1,0:T(8,128)(2,1)S(1)}, bf16[128,2048]{1,0:T(8,128)(2,1)}, u32[]{:S(2)}) copy-start(bf16[128,2048]{1,0:T(8,128)(2,1)} %get-tuple-element.85) | copy-start | bytes 1572868
  484.9 6.7 %copy-start.7 = (bf16[128,2048]{1,0:T(8,128)(2,1)S(1)}, bf16[128,2048]{1,0:T(8,128)(2,1)}, u32[]{:S(2)}) copy-start(bf16[128,2048]{1,0:T(8,128)(2,1)} %get-tuple-element.84) | copy-start | bytes 1572868
  493.1 109.9 %copy-start.3 = (f32[4000,128]{1,0:T(8,128)S(1)}, f32[4000,128]{1,0:T(8,128)}, u32[]{:S(2)}) copy-start(f32[4000,128]{1,0:T(8,128)} %param.28) | copy-start | bytes 6144004
Sparse Core Ops, SparseCore 0:
  205.4 134.1 all-gather.1

commit v8 on v7

--- a/solution.py
+++ b/solution.py
@@ -675,11 +675,19 @@
     ):
         post = Post(sem, 60)
         me = fsdp_me()
-        load = pltpu.make_async_copy(head_hbm, hd.at[pl.ds(0, vocab)], lsem)
-        load.start()
+        last = (tiles - 1) * 512
+
+        def load(n):
+            at = pl.ds(pl.multiple_of(n * 512, 512), 512)
+            return pltpu.make_async_copy(head_hbm.at[at], hd.at[at], lsem.at[n])
+
+        rest = pl.ds(last, vocab - last)
+        load_last = pltpu.make_async_copy(head_hbm.at[rest], hd.at[rest], lsem.at[tiles - 1])
+        for n in range(tiles - 1):
+            load(n).start()
+        load_last.start()
         greet_devices(fsdp_peers())
         hd[vocab:, :] = jnp.zeros((padded - vocab, width), jnp.bfloat16)
-        load.wait()
         target_at = target_ref[...]
 
         def logits(n, carry):
@@ -693,9 +701,16 @@
             hit = jnp.where(column == target_at, tile, 0.0)
             return top, picked + jnp.sum(hit, axis=1, keepdims=True)
 
+        def loaded(n, carry):
+            load(n).wait()
+            return logits(n, carry)
+
         top, picked = lax.fori_loop(
-            0, tiles, logits, (jnp.full((512, 1), -1e30, jnp.float32), jnp.zeros((512, 1), jnp.float32))
+            0, tiles - 1, loaded,
+            (jnp.full((512, 1), -1e30, jnp.float32), jnp.zeros((512, 1), jnp.float32)),
         )
+        load_last.wait()
+        top, picked = logits(tiles - 1, (top, picked))
 
         def exponents(n, total):
             at = pl.ds(pl.multiple_of(n * 512, 512), 512)
@@ -775,7 +790,7 @@
             pltpu.VMEM((8, 512), jnp.float32),
             pltpu.VMEM((7, 8, 512), jnp.float32),
             DMA((60,)),
-            DMA,
+            DMA((tiles,)),
         ],
         collective_id,
         "head_step",

time: 627 us -> 623 us (level)
  no operation moved by 1% of the time
where the time goes in v8:
time: 623 us; the launch traced here: 613 us
  Pallas kernels  522 us (84%)
  local copies, waits for them, and re-layouts  24 us (4%)
  matrix products  23.3 us (4%)
  other arithmetic  22.8 us (4%)
  between operations  15.1 us (2%)
    pallas_call x1, Pallas kernels, gather_weights(): remote_call(body, out_shape, [ANY] * 4 + [VMEM, ANY], [ANY] * 6, [pltpu.V...  190 us
    pallas_call x1, Pallas kernels, token_gradients(): remote_call(body, [jax.ShapeDtypeStruct((vocab, width), jnp.float32), jax...  90.9 us
    pallas_call x1, Pallas kernels, head_step(): remote_call(body, [jax.ShapeDtypeStruct((64, width), jnp.float32), jax.Sh...  59.8 us
    pallas_call x1, Pallas kernels, attention_block(): remote_call(body, [shape(rows_n, 2048, dtype=jnp.float32), shape(rows_n,...  56.3 us
    pallas_call x1, Pallas kernels, feed_forward(): remote_call(body, total, [VMEM] + [ANY] * (2 * parts_n + 1), VMEM, scratc...  40.4 us
    pallas_call x1, Pallas kernels, feed_forward(): remote_call(body, [total, products], [VMEM] + [ANY] * (2 * parts_n), [VME...  32.4 us
    pallas_call x1, Pallas kernels, chosen_rows(): remote_call(body, jax.ShapeDtypeStruct((FSDP_N, *chosen.shape), chosen.dt...  22.3 us
    dot_general x4, matrix products, nt(): lax.dot_general(left, right, (((1,), (1,)), ((), ())), preferred_element_...  14.4 us
  transfers between devices with their start and end apart: 1, of which 1 were waited for; matrix products, arithmetic and copies ran while one was open for 3% of the time, Pallas kernels for 18%

profile of v8, /device:TPU:1, one launch (start us, length us, event | category | flops | bytes accessed | tf_op | source)
XLA Modules:
  0.0 612.8 jit_solution(4072498834117878648)
XLA Ops:
  9.7 2.6 convert_element_type.100.refs_2_
  15.0 190.3 %gather_weights.1 = (bf16[2,4,2,4,2,16,4608]{6,5,4,3,2,1,0:T(8,128)(2,1)}, f32[2,4,2,4,2,8,128]{6,5,4,3,2,1,0:T(8,128)}, bf16[8,4000,128]{2,1,0:T(8,128)(2,1)}, ...) custom-call(bf16[16,4608]{1,0:T(8,128)(2,1)} %pad_maximum_fusion.3.ref, ...), custom_call_target="tpu_custom_call" | custom-call | tf_op jit(solution)/shard_map/gather_weights/pallas_call | solution.py:470
  205.3 1.1 copy.144
  214.8 56.3 %attention_block.1 = (f32[128,2048]{1,0:T(8,128)}, bf16[128,2048]{1,0:T(8,128)(2,1)}, bf16[128,24]{1,0:T(8,128)(2,1)}, bf16[128,2048]{1,0:T(8,128)(2,1)}, bf16[2...) custom-call(bf16[8,4000,128]{2,1,0:T(8,128)(2,1)} %get-tuple-element, ...), custom_call_target="tpu_custom_call" | custom-call | tf_op jit(solution)/shard_map/attention_block/pallas_call | solution.py:617
  271.1 32.4 %feed_forward.1 = (f32[128,2048]{1,0:T(8,128)}, f32[512,3072]{1,0:T(8,128)}) custom-call(bf16[128,2048]{1,0:T(8,128)(2,1)} %get-tuple-element.69.refs_0_, bf16[2048,3072]{1,0:T(8,128)(2,1)} %bitcast.64, bf16[1536,2048]{1,0:T(8,128)(2,1)} %bitcast.66), custom_call_target="tpu_custom_call" | custom-call | tf_op jit(solution)/shard_map/feed_forward/pallas_call | solution.py:1172
  303.5 1.5 multiply_reduce_fusion.8
  306.1 22.3 %chosen_rows.1 = bf16[8,64,2048]{2,1,0:T(8,128)(2,1)} custom-call(bf16[64,2048]{1,0:T(8,128)(2,1)} %convolution_convert_fusion.src), custom_call_target="tpu_custom_call" | custom-call | tf_op jit(solution)/shard_map/chosen_rows/pallas_call | solution.py:660
  333.6 1.4 broadcast_divide_fusion.scaled_ref
  334.9 5.1 all-gather.2.cloned.1.call-done.head_hbm
  340.0 59.8 %head_step.1 = (f32[64,2048]{1,0:T(8,128)}, f32[8,128]{1,0:T(8,128)}) custom-call(bf16[512,2048]{1,0:T(8,128)(2,1)} %bitcast.71, bf16[4000,2048]{1,0:T(8,128)(2,1)} %all-gather.2.cloned.1.call-done.head_hbm, s32[512,1]{1,0:T(8,128)} %compare_select_fusion.target_ref, f32[512,1]{1,0:T(8,128)} %copy-done.4, f32[512,1]{1,0:T(8,128)} %broadcast_divide_fusion.scaled_ref), custom_call_target="tpu_custom_call" | custom-call | tf_op jit(solution)/shard_map/head_step/pallas_call | solution.py:776
  399.9 2.0 multiply_reduce_fusion
  403.0 40.4 %feed_forward_back.1 = f32[128,2048]{1,0:T(8,128)} custom-call(bf16[128,2048]{1,0:T(8,128)(2,1)} %fusion.37.refs_0_, bf16[2048,3072]{1,0:T(8,128)(2,1)} %bitcast.65, bf16[1536,2048]{1,0:T(8,128)(2,1)} %bitcast.67, f32[512,3072]{1,0:T(8,128)} %get-tuple-element.77.refs_3_), custom_call_target="tpu_custom_call" | custom-call | tf_op jit(solution)/shard_map/feed_forward_back/pallas_call | solution.py:1176
  443.4 1.6 multiply_reduce_fusion.1
  445.8 6.3 %fusion.2 = f32[128,2048]{1,0:T(8,128)S(1)} fusion(bf16[2048,4608]{1,0:T(8,128)(2,1)} %bitcast.69, f32[128,2048]{1,0:T(8,128)S(1)} %subtract_add_fusion), kind=kOutput, calls=%fused_computation.2 | convolution fusion | flops 1074003968 | bytes 10485760 | tf_op jit(solution)/shard_map/dot_general | solution.py:1252
  452.1 1.3 fusion.4.g_ref
  453.4 11.1 %attend_back.1 = (bf16[128,2048]{1,0:T(8,128)(2,1)}, bf16[2,256,512]{2,1,0:T(8,128)(2,1)}, f32[2,64,512]{2,1,0:T(8,128)}) custom-call(s32[1]{0:T(128)} %bitcast.22.start_ref, s32[4]{0:T(128)} %shift_ref.3, bf16[128,2048]{1,0:T(8,128)(2,1)} %get-tuple-element.79.q_ref, bf16[2,320,512]{2,1,0:T(8,128)(2,1)} %get-tuple-element.80.kv_ref, ...), custom_call_target="tpu_custom_call" | custom-call | tf_op jit(solution)/shard_map/attend_back/pallas_call | solution.py:1295
  464.5 11.0 %key_value_back.1 = bf16[128,512]{1,0:T(8,128)(2,1)} custom-call(bf16[2,256,512]{2,1,0:T(8,128)(2,1)} %get-tuple-element.82.far_ref, f32[2,64,512]{2,1,0:T(8,128)} %get-tuple-element.83.own_ref, f32[64,512]{1,0:T(8,128)} %copy.112.cos_ref, f32[64,512]{1,0:T(8,128)} %tile.21.sin_ref), custom_call_target="tpu_custom_call" | custom-call | tf_op jit(solution)/shard_map/key_value_back/pallas_call | solution.py:1220
  475.5 1.1 fusion.20
  477.7 1.3 fusion.24
  479.0 1.4 fusion.11
  480.5 6.5 %fusion = f32[128,2048]{1,0:T(8,128)S(1)} fusion(bf16[2048,4608]{1,0:T(8,128)(2,1)} %bitcast.70, bf16[128,512]{1,0:T(8,128)(2,1)S(1)} %copy-done.9, bf16[128,2048]{1,0:T(8,128)(2,1)S(1)} %copy-done.6), kind=kOutput, calls=%fused_computation | convolution fusion | flops 1343488000 | bytes 12189696 | tf_op jit(solution)/shard_map/dot_general | solution.py:1252
  488.9 1.1 add_convert_fusion.src
  490.0 2.0 concatenate.33.left_ref
  492.0 90.9 %token_gradients.1 = (f32[4000,128]{1,0:T(8,128)}, f32[40,128]{1,0:T(8,128)}, f32[8,384]{1,0:T(8,128)}, f32[8,128]{1,0:T(8,128)}) custom-call(bf16[128,2048]{1,0:T(8,128)(2,1)} %add_convert_fusion.src, f32[40,2048]{1,0:T(8,128)} %concatenate.33.left_ref, f32[8,4608]{1,0:T(8,128)} %pad_maximum_fusion.4.right_ref, s32[16,1024]{1,0:T(8,128)} %sub.57.ids_ref, ...), custom_call_target="tpu_custom_call" | custom-call | tf_op jit(solution)/shard_map/token_gradients/pallas_call | solution.py:957
  582.9 1.3 slice.88
  584.2 1.4 constant_dynamic-slice_fusion.r_ref
  585.5 1.4 constant_dynamic-slice_fusion.1.l_ref
  587.0 7.9 %small_updates.1 = (f32[8,128]{1,0:T(8,128)}, f32[32,16]{1,0:T(8,128)}, f32[8,36]{1,0:T(8,128)}, f32[3,16]{1,0:T(4,128)}, f32[3,16]{1,0:T(4,128)}, /*index=5*/f3...) custom-call(f32[8,128]{1,0:T(8,128)} %get-tuple-element.89.t_ref, ...), custom_call_target="tpu_custom_call" | custom-call | tf_op jit(solution)/shard_map/small_updates/pallas_call | solution.py:1409
  594.8 1.3 fusion.40
  596.2 1.4 copy.133
  597.5 1.4 copy.134
  598.9 6.6 %fusion.10 = (f32[4000,128]{1,0:T(8,128)}, f32[4000,128]{1,0:T(8,128)}, f32[4000,128]{1,0:T(8,128)}) fusion(f32[4000,128]{1,0:T(8,128)S(1)} %copy-done.3, f32[4000,128]{1,0:T(8,128)} %param.29, f32[4000,128]{1,0:T(8,128)} %param.30, f32[4000,128]{1,0:T(8,128)} %get-tuple-element.93, f32[]{:T(128)} %bitcast.30), kind=kLoop, calls=%fused_computation.16 | loop fusion | flops 7680000 | bytes 14336004 | tf_op jit(solution)/shard_map/sub | solution.py:1451
  (141 shorter events, 24.3 us)
Async XLA Ops:
  7.2 5.2 copy-start.12
  7.2 5.9 copy-start.15
  7.2 5.9 copy-start.16
  7.2 6.5 %copy-start.20 = (s32[2,8,64]{2,1,0:T(8,128)S(1)}, s32[2,8,64]{2,1,0:T(8,128)}, u32[]{:S(2)}) copy-start(s32[2,8,64]{2,1,0:T(8,128)} %param.22) | copy-start | bytes 12292
  7.2 332.8 %all-gather.2.cloned.1.call-start = ((), (), s32[]{:S(2)}) async-start(), calls=%async_computation | async-start | bytes 17408000 | tf_op jit(solution)/shard_map/all_gather | solution.py:1506
  8.1 197.2 %copy-start.13 = (f32[32,16]{1,0:T(8,128)}, f32[32,16]{1,0:T(8,128)S(1)}, u32[]{:S(2)}) copy-start(f32[32,16]{1,0:T(8,128)S(1)} %copy.104.a_ref) | copy-start | bytes 6148
  206.5 2.9 copy-start.14
  206.5 3.8 copy-start.8
  207.3 6.4 %copy-start.18 = (s32[2,8,512]{2,1,0:T(8,128)S(1)}, s32[2,8,512]{2,1,0:T(8,128)}, u32[]{:S(2)}) copy-start(s32[2,8,512]{2,1,0:T(8,128)} %param.24) | copy-start | bytes 98308
  209.5 5.3 copy-start.17
  271.1 32.4 %copy-start.2 = (f32[128,2048]{1,0:T(8,128)S(1)}, f32[128,2048]{1,0:T(8,128)}, u32[]{:S(2)}) copy-start(f32[128,2048]{1,0:T(8,128)} %get-tuple-element.68) | copy-start | bytes 3145732
  303.5 1.5 copy-start.11
  305.0 23.5 %copy-start.22 = (s32[2,8]{1,0:T(2,128)S(1)}, s32[2,8]{1,0:T(2,128)}, u32[]{:S(2)}) copy-start(s32[2,8]{1,0:T(2,128)} %param.26) | copy-start | bytes 196
  306.1 24.4 %copy-start.21 = (s32[2,8,32]{2,1,0:T(8,128)S(1)}, s32[2,8,32]{2,1,0:T(8,128)}, u32[]{:S(2)}) copy-start(s32[2,8,32]{2,1,0:T(8,128)} %param.23) | copy-start | bytes 6148
  330.5 9.6 %copy-start.4 = (f32[512,1]{1,0:T(8,128)}, f32[512,1]{1,0:T(8,128)S(1)}, u32[]{:S(2)}) copy-start(f32[512,1]{1,0:T(8,128)S(1)} %reshape_reshape.4.weight_ref) | copy-start | bytes 6148
  403.0 40.4 %copy-start = (f32[128,2048]{1,0:T(8,128)S(1)}, f32[128,2048]{1,0:T(8,128)}, u32[]{:S(2)}) copy-start(f32[128,2048]{1,0:T(8,128)} %get-tuple-element.78) | copy-start | bytes 3145732
  443.4 1.7 copy-start.1
  453.4 22.1 %copy-start.10 = (bf16[128,24]{1,0:T(8,128)(2,1)S(1)}, bf16[128,24]{1,0:T(8,128)(2,1)}, u32[]{:S(2)}) copy-start(bf16[128,24]{1,0:T(8,128)(2,1)} %get-tuple-element.86) | copy-start | bytes 18436
  464.5 16.0 %copy-start.6 = (bf16[128,2048]{1,0:T(8,128)(2,1)S(1)}, bf16[128,2048]{1,0:T(8,128)(2,1)}, u32[]{:S(2)}) copy-start(bf16[128,2048]{1,0:T(8,128)(2,1)} %get-tuple-element.81) | copy-start | bytes 1572868
  475.5 5.0 copy-start.9
  480.5 6.5 %copy-start.19 = (bf16[128,8]{1,0:T(8,128)(2,1)S(1)}, bf16[128,8]{1,0:T(8,128)(2,1)}, u32[]{:S(2)}) copy-start(bf16[128,8]{1,0:T(8,128)(2,1)} %get-tuple-element.87) | copy-start | bytes 6148
  480.5 6.7 %copy-start.5 = (bf16[128,2048]{1,0:T(8,128)(2,1)S(1)}, bf16[128,2048]{1,0:T(8,128)(2,1)}, u32[]{:S(2)}) copy-start(bf16[128,2048]{1,0:T(8,128)(2,1)} %get-tuple-element.85) | copy-start | bytes 1572868
  480.5 6.9 %copy-start.7 = (bf16[128,2048]{1,0:T(8,128)(2,1)S(1)}, bf16[128,2048]{1,0:T(8,128)(2,1)}, u32[]{:S(2)}) copy-start(bf16[128,2048]{1,0:T(8,128)(2,1)} %get-tuple-element.84) | copy-start | bytes 1572868
  488.9 110.0 %copy-start.3 = (f32[4000,128]{1,0:T(8,128)S(1)}, f32[4000,128]{1,0:T(8,128)}, u32[]{:S(2)}) copy-start(f32[4000,128]{1,0:T(8,128)} %param.28) | copy-start | bytes 6144004
Sparse Core Ops, SparseCore 0:
  205.4 134.5 all-gather.1
